TPU v7x, 128 devices: a whole 4x4x4 slice. The times are simulated.
128 devices in a mesh: march: 32 (over x, y, core), cross: 4 (over z).
Axes of the slice: x: 4, y: 4, z: 4, core: 2. Of those that a mesh axis runs over, the one named last changes fastest.
Arguments:
- velocity_guess: float32 [128, 512, 512], P('march', 'cross'), may hold values from -6 to 6
- damping: float32 [128, 512, 512], P('march', 'cross'), may hold values from 0.001 to 0.5
- inflow: float32 [512, 512], P('cross'), may hold values from -6 to 6
- disc_rows: int32 [256], replicated, may hold values from 0 to 511, as said below
- owner: int32 [256], replicated, may hold values from 0 to 31, as said below
- blade: bfloat16 [32, 512, 512], P('march', None, 'cross'), may hold values from -0.25 to 0.25
Outputs:
- velocity: float32 [128, 512, 512], P('march', 'cross')
- pressure: float32 [128, 512, 512], P('march', 'cross')
Inputs may be any that keep to these rules, and one draw needn't show every extreme that they name: `disc_rows`: the 256 disc rows are distinct. Every owner owns at least one disc row.
All inputs are finite; a program needn't handle non-finite values.
Results may differ from a plain program's by a relative error of at most 0.001.
Values may be sent and summed in bfloat16 or wider, within the bound.
No kernel may reach another device: no remote copies, remote signals or barrier semaphores. Data moves between devices by JAX's collectives and lax.ppermute only.
A program may use at most 128 MiB of HBM per device.

v0:
```python
import jax
import jax.numpy as jnp
from jax import lax
from jax.sharding import PartitionSpec as P

SWEEPS = 2


SOURCE_GAIN = 0.04
SCREENING = 0.001
VISCOSITY = 0.1
DRAG_RATE = 0.01


def passed_along(value, axis, steps):
    count = lax.axis_size(axis)
    initial, last = (max(0, -steps), min(count, count - steps))
    return lax.ppermute(value, axis, [(source, source + steps) for source in range(initial, last)])


def extended(block, sides, width):
    for axis, dim in sides:
        count = lax.axis_size(axis)
        forward = [(i, i + 1) for i in range(count - 1)]
        backward = [(target, source) for source, target in forward]
        low = lax.ppermute(
            lax.slice_in_dim(block, block.shape[dim] - width, None, axis=dim), axis, forward
        )
        high = lax.ppermute(lax.slice_in_dim(block, 0, width, axis=dim), axis, backward)
        block = jnp.concatenate([low, block, high], axis=dim)
    return block


def broadcast(shard, axis, root):
    mine = lax.axis_index(axis) == root
    return lax.psum(jnp.where(mine, shard, jnp.zeros_like(shard)), axis)


def sine_table(length):
    ordinal = jnp.arange(length, dtype=jnp.int32) + 1
    product = ordinal[:, None] * ordinal[None, :] % (2 * (length + 1))
    return jnp.sqrt(2.0 / (length + 1)) * jnp.sin(
        jnp.pi * product.astype(jnp.float32) / (length + 1)
    )


def eigen_values(length):
    ordinal = jnp.arange(length, dtype=jnp.int32) + 1
    return 2.0 - 2.0 * jnp.cos(jnp.pi * ordinal.astype(jnp.float32) / (length + 1))


def local(velocity_guess, damping, inflow, disc_rows, owner, blade):
    highest = lax.Precision.HIGHEST
    stations, rows, width = velocity_guess.shape
    march_size = lax.axis_size("march")
    cross_size = lax.axis_size("cross")
    march_index = lax.axis_index("march")
    cross_index = lax.axis_index("cross")
    block_cols = width // cross_size
    disc_global = stations * march_size // 2
    disc_owner = disc_global // stations
    disc_local = disc_global % stations
    transform = sine_table(width)
    spectrum = eigen_values(width)
    column_values = lax.dynamic_slice_in_dim(spectrum, cross_index * block_cols, block_cols)
    divisor = SCREENING + spectrum[:, None] + column_values[None, :]
    row_ids = cross_index * rows + jnp.arange(rows, dtype=jnp.int32)
    selector = (disc_rows[:, None] == row_ids[None, :]).astype(jnp.float32)
    owned = (owner == march_index).astype(jnp.float32)[:, None]
    at_disc = (march_index == disc_owner).astype(jnp.float32)
    first_slab = march_index == 0
    current = velocity_guess
    pressure = jnp.zeros_like(velocity_guess)
    for sweep_index in range(SWEEPS):
        upstream = passed_along(current[-1], "march", 1)
        upstream = jnp.where(first_slab, inflow, upstream)
        shifted = jnp.concatenate([upstream[None], current[:-1]], axis=0)
        source = SOURCE_GAIN * (current - shifted)
        spectral = jnp.einsum("sjk,kl->sjl", source, transform, precision=highest)
        solved = (
            jnp.einsum(
                "ij,sjl->sil",
                transform,
                lax.all_to_all(spectral, "cross", split_axis=2, concat_axis=1, tiled=True),
                precision=highest,
            )
            / divisor
        )
        solved = jnp.einsum("ij,sjl->sil", transform, solved, precision=highest)
        spectral = lax.all_to_all(solved, "cross", split_axis=1, concat_axis=2, tiled=True)
        pressure = jnp.einsum("sjk,kl->sjl", spectral, transform, precision=highest)
        following = passed_along(pressure[0], "march", -1)
        gradient = jnp.concatenate([pressure[1:], following[None]], axis=0) - pressure
        padded = extended(current, (("cross", 1),), 1)
        padded = jnp.pad(padded, ((0, 0), (0, 0), (1, 1)))
        laplace = (
            padded[:, 2:, 1:-1]
            + padded[:, :-2, 1:-1]
            + padded[:, 1:-1, 2:]
            + padded[:, 1:-1, :-2]
            - 4.0 * current
        )
        picked = jnp.dot(
            selector, current[disc_local], precision=highest, preferred_element_type=jnp.float32
        ).astype(jnp.bfloat16)
        slab_rows = broadcast(picked, "march", disc_owner)
        row_blocks = lax.all_gather(slab_rows[None], "cross", axis=0, tiled=True)
        disc_velocity = jnp.sum(row_blocks.astype(jnp.float32), axis=0).astype(jnp.bfloat16)
        response = (
            jnp.tanh(jnp.dot(disc_velocity, blade[0], preferred_element_type=jnp.float32)) * owned
        )
        placed = lax.dynamic_update_slice(
            jnp.zeros((response.shape[0], width), jnp.float32),
            response,
            (0, cross_index * block_cols),
        )
        forces = lax.psum(placed, ("march", "cross"))
        force_plane = (
            jnp.dot(selector.T, forces, precision=highest, preferred_element_type=jnp.float32)
            * at_disc
        )
        forcing = jnp.zeros_like(current).at[disc_local].set(force_plane)
        decay = 1.0 - (damping + DRAG_RATE * jnp.abs(current))
        increment = VISCOSITY * laplace - gradient + forcing

        def compose(carried, scanned):
            decay_k, term_k = scanned
            return ((decay_k * carried[0], decay_k * carried[1] + term_k), None)

        (scale, offset), _ = lax.scan(
            compose, (jnp.ones_like(inflow), jnp.zeros_like(inflow)), (decay, increment)
        )

        def relay_step(unused, incoming):
            outgoing = scale * incoming + offset
            arrived = passed_along(outgoing, "march", 1)
            return jnp.where(first_slab, inflow, arrived)

        incoming = lax.fori_loop(0, march_size - 1, relay_step, inflow)

        def advance(state_plane, scanned):
            decay_k, term_k = scanned
            state_plane = decay_k * state_plane + term_k
            return (state_plane, state_plane)

        _, current = lax.scan(advance, incoming, (decay, increment))
    return (current, pressure)


def solution(mesh):
    in_specs = (
        P("march", "cross", None),
        P("march", "cross", None),
        P("cross", None),
        P(),
        P(),
        P("march", None, "cross"),
    )
    out_specs = (P("march", "cross", None), P("march", "cross", None))
    return jax.shard_map(local, mesh=mesh, in_specs=in_specs, out_specs=out_specs, check_vma=False)
```

profile of v0, /device:TPU:2, one launch (start us, length us, event | category | flops | bytes accessed | tf_op | source)
XLA Modules:
  0.0 1310.4 jit_solution(8215345266207167384)
XLA Ops:
  32.6 103.3 %all-reduce.7.cloned.1.call-done = bf16[1,256,512]{2,1,0:T(8,128)(2,1)} async-done(((bf16[1,256,512]{2,1,0:T(8,128)(2,1)}), bf16[1,256,512]{2,1,0:T(8,128)(2,1)}) %all-reduce.7.cloned.1.call-update) | async-done | bytes 262160 | tf_op jit(solution)/shard_map/psum | solution.py:36
  164.5 9.2 all-to-all-done.1
  200.3 138.5 %all-reduce.9.cloned.1.call-done = f32[256,512]{1,0:T(8,128)} async-done(((f32[256,512]{1,0:T(8,128)}), f32[256,512]{1,0:T(8,128)}) %all-reduce.9.cloned.1.call-update) | async-done | bytes 524304 | tf_op jit(solution)/shard_map/psum | solution.py:117
  344.9 307.5 %while.72 = (s32[]{:T(128)}, f32[128,512]{1,0:T(8,128)S(1)}, pred[]{:T(512)}, f32[128,512]{1,0:T(8,128)S(1)}, f32[128,512]{1,0:T(8,128)S(1)}, /*index=5*/f32[128,512]{1,0:T(8,128)S(1)}, s32[]{:T(128)}) while((s32[]{:T(128)}, f32[128,512]{1,0:T(8,128)S(1)}, pred[]{:T(512)}, f32[128,512]{1,0:T(8,128)S(1)}, f32[128,512]{1,0:T(8,128)S(1)}, ...), condition=%wide.region_6.7_spmd, body=%wide.region_5.6_spmd.sunk | while | flops 196610 | bytes 2883702 | solution.py:139
  346.9 7.9 collective-permute-done
  356.9 7.9 collective-permute-done
  366.8 7.9 collective-permute-done
  376.7 7.9 collective-permute-done
  386.6 7.9 collective-permute-done
  396.5 7.9 collective-permute-done
  406.5 7.9 collective-permute-done
  416.4 7.9 collective-permute-done
  426.3 7.9 collective-permute-done
  436.2 7.9 collective-permute-done
  446.1 7.9 collective-permute-done
  456.1 7.9 collective-permute-done
  466.0 7.9 collective-permute-done
  475.9 7.9 collective-permute-done
  485.8 7.9 collective-permute-done
  495.7 7.9 collective-permute-done
  505.7 7.9 collective-permute-done
  515.6 7.9 collective-permute-done
  525.5 7.9 collective-permute-done
  535.4 7.9 collective-permute-done
  545.3 7.9 collective-permute-done
  555.2 7.9 collective-permute-done
  565.2 7.9 collective-permute-done
  575.1 7.9 collective-permute-done
  585.0 7.9 collective-permute-done
  594.9 7.9 collective-permute-done
  604.8 7.9 collective-permute-done
  614.8 7.9 collective-permute-done
  624.7 7.9 collective-permute-done
  644.5 7.9 collective-permute-done
  679.5 102.2 %all-reduce.11.cloned.1.call-done = bf16[1,256,512]{2,1,0:T(8,128)(2,1)} async-done(((bf16[1,256,512]{2,1,0:T(8,128)(2,1)}), bf16[1,256,512]{2,1,0:T(8,128)(2,1)}) %all-reduce.11.cloned.1.call-update) | async-done | bytes 262160 | tf_op jit(solution)/shard_map/psum | solution.py:36
  782.2 8.3 fusion.1
  808.2 10.0 all-to-all-done.3
  843.6 140.0 %all-reduce.13.cloned.1.call-done = f32[256,512]{1,0:T(8,128)} async-done(((f32[256,512]{1,0:T(8,128)}), f32[256,512]{1,0:T(8,128)}) %all-reduce.13.cloned.1.call-update) | async-done | bytes 524304 | tf_op jit(solution)/shard_map/psum | solution.py:117
  989.8 307.5 %while.74 = (s32[]{:T(128)}, f32[128,512]{1,0:T(8,128)S(1)}, pred[]{:T(512)}, f32[128,512]{1,0:T(8,128)S(1)}, f32[128,512]{1,0:T(8,128)S(1)}, /*index=5*/f32[128,512]{1,0:T(8,128)S(1)}, s32[]{:T(128)}) while((s32[]{:T(128)}, f32[128,512]{1,0:T(8,128)S(1)}, pred[]{:T(512)}, f32[128,512]{1,0:T(8,128)S(1)}, f32[128,512]{1,0:T(8,128)S(1)}, ...), condition=%wide.region_15.16_spmd, body=%wide.region_14.15_spmd.sunk | while | flops 196610 | bytes 2883702 | solution.py:139
  991.8 7.9 collective-permute-done.1
  1041.4 7.9 collective-permute-done.1
  1071.1 7.9 collective-permute-done.1
  1100.9 7.9 collective-permute-done.1
  1150.5 7.9 collective-permute-done.1
  1180.2 7.9 collective-permute-done.1
  1229.8 7.9 collective-permute-done.1
  1259.6 7.9 collective-permute-done.1
  1289.3 7.9 collective-permute-done.1
  (373 shorter events, 492.9 us)
Async XLA Ops:
  8.3 9.8 collective-permute-start.4
  25.5 110.5 %all-to-all-start = ((f32[4,128,512]{1,0,2:T(4,128)}), f32[4,128,512]{1,0,2:T(4,128)S(1)}, u32[]{:S(2)}, u32[]{:S(2)}) async-start(f32[4,128,512]{1,0,2:T(4,128)} %copy.22), calls=%async_computation | async-start | bytes 2097152 | tf_op jit(solution)/shard_map/all_to_all | solution.py:84
  30.9 105.0 %all-reduce.7.cloned.1.call-start = ((), (), s32[]{:S(2)}) async-start(), calls=%async_computation.4 | async-start | bytes 524288 | tf_op jit(solution)/shard_map/psum | solution.py:36
  32.1 160.1 %all-gather.3.cloned.1.call-start = ((), (), s32[]{:S(2)}) async-start(), calls=%async_computation.5 | async-start | bytes 1310720 | tf_op jit(solution)/shard_map/all_gather | solution.py:107
  153.5 20.2 %all-to-all-start.1 = ((f32[4,512,128]{2,0,1:T(4,128)}), f32[4,512,128]{2,0,1:T(4,128)}, u32[]{:S(2)}, u32[]{:S(2)}) async-start(f32[4,512,128]{2,0,1:T(4,128)} %copy.26), calls=%async_computation.1 | async-start | bytes 2097152 | tf_op jit(solution)/shard_map/all_to_all | solution.py:90
  158.0 180.8 %all-reduce.9.cloned.1.call-start = ((), (), s32[]{:S(2)}) async-start(), calls=%async_computation.6 | async-start | bytes 1048576 | tf_op jit(solution)/shard_map/psum | solution.py:117
  158.0 32.5 %collective-permute-start.2 = (f32[4,1,512]{2,1,0:T(1,128)S(1)}, f32[4,1,512]{2,1,0:T(1,128)S(1)}, u32[]{:S(2)}, u32[]{:S(2)}) collective-permute-start(f32[4,1,512]{2,1,0:T(1,128)S(1)} %get-tuple-element.323), channel_id=1, source_target_pairs={{1,0},{2,1},{3,2},{5,4},{6,5},{7,6},{9,8},{10,9},{11,10},{13,12},{... | collective-permute-start | bytes 24584 | tf_op jit(solution)/shard_map/ppermute | solution.py:29
  159.3 31.2 %collective-permute-start.3 = (f32[4,1,512]{2,1,0:T(1,128)S(1)}, f32[4,1,512]{2,1,0:T(1,128)S(1)}, u32[]{:S(2)}, u32[]{:S(2)}) collective-permute-start(f32[4,1,512]{2,1,0:T(1,128)S(1)} %get-tuple-element.322), channel_id=1, source_target_pairs={{0,1},{1,2},{2,3},{4,5},{5,6},{6,7},{8,9},{9,10},{10,11},{12,13},{... | collective-permute-start | bytes 24584 | tf_op jit(solution)/shard_map/ppermute | solution.py:26
  345.0 9.8 collective-permute-start
  354.9 9.8 collective-permute-start
  364.9 9.8 collective-permute-start
  374.8 9.8 collective-permute-start
  384.7 9.8 collective-permute-start
  394.6 9.8 collective-permute-start
  404.5 9.8 collective-permute-start
  414.5 9.8 collective-permute-start
  424.4 9.8 collective-permute-start
  434.3 9.8 collective-permute-start
  444.2 9.8 collective-permute-start
  454.1 9.8 collective-permute-start
  464.0 9.8 collective-permute-start
  474.0 9.8 collective-permute-start
  483.9 9.8 collective-permute-start
  493.8 9.8 collective-permute-start
  533.5 9.8 collective-permute-start
  563.2 9.8 collective-permute-start
  593.0 9.8 collective-permute-start
  612.8 9.8 collective-permute-start
  642.6 9.8 collective-permute-start
  657.3 9.8 collective-permute-start.8
  674.4 107.4 %all-to-all-start.2 = ((f32[4,128,512]{1,0,2:T(4,128)}), f32[4,128,512]{1,0,2:T(4,128)S(1)}, u32[]{:S(2)}, u32[]{:S(2)}) async-start(f32[4,128,512]{1,0,2:T(4,128)} %copy.28), calls=%async_computation.2 | async-start | bytes 2097152 | tf_op jit(solution)/shard_map/all_to_all | solution.py:84
  678.1 103.7 %all-reduce.11.cloned.1.call-start = ((), (), s32[]{:S(2)}) async-start(), calls=%async_computation.7 | async-start | bytes 524288 | tf_op jit(solution)/shard_map/psum | solution.py:36
  679.3 155.7 %all-gather.5.cloned.1.call-start = ((), (), s32[]{:S(2)}) async-start(), calls=%async_computation.8 | async-start | bytes 1310720 | tf_op jit(solution)/shard_map/all_gather | solution.py:107
  797.9 20.3 %all-to-all-start.3 = ((f32[4,512,128]{2,0,1:T(4,128)}), f32[4,512,128]{2,0,1:T(4,128)S(1)}, u32[]{:S(2)}, u32[]{:S(2)}) async-start(f32[4,512,128]{2,0,1:T(4,128)} %copy.32), calls=%async_computation.3 | async-start | bytes 2097152 | tf_op jit(solution)/shard_map/all_to_all | solution.py:90
  802.3 181.3 %all-reduce.13.cloned.1.call-start = ((), (), s32[]{:S(2)}) async-start(), calls=%async_computation.9 | async-start | bytes 1048576 | tf_op jit(solution)/shard_map/psum | solution.py:117
  802.4 30.9 %collective-permute-start.6 = (f32[4,1,512]{2,1,0:T(1,128)S(1)}, f32[4,1,512]{2,1,0:T(1,128)S(1)}, u32[]{:S(2)}, u32[]{:S(2)}) collective-permute-start(f32[4,1,512]{2,1,0:T(1,128)S(1)} %get-tuple-element.319), channel_id=1, source_target_pairs={{1,0},{2,1},{3,2},{5,4},{6,5},{7,6},{9,8},{10,9},{11,10},{13,12},{... | collective-permute-start | bytes 24584 | tf_op jit(solution)/shard_map/ppermute | solution.py:29
  803.7 29.6 %collective-permute-start.7 = (f32[4,1,512]{2,1,0:T(1,128)S(1)}, f32[4,1,512]{2,1,0:T(1,128)S(1)}, u32[]{:S(2)}, u32[]{:S(2)}) collective-permute-start(f32[4,1,512]{2,1,0:T(1,128)S(1)} %get-tuple-element.318), channel_id=1, source_target_pairs={{0,1},{1,2},{2,3},{4,5},{5,6},{6,7},{8,9},{9,10},{10,11},{12,13},{... | collective-permute-start | bytes 24584 | tf_op jit(solution)/shard_map/ppermute | solution.py:26
  989.8 9.8 collective-permute-start.1
  1019.6 9.8 collective-permute-start.1
  1039.4 9.8 collective-permute-start.1
  1069.2 9.8 collective-permute-start.1
  1099.0 9.8 collective-permute-start.1
  1148.6 9.8 collective-permute-start.1
  1178.3 9.8 collective-permute-start.1
  1208.1 9.8 collective-permute-start.1
  1227.9 9.8 collective-permute-start.1
  1257.7 9.8 collective-permute-start.1
  1287.4 9.8 collective-permute-start.1
  (57 other events, 1401.1 us)
Sparse Core Ops, SparseCore 0:
  35.5 100.3 all-reduce.6
  137.7 24.4 all-gather.2
  194.9 143.8 all-reduce.8
  682.4 99.3 all-reduce.10
  783.3 25.4 all-gather.4
  838.9 144.6 all-reduce.12
where the time goes:
time: 1320 us; the launch traced here: 1310 us
  waiting for transfers between devices  1010 us (77%)
  starting transfers between devices  159 us (12%)
  matrix products  61.1 us (5%)
  other arithmetic  40 us (3%)
  local copies, waits for them, and re-layouts  26.1 us (2%)
  between operations  15.2 us (1%)
    ppermute x66, waiting for transfers between devices, passed_along(): lax.ppermute(value, axis, [(source, source + steps) for source in range(i...  504 us
    psum x2, waiting for transfers between devices, local(): forces = lax.psum(placed, ('march', 'cross'))  278 us
    psum x2, waiting for transfers between devices, broadcast(): return lax.psum(jnp.where(mine, shard, jnp.zeros_like(shard)), axis)  205 us
    ppermute x66, starting transfers between devices, passed_along(): lax.ppermute(value, axis, [(source, source + steps) for source in range(i...  128 us
  transfers between devices with their start and end apart: 80, of which 70 were waited for; matrix products, arithmetic and copies ran while one was open for 6% of the time, Pallas kernels for 0%

commit v1 on v0

v1 whole, which is shorter than its diff:
```python
import ml_dtypes
import numpy as np
import jax
import jax.numpy as jnp
from jax import lax
from jax.experimental import pallas as pl
from jax.experimental.pallas import tpu as pltpu
from jax.sharding import PartitionSpec as P

SWEEPS = 2
SOURCE_GAIN = 0.04
SCREENING = 0.001
VISCOSITY = 0.1
DRAG_RATE = 0.01

F32 = jnp.float32
BF16 = jnp.bfloat16
SUB = 8
LANE = 128
PARAMS = pltpu.CompilerParams(vmem_limit_bytes=32 * 1024 * 1024)
VMEM = pl.BlockSpec(memory_space=pltpu.VMEM)
SMEM = pl.BlockSpec(memory_space=pltpu.SMEM)


def tables(length):
    ordinal = np.arange(1, length + 1)
    product = np.outer(ordinal, ordinal) % (2 * (length + 1))
    sine = np.sqrt(2.0 / (length + 1)) * np.sin(np.pi * product / (length + 1))
    high = sine.astype(np.float32).astype(ml_dtypes.bfloat16)
    low = (sine - high.astype(np.float64)).astype(np.float32).astype(ml_dtypes.bfloat16)
    values = 2.0 - 2.0 * np.cos(np.pi * ordinal / (length + 1))
    inverse = 1.0 / (SCREENING + values[:, None] + values[None, :])
    return high, low, inverse.astype(np.float32)


def split(value):
    high = value.astype(BF16)
    return high, (value - high.astype(F32)).astype(BF16)


def groups(rows):
    return [(g, slice(SUB * g, SUB * g + SUB)) for g in range(rows // SUB)]


def to_chunks(ref, g, value):
    for h in range(2):
        for q in range(2):
            at = (2 * h + q) * LANE
            ref[2 * g + h, SUB * q : SUB * q + SUB, :] = value[:, at : at + LANE]


def from_chunks(ref, g):
    parts = []
    for h in range(2):
        for q in range(2):
            parts.append(ref[2 * g + h, SUB * q : SUB * q + SUB, :])
    return jnp.concatenate(parts, axis=1)


def decay_of(value, damping):
    return 1.0 - (damping + DRAG_RATE * jnp.abs(value))


def source_kernel(place, current, upstream, *outs):
    c = place[0]
    stations = current.shape[0]
    for r in range(stations):
        s = lax.rem(c + r, stations)
        before = jnp.maximum(s - 1, 0)
        for _, rows in groups(current.shape[1]):
            previous = jnp.where(s == 0, upstream[rows], current[before, rows])
            outs[r][rows] = SOURCE_GAIN * (current[s, rows] - previous)


def decay_kernel(current, damping, decay, scale):
    for g, rows in groups(current.shape[1]):
        product = None
        for s in range(current.shape[0]):
            d = decay_of(current[s, rows], damping[s, rows])
            decay[s, rows] = d
            product = d if product is None else product * d
        to_chunks(scale, g, product)


def laplace_kernel(current, above, below, term):
    stations, height, width = current.shape
    lane = lax.broadcasted_iota(jnp.int32, (SUB, width), 1)
    for s in range(stations):
        for g, rows in groups(height):
            here = current[s, rows]
            lo, hi = SUB * g, SUB * g + SUB
            if g == 0:
                up = jnp.concatenate([above[s : s + 1], current[s, 0 : SUB - 1]], axis=0)
            else:
                up = current[s, lo - 1 : hi - 1]
            if hi == height:
                down = jnp.concatenate([current[s, lo + 1 : hi], below[s : s + 1]], axis=0)
            else:
                down = current[s, lo + 1 : hi + 1]
            left = jnp.where(lane == 0, 0.0, pltpu.roll(here, 1, 1))
            right = jnp.where(lane == width - 1, 0.0, pltpu.roll(here, width - 1, 1))
            term[s, rows] = VISCOSITY * (up + down + left + right - 4.0 * here)


def solve_kernel(place, x0, x1, x2, x3, high, low, inverse, p0, p1, p2, p3, plane):
    c = place[0]
    inputs, outputs = (x0, x1, x2, x3), (p0, p1, p2, p3)
    count = len(inputs)
    height = x0.shape[0]
    for r, ref in enumerate(inputs):
        b = lax.rem(c - r + count, count)
        plane[pl.ds(pl.multiple_of(b * height, height), height), :] = ref[...]
    sh, sl = high[...], low[...]
    by_left = jnp.concatenate([sh, sh, sl], axis=1)
    by_right = jnp.concatenate([sh, sl, sh], axis=0)

    def right(value):
        vh, vl = split(value)
        return jnp.dot(
            jnp.concatenate([vh, vh, vl], axis=1), by_right, preferred_element_type=F32
        )

    def left(value):
        vh, vl = split(value)
        return jnp.dot(
            by_left, jnp.concatenate([vh, vl, vh], axis=0), preferred_element_type=F32
        )

    modes = left(right(plane[...])) * inverse[...]
    plane[...] = right(left(modes))
    for r, ref in enumerate(outputs):
        b = lax.rem(c + r, count)
        ref[...] = plane[pl.ds(pl.multiple_of(b * height, height), height), :]


def disc_kernel(d0, d1, d2, d3, owners, blade, f0, f1, f2, f3, rows, total):
    step = pl.program_id(0)
    height = d0.shape[0]

    @pl.when(step == 0)
    def _():
        for r, ref in enumerate((d0, d1, d2, d3)):
            rows[height * r : height * (r + 1)] = ref[...]
        total[...] = jnp.zeros_like(total)

    per_step = blade.shape[0]
    for j in range(0, per_step, 2):
        pair = jnp.concatenate([blade[j], blade[j + 1]], axis=1)
        response = jnp.dot(rows[...], pair, preferred_element_type=F32)
        first = step * per_step + j
        kept = jnp.where(owners[...] == first, response[:, :LANE], total[...])
        total[...] = jnp.where(owners[...] == first + 1, response[:, LANE:], kept)

    @pl.when(step == pl.num_programs(0) - 1)
    def _():
        for r, ref in enumerate((f0, f1, f2, f3)):
            ref[...] = jnp.tanh(total[height * r : height * (r + 1)])


def offset_kernel(
    place, p0, p1, p2, p3, f0, f1, f2, f3, decay, term, inflow, pressure, lead, force, offset
):
    c = place[0]
    first = place[1]
    pieces, forces = (p0, p1, p2, p3), (f0, f1, f2, f3)
    count = len(pieces)
    width = inflow.shape[1] // count
    for r in range(count):
        s = lax.rem(c - r + count, count)
        pressure[s] = pieces[r][...]
        b = lax.rem(c + r, count)
        force[:, pl.ds(pl.multiple_of(b * width, width), width)] = forces[r][...]
    for g, rows in groups(inflow.shape[0]):
        start = pressure[0, rows]
        lead[rows] = start
        state = jnp.where(first == 1, inflow[rows] + start, 0.0)
        for s in range(count):
            d = decay[s, rows]
            t = term[s, rows]
            if s == 0:
                t = t + force[rows]
            state = d * state + (t + (1.0 - d) * pressure[s, rows])
        to_chunks(offset, g, state)


def scan_kernel(scale, offset, entering):
    entering[0] = jnp.zeros_like(entering[0])
    state = offset[0]
    for m in range(1, scale.shape[0]):
        entering[m] = state
        state = scale[m] * state + offset[m]


def march_rows(first, g, rows, entering, pressure, following, decay, term, force, inflow):
    stations = decay.shape[0]
    ahead = pressure[0, rows]
    state = jnp.where(first == 1, inflow[rows], from_chunks(entering, g) - ahead)
    states = [state]
    for s in range(stations):
        here = ahead
        ahead = following[rows] if s == stations - 1 else pressure[s + 1, rows]
        t = term[s, rows]
        if s == 0:
            t = t + force[rows]
        state = decay[s, rows] * state + (t - (ahead - here))
        states.append(state)
    return states


def middle_kernel(
    place, entering, pressure, following, decay, term, force, inflow, damping,
    current, decay_new, scale, s0, s1, s2, s3, top, bottom, disc, source,
):
    c = place[0]
    first = place[1]
    stations, height, _ = current.shape
    for g, rows in groups(height):
        states = march_rows(
            first, g, rows, entering, pressure, following, decay, term, force, inflow
        )
        product = None
        for s in range(stations):
            value = states[s + 1]
            current[s, rows] = value
            source[s, rows] = SOURCE_GAIN * (value - states[s])
            d = decay_of(value, damping[s, rows])
            decay_new[s, rows] = d
            product = d if product is None else product * d
            if g == 0:
                top[s : s + 1] = value[0:1]
            if SUB * (g + 1) == height:
                bottom[s : s + 1] = value[SUB - 1 : SUB]
        to_chunks(scale, g, product)
    disc[...] = current[0].astype(BF16)
    for r, ref in enumerate((s0, s1, s2, s3)):
        ref[...] = source[lax.rem(c + r, stations)]


def last_kernel(
    place, entering, pressure, following, decay, term, force, inflow, current
):
    first = place[1]
    for g, rows in groups(current.shape[1]):
        states = march_rows(
            first, g, rows, entering, pressure, following, decay, term, force, inflow
        )
        for s in range(current.shape[0]):
            current[s, rows] = states[s + 1]


def call(kernel, outs, args, scratch=(), cost=None, scalars=0):
    return pl.pallas_call(
        kernel,
        out_shape=[jax.ShapeDtypeStruct(shape, dtype) for shape, dtype in outs],
        in_specs=[SMEM] * scalars + [VMEM] * (len(args) - scalars),
        out_specs=[VMEM] * len(outs),
        scratch_shapes=list(scratch),
        compiler_params=PARAMS,
        cost_estimate=cost,
    )(*args)


def cost(flops, size):
    return pl.CostEstimate(flops=int(flops), bytes_accessed=int(size), transcendentals=0)


def local(velocity_guess, damping, inflow, disc_rows, owner, blade):
    stations, height, width = velocity_guess.shape
    march_size = lax.axis_size("march")
    cross_size = lax.axis_size("cross")
    march_index = lax.axis_index("march")
    cross_index = lax.axis_index("cross")
    disc_slab = stations * march_size // 2 // stations
    at_disc = march_index == disc_slab
    first = (march_index == 0).astype(jnp.int32)
    place = jnp.stack([cross_index.astype(jnp.int32), first])
    high, low, inverse = (jnp.asarray(t) for t in tables(width))

    slab = (stations, height, width)
    plane = (height, width)
    chunks = (march_size, height * width // march_size // LANE, LANE)
    mib = 4 * stations * height * width

    def turn(value, steps):
        return lax.ppermute(
            value, "cross", [(i, (i + steps) % cross_size) for i in range(cross_size)]
        )

    def turn_disc(value, steps):
        base = disc_slab * cross_size
        return lax.ppermute(
            value,
            ("march", "cross"),
            [(base + i, base + (i + steps) % cross_size) for i in range(cross_size)],
        )

    def exchange(blocks):
        return [blocks[0]] + [turn(blocks[r], r) for r in range(1, cross_size)]

    def along(value, axis, steps):
        count = lax.axis_size(axis)
        return lax.ppermute(
            value, axis, [(i, i + steps) for i in range(count) if 0 <= i + steps < count]
        )

    def across_march(value):
        return lax.all_to_all(value, "march", split_axis=0, concat_axis=0, tiled=True)

    turns = jnp.repeat(jnp.arange(cross_size, dtype=jnp.int32), height)
    ids = (cross_index - turns + cross_size) % cross_size * height + jnp.tile(
        jnp.arange(height, dtype=jnp.int32), cross_size
    )
    owners = jnp.max(
        jnp.where(ids[:, None] == disc_rows[None, :], owner[None, :], -1), axis=1
    )
    owners = jnp.where(at_disc, owners, -1)
    owners = jnp.broadcast_to(owners[:, None], (cross_size * height, LANE))
    blades = lax.all_gather(blade, "march", axis=0, tiled=True)

    upstream = along(velocity_guess[-1], "march", 1)
    upstream = jnp.where(first == 1, inflow, upstream)
    current = velocity_guess
    disc = current[0].astype(BF16)
    top, bottom = current[:, 0], current[:, -1]
    decay, scale = call(
        decay_kernel, [(slab, F32), (chunks, F32)], (current, damping), cost=cost(4e6, 3.25 * mib)
    )
    source = call(
        source_kernel,
        [(plane, F32)] * stations,
        (place, current, upstream),
        cost=cost(1e6, 2 * mib),
        scalars=1,
    )
    for sweep_index in range(SWEEPS):
        arrived = exchange(source)
        scales = across_march(scale)
        above = along(bottom, "cross", 1)
        below = along(top, "cross", -1)
        rows = [disc] + [turn_disc(disc, r) for r in range(1, cross_size)]
        (term,) = call(
            laplace_kernel, [(slab, F32)], (current, above, below), cost=cost(4e6, 2 * mib)
        )
        solved = call(
            solve_kernel,
            [(plane, F32)] * cross_size,
            (place, *arrived, high, low, inverse),
            scratch=[pltpu.VMEM((width, width), F32)],
            cost=cost(3 * 8 * width**3, 5 * mib),
            scalars=1,
        )
        piece = (height, LANE)
        per_step = 4
        fixed = lambda shape: pl.BlockSpec(shape, lambda i: (0,) * len(shape))
        forces = pl.pallas_call(
            disc_kernel,
            grid=(march_size // per_step,),
            out_shape=[jax.ShapeDtypeStruct(piece, F32)] * cross_size,
            in_specs=[fixed(plane)] * cross_size
            + [
                fixed(owners.shape),
                pl.BlockSpec((per_step, width, LANE), lambda i: (i, 0, 0)),
            ],
            out_specs=[fixed(piece)] * cross_size,
            scratch_shapes=[
                pltpu.VMEM((width, width), BF16),
                pltpu.VMEM((width, LANE), F32),
            ],
            compiler_params=PARAMS,
            cost_estimate=cost(2 * march_size * width * width * LANE, 5 * mib),
        )(*rows, owners, blades)
        forces = [forces[0]] + [turn_disc(forces[r], -r) for r in range(1, cross_size)]
        pieces = exchange(solved)
        pressure, lead, force, offset = call(
            offset_kernel,
            [(slab, F32), (plane, F32), (plane, F32), (chunks, F32)],
            (place, *pieces, *forces, decay, term, inflow),
            cost=cost(4e6, 5 * mib),
            scalars=1,
        )
        following = along(lead, "march", -1)
        (entering,) = call(
            scan_kernel,
            [(chunks, F32)],
            (scales, across_march(offset)),
            cost=cost(1e5, mib),
        )
        entering = across_march(entering)
        common = (place, entering, pressure, following, decay, term, force, inflow)
        if sweep_index < SWEEPS - 1:
            outs = call(
                middle_kernel,
                [(slab, F32), (slab, F32), (chunks, F32)]
                + [(plane, F32)] * stations
                + [((stations, width), F32)] * 2
                + [(plane, BF16)],
                common + (damping,),
                scratch=[pltpu.VMEM(slab, F32)],
                cost=cost(8e6, 8 * mib),
                scalars=1,
            )
            current, decay, scale = outs[:3]
            source = outs[3 : 3 + stations]
            top, bottom, disc = outs[3 + stations :]
        else:
            (current,) = call(
                last_kernel, [(slab, F32)], common, cost=cost(4e6, 5 * mib), scalars=1
            )
    return (current, pressure)


def solution(mesh):
    in_specs = (
        P("march", "cross", None),
        P("march", "cross", None),
        P("cross", None),
        P(),
        P(),
        P("march", None, "cross"),
    )
    out_specs = (P("march", "cross", None), P("march", "cross", None))
    return jax.shard_map(local, mesh=mesh, in_specs=in_specs, out_specs=out_specs, check_vma=False)
```

time: 1320 us -> 229 us (0.17)
  waiting for transfers between devices: 1010 us -> 37.6 us
  matrix products: 61.1 us -> 0 us
  starting transfers between devices: 159 us -> 117 us
  other arithmetic: 40 us -> 0.38 us
  Pallas kernels: 0 us -> 30 us
    ppermute x70 -> x31, waiting for transfers between devices: 504 us -> 14.6 us  [the longest x12 8.69 us: turn(): lax.ppermute(value, 'cross', [(i, (i + steps) % cross_size) for i in rang...]
    psum x4 -> x0, waiting for transfers between devices: 484 us -> none  [the longest x2 278 us: local(): forces = lax.psum(placed, ('march', 'cross'))]
    ppermute x70 -> x31, starting transfers between devices: 140 us -> 48.7 us  [the longest x12 21.6 us: turn(): lax.ppermute(value, 'cross', [(i, (i + steps) % cross_size) for i in rang...]
    dot_general x14 -> x0, matrix products: 61.1 us -> none  [the longest x2 15.6 us: local(): jnp.einsum('ij,sjl->sil', transform, lax.all_to_all(spectral, 'cross', sp...]
    all_to_all x4 -> x6, starting transfers between devices: 18 us -> 67.9 us  [across_march(): lax.all_to_all(value, 'march', split_axis=0, concat_axis=0, tiled=True)]
    pallas_call x0 -> x14, Pallas kernels: none -> 30 us  [the longest x12 22.5 us: call(): pl.pallas_call(kernel, out_shape=[jax.ShapeDtypeStruct(shape, dtype) for...]
    unnamed x48 -> x72, local copies, waits for them, and re-layouts: 4.1 us -> 23.8 us
  transfers between devices with their start and end apart: 80 -> 38, of which waited for: 70 -> 8; matrix products, arithmetic and copies ran while one was open for 6% -> 1% of each run, Pallas kernels for 0% -> 12%
where the time goes in v1:
time: 229 us; the launch traced here: 225 us
  starting transfers between devices  117 us (51%)
  waiting for transfers between devices  37.6 us (16%)
  Pallas kernels  30 us (13%)
  local copies, waits for them, and re-layouts  25.9 us (11%)
  between operations  14.7 us (6%)
    all_to_all x6, starting transfers between devices, across_march(): lax.all_to_all(value, 'march', split_axis=0, concat_axis=0, tiled=True)  67.9 us
    unnamed x72, local copies, waits for them, and re-layouts  23.8 us
    pallas_call x12, Pallas kernels, call(): pl.pallas_call(kernel, out_shape=[jax.ShapeDtypeStruct(shape, dtype) for...  22.5 us
    all_to_all x6, waiting for transfers between devices, across_march(): lax.all_to_all(value, 'march', split_axis=0, concat_axis=0, tiled=True)  22.3 us
    ppermute x12, starting transfers between devices, turn(): lax.ppermute(value, 'cross', [(i, (i + steps) % cross_size) for i in rang...  21.6 us
    ppermute x7, starting transfers between devices, along(): lax.ppermute(value, axis, [(i, i + steps) for i in range(count) if 0 <= i...  18.9 us
    ppermute x12, waiting for transfers between devices, turn(): lax.ppermute(value, 'cross', [(i, (i + steps) % cross_size) for i in rang...  8.69 us
    ppermute x12, starting transfers between devices, turn_disc(): lax.ppermute(value, ('march', 'cross'), [(base + i, base + (i + steps) %...  8.27 us
  transfers between devices with their start and end apart: 38, of which 8 were waited for; matrix products, arithmetic and copies ran while one was open for 1% of the time, Pallas kernels for 12%

profile of v1, /device:TPU:2, one launch (start us, length us, event | category | flops | bytes accessed | tf_op | source)
XLA Modules:
  0.0 225.3 jit_solution(8708498480325902789)
XLA Ops:
  8.9 1.9 collective-permute-start
  13.2 1.2 copy-done
  14.4 1.2 copy-done.4
  17.5 11.6 %all-to-all-start = ((f32[32,16,128]{2,1,0:T(8,128)}), f32[32,16,128]{2,1,0:T(8,128)}, u32[]{:S(2)}, u32[]{:S(2)}) async-start(f32[32,16,128]{2,1,0:T(8,128)} %get-tuple-element.42), calls=%async_computation | async-start | bytes 524288 | tf_op jit(solution)/shard_map/all_to_all | solution.py:307
  29.2 1.2 copy-done.1
  31.1 1.3 collective-permute-start.1
  32.4 2.4 %collective-permute-start.2 = (f32[128,512]{1,0:T(8,128)S(1)}, f32[128,512]{1,0:T(8,128)S(1)}, u32[]{:S(2)}, u32[]{:S(2)}) collective-permute-start(f32[128,512]{1,0:T(8,128)S(1)} %get-tuple-element.45), channel_id=1, source_target_pairs={{0,2},{1,3},{2,0},{3,1},{4,6},{5,7},{6,4},{7,5},{8,10},{9,11},{10,... | collective-permute-start | bytes 786440 | tf_op jit(solution)/shard_map/ppermute | solution.py:285
  34.8 2.5 %collective-permute-start.3 = (f32[128,512]{1,0:T(8,128)S(1)}, f32[128,512]{1,0:T(8,128)S(1)}, u32[]{:S(2)}, u32[]{:S(2)}) collective-permute-start(f32[128,512]{1,0:T(8,128)S(1)} %get-tuple-element.46), channel_id=1, source_target_pairs={{0,3},{1,0},{2,1},{3,2},{4,7},{5,4},{6,5},{7,6},{8,11},{9,8},{10,9... | collective-permute-start | bytes 786440 | tf_op jit(solution)/shard_map/ppermute | solution.py:285
  37.7 3.1 %collective-permute-done.1.x1 = f32[128,512]{1,0:T(8,128)S(1)} collective-permute-done((f32[128,512]{1,0:T(8,128)S(1)}, f32[128,512]{1,0:T(8,128)S(1)}, u32[]{:S(2)}, u32[]{:S(2)}) %collective-permute-start.1) | collective-permute-done | bytes 262176 | tf_op jit(solution)/shard_map/ppermute | solution.py:285
  41.4 5.5 %collective-permute-done.2.x2 = f32[128,512]{1,0:T(8,128)S(1)} collective-permute-done((f32[128,512]{1,0:T(8,128)S(1)}, f32[128,512]{1,0:T(8,128)S(1)}, u32[]{:S(2)}, u32[]{:S(2)}) %collective-permute-start.2) | collective-permute-done | bytes 262176 | tf_op jit(solution)/shard_map/ppermute | solution.py:285
  47.0 1.8 collective-permute-start.13
  48.8 1.3 copy-done.27
  51.1 1.1 copy-done.31
  52.2 5.1 %shard_map.106 = (f32[128,512]{1,0:T(8,128)S(1)}, f32[128,512]{1,0:T(8,128)S(1)}, f32[128,512]{1,0:T(8,128)}, f32[128,512]{1,0:T(8,128)}) custom-call(s32[2]{0:T(128)S(1)} %pad_add_fusion.place, f32[128,512]{1,0:T(8,128)S(1)} %get-tuple-element.43.x0, f32[128,512]{1,0:T(8,128)S(1)} %collective-permute-done.1.x1, f32[128,512]{1,0:T(8,128)S(1)} %collective-permute-done.2.x2, ...), custom_call_target="tpu_custom_call" | custom-call | flops 3221225472 | bytes 5242880 | tf_op jit(solution)/shard_map/pallas_call | solution.py:252
  58.0 2.5 %collective-permute-start.4 = (f32[128,512]{1,0:T(8,128)S(1)}, f32[128,512]{1,0:T(8,128)S(1)}, u32[]{:S(2)}, u32[]{:S(2)}) collective-permute-start(f32[128,512]{1,0:T(8,128)S(1)} %get-tuple-element.48), channel_id=1, source_target_pairs={{0,1},{1,2},{2,3},{3,0},{4,5},{5,6},{6,7},{7,4},{8,9},{9,10},{10,1... | collective-permute-start | bytes 786440 | tf_op jit(solution)/shard_map/ppermute | solution.py:285
  60.6 1.3 collective-permute-start.14
  61.9 2.9 %collective-permute-start.5 = (f32[128,512]{1,0:T(8,128)}, f32[128,512]{1,0:T(8,128)}, u32[]{:S(2)}, u32[]{:S(2)}) collective-permute-start(f32[128,512]{1,0:T(8,128)} %get-tuple-element.49), channel_id=1, source_target_pairs={{0,2},{1,3},{2,0},{3,1},{4,6},{5,7},{6,4},{7,5},{8,10},{9,11},{10,... | collective-permute-start | bytes 786440 | tf_op jit(solution)/shard_map/ppermute | solution.py:285
  64.8 2.5 %collective-permute-start.6 = (f32[128,512]{1,0:T(8,128)}, f32[128,512]{1,0:T(8,128)}, u32[]{:S(2)}, u32[]{:S(2)}) collective-permute-start(f32[128,512]{1,0:T(8,128)} %get-tuple-element.50), channel_id=1, source_target_pairs={{0,3},{1,0},{2,1},{3,2},{4,7},{5,4},{6,5},{7,6},{8,11},{9,8},{10,9... | collective-permute-start | bytes 786440 | tf_op jit(solution)/shard_map/ppermute | solution.py:285
  67.4 2.2 copy-done.22
  69.6 3.7 %shard_map.107 = (f32[128,128]{1,0:T(8,128)S(1)}, f32[128,128]{1,0:T(8,128)S(1)}, f32[128,128]{1,0:T(8,128)S(1)}, f32[128,128]{1,0:T(8,128)S(1)}) custom-call(bf16[128,512]{1,0:T(8,128)(2,1)S(1)} %fusion.d0, bf16[128,512]{1,0:T(8,128)(2,1)S(1)} %collective-permute-done.7.d1, bf16[128,512]{1,0:T(8,128)(2,1)S(1)} %collective-permute-done.8.d2, ...), custom_call_target="tpu_custom_call" | custom-call | flops 2147483648 | bytes 5242880 | tf_op jit(solution)/shard_map/pallas_call | solution.py:355
  78.1 2.1 shard_map.109
  81.1 16.0 %all-to-all-start.1 = ((f32[32,16,128]{2,1,0:T(8,128)}), f32[32,16,128]{2,1,0:T(8,128)S(1)}, u32[]{:S(2)}, u32[]{:S(2)}) async-start(f32[32,16,128]{2,1,0:T(8,128)} %get-tuple-element.56), calls=%async_computation.1 | async-start | bytes 524288 | tf_op jit(solution)/shard_map/all_to_all | solution.py:307
  97.2 4.3 %collective-permute-start.15 = (f32[128,512]{1,0:T(8,128)S(1)}, f32[128,512]{1,0:T(8,128)S(1)}, u32[]{:S(2)}, u32[]{:S(2)}) collective-permute-start(f32[128,512]{1,0:T(8,128)S(1)} %get-tuple-element.58), channel_id=1, source_target_pairs={{4,0},{8,4},{12,8},{16,12},{20,16},{24,20},{28,24},{32,28},{36,32}... | collective-permute-start | bytes 786440 | tf_op jit(solution)/shard_map/ppermute | solution.py:302
  101.5 3.4 %all-to-all-done.1.offset = f32[32,16,128]{2,1,0:T(8,128)S(1)} async-done(((f32[32,16,128]{2,1,0:T(8,128)}), f32[32,16,128]{2,1,0:T(8,128)S(1)}, u32[]{:S(2)}, u32[]{:S(2)}) %all-to-all-start.1) | async-done | bytes 262176 | tf_op jit(solution)/shard_map/all_to_all | solution.py:307
  104.9 1.7 shard_map.110
  106.6 5.0 %all-to-all-start.2 = ((f32[32,16,128]{2,1,0:T(8,128)}), f32[32,16,128]{2,1,0:T(8,128)S(1)}, u32[]{:S(2)}, u32[]{:S(2)}) async-start(f32[32,16,128]{2,1,0:T(8,128)} %shard_map.110), calls=%async_computation.2 | async-start | bytes 524288 | tf_op jit(solution)/shard_map/all_to_all | solution.py:307
  111.7 7.8 %all-to-all-done.2.entering = f32[32,16,128]{2,1,0:T(8,128)S(1)} async-done(((f32[32,16,128]{2,1,0:T(8,128)}), f32[32,16,128]{2,1,0:T(8,128)S(1)}, u32[]{:S(2)}, u32[]{:S(2)}) %all-to-all-start.2) | async-done | bytes 262176 | tf_op jit(solution)/shard_map/all_to_all | solution.py:307
  119.5 1.2 copy-done.8
  120.7 1.2 copy-done.14
  121.9 2.0 shard_map.111
  126.5 3.5 %collective-permute-start.17 = (f32[128,512]{1,0:T(8,128)}, f32[128,512]{1,0:T(8,128)S(1)}, u32[]{:S(2)}, u32[]{:S(2)}) collective-permute-start(f32[128,512]{1,0:T(8,128)} %get-tuple-element.63), channel_id=1, source_target_pairs={{0,2},{1,3},{2,0},{3,1},{4,6},{5,7},{6,4},{7,5},{8,10},{9,11},{10,... | collective-permute-start | bytes 786440 | tf_op jit(solution)/shard_map/ppermute | solution.py:285
  131.5 10.6 %all-to-all-start.3 = ((f32[32,16,128]{2,1,0:T(8,128)}), f32[32,16,128]{2,1,0:T(8,128)S(1)}, u32[]{:S(2)}, u32[]{:S(2)}) async-start(f32[32,16,128]{2,1,0:T(8,128)} %get-tuple-element.60), calls=%async_computation.3 | async-start | bytes 524288 | tf_op jit(solution)/shard_map/all_to_all | solution.py:307
  143.0 1.2 copy-done.28
  146.3 4.3 %shard_map.112 = (f32[128,512]{1,0:T(8,128)S(1)}, f32[128,512]{1,0:T(8,128)S(1)}, f32[128,512]{1,0:T(8,128)S(1)}, f32[128,512]{1,0:T(8,128)S(1)}) custom-call(s32[2]{0:T(128)S(1)} %pad_add_fusion.place, f32[128,512]{1,0:T(8,128)S(1)} %get-tuple-element.61.x0, f32[128,512]{1,0:T(8,128)S(1)} %collective-permute-done.16.x1, ...), custom_call_target="tpu_custom_call" | custom-call | flops 3221225472 | bytes 5242880 | tf_op jit(solution)/shard_map/pallas_call | solution.py:252
  150.8 3.6 %collective-permute-start.20 = (f32[128,512]{1,0:T(8,128)S(1)}, f32[128,512]{1,0:T(8,128)S(1)}, u32[]{:S(2)}, u32[]{:S(2)}) collective-permute-start(f32[128,512]{1,0:T(8,128)S(1)} %get-tuple-element.67), channel_id=1, source_target_pairs={{0,2},{1,3},{2,0},{3,1},{4,6},{5,7},{6,4},{7,5},{8,10},{9,11},{10,... | collective-permute-start | bytes 786440 | tf_op jit(solution)/shard_map/ppermute | solution.py:285
  154.4 3.7 %shard_map.113 = (f32[128,128]{1,0:T(8,128)S(1)}, f32[128,128]{1,0:T(8,128)S(1)}, f32[128,128]{1,0:T(8,128)S(1)}, f32[128,128]{1,0:T(8,128)S(1)}) custom-call(bf16[128,512]{1,0:T(8,128)(2,1)S(1)} %get-tuple-element.69.d0, bf16[128,512]{1,0:T(8,128)(2,1)S(1)} %collective-permute-done.22.d1, bf16[128,512]{1,0:T(8,128)(2,1)S(1)} %collective-permute-done.23.d2, ...), custom_call_target="tpu_custom_call" | custom-call | flops 2147483648 | bytes 5242880 | tf_op jit(solution)/shard_map/pallas_call | solution.py:355
  158.8 3.9 %collective-permute-start.28 = (f32[4,512]{1,0:T(4,128)S(1)}, f32[4,512]{1,0:T(4,128)S(1)}, u32[]{:S(2)}, u32[]{:S(2)}) collective-permute-start(f32[4,512]{1,0:T(4,128)S(1)} %copy-done.26), channel_id=1, source_target_pairs={{0,1},{1,2},{2,3},{4,5},{5,6},{6,7},{8,9},{9,10},{10,11},{12,13},{... | collective-permute-start | bytes 24584 | tf_op jit(solution)/shard_map/ppermute | solution.py:302
  162.7 1.3 collective-permute-done.28.above
  164.1 1.3 collective-permute-start.29
  165.4 4.5 %collective-permute-done.29.below = f32[4,512]{1,0:T(4,128)S(1)} collective-permute-done((f32[4,512]{1,0:T(4,128)S(1)}, f32[4,512]{1,0:T(4,128)S(1)}, u32[]{:S(2)}, u32[]{:S(2)}) %collective-permute-start.29) | collective-permute-done | bytes 8224 | tf_op jit(solution)/shard_map/ppermute | solution.py:302
  172.1 1.7 shard_map.115
  174.5 19.7 %all-to-all-start.4 = ((f32[32,16,128]{2,1,0:T(8,128)}), f32[32,16,128]{2,1,0:T(8,128)S(1)}, u32[]{:S(2)}, u32[]{:S(2)}) async-start(f32[32,16,128]{2,1,0:T(8,128)} %get-tuple-element.78), calls=%async_computation.4 | async-start | bytes 524288 | tf_op jit(solution)/shard_map/all_to_all | solution.py:307
  194.2 4.3 %collective-permute-start.30 = (f32[128,512]{1,0:T(8,128)}, f32[128,512]{1,0:T(8,128)S(1)}, u32[]{:S(2)}, u32[]{:S(2)}) collective-permute-start(f32[128,512]{1,0:T(8,128)} %copy-done.24), channel_id=1, source_target_pairs={{4,0},{8,4},{12,8},{16,12},{20,16},{24,20},{28,24},{32,28},{36,32}... | collective-permute-start | bytes 786440 | tf_op jit(solution)/shard_map/ppermute | solution.py:302
  198.5 3.4 %all-to-all-done.4.offset = f32[32,16,128]{2,1,0:T(8,128)S(1)} async-done(((f32[32,16,128]{2,1,0:T(8,128)}), f32[32,16,128]{2,1,0:T(8,128)S(1)}, u32[]{:S(2)}, u32[]{:S(2)}) %all-to-all-start.4) | async-done | bytes 262176 | tf_op jit(solution)/shard_map/all_to_all | solution.py:307
  202.7 5.0 %all-to-all-start.5 = ((f32[32,16,128]{2,1,0:T(8,128)}), f32[32,16,128]{2,1,0:T(8,128)S(1)}, u32[]{:S(2)}, u32[]{:S(2)}) async-start(f32[32,16,128]{2,1,0:T(8,128)} %shard_map.116), calls=%async_computation.5 | async-start | bytes 524288 | tf_op jit(solution)/shard_map/all_to_all | solution.py:307
  207.7 7.8 %all-to-all-done.5.entering = f32[32,16,128]{2,1,0:T(8,128)S(1)} async-done(((f32[32,16,128]{2,1,0:T(8,128)}), f32[32,16,128]{2,1,0:T(8,128)S(1)}, u32[]{:S(2)}, u32[]{:S(2)}) %all-to-all-start.5) | async-done | bytes 262176 | tf_op jit(solution)/shard_map/all_to_all | solution.py:307
  215.5 1.2 copy-done.15
  216.7 1.7 shard_map.117
  (124 shorter events, 26.7 us)
Async XLA Ops:
  7.2 30.2 %copy-start.33 = (s32[256]{0:T(256)S(1)}, s32[256]{0:T(256)}, u32[]{:S(2)}) copy-start(s32[256]{0:T(256)} %param.13) | copy-start | bytes 3076
  7.2 30.2 %copy-start.34 = (s32[256]{0:T(256)S(1)}, s32[256]{0:T(256)}, u32[]{:S(2)}) copy-start(s32[256]{0:T(256)} %param.12) | copy-start | bytes 3076
  7.2 60.1 %all-gather.2.cloned.1.call-start = ((), (), s32[]{:S(2)}) async-start(), calls=%async_computation.6 | async-start | bytes 4325376 | tf_op jit(solution)/shard_map/all_gather | solution.py:318
  8.9 20.3 %collective-permute-start = (f32[128,512]{1,0:T(8,128)S(1)}, f32[128,512]{1,0:T(8,128)S(1)}, u32[]{:S(2)}, u32[]{:S(2)}) collective-permute-start(f32[128,512]{1,0:T(8,128)S(1)} %slice_bitcast_fusion), channel_id=1, source_target_pairs={{0,4},{4,8},{8,12},{12,16},{16,20},{20,24},{24,28},{28,32},{32,36}... | collective-permute-start | bytes 786440 | tf_op jit(solution)/shard_map/ppermute | solution.py:302
  11.8 48.8 %collective-permute-start.9 = (bf16[128,512]{1,0:T(8,128)(2,1)S(1)}, bf16[128,512]{1,0:T(8,128)(2,1)S(1)}, u32[]{:S(2)}, u32[]{:S(2)}) collective-permute-start(bf16[128,512]{1,0:T(8,128)(2,1)S(1)} %fusion.d0), channel_id=1, source_target_pairs={{64,67},{65,64},{66,65},{67,66}} | collective-permute-start | bytes 393224 | tf_op jit(solution)/shard_map/ppermute | solution.py:291
  12.5 49.4 %collective-permute-start.8 = (bf16[128,512]{1,0:T(8,128)(2,1)S(1)}, bf16[128,512]{1,0:T(8,128)(2,1)S(1)}, u32[]{:S(2)}, u32[]{:S(2)}) collective-permute-start(bf16[128,512]{1,0:T(8,128)(2,1)S(1)} %fusion.d0), channel_id=1, source_target_pairs={{64,66},{65,67},{66,64},{67,65}} | collective-permute-start | bytes 393224 | tf_op jit(solution)/shard_map/ppermute | solution.py:291
  17.5 63.7 %all-to-all-start = ((f32[32,16,128]{2,1,0:T(8,128)}), f32[32,16,128]{2,1,0:T(8,128)}, u32[]{:S(2)}, u32[]{:S(2)}) async-start(f32[32,16,128]{2,1,0:T(8,128)} %get-tuple-element.42), calls=%async_computation | async-start | bytes 524288 | tf_op jit(solution)/shard_map/all_to_all | solution.py:307
  31.1 9.6 %collective-permute-start.1 = (f32[128,512]{1,0:T(8,128)S(1)}, f32[128,512]{1,0:T(8,128)S(1)}, u32[]{:S(2)}, u32[]{:S(2)}) collective-permute-start(f32[128,512]{1,0:T(8,128)S(1)} %get-tuple-element.44), channel_id=1, source_target_pairs={{0,1},{1,2},{2,3},{3,0},{4,5},{5,6},{6,7},{7,4},{8,9},{9,10},{10,1... | collective-permute-start | bytes 786440 | tf_op jit(solution)/shard_map/ppermute | solution.py:285
  32.4 14.6 %collective-permute-start.2 = (f32[128,512]{1,0:T(8,128)S(1)}, f32[128,512]{1,0:T(8,128)S(1)}, u32[]{:S(2)}, u32[]{:S(2)}) collective-permute-start(f32[128,512]{1,0:T(8,128)S(1)} %get-tuple-element.45), channel_id=1, source_target_pairs={{0,2},{1,3},{2,0},{3,1},{4,6},{5,7},{6,4},{7,5},{8,10},{9,11},{10,... | collective-permute-start | bytes 786440 | tf_op jit(solution)/shard_map/ppermute | solution.py:285
  34.8 14.0 %collective-permute-start.3 = (f32[128,512]{1,0:T(8,128)S(1)}, f32[128,512]{1,0:T(8,128)S(1)}, u32[]{:S(2)}, u32[]{:S(2)}) collective-permute-start(f32[128,512]{1,0:T(8,128)S(1)} %get-tuple-element.46), channel_id=1, source_target_pairs={{0,3},{1,0},{2,1},{3,2},{4,7},{5,4},{6,5},{7,6},{8,11},{9,8},{10,9... | collective-permute-start | bytes 786440 | tf_op jit(solution)/shard_map/ppermute | solution.py:285
  40.8 24.0 %collective-permute-start.7 = (bf16[128,512]{1,0:T(8,128)(2,1)S(1)}, bf16[128,512]{1,0:T(8,128)(2,1)S(1)}, u32[]{:S(2)}, u32[]{:S(2)}) collective-permute-start(bf16[128,512]{1,0:T(8,128)(2,1)S(1)} %fusion.d0), channel_id=1, source_target_pairs={{64,65},{65,66},{66,67},{67,64}} | collective-permute-start | bytes 393224 | tf_op jit(solution)/shard_map/ppermute | solution.py:291
  47.0 26.4 %collective-permute-start.13 = (f32[4,512]{1,0:T(4,128)S(1)}, f32[4,512]{1,0:T(4,128)S(1)}, u32[]{:S(2)}, u32[]{:S(2)}) collective-permute-start(f32[4,512]{1,0:T(4,128)S(1)} %bitcast.18), channel_id=1, source_target_pairs={{0,1},{1,2},{2,3},{4,5},{5,6},{6,7},{8,9},{9,10},{10,11},{12,13},{... | collective-permute-start | bytes 24584 | tf_op jit(solution)/shard_map/ppermute | solution.py:302
  58.0 18.2 %copy-start.2 = (f32[4,128,512]{2,1,0:T(8,128)S(1)}, f32[4,128,512]{2,1,0:T(8,128)}, u32[]{:S(2)}) copy-start(f32[4,128,512]{2,1,0:T(8,128)} %current.5) | copy-start | bytes 3145732
  58.0 16.8 %collective-permute-start.4 = (f32[128,512]{1,0:T(8,128)S(1)}, f32[128,512]{1,0:T(8,128)S(1)}, u32[]{:S(2)}, u32[]{:S(2)}) collective-permute-start(f32[128,512]{1,0:T(8,128)S(1)} %get-tuple-element.48), channel_id=1, source_target_pairs={{0,1},{1,2},{2,3},{3,0},{4,5},{5,6},{6,7},{7,4},{8,9},{9,10},{10,1... | collective-permute-start | bytes 786440 | tf_op jit(solution)/shard_map/ppermute | solution.py:285
  60.6 13.6 %collective-permute-start.14 = (f32[4,512]{1,0:T(4,128)S(1)}, f32[4,512]{1,0:T(4,128)S(1)}, u32[]{:S(2)}, u32[]{:S(2)}) collective-permute-start(f32[4,512]{1,0:T(4,128)S(1)} %bitcast.19), channel_id=1, source_target_pairs={{1,0},{2,1},{3,2},{5,4},{6,5},{7,6},{9,8},{10,9},{11,10},{13,12},{... | collective-permute-start | bytes 24584 | tf_op jit(solution)/shard_map/ppermute | solution.py:302
  61.9 15.2 %collective-permute-start.5 = (f32[128,512]{1,0:T(8,128)}, f32[128,512]{1,0:T(8,128)}, u32[]{:S(2)}, u32[]{:S(2)}) collective-permute-start(f32[128,512]{1,0:T(8,128)} %get-tuple-element.49), channel_id=1, source_target_pairs={{0,2},{1,3},{2,0},{3,1},{4,6},{5,7},{6,4},{7,5},{8,10},{9,11},{10,... | collective-permute-start | bytes 786440 | tf_op jit(solution)/shard_map/ppermute | solution.py:285
  64.8 12.3 %collective-permute-start.6 = (f32[128,512]{1,0:T(8,128)}, f32[128,512]{1,0:T(8,128)}, u32[]{:S(2)}, u32[]{:S(2)}) collective-permute-start(f32[128,512]{1,0:T(8,128)} %get-tuple-element.50), channel_id=1, source_target_pairs={{0,3},{1,0},{2,1},{3,2},{4,7},{5,4},{6,5},{7,6},{8,11},{9,8},{10,9... | collective-permute-start | bytes 786440 | tf_op jit(solution)/shard_map/ppermute | solution.py:285
  69.6 7.5 %copy-start.19 = (f32[128,512]{1,0:T(8,128)S(1)}, f32[128,512]{1,0:T(8,128)}, u32[]{:S(2)}) copy-start(f32[128,512]{1,0:T(8,128)} %copy-done.18) | copy-start | bytes 786436
  73.3 46.1 %copy-start.5 = (f32[4,128,512]{2,1,0:T(8,128)S(1)}, f32[4,128,512]{2,1,0:T(8,128)}, u32[]{:S(2)}) copy-start(f32[4,128,512]{2,1,0:T(8,128)} %damping.3) | copy-start | bytes 3145732
  73.4 3.7 %collective-permute-start.10 = (f32[128,128]{1,0:T(8,128)S(1)}, f32[128,128]{1,0:T(8,128)S(1)}, u32[]{:S(2)}, u32[]{:S(2)}) collective-permute-start(f32[128,128]{1,0:T(8,128)S(1)} %get-tuple-element.52), channel_id=1, source_target_pairs={{64,67},{65,64},{66,65},{67,66}} | collective-permute-start | bytes 196616 | tf_op jit(solution)/shard_map/ppermute | solution.py:291
  74.2 2.9 %collective-permute-start.11 = (f32[128,128]{1,0:T(8,128)S(1)}, f32[128,128]{1,0:T(8,128)S(1)}, u32[]{:S(2)}, u32[]{:S(2)}) collective-permute-start(f32[128,128]{1,0:T(8,128)S(1)} %get-tuple-element.53), channel_id=1, source_target_pairs={{64,66},{65,67},{66,64},{67,65}} | collective-permute-start | bytes 196616 | tf_op jit(solution)/shard_map/ppermute | solution.py:291
  75.6 1.5 collective-permute-start.12
  81.1 23.8 %all-to-all-start.1 = ((f32[32,16,128]{2,1,0:T(8,128)}), f32[32,16,128]{2,1,0:T(8,128)S(1)}, u32[]{:S(2)}, u32[]{:S(2)}) async-start(f32[32,16,128]{2,1,0:T(8,128)} %get-tuple-element.56), calls=%async_computation.1 | async-start | bytes 524288 | tf_op jit(solution)/shard_map/all_to_all | solution.py:307
  97.2 14.5 %collective-permute-start.15 = (f32[128,512]{1,0:T(8,128)S(1)}, f32[128,512]{1,0:T(8,128)S(1)}, u32[]{:S(2)}, u32[]{:S(2)}) collective-permute-start(f32[128,512]{1,0:T(8,128)S(1)} %get-tuple-element.58), channel_id=1, source_target_pairs={{4,0},{8,4},{12,8},{16,12},{20,16},{24,20},{28,24},{32,28},{36,32}... | collective-permute-start | bytes 786440 | tf_op jit(solution)/shard_map/ppermute | solution.py:302
  106.6 12.8 %all-to-all-start.2 = ((f32[32,16,128]{2,1,0:T(8,128)}), f32[32,16,128]{2,1,0:T(8,128)S(1)}, u32[]{:S(2)}, u32[]{:S(2)}) async-start(f32[32,16,128]{2,1,0:T(8,128)} %shard_map.110), calls=%async_computation.2 | async-start | bytes 524288 | tf_op jit(solution)/shard_map/all_to_all | solution.py:307
  126.5 15.6 %collective-permute-start.16 = (f32[128,512]{1,0:T(8,128)}, f32[128,512]{1,0:T(8,128)S(1)}, u32[]{:S(2)}, u32[]{:S(2)}) collective-permute-start(f32[128,512]{1,0:T(8,128)} %get-tuple-element.62), channel_id=1, source_target_pairs={{0,1},{1,2},{2,3},{3,0},{4,5},{5,6},{6,7},{7,4},{8,9},{9,10},{10,1... | collective-permute-start | bytes 786440 | tf_op jit(solution)/shard_map/ppermute | solution.py:285
  126.5 16.5 %collective-permute-start.17 = (f32[128,512]{1,0:T(8,128)}, f32[128,512]{1,0:T(8,128)S(1)}, u32[]{:S(2)}, u32[]{:S(2)}) collective-permute-start(f32[128,512]{1,0:T(8,128)} %get-tuple-element.63), channel_id=1, source_target_pairs={{0,2},{1,3},{2,0},{3,1},{4,6},{5,7},{6,4},{7,5},{8,10},{9,11},{10,... | collective-permute-start | bytes 786440 | tf_op jit(solution)/shard_map/ppermute | solution.py:285
  129.9 13.1 %collective-permute-start.18 = (f32[128,512]{1,0:T(8,128)}, f32[128,512]{1,0:T(8,128)S(1)}, u32[]{:S(2)}, u32[]{:S(2)}) collective-permute-start(f32[128,512]{1,0:T(8,128)} %get-tuple-element.64), channel_id=1, source_target_pairs={{0,3},{1,0},{2,1},{3,2},{4,7},{5,4},{6,5},{7,6},{8,11},{9,8},{10,9... | collective-permute-start | bytes 786440 | tf_op jit(solution)/shard_map/ppermute | solution.py:285
  130.2 24.1 %collective-permute-start.24 = (bf16[128,512]{1,0:T(8,128)(2,1)S(1)}, bf16[128,512]{1,0:T(8,128)(2,1)S(1)}, u32[]{:S(2)}, u32[]{:S(2)}) collective-permute-start(bf16[128,512]{1,0:T(8,128)(2,1)S(1)} %get-tuple-element.69.d0), channel_id=1, source_target_pairs={{64,67},{65,64},{66,65},{67,66}} | collective-permute-start | bytes 393224 | tf_op jit(solution)/shard_map/ppermute | solution.py:291
  130.9 23.5 %collective-permute-start.23 = (bf16[128,512]{1,0:T(8,128)(2,1)S(1)}, bf16[128,512]{1,0:T(8,128)(2,1)S(1)}, u32[]{:S(2)}, u32[]{:S(2)}) collective-permute-start(bf16[128,512]{1,0:T(8,128)(2,1)S(1)} %get-tuple-element.69.d0), channel_id=1, source_target_pairs={{64,66},{65,67},{66,64},{67,65}} | collective-permute-start | bytes 393224 | tf_op jit(solution)/shard_map/ppermute | solution.py:291
  131.5 43.0 %all-to-all-start.3 = ((f32[32,16,128]{2,1,0:T(8,128)}), f32[32,16,128]{2,1,0:T(8,128)S(1)}, u32[]{:S(2)}, u32[]{:S(2)}) async-start(f32[32,16,128]{2,1,0:T(8,128)} %get-tuple-element.60), calls=%async_computation.3 | async-start | bytes 524288 | tf_op jit(solution)/shard_map/all_to_all | solution.py:307
  142.1 12.3 %collective-permute-start.22 = (bf16[128,512]{1,0:T(8,128)(2,1)S(1)}, bf16[128,512]{1,0:T(8,128)(2,1)S(1)}, u32[]{:S(2)}, u32[]{:S(2)}) collective-permute-start(bf16[128,512]{1,0:T(8,128)(2,1)S(1)} %get-tuple-element.69.d0), channel_id=1, source_target_pairs={{64,65},{65,66},{66,67},{67,64}} | collective-permute-start | bytes 393224 | tf_op jit(solution)/shard_map/ppermute | solution.py:291
  146.3 8.1 %copy-start.17 = (s32[512,128]{1,0:T(8,128)S(1)}, s32[512,128]{1,0:T(8,128)}, u32[]{:S(2)}) copy-start(s32[512,128]{1,0:T(8,128)} %copy-done.16) | copy-start | bytes 786436
  146.3 8.1 %copy-start.23 = (bf16[32,512,128]{2,1,0:T(8,128)(2,1)S(1)}, bf16[32,512,128]{2,1,0:T(8,128)(2,1)}, u32[]{:S(2)}) copy-start(bf16[32,512,128]{2,1,0:T(8,128)(2,1)} %all-gather.2.cloned.1.call-done.blade) | copy-start | bytes 12582916
  150.6 8.2 %copy-start.26 = (f32[4,512]{1,0:T(4,128)S(1)}, f32[4,512]{1,0:T(4,128)}, u32[]{:S(2)}) copy-start(f32[4,512]{1,0:T(4,128)} %copy-done.25) | copy-start | bytes 24580
  150.6 20.6 %copy-start.12 = (f32[4,128,512]{2,1,0:T(8,128)S(1)}, f32[4,128,512]{2,1,0:T(8,128)}, u32[]{:S(2)}) copy-start(f32[4,128,512]{2,1,0:T(8,128)} %copy-done.11) | copy-start | bytes 3145732
  150.6 21.5 %collective-permute-start.19 = (f32[128,512]{1,0:T(8,128)S(1)}, f32[128,512]{1,0:T(8,128)S(1)}, u32[]{:S(2)}, u32[]{:S(2)}) collective-permute-start(f32[128,512]{1,0:T(8,128)S(1)} %get-tuple-element.66), channel_id=1, source_target_pairs={{0,1},{1,2},{2,3},{3,0},{4,5},{5,6},{6,7},{7,4},{8,9},{9,10},{10,1... | collective-permute-start | bytes 786440 | tf_op jit(solution)/shard_map/ppermute | solution.py:285
  150.8 21.3 %collective-permute-start.20 = (f32[128,512]{1,0:T(8,128)S(1)}, f32[128,512]{1,0:T(8,128)S(1)}, u32[]{:S(2)}, u32[]{:S(2)}) collective-permute-start(f32[128,512]{1,0:T(8,128)S(1)} %get-tuple-element.67), channel_id=1, source_target_pairs={{0,2},{1,3},{2,0},{3,1},{4,6},{5,7},{6,4},{7,5},{8,10},{9,11},{10,... | collective-permute-start | bytes 786440 | tf_op jit(solution)/shard_map/ppermute | solution.py:285
  154.3 17.8 %copy-start.10 = (f32[4,128,512]{2,1,0:T(8,128)S(1)}, f32[4,128,512]{2,1,0:T(8,128)}, u32[]{:S(2)}) copy-start(f32[4,128,512]{2,1,0:T(8,128)} %copy-done.9) | copy-start | bytes 3145732
  154.4 17.8 %collective-permute-start.21 = (f32[128,512]{1,0:T(8,128)S(1)}, f32[128,512]{1,0:T(8,128)S(1)}, u32[]{:S(2)}, u32[]{:S(2)}) collective-permute-start(f32[128,512]{1,0:T(8,128)S(1)} %get-tuple-element.68), channel_id=1, source_target_pairs={{0,3},{1,0},{2,1},{3,2},{4,7},{5,4},{6,5},{7,6},{8,11},{9,8},{10,9... | collective-permute-start | bytes 786440 | tf_op jit(solution)/shard_map/ppermute | solution.py:285
  158.1 12.4 %collective-permute-start.25 = (f32[128,128]{1,0:T(8,128)S(1)}, f32[128,128]{1,0:T(8,128)S(1)}, u32[]{:S(2)}, u32[]{:S(2)}) collective-permute-start(f32[128,128]{1,0:T(8,128)S(1)} %get-tuple-element.71), channel_id=1, source_target_pairs={{64,67},{65,64},{66,65},{67,66}} | collective-permute-start | bytes 196616 | tf_op jit(solution)/shard_map/ppermute | solution.py:291
  158.8 5.3 %collective-permute-start.28 = (f32[4,512]{1,0:T(4,128)S(1)}, f32[4,512]{1,0:T(4,128)S(1)}, u32[]{:S(2)}, u32[]{:S(2)}) collective-permute-start(f32[4,512]{1,0:T(4,128)S(1)} %copy-done.26), channel_id=1, source_target_pairs={{0,1},{1,2},{2,3},{4,5},{5,6},{6,7},{8,9},{9,10},{10,11},{12,13},{... | collective-permute-start | bytes 24584 | tf_op jit(solution)/shard_map/ppermute | solution.py:302
  164.1 5.8 %collective-permute-start.29 = (f32[4,512]{1,0:T(4,128)S(1)}, f32[4,512]{1,0:T(4,128)S(1)}, u32[]{:S(2)}, u32[]{:S(2)}) collective-permute-start(f32[4,512]{1,0:T(4,128)S(1)} %get-tuple-element.77), channel_id=1, source_target_pairs={{1,0},{2,1},{3,2},{5,4},{6,5},{7,6},{9,8},{10,9},{11,10},{13,12},{... | collective-permute-start | bytes 24584 | tf_op jit(solution)/shard_map/ppermute | solution.py:302
  169.9 2.2 collective-permute-start.26
  170.6 1.5 collective-permute-start.27
  174.5 27.4 %all-to-all-start.4 = ((f32[32,16,128]{2,1,0:T(8,128)}), f32[32,16,128]{2,1,0:T(8,128)S(1)}, u32[]{:S(2)}, u32[]{:S(2)}) async-start(f32[32,16,128]{2,1,0:T(8,128)} %get-tuple-element.78), calls=%async_computation.4 | async-start | bytes 524288 | tf_op jit(solution)/shard_map/all_to_all | solution.py:307
  194.2 13.5 %collective-permute-start.30 = (f32[128,512]{1,0:T(8,128)}, f32[128,512]{1,0:T(8,128)S(1)}, u32[]{:S(2)}, u32[]{:S(2)}) collective-permute-start(f32[128,512]{1,0:T(8,128)} %copy-done.24), channel_id=1, source_target_pairs={{4,0},{8,4},{12,8},{16,12},{20,16},{24,20},{28,24},{32,28},{36,32}... | collective-permute-start | bytes 786440 | tf_op jit(solution)/shard_map/ppermute | solution.py:302
  202.7 12.8 %all-to-all-start.5 = ((f32[32,16,128]{2,1,0:T(8,128)}), f32[32,16,128]{2,1,0:T(8,128)S(1)}, u32[]{:S(2)}, u32[]{:S(2)}) async-start(f32[32,16,128]{2,1,0:T(8,128)} %shard_map.116), calls=%async_computation.5 | async-start | bytes 524288 | tf_op jit(solution)/shard_map/all_to_all | solution.py:307
  (25 other events, 46.4 us)
Sparse Core Ops, SparseCore 0:
  10.3 49.7 all-gather.1

commit v2 on v1

v2 whole, which is shorter than its diff:
```python
import ml_dtypes
import numpy as np
import jax
import jax.numpy as jnp
from jax import lax
from jax.experimental import pallas as pl
from jax.experimental.pallas import tpu as pltpu
from jax.sharding import PartitionSpec as P

SWEEPS = 2
SOURCE_GAIN = 0.04
SCREENING = 0.001
VISCOSITY = 0.1
DRAG_RATE = 0.01

F32 = jnp.float32
BF16 = jnp.bfloat16
SUB = 8
LANE = 128
EDGE = 8
STEPS = 4
MIB = 1024 * 1024
VMEM = pl.BlockSpec(memory_space=pltpu.VMEM)
SMEM = pl.BlockSpec(memory_space=pltpu.SMEM)


def tables(length):
    ordinal = np.arange(1, length + 1)
    product = np.outer(ordinal, ordinal) % (2 * (length + 1))
    sine = np.sqrt(2.0 / (length + 1)) * np.sin(np.pi * product / (length + 1))
    high = sine.astype(np.float32).astype(ml_dtypes.bfloat16)
    low = (sine - high.astype(np.float64)).astype(np.float32).astype(ml_dtypes.bfloat16)
    values = 2.0 - 2.0 * np.cos(np.pi * ordinal / (length + 1))
    inverse = 1.0 / (SCREENING + values[:, None] + values[None, :])
    return high, low, inverse.astype(np.float32)


def split(value):
    high = value.astype(BF16)
    return high, (value - high.astype(F32)).astype(BF16)


def groups(rows):
    return [(g, slice(SUB * g, SUB * g + SUB)) for g in range(rows // SUB)]


def to_chunks(ref, g, value):
    for h in range(2):
        for q in range(2):
            at = (2 * h + q) * LANE
            ref[2 * g + h, SUB * q : SUB * q + SUB, :] = value[:, at : at + LANE]


def from_chunks(ref, g):
    parts = []
    for h in range(2):
        for q in range(2):
            parts.append(ref[2 * g + h, SUB * q : SUB * q + SUB, :])
    return jnp.concatenate(parts, axis=1)


def decay_of(value, damping):
    return 1.0 - (damping + DRAG_RATE * jnp.abs(value))


def send_order(place, i, source, outs):
    count, height, _ = source.shape
    at = pl.multiple_of(i * height, height)
    for r, ref in enumerate(outs):
        ref[pl.ds(at, height), :] = source[lax.rem(place[0] + r, count)]


def send_edges(current, outs):
    stations, height, width = current.shape
    i = pl.program_id(0)
    total = outs[1].shape[0]
    empty = jnp.zeros((EDGE - stations, width), F32)

    @pl.when(i == pl.num_programs(0) - 1)
    def _():
        rows = [current[s, height - 1 : height] for s in range(stations)]
        outs[1][total - EDGE : total] = jnp.concatenate(rows + [empty], axis=0)

    @pl.when(i == 0)
    def _():
        rows = [current[s, 0:1] for s in range(stations)]
        outs[-1][total - EDGE : total] = jnp.concatenate(rows + [empty], axis=0)


def source_kernel(place, current, upstream, inflow, x0, x1, x2, x3, source):
    stations, height, _ = current.shape
    for _, rows in groups(height):
        previous = jnp.where(place[1] == 1, inflow[rows], upstream[rows])
        for s in range(stations):
            here = current[s, rows]
            source[s, rows] = SOURCE_GAIN * (here - previous)
            previous = here
    outs = (x0, x1, x2, x3)
    send_order(place, pl.program_id(0), source, outs)
    send_edges(current, outs)


def decay_kernel(place, current, damping, decay, scale):
    for g, rows in groups(current.shape[1]):
        product = None
        for s in range(current.shape[0]):
            d = decay_of(current[s, rows], damping[s, rows])
            decay[s, rows] = d
            product = d if product is None else product * d
        to_chunks(scale, g, product)


def laplace_kernel(place, current, before, after, term):
    stations, height, width = current.shape
    above = jnp.where(place[2] == 1, 0.0, before[height : height + EDGE])
    below = jnp.where(place[3] == 1, 0.0, after[height : height + EDGE])
    lane = lax.broadcasted_iota(jnp.int32, (SUB, width), 1)
    for s in range(stations):
        for g, rows in groups(height):
            here = current[s, rows]
            lo, hi = SUB * g, SUB * g + SUB
            if g == 0:
                up = jnp.concatenate([above[s : s + 1], current[s, 0 : SUB - 1]], axis=0)
            else:
                up = current[s, lo - 1 : hi - 1]
            if hi == height:
                down = jnp.concatenate([current[s, lo + 1 : hi], below[s : s + 1]], axis=0)
            else:
                down = current[s, lo + 1 : hi + 1]
            left = jnp.where(lane == 0, 0.0, pltpu.roll(here, 1, 1))
            right = jnp.where(lane == width - 1, 0.0, pltpu.roll(here, width - 1, 1))
            term[s, rows] = VISCOSITY * (up + down + left + right - 4.0 * here)


def solve_kernel(
    place, x0, x1, x2, x3, high_far, low_far, inverse_far, p0, p1, p2, p3,
    plane, high, low, inverse, arrivals,
):
    c = place[0]
    copies = [
        pltpu.make_async_copy(far_ref, ref, arrivals.at[i])
        for i, (far_ref, ref) in enumerate(
            ((high_far, high), (low_far, low), (inverse_far, inverse))
        )
    ]
    for copy in copies:
        copy.start()
    inputs, outputs = (x0, x1, x2, x3), (p0, p1, p2, p3)
    count = len(inputs)
    height = p0.shape[0]
    for r, ref in enumerate(inputs):
        b = lax.rem(c - r + count, count)
        plane[pl.ds(pl.multiple_of(b * height, height), height), :] = ref[0:height]
    copies[0].wait()
    copies[1].wait()
    sh, sl = high[...], low[...]
    by_left = jnp.concatenate([sh, sh, sl], axis=1)
    by_right = jnp.concatenate([sh, sl, sh], axis=0)

    def right(value):
        vh, vl = split(value)
        return jnp.dot(
            jnp.concatenate([vh, vh, vl], axis=1), by_right, preferred_element_type=F32
        )

    def left(value):
        vh, vl = split(value)
        return jnp.dot(
            by_left, jnp.concatenate([vh, vl, vh], axis=0), preferred_element_type=F32
        )

    modes = left(right(plane[...]))
    copies[2].wait()
    modes = modes * inverse[...]
    plane[...] = right(left(modes))
    for r, ref in enumerate(outputs):
        b = lax.rem(c + r, count)
        ref[...] = plane[pl.ds(pl.multiple_of(b * height, height), height), :]


def disc_kernel(d0, d1, d2, d3, owners, blade_a, blade_b, f0, f1, f2, f3, plane, total):
    step = pl.program_id(0)
    height = d0.shape[0]

    @pl.when(step == 0)
    def _():
        for r, ref in enumerate((d0, d1, d2, d3)):
            plane[height * r : height * (r + 1)] = ref[...]
        total[...] = jnp.zeros_like(total)

    per_step = blade_a.shape[0]
    for i in range(0, per_step, 2):
        pair = jnp.concatenate(
            [
                jnp.concatenate([blade_a[i], blade_b[i]], axis=0),
                jnp.concatenate([blade_a[i + 1], blade_b[i + 1]], axis=0),
            ],
            axis=1,
        )
        response = jnp.dot(plane[...], pair, preferred_element_type=F32)
        first = step * per_step + i
        kept = jnp.where(owners[...] == first, response[:, :LANE], total[...])
        total[...] = jnp.where(owners[...] == first + 1, response[:, LANE:], kept)

    @pl.when(step == pl.num_programs(0) - 1)
    def _():
        for r, ref in enumerate((f0, f1, f2, f3)):
            ref[...] = jnp.tanh(total[height * r : height * (r + 1)])


def offset_kernel(
    place, p0, p1, p2, p3, f0, f1, f2, f3, decay, term, inflow, pressure, lead, force, offset
):
    c = place[0]
    first = place[1]
    pieces, forces = (p0, p1, p2, p3), (f0, f1, f2, f3)
    count = len(pieces)
    width = inflow.shape[1] // count
    for r in range(count):
        s = lax.rem(c - r + count, count)
        pressure[s] = pieces[r][...]
        b = lax.rem(c + r, count)
        force[:, pl.ds(pl.multiple_of(b * width, width), width)] = forces[r][...]
    for g, rows in groups(inflow.shape[0]):
        start = pressure[0, rows]
        lead[rows] = start
        state = jnp.where(first == 1, inflow[rows] + start, 0.0)
        for s in range(count):
            p = pressure[s, rows]
            t = term[s, rows]
            if s == 0:
                t = t + force[rows]
            d = decay[s, rows]
            state = d * state + (t + (1.0 - d) * p)
        to_chunks(offset, g, state)


def scan_kernel(scale, offset, entering):
    entering[0] = jnp.zeros_like(entering[0])
    state = offset[0]
    for m in range(1, scale.shape[0]):
        entering[m] = state
        state = scale[m] * state + offset[m]


def march_rows(first, g, rows, entering, pressure, following, decay, term, force, inflow):
    stations = decay.shape[0]
    ahead = pressure[0, rows]
    state = jnp.where(first == 1, inflow[rows], from_chunks(entering, g) - ahead)
    states = [state]
    for s in range(stations):
        here = ahead
        ahead = following[rows] if s == stations - 1 else pressure[s + 1, rows]
        t = term[s, rows]
        if s == 0:
            t = t + force[rows]
        state = decay[s, rows] * state + (t - (ahead - here))
        states.append(state)
    return states


def middle_kernel(
    place, entering, pressure, following, decay, term, force, inflow, damping,
    current, decay_new, scale, disc, x0, x1, x2, x3, source,
):
    first = place[1]
    stations, height, _ = current.shape
    for g, rows in groups(height):
        states = march_rows(
            first, g, rows, entering, pressure, following, decay, term, force, inflow
        )
        product = None
        for s in range(stations):
            value = states[s + 1]
            current[s, rows] = value
            source[s, rows] = SOURCE_GAIN * (value - states[s])
            d = decay_of(value, damping[s, rows])
            decay_new[s, rows] = d
            product = d if product is None else product * d
        to_chunks(scale, g, product)
    outs = (x0, x1, x2, x3)
    send_order(place, pl.program_id(0), source, outs)
    send_edges(current, outs)
    disc[...] = current[0].astype(BF16)


def last_kernel(
    place, entering, pressure, following, decay, term, force, inflow, current
):
    first = place[1]
    for g, rows in groups(current.shape[1]):
        states = march_rows(
            first, g, rows, entering, pressure, following, decay, term, force, inflow
        )
        for s in range(current.shape[0]):
            current[s, rows] = states[s + 1]


def cost(flops, size):
    return pl.CostEstimate(flops=int(flops), bytes_accessed=int(size), transcendentals=0)


def near(shape, dtype=F32):
    return pltpu.VMEM(shape, dtype)


def far(shape, dtype=F32):
    return pltpu.HBM(shape, dtype)


def stay(value):
    return pltpu.with_memory_space_constraint(value, pltpu.HBM)


def call(kernel, outs, args, work, scalars=0, limit=8, scratch=()):
    return pl.pallas_call(
        kernel,
        out_shape=outs,
        in_specs=[SMEM] * scalars + [VMEM] * (len(args) - scalars),
        out_specs=[VMEM] * len(outs),
        scratch_shapes=list(scratch),
        compiler_params=pltpu.CompilerParams(vmem_limit_bytes=limit * MIB),
        cost_estimate=work,
    )(*args)


def by_rows(kernel, height, outs, place, args, work, whole=(), scratch=()):
    part = height // STEPS

    def spec(shape, index):
        if index in whole:
            return pl.BlockSpec(shape, lambda i, p: (0,) * len(shape))
        if shape[-1] == LANE and len(shape) == 3:
            return pl.BlockSpec((shape[0] // STEPS,) + shape[1:], lambda i, p: (i, 0, 0))
        if len(shape) == 3:
            return pl.BlockSpec((shape[0], part, shape[2]), lambda i, p: (0, i, 0))
        return pl.BlockSpec((part, shape[1]), lambda i, p: (i, 0))

    count = len(args)
    return pl.pallas_call(
        kernel,
        grid_spec=pltpu.PrefetchScalarGridSpec(
            num_scalar_prefetch=1,
            grid=(STEPS,),
            in_specs=[spec(a.shape, None) for a in args],
            out_specs=[spec(a.inner_aval.shape, i) for i, a in enumerate(outs)],
            scratch_shapes=list(scratch),
        ),
        out_shape=outs,
        compiler_params=pltpu.CompilerParams(vmem_limit_bytes=12 * MIB),
        cost_estimate=work,
    )(place, *args)


def disc_forces(rows, owners, blades):
    height, width = rows[0].shape
    count = len(rows)
    number, half, _ = blades[0].shape
    per_step = 4
    fixed = lambda shape: pl.BlockSpec(shape, lambda i: (0,) * len(shape))
    table = pl.BlockSpec((per_step, half, LANE), lambda i: (i, 0, 0))
    blades = [stay(b) for b in blades]
    return pl.pallas_call(
        disc_kernel,
        grid=(number // per_step,),
        out_shape=[near((height, LANE))] * count,
        in_specs=[fixed((height, width))] * count + [fixed(owners.shape), table, table],
        out_specs=[fixed((height, LANE))] * count,
        scratch_shapes=[
            pltpu.VMEM((count * height, width), BF16),
            pltpu.VMEM((count * height, LANE), F32),
        ],
        compiler_params=pltpu.CompilerParams(vmem_limit_bytes=16 * MIB),
        cost_estimate=cost(2 * number * width * width * LANE, 5 * MIB),
    )(*rows, stay(owners), *blades)


def local(velocity_guess, damping, inflow, disc_rows, owner, blade):
    stations, height, width = velocity_guess.shape
    march_size = lax.axis_size("march")
    cross_size = lax.axis_size("cross")
    march_index = lax.axis_index("march")
    cross_index = lax.axis_index("cross")
    disc_slab = stations * march_size // 2 // stations
    at_disc = march_index == disc_slab
    first = march_index == 0
    place = jnp.stack(
        [
            cross_index.astype(jnp.int32),
            first.astype(jnp.int32),
            (cross_index == 0).astype(jnp.int32),
            (cross_index == cross_size - 1).astype(jnp.int32),
        ]
    )
    tabled = [stay(jnp.asarray(t)) for t in tables(width)]

    slab = (stations, height, width)
    plane = (height, width)
    edged = (height + EDGE, width)
    chunks = (march_size, height * width // march_size // LANE, LANE)
    sources = [near(plane), near(edged), near(plane), near(edged)]

    def turn(value, steps):
        return lax.ppermute(
            value, "cross", [(i, (i + steps) % cross_size) for i in range(cross_size)]
        )

    def turns(blocks, sign=1):
        return [blocks[0]] + [turn(blocks[r], sign * r) for r in range(1, cross_size)]

    def along_march(value, steps):
        count = march_size
        return lax.ppermute(
            value, "march", [(i, i + steps) for i in range(count) if 0 <= i + steps < count]
        )

    def across_march(value):
        return lax.all_to_all(value, "march", split_axis=0, concat_axis=0, tiled=True)

    half = width // 2
    blades = [
        lax.all_gather(blade[:, half * i : half * (i + 1)], "march", axis=0, tiled=True)
        for i in range(2)
    ]
    blocks = (cross_index - jnp.arange(cross_size, dtype=jnp.int32) + cross_size) % cross_size
    ids = (blocks[:, None] * height + jnp.arange(height, dtype=jnp.int32)[None, :]).reshape(-1)
    owners = jnp.max(
        jnp.where(ids[:, None] == disc_rows[None, :], owner[None, :], -1), axis=1
    )
    owners = jnp.where(at_disc, owners, -1)
    owners = jnp.broadcast_to(owners[:, None], (cross_size * height, LANE))

    step = (stations, height // STEPS, width)
    turned = range(4, 8)
    near_inflow = stay(inflow)
    upstream = along_march(velocity_guess[-1], 1)
    current = stay(velocity_guess)
    disc = velocity_guess[0].astype(BF16)
    rows = turns([disc] * cross_size)
    source = by_rows(
        source_kernel,
        height,
        sources,
        place,
        (current, upstream, near_inflow),
        cost(1e6, 2 * MIB),
        whole=range(4),
        scratch=[pltpu.VMEM(step, F32)],
    )
    guess, damp, *source = lax.optimization_barrier((velocity_guess, damping, *source))
    decay, scale = by_rows(
        decay_kernel,
        height,
        [far(slab), far(chunks)],
        place,
        (stay(guess), stay(damp)),
        cost(4e6, 3 * MIB),
    )
    for sweep_index in range(SWEEPS):
        arrived = turns(source)
        scales = across_march(scale)
        if sweep_index > 0:
            disc, *arrived = lax.optimization_barrier((disc, *arrived))
            rows = turns([disc] * cross_size)
        solved = pl.pallas_call(
            solve_kernel,
            out_shape=[near(plane)] * cross_size,
            in_specs=[SMEM] + [VMEM] * cross_size + [pl.BlockSpec(memory_space=pltpu.HBM)] * 3,
            out_specs=[VMEM] * cross_size,
            scratch_shapes=[pltpu.VMEM((width, width), F32)]
            + [pltpu.VMEM((width, width), BF16)] * 2
            + [pltpu.VMEM((width, width), F32), pltpu.SemaphoreType.DMA((3,))],
            compiler_params=pltpu.CompilerParams(vmem_limit_bytes=20 * MIB),
            cost_estimate=cost(3 * 8 * width**3, 5 * MIB),
        )(place, *arrived, *tabled)
        rows, solved = lax.optimization_barrier((rows, solved))
        pieces = turns(solved)
        forces = turns(disc_forces(rows, owners, blades), -1)
        (term,) = call(
            laplace_kernel,
            [far(slab)],
            (place, current, arrived[1], arrived[-1]),
            cost(4e6, 2 * MIB),
            scalars=1,
        )
        decay, term = stay(decay), stay(term)
        pressure, lead, force, offset = by_rows(
            offset_kernel,
            height,
            [far(slab), near(plane), far(plane), far(chunks)],
            place,
            (*pieces, *forces, decay, term, near_inflow),
            cost(4e6, 5 * MIB),
        )
        following = along_march(lead, -1)
        (entering,) = call(
            scan_kernel,
            [far(chunks)],
            (stay(scales), across_march(offset)),
            cost(1e5, MIB),
        )
        entering = across_march(entering)
        common = (entering, stay(pressure), stay(following), decay, term, stay(force), near_inflow)
        if sweep_index == SWEEPS - 1:
            (current,) = by_rows(
                last_kernel, height, [far(slab)], place, common, cost(4e6, 5 * MIB)
            )
            return (current, pressure)
        current, decay, scale, disc, *source = by_rows(
            middle_kernel,
            height,
            [far(slab), far(slab), far(chunks), near(plane, BF16)] + sources,
            place,
            common + (stay(damping),),
            cost(8e6, 8 * MIB),
            whole=turned,
            scratch=[pltpu.VMEM(step, F32)],
        )
        current = stay(current)


def solution(mesh):
    in_specs = (
        P("march", "cross", None),
        P("march", "cross", None),
        P("cross", None),
        P(),
        P(),
        P("march", None, "cross"),
    )
    out_specs = (P("march", "cross", None), P("march", "cross", None))
    return jax.shard_map(local, mesh=mesh, in_specs=in_specs, out_specs=out_specs, check_vma=False)
```

time: 229 us -> 253 us (1.10)
  waiting for transfers between devices: 37.6 us -> 91.6 us
  starting transfers between devices: 117 us -> 79.8 us
  Pallas kernels: 30 us -> 59.2 us
  local copies, waits for them, and re-layouts: 25.9 us -> 4.37 us
    all_gather x1 -> x2, waiting for transfers between devices: 0.01 us -> 41.1 us  [local(): lax.all_gather(blade[:, half * i:half * (i + 1)], 'march', axis=0, tiled=...]
    all_to_all x6, starting transfers between devices: 67.9 us -> 33.1 us  [across_march(): lax.all_to_all(value, 'march', split_axis=0, concat_axis=0, tiled=True)]
    pallas_call x14, Pallas kernels: 30 us -> 59.2 us  [the longest x6 25.2 us: by_rows(): pl.pallas_call(kernel, grid_spec=pltpu.PrefetchScalarGridSpec(num_scalar_...]
    unnamed x72 -> x12, local copies, waits for them, and re-layouts: 23.8 us -> 0.02 us
    ppermute x19 -> x3, starting transfers between devices: 27.1 us -> 10.6 us  [along_march(): lax.ppermute(value, 'march', [(i, i + steps) for i in range(count) if 0 <...]
    ppermute x12 -> x24, waiting for transfers between devices: 8.69 us -> 24.7 us  [turn(): lax.ppermute(value, 'cross', [(i, (i + steps) % cross_size) for i in rang...]
    ppermute x12 -> x24, starting transfers between devices: 21.6 us -> 36 us  [turn(): lax.ppermute(value, 'cross', [(i, (i + steps) % cross_size) for i in rang...]
    ppermute x19 -> x3, waiting for transfers between devices: 5.91 us -> 2.7 us  [along_march(): lax.ppermute(value, 'march', [(i, i + steps) for i in range(count) if 0 <...]
  transfers between devices with their start and end apart: 38 -> 35, of which waited for: 8 -> 16; matrix products, arithmetic and copies ran while one was open for 1% -> 1% of each run, Pallas kernels for 12% -> 20%
where the time goes in v2:
time: 253 us; the launch traced here: 250 us
  waiting for transfers between devices  91.6 us (36%)
  starting transfers between devices  79.8 us (32%)
  Pallas kernels  59.2 us (23%)
  between operations  14.3 us (6%)
  local copies, waits for them, and re-layouts  4.37 us (2%)
    all_gather x2, waiting for transfers between devices, local(): lax.all_gather(blade[:, half * i:half * (i + 1)], 'march', axis=0, tiled=...  41.1 us
    ppermute x24, starting transfers between devices, turn(): lax.ppermute(value, 'cross', [(i, (i + steps) % cross_size) for i in rang...  36 us
    all_to_all x6, starting transfers between devices, across_march(): lax.all_to_all(value, 'march', split_axis=0, concat_axis=0, tiled=True)  33.1 us
    pallas_call x6, Pallas kernels, by_rows(): pl.pallas_call(kernel, grid_spec=pltpu.PrefetchScalarGridSpec(num_scalar_...  25.2 us
    ppermute x24, waiting for transfers between devices, turn(): lax.ppermute(value, 'cross', [(i, (i + steps) % cross_size) for i in rang...  24.7 us
    all_to_all x6, waiting for transfers between devices, across_march(): lax.all_to_all(value, 'march', split_axis=0, concat_axis=0, tiled=True)  22.4 us
    pallas_call x2, Pallas kernels, disc_forces(): pl.pallas_call(disc_kernel, grid=(number // per_step,), out_shape=[near((...  13.4 us
    pallas_call x2, Pallas kernels, local(): pl.pallas_call(solve_kernel, out_shape=[near(plane)] * cross_size, in_spe...  11.1 us
  transfers between devices with their start and end apart: 35, of which 16 were waited for; matrix products, arithmetic and copies ran while one was open for 1% of the time, Pallas kernels for 20%

profile of v2, /device:TPU:2, one launch (start us, length us, event | category | flops | bytes accessed | tf_op | source)
XLA Modules:
  0.0 249.6 jit_solution(15150480567910821016)
XLA Ops:
  7.2 1.5 fusion.3
  10.5 1.9 collective-permute-start
  13.4 4.1 %collective-permute-start.3 = (bf16[128,512]{1,0:T(8,128)(2,1)S(1)}, bf16[128,512]{1,0:T(8,128)(2,1)S(1)}, u32[]{:S(2)}, u32[]{:S(2)}) collective-permute-start(bf16[128,512]{1,0:T(8,128)(2,1)S(1)} %fusion.d0), channel_id=1, source_target_pairs={{0,3},{1,0},{2,1},{3,2},{4,7},{5,4},{6,5},{7,6},{8,11},{9,8},{10,9... | collective-permute-start | bytes 393224 | tf_op jit(solution)/shard_map/ppermute | solution.py:404
  17.6 2.7 %collective-permute-done.upstream = f32[128,512]{1,0:T(8,128)S(1)} collective-permute-done((f32[128,512]{1,0:T(8,128)S(1)}, f32[128,512]{1,0:T(8,128)S(1)}, u32[]{:S(2)}, u32[]{:S(2)}) %collective-permute-start) | collective-permute-done | bytes 262176 | tf_op jit(solution)/shard_map/ppermute | solution.py:413
  20.3 2.8 %shard_map.104 = (f32[128,512]{1,0:T(8,128)S(1)}, f32[136,512]{1,0:T(8,128)S(1)}, f32[128,512]{1,0:T(8,128)S(1)}, f32[136,512]{1,0:T(8,128)S(1)}) custom-call(s32[4]{0:T(128)S(1)} %pad_add_fusion.place, f32[4,128,512]{2,1,0:T(8,128)} %current.4, f32[128,512]{1,0:T(8,128)S(1)} %collective-permute-done.upstream, f32[128,512]{1,0:T(8,128)} %inflow.9), custom_call_target="tpu_custom_call" | custom-call | flops 1000000 | bytes 2097152 | tf_op jit(solution)/shard_map/pallas_call | solution.py:340
  23.1 4.0 %collective-permute-start.5 = (f32[128,512]{1,0:T(8,128)S(1)}, f32[128,512]{1,0:T(8,128)S(1)}, u32[]{:S(2)}, u32[]{:S(2)}) collective-permute-start(f32[128,512]{1,0:T(8,128)S(1)} %get-tuple-element.76), channel_id=1, source_target_pairs={{0,2},{1,3},{2,0},{3,1},{4,6},{5,7},{6,4},{7,5},{8,10},{9,11},{10,... | collective-permute-start | bytes 786440 | tf_op jit(solution)/shard_map/ppermute | solution.py:404
  28.1 2.2 collective-permute-start.6
  30.6 3.7 %collective-permute-done.5.x2 = f32[128,512]{1,0:T(8,128)S(1)} collective-permute-done((f32[128,512]{1,0:T(8,128)S(1)}, f32[128,512]{1,0:T(8,128)S(1)}, u32[]{:S(2)}, u32[]{:S(2)}) %collective-permute-start.5) | collective-permute-done | bytes 262176 | tf_op jit(solution)/shard_map/ppermute | solution.py:404
  34.3 1.3 collective-permute-start.1
  35.6 3.3 %collective-permute-done.4.x1.before = f32[136,512]{1,0:T(8,128)S(1)} collective-permute-done((f32[136,512]{1,0:T(8,128)S(1)}, f32[136,512]{1,0:T(8,128)S(1)}, u32[]{:S(2)}, u32[]{:S(2)}) %collective-permute-start.4) | collective-permute-done | bytes 278560 | tf_op jit(solution)/shard_map/ppermute | solution.py:404
  39.0 5.6 %shard_map.106 = (f32[128,512]{1,0:T(8,128)S(1)}, f32[128,512]{1,0:T(8,128)S(1)}, f32[128,512]{1,0:T(8,128)S(1)}, f32[128,512]{1,0:T(8,128)S(1)}) custom-call(s32[4]{0:T(128)S(1)} %pad_add_fusion.place, f32[128,512]{1,0:T(8,128)S(1)} %get-tuple-element.74.x0, f32[136,512]{1,0:T(8,128)S(1)} %collective-permute-done.4.x1.before, ...), custom_call_target="tpu_custom_call" | custom-call | flops 3221225472 | bytes 5242880 | tf_op jit(solution)/shard_map/pallas_call | solution.py:465
  44.6 1.9 collective-permute-start.7
  46.4 4.2 %shard_map.105 = (f32[4,128,512]{2,1,0:T(8,128)}, f32[32,16,128]{2,1,0:T(8,128)}) custom-call(s32[4]{0:T(128)S(1)} %pad_add_fusion.place, f32[4,128,512]{2,1,0:T(8,128)} %current.4, f32[4,128,512]{2,1,0:T(8,128)} %damping.2), custom_call_target="tpu_custom_call" | custom-call | flops 4000000 | bytes 3145728 | tf_op jit(solution)/shard_map/pallas_call | solution.py:340
  50.6 7.0 %all-to-all-start = ((f32[32,16,128]{2,1,0:T(8,128)}), f32[32,16,128]{2,1,0:T(8,128)S(1)}, u32[]{:S(2)}, u32[]{:S(2)}) async-start(f32[32,16,128]{2,1,0:T(8,128)} %get-tuple-element.73), calls=%async_computation | async-start | bytes 524288 | tf_op jit(solution)/shard_map/all_to_all | solution.py:418
  58.7 1.9 collective-permute-start.9
  60.7 41.1 %all-gather.3.cloned.1.call-done.blade_a = bf16[32,256,128]{2,1,0:T(8,128)(2,1)} async-done(((bf16[1,256,128]{2,1,0:T(8,128)(2,1)}), bf16[32,256,128]{2,1,0:T(8,128)(2,1)}) %all-gather.3.cloned.1.call-update) | async-done | bytes 2097168 | tf_op jit(solution)/shard_map/all_gather | solution.py:422
  102.6 6.7 %shard_map.107 = (f32[128,128]{1,0:T(8,128)S(1)}, f32[128,128]{1,0:T(8,128)S(1)}, f32[128,128]{1,0:T(8,128)S(1)}, f32[128,128]{1,0:T(8,128)S(1)}) custom-call(bf16[128,512]{1,0:T(8,128)(2,1)S(1)} %fusion.d0, bf16[128,512]{1,0:T(8,128)(2,1)S(1)} %collective-permute-done.1.d1, bf16[128,512]{1,0:T(8,128)(2,1)S(1)} %collective-permute-done.2.d2, ...), custom_call_target="tpu_custom_call" | custom-call | flops 2147483648 | bytes 5242880 | tf_op jit(solution)/shard_map/pallas_call | solution.py:363
  109.3 3.0 %collective-permute-start.10 = (f32[128,128]{1,0:T(8,128)S(1)}, f32[128,128]{1,0:T(8,128)S(1)}, u32[]{:S(2)}, u32[]{:S(2)}) collective-permute-start(f32[128,128]{1,0:T(8,128)S(1)} %get-tuple-element.91), channel_id=1, source_target_pairs={{0,3},{1,0},{2,1},{3,2},{4,7},{5,4},{6,5},{7,6},{8,11},{9,8},{10,9... | collective-permute-start | bytes 196616 | tf_op jit(solution)/shard_map/ppermute | solution.py:404
  114.0 3.0 %shard_map.108.term = f32[4,128,512]{2,1,0:T(8,128)} custom-call(s32[4]{0:T(128)S(1)} %pad_add_fusion.place, f32[4,128,512]{2,1,0:T(8,128)} %current.4, f32[136,512]{1,0:T(8,128)S(1)} %collective-permute-done.4.x1.before, f32[136,512]{1,0:T(8,128)S(1)} %collective-permute-done.6.x3.after), custom_call_target="tpu_custom_call" | custom-call | flops 4000000 | bytes 2097152 | tf_op jit(solution)/shard_map/pallas_call | solution.py:316
  117.0 1.6 collective-permute-done.11.f2
  119.2 4.4 %shard_map.109 = (f32[4,128,512]{2,1,0:T(8,128)}, f32[128,512]{1,0:T(8,128)S(1)}, f32[128,512]{1,0:T(8,128)}, f32[32,16,128]{2,1,0:T(8,128)}) custom-call(s32[4]{0:T(128)S(1)} %pad_add_fusion.place, f32[128,512]{1,0:T(8,128)S(1)} %get-tuple-element.82.p0, f32[128,512]{1,0:T(8,128)S(1)} %collective-permute-done.7.p1, ...), custom_call_target="tpu_custom_call" | custom-call | flops 4000000 | bytes 5242880 | tf_op jit(solution)/shard_map/pallas_call | solution.py:340
  123.6 5.9 %all-to-all-start.1 = ((f32[32,16,128]{2,1,0:T(8,128)}), f32[32,16,128]{2,1,0:T(8,128)S(1)}, u32[]{:S(2)}, u32[]{:S(2)}) async-start(f32[32,16,128]{2,1,0:T(8,128)} %get-tuple-element.95), calls=%async_computation.1 | async-start | bytes 524288 | tf_op jit(solution)/shard_map/all_to_all | solution.py:418
  129.5 4.3 %collective-permute-start.13 = (f32[128,512]{1,0:T(8,128)S(1)}, f32[128,512]{1,0:T(8,128)S(1)}, u32[]{:S(2)}, u32[]{:S(2)}) collective-permute-start(f32[128,512]{1,0:T(8,128)S(1)} %get-tuple-element.97), channel_id=1, source_target_pairs={{4,0},{8,4},{12,8},{16,12},{20,16},{24,20},{28,24},{32,28},{36,32}... | collective-permute-start | bytes 786440 | tf_op jit(solution)/shard_map/ppermute | solution.py:413
  133.9 3.4 %all-to-all-done.1.offset = f32[32,16,128]{2,1,0:T(8,128)S(1)} async-done(((f32[32,16,128]{2,1,0:T(8,128)}), f32[32,16,128]{2,1,0:T(8,128)S(1)}, u32[]{:S(2)}, u32[]{:S(2)}) %all-to-all-start.1) | async-done | bytes 262176 | tf_op jit(solution)/shard_map/all_to_all | solution.py:418
  137.2 1.7 shard_map.110
  139.0 5.0 %all-to-all-start.2 = ((f32[32,16,128]{2,1,0:T(8,128)}), f32[32,16,128]{2,1,0:T(8,128)S(1)}, u32[]{:S(2)}, u32[]{:S(2)}) async-start(f32[32,16,128]{2,1,0:T(8,128)} %shard_map.110), calls=%async_computation.2 | async-start | bytes 524288 | tf_op jit(solution)/shard_map/all_to_all | solution.py:418
  144.0 7.8 %all-to-all-done.2.entering = f32[32,16,128]{2,1,0:T(8,128)S(1)} async-done(((f32[32,16,128]{2,1,0:T(8,128)}), f32[32,16,128]{2,1,0:T(8,128)S(1)}, u32[]{:S(2)}, u32[]{:S(2)}) %all-to-all-start.2) | async-done | bytes 262176 | tf_op jit(solution)/shard_map/all_to_all | solution.py:418
  151.8 5.2 %shard_map.111 = (f32[4,128,512]{2,1,0:T(8,128)}, f32[4,128,512]{2,1,0:T(8,128)}, f32[32,16,128]{2,1,0:T(8,128)}, bf16[128,512]{1,0:T(8,128)(2,1)S(1)}, f32[128,...) custom-call(s32[4]{0:T(128)S(1)} %pad_add_fusion.place, ...), custom_call_target="tpu_custom_call" | custom-call | flops 8000000 | bytes 8388608 | tf_op jit(solution)/shard_map/pallas_call | solution.py:340
  157.0 3.2 %collective-permute-start.16 = (f32[136,512]{1,0:T(8,128)S(1)}, f32[136,512]{1,0:T(8,128)S(1)}, u32[]{:S(2)}, u32[]{:S(2)}) collective-permute-start(f32[136,512]{1,0:T(8,128)S(1)} %get-tuple-element.104), channel_id=1, source_target_pairs={{0,3},{1,0},{2,1},{3,2},{4,7},{5,4},{6,5},{7,6},{8,11},{9,8},{10,9... | collective-permute-start | bytes 835592 | tf_op jit(solution)/shard_map/ppermute | solution.py:404
  160.2 5.0 %all-to-all-start.3 = ((f32[32,16,128]{2,1,0:T(8,128)}), f32[32,16,128]{2,1,0:T(8,128)S(1)}, u32[]{:S(2)}, u32[]{:S(2)}) async-start(f32[32,16,128]{2,1,0:T(8,128)} %get-tuple-element.99), calls=%async_computation.3 | async-start | bytes 524288 | tf_op jit(solution)/shard_map/all_to_all | solution.py:418
  165.2 6.3 %collective-permute-done.15.x2 = f32[128,512]{1,0:T(8,128)S(1)} collective-permute-done((f32[128,512]{1,0:T(8,128)S(1)}, f32[128,512]{1,0:T(8,128)S(1)}, u32[]{:S(2)}, u32[]{:S(2)}) %collective-permute-start.15) | collective-permute-done | bytes 262176 | tf_op jit(solution)/shard_map/ppermute | solution.py:404
  172.6 3.0 %collective-permute-start.19 = (bf16[128,512]{1,0:T(8,128)(2,1)S(1)}, bf16[128,512]{1,0:T(8,128)(2,1)S(1)}, u32[]{:S(2)}, u32[]{:S(2)}) collective-permute-start(bf16[128,512]{1,0:T(8,128)(2,1)S(1)} %get-tuple-element.118.d0), channel_id=1, source_target_pairs={{0,3},{1,0},{2,1},{3,2},{4,7},{5,4},{6,5},{7,6},{8,11},{9,8},{10,9... | collective-permute-start | bytes 393224 | tf_op jit(solution)/shard_map/ppermute | solution.py:404
  176.5 5.6 %shard_map.112 = (f32[128,512]{1,0:T(8,128)S(1)}, f32[128,512]{1,0:T(8,128)S(1)}, f32[128,512]{1,0:T(8,128)S(1)}, f32[128,512]{1,0:T(8,128)S(1)}) custom-call(s32[4]{0:T(128)S(1)} %pad_add_fusion.place, f32[128,512]{1,0:T(8,128)S(1)} %get-tuple-element.106.x0, f32[136,512]{1,0:T(8,128)S(1)} %collective-permute-done.14.x1.before, ...), custom_call_target="tpu_custom_call" | custom-call | flops 3221225472 | bytes 5242880 | tf_op jit(solution)/shard_map/pallas_call | solution.py:465
  184.7 1.5 collective-permute-start.21
  187.5 6.7 %shard_map.113 = (f32[128,128]{1,0:T(8,128)S(1)}, f32[128,128]{1,0:T(8,128)S(1)}, f32[128,128]{1,0:T(8,128)S(1)}, f32[128,128]{1,0:T(8,128)S(1)}) custom-call(bf16[128,512]{1,0:T(8,128)(2,1)S(1)} %get-tuple-element.118.d0, bf16[128,512]{1,0:T(8,128)(2,1)S(1)} %collective-permute-done.17.d1, bf16[128,512]{1,0:T(8,128)(2,1)S(1)} %collective-permute-done.18.d2, ...), custom_call_target="tpu_custom_call" | custom-call | flops 2147483648 | bytes 5242880 | tf_op jit(solution)/shard_map/pallas_call | solution.py:363
  194.2 1.4 collective-permute-start.23
  195.6 1.5 collective-permute-start.24
  197.1 3.9 %collective-permute-done.23.f1 = f32[128,128]{1,0:T(8,128)S(1)} collective-permute-done((f32[128,128]{1,0:T(8,128)S(1)}, f32[128,128]{1,0:T(8,128)S(1)}, u32[]{:S(2)}, u32[]{:S(2)}) %collective-permute-start.23) | collective-permute-done | bytes 65568 | tf_op jit(solution)/shard_map/ppermute | solution.py:404
  201.3 3.0 %shard_map.114.term = f32[4,128,512]{2,1,0:T(8,128)} custom-call(s32[4]{0:T(128)S(1)} %pad_add_fusion.place, f32[4,128,512]{2,1,0:T(8,128)} %get-tuple-element.127.current, f32[136,512]{1,0:T(8,128)S(1)} %collective-permute-done.14.x1.before, f32[136,512]{1,0:T(8,128)S(1)} %collective-permute-done.16.x3.after), custom_call_target="tpu_custom_call" | custom-call | flops 4000000 | bytes 2097152 | tf_op jit(solution)/shard_map/pallas_call | solution.py:316
  204.3 2.2 collective-permute-done.25.f3
  206.5 4.3 %shard_map.115 = (f32[4,128,512]{2,1,0:T(8,128)}, f32[128,512]{1,0:T(8,128)S(1)}, f32[128,512]{1,0:T(8,128)}, f32[32,16,128]{2,1,0:T(8,128)}) custom-call(s32[4]{0:T(128)S(1)} %pad_add_fusion.place, f32[128,512]{1,0:T(8,128)S(1)} %get-tuple-element.114.p0, f32[128,512]{1,0:T(8,128)S(1)} %collective-permute-done.20.p1, ...), custom_call_target="tpu_custom_call" | custom-call | flops 4000000 | bytes 5242880 | tf_op jit(solution)/shard_map/pallas_call | solution.py:340
  210.8 5.2 %all-to-all-start.4 = ((f32[32,16,128]{2,1,0:T(8,128)}), f32[32,16,128]{2,1,0:T(8,128)S(1)}, u32[]{:S(2)}, u32[]{:S(2)}) async-start(f32[32,16,128]{2,1,0:T(8,128)} %get-tuple-element.128), calls=%async_computation.4 | async-start | bytes 524288 | tf_op jit(solution)/shard_map/all_to_all | solution.py:418
  216.0 4.3 %collective-permute-start.26 = (f32[128,512]{1,0:T(8,128)S(1)}, f32[128,512]{1,0:T(8,128)S(1)}, u32[]{:S(2)}, u32[]{:S(2)}) collective-permute-start(f32[128,512]{1,0:T(8,128)S(1)} %get-tuple-element.130), channel_id=1, source_target_pairs={{4,0},{8,4},{12,8},{16,12},{20,16},{24,20},{28,24},{32,28},{36,32}... | collective-permute-start | bytes 786440 | tf_op jit(solution)/shard_map/ppermute | solution.py:413
  220.3 3.4 %all-to-all-done.4.offset = f32[32,16,128]{2,1,0:T(8,128)S(1)} async-done(((f32[32,16,128]{2,1,0:T(8,128)}), f32[32,16,128]{2,1,0:T(8,128)S(1)}, u32[]{:S(2)}, u32[]{:S(2)}) %all-to-all-start.4) | async-done | bytes 262176 | tf_op jit(solution)/shard_map/all_to_all | solution.py:418
  223.8 1.7 shard_map.116
  225.5 5.0 %all-to-all-start.5 = ((f32[32,16,128]{2,1,0:T(8,128)}), f32[32,16,128]{2,1,0:T(8,128)S(1)}, u32[]{:S(2)}, u32[]{:S(2)}) async-start(f32[32,16,128]{2,1,0:T(8,128)} %shard_map.116), calls=%async_computation.5 | async-start | bytes 524288 | tf_op jit(solution)/shard_map/all_to_all | solution.py:418
  230.6 7.8 %all-to-all-done.5.entering = f32[32,16,128]{2,1,0:T(8,128)S(1)} async-done(((f32[32,16,128]{2,1,0:T(8,128)}), f32[32,16,128]{2,1,0:T(8,128)S(1)}, u32[]{:S(2)}, u32[]{:S(2)}) %all-to-all-start.5) | async-done | bytes 262176 | tf_op jit(solution)/shard_map/all_to_all | solution.py:418
  238.3 4.4 %shard_map.117 = f32[4,128,512]{2,1,0:T(8,128)} custom-call(s32[4]{0:T(128)S(1)} %pad_add_fusion.place, f32[32,16,128]{2,1,0:T(8,128)S(1)} %all-to-all-done.5.entering, f32[4,128,512]{2,1,0:T(8,128)} %get-tuple-element.66.pressure, f32[128,512]{1,0:T(8,128)} %copy-done.3, f32[4,128,512]{2,1,0:T(8,128)} %get-tuple-element.126.decay, ...), custom_call_target="tpu_custom_call" | custom-call | flops 4000000 | bytes 5242880 | tf_op jit(solution)/shard_map/pallas_call | solution.py:340
  (59 shorter events, 14.8 us)
Async XLA Ops:
  7.2 23.2 %copy-start.4 = (s32[256]{0:T(256)S(1)}, s32[256]{0:T(256)}, u32[]{:S(2)}) copy-start(s32[256]{0:T(256)} %param.13) | copy-start | bytes 3076
  7.2 23.2 %copy-start.5 = (s32[256]{0:T(256)S(1)}, s32[256]{0:T(256)}, u32[]{:S(2)}) copy-start(s32[256]{0:T(256)} %param.12) | copy-start | bytes 3076
  7.2 53.5 %all-gather.5.cloned.1.call-start = ((), (), s32[]{:S(2)}) async-start(), calls=%async_computation.7 | async-start | bytes 2162688 | tf_op jit(solution)/shard_map/all_gather | solution.py:422
  8.8 93.0 %all-gather.3.cloned.1.call-start = ((), (), s32[]{:S(2)}) async-start(), calls=%async_computation.6 | async-start | bytes 2162688 | tf_op jit(solution)/shard_map/all_gather | solution.py:422
  10.5 9.8 %collective-permute-start = (f32[128,512]{1,0:T(8,128)S(1)}, f32[128,512]{1,0:T(8,128)S(1)}, u32[]{:S(2)}, u32[]{:S(2)}) collective-permute-start(f32[128,512]{1,0:T(8,128)S(1)} %slice_bitcast_fusion), channel_id=1, source_target_pairs={{0,4},{4,8},{8,12},{12,16},{16,20},{20,24},{24,28},{28,32},{32,36}... | collective-permute-start | bytes 786440 | tf_op jit(solution)/shard_map/ppermute | solution.py:413
  13.4 31.1 %collective-permute-start.3 = (bf16[128,512]{1,0:T(8,128)(2,1)S(1)}, bf16[128,512]{1,0:T(8,128)(2,1)S(1)}, u32[]{:S(2)}, u32[]{:S(2)}) collective-permute-start(bf16[128,512]{1,0:T(8,128)(2,1)S(1)} %fusion.d0), channel_id=1, source_target_pairs={{0,3},{1,0},{2,1},{3,2},{4,7},{5,4},{6,5},{7,6},{8,11},{9,8},{10,9... | collective-permute-start | bytes 393224 | tf_op jit(solution)/shard_map/ppermute | solution.py:404
  17.5 27.0 %collective-permute-start.2 = (bf16[128,512]{1,0:T(8,128)(2,1)S(1)}, bf16[128,512]{1,0:T(8,128)(2,1)S(1)}, u32[]{:S(2)}, u32[]{:S(2)}) collective-permute-start(bf16[128,512]{1,0:T(8,128)(2,1)S(1)} %fusion.d0), channel_id=1, source_target_pairs={{0,2},{1,3},{2,0},{3,1},{4,6},{5,7},{6,4},{7,5},{8,10},{9,11},{10,... | collective-permute-start | bytes 393224 | tf_op jit(solution)/shard_map/ppermute | solution.py:404
  23.1 11.2 %collective-permute-start.5 = (f32[128,512]{1,0:T(8,128)S(1)}, f32[128,512]{1,0:T(8,128)S(1)}, u32[]{:S(2)}, u32[]{:S(2)}) collective-permute-start(f32[128,512]{1,0:T(8,128)S(1)} %get-tuple-element.76), channel_id=1, source_target_pairs={{0,2},{1,3},{2,0},{3,1},{4,6},{5,7},{6,4},{7,5},{8,10},{9,11},{10,... | collective-permute-start | bytes 786440 | tf_op jit(solution)/shard_map/ppermute | solution.py:404
  27.0 11.9 %collective-permute-start.4 = (f32[136,512]{1,0:T(8,128)S(1)}, f32[136,512]{1,0:T(8,128)S(1)}, u32[]{:S(2)}, u32[]{:S(2)}) collective-permute-start(f32[136,512]{1,0:T(8,128)S(1)} %get-tuple-element.75), channel_id=1, source_target_pairs={{0,1},{1,2},{2,3},{3,0},{4,5},{5,6},{6,7},{7,4},{8,9},{9,10},{10,1... | collective-permute-start | bytes 835592 | tf_op jit(solution)/shard_map/ppermute | solution.py:404
  28.1 10.9 %collective-permute-start.6 = (f32[136,512]{1,0:T(8,128)S(1)}, f32[136,512]{1,0:T(8,128)S(1)}, u32[]{:S(2)}, u32[]{:S(2)}) collective-permute-start(f32[136,512]{1,0:T(8,128)S(1)} %get-tuple-element.77), channel_id=1, source_target_pairs={{0,3},{1,0},{2,1},{3,2},{4,7},{5,4},{6,5},{7,6},{8,11},{9,8},{10,9... | collective-permute-start | bytes 835592 | tf_op jit(solution)/shard_map/ppermute | solution.py:404
  34.3 10.3 %collective-permute-start.1 = (bf16[128,512]{1,0:T(8,128)(2,1)S(1)}, bf16[128,512]{1,0:T(8,128)(2,1)S(1)}, u32[]{:S(2)}, u32[]{:S(2)}) collective-permute-start(bf16[128,512]{1,0:T(8,128)(2,1)S(1)} %fusion.d0), channel_id=1, source_target_pairs={{0,1},{1,2},{2,3},{3,0},{4,5},{5,6},{6,7},{7,4},{8,9},{9,10},{10,1... | collective-permute-start | bytes 393224 | tf_op jit(solution)/shard_map/ppermute | solution.py:404
  44.6 68.5 %collective-permute-start.7 = (f32[128,512]{1,0:T(8,128)S(1)}, f32[128,512]{1,0:T(8,128)S(1)}, u32[]{:S(2)}, u32[]{:S(2)}) collective-permute-start(f32[128,512]{1,0:T(8,128)S(1)} %get-tuple-element.83), channel_id=1, source_target_pairs={{0,1},{1,2},{2,3},{3,0},{4,5},{5,6},{6,7},{7,4},{8,9},{9,10},{10,1... | collective-permute-start | bytes 786440 | tf_op jit(solution)/shard_map/ppermute | solution.py:404
  50.6 73.0 %all-to-all-start = ((f32[32,16,128]{2,1,0:T(8,128)}), f32[32,16,128]{2,1,0:T(8,128)S(1)}, u32[]{:S(2)}, u32[]{:S(2)}) async-start(f32[32,16,128]{2,1,0:T(8,128)} %get-tuple-element.73), calls=%async_computation | async-start | bytes 524288 | tf_op jit(solution)/shard_map/all_to_all | solution.py:418
  57.6 59.4 %collective-permute-start.8 = (f32[128,512]{1,0:T(8,128)S(1)}, f32[128,512]{1,0:T(8,128)S(1)}, u32[]{:S(2)}, u32[]{:S(2)}) collective-permute-start(f32[128,512]{1,0:T(8,128)S(1)} %get-tuple-element.84), channel_id=1, source_target_pairs={{0,2},{1,3},{2,0},{3,1},{4,6},{5,7},{6,4},{7,5},{8,10},{9,11},{10,... | collective-permute-start | bytes 786440 | tf_op jit(solution)/shard_map/ppermute | solution.py:404
  58.7 58.3 %collective-permute-start.9 = (f32[128,512]{1,0:T(8,128)S(1)}, f32[128,512]{1,0:T(8,128)S(1)}, u32[]{:S(2)}, u32[]{:S(2)}) collective-permute-start(f32[128,512]{1,0:T(8,128)S(1)} %get-tuple-element.85), channel_id=1, source_target_pairs={{0,3},{1,0},{2,1},{3,2},{4,7},{5,4},{6,5},{7,6},{8,11},{9,8},{10,9... | collective-permute-start | bytes 786440 | tf_op jit(solution)/shard_map/ppermute | solution.py:404
  109.3 7.7 %collective-permute-start.10 = (f32[128,128]{1,0:T(8,128)S(1)}, f32[128,128]{1,0:T(8,128)S(1)}, u32[]{:S(2)}, u32[]{:S(2)}) collective-permute-start(f32[128,128]{1,0:T(8,128)S(1)} %get-tuple-element.91), channel_id=1, source_target_pairs={{0,3},{1,0},{2,1},{3,2},{4,7},{5,4},{6,5},{7,6},{8,11},{9,8},{10,9... | collective-permute-start | bytes 196616 | tf_op jit(solution)/shard_map/ppermute | solution.py:404
  112.4 6.2 %collective-permute-start.11 = (f32[128,128]{1,0:T(8,128)S(1)}, f32[128,128]{1,0:T(8,128)S(1)}, u32[]{:S(2)}, u32[]{:S(2)}) collective-permute-start(f32[128,128]{1,0:T(8,128)S(1)} %get-tuple-element.92), channel_id=1, source_target_pairs={{0,2},{1,3},{2,0},{3,1},{4,6},{5,7},{6,4},{7,5},{8,10},{9,11},{10,... | collective-permute-start | bytes 196616 | tf_op jit(solution)/shard_map/ppermute | solution.py:404
  113.0 6.2 %collective-permute-start.12 = (f32[128,128]{1,0:T(8,128)S(1)}, f32[128,128]{1,0:T(8,128)S(1)}, u32[]{:S(2)}, u32[]{:S(2)}) collective-permute-start(f32[128,128]{1,0:T(8,128)S(1)} %get-tuple-element.93), channel_id=1, source_target_pairs={{0,1},{1,2},{2,3},{3,0},{4,5},{5,6},{6,7},{7,4},{8,9},{9,10},{10,1... | collective-permute-start | bytes 196616 | tf_op jit(solution)/shard_map/ppermute | solution.py:404
  123.6 13.6 %copy-start.1 = (f32[32,16,128]{2,1,0:T(8,128)}, f32[32,16,128]{2,1,0:T(8,128)S(1)}, u32[]{:S(2)}) copy-start(f32[32,16,128]{2,1,0:T(8,128)S(1)} %all-to-all-done.scale) | copy-start | bytes 786436
  123.6 13.6 %all-to-all-start.1 = ((f32[32,16,128]{2,1,0:T(8,128)}), f32[32,16,128]{2,1,0:T(8,128)S(1)}, u32[]{:S(2)}, u32[]{:S(2)}) async-start(f32[32,16,128]{2,1,0:T(8,128)} %get-tuple-element.95), calls=%async_computation.1 | async-start | bytes 524288 | tf_op jit(solution)/shard_map/all_to_all | solution.py:418
  129.5 14.5 %collective-permute-start.13 = (f32[128,512]{1,0:T(8,128)S(1)}, f32[128,512]{1,0:T(8,128)S(1)}, u32[]{:S(2)}, u32[]{:S(2)}) collective-permute-start(f32[128,512]{1,0:T(8,128)S(1)} %get-tuple-element.97), channel_id=1, source_target_pairs={{4,0},{8,4},{12,8},{16,12},{20,16},{24,20},{28,24},{32,28},{36,32}... | collective-permute-start | bytes 786440 | tf_op jit(solution)/shard_map/ppermute | solution.py:413
  139.0 12.8 %all-to-all-start.2 = ((f32[32,16,128]{2,1,0:T(8,128)}), f32[32,16,128]{2,1,0:T(8,128)S(1)}, u32[]{:S(2)}, u32[]{:S(2)}) async-start(f32[32,16,128]{2,1,0:T(8,128)} %shard_map.110), calls=%async_computation.2 | async-start | bytes 524288 | tf_op jit(solution)/shard_map/all_to_all | solution.py:418
  144.0 7.8 %copy-start.2 = (f32[128,512]{1,0:T(8,128)}, f32[128,512]{1,0:T(8,128)S(1)}, u32[]{:S(2)}) copy-start(f32[128,512]{1,0:T(8,128)S(1)} %collective-permute-done.13.following) | copy-start | bytes 786436
  157.0 15.7 %collective-permute-start.14 = (f32[136,512]{1,0:T(8,128)S(1)}, f32[136,512]{1,0:T(8,128)S(1)}, u32[]{:S(2)}, u32[]{:S(2)}) collective-permute-start(f32[136,512]{1,0:T(8,128)S(1)} %get-tuple-element.102), channel_id=1, source_target_pairs={{0,1},{1,2},{2,3},{3,0},{4,5},{5,6},{6,7},{7,4},{8,9},{9,10},{10,1... | collective-permute-start | bytes 835592 | tf_op jit(solution)/shard_map/ppermute | solution.py:404
  157.0 15.7 %collective-permute-start.16 = (f32[136,512]{1,0:T(8,128)S(1)}, f32[136,512]{1,0:T(8,128)S(1)}, u32[]{:S(2)}, u32[]{:S(2)}) collective-permute-start(f32[136,512]{1,0:T(8,128)S(1)} %get-tuple-element.104), channel_id=1, source_target_pairs={{0,3},{1,0},{2,1},{3,2},{4,7},{5,4},{6,5},{7,6},{8,11},{9,8},{10,9... | collective-permute-start | bytes 835592 | tf_op jit(solution)/shard_map/ppermute | solution.py:404
  160.2 11.3 %collective-permute-start.15 = (f32[128,512]{1,0:T(8,128)S(1)}, f32[128,512]{1,0:T(8,128)S(1)}, u32[]{:S(2)}, u32[]{:S(2)}) collective-permute-start(f32[128,512]{1,0:T(8,128)S(1)} %get-tuple-element.103), channel_id=1, source_target_pairs={{0,2},{1,3},{2,0},{3,1},{4,6},{5,7},{6,4},{7,5},{8,10},{9,11},{10,... | collective-permute-start | bytes 786440 | tf_op jit(solution)/shard_map/ppermute | solution.py:404
  160.2 50.6 %all-to-all-start.3 = ((f32[32,16,128]{2,1,0:T(8,128)}), f32[32,16,128]{2,1,0:T(8,128)S(1)}, u32[]{:S(2)}, u32[]{:S(2)}) async-start(f32[32,16,128]{2,1,0:T(8,128)} %get-tuple-element.99), calls=%async_computation.3 | async-start | bytes 524288 | tf_op jit(solution)/shard_map/all_to_all | solution.py:418
  172.6 9.4 %collective-permute-start.19 = (bf16[128,512]{1,0:T(8,128)(2,1)S(1)}, bf16[128,512]{1,0:T(8,128)(2,1)S(1)}, u32[]{:S(2)}, u32[]{:S(2)}) collective-permute-start(bf16[128,512]{1,0:T(8,128)(2,1)S(1)} %get-tuple-element.118.d0), channel_id=1, source_target_pairs={{0,3},{1,0},{2,1},{3,2},{4,7},{5,4},{6,5},{7,6},{8,11},{9,8},{10,9... | collective-permute-start | bytes 393224 | tf_op jit(solution)/shard_map/ppermute | solution.py:404
  175.6 7.3 %collective-permute-start.18 = (bf16[128,512]{1,0:T(8,128)(2,1)S(1)}, bf16[128,512]{1,0:T(8,128)(2,1)S(1)}, u32[]{:S(2)}, u32[]{:S(2)}) collective-permute-start(bf16[128,512]{1,0:T(8,128)(2,1)S(1)} %get-tuple-element.118.d0), channel_id=1, source_target_pairs={{0,2},{1,3},{2,0},{3,1},{4,6},{5,7},{6,4},{7,5},{8,10},{9,11},{10,... | collective-permute-start | bytes 393224 | tf_op jit(solution)/shard_map/ppermute | solution.py:404
  175.6 8.3 %collective-permute-start.17 = (bf16[128,512]{1,0:T(8,128)(2,1)S(1)}, bf16[128,512]{1,0:T(8,128)(2,1)S(1)}, u32[]{:S(2)}, u32[]{:S(2)}) collective-permute-start(bf16[128,512]{1,0:T(8,128)(2,1)S(1)} %get-tuple-element.118.d0), channel_id=1, source_target_pairs={{0,1},{1,2},{2,3},{3,0},{4,5},{5,6},{6,7},{7,4},{8,9},{9,10},{10,1... | collective-permute-start | bytes 393224 | tf_op jit(solution)/shard_map/ppermute | solution.py:404
  183.9 22.6 %collective-permute-start.20 = (f32[128,512]{1,0:T(8,128)S(1)}, f32[128,512]{1,0:T(8,128)S(1)}, u32[]{:S(2)}, u32[]{:S(2)}) collective-permute-start(f32[128,512]{1,0:T(8,128)S(1)} %get-tuple-element.115), channel_id=1, source_target_pairs={{0,1},{1,2},{2,3},{3,0},{4,5},{5,6},{6,7},{7,4},{8,9},{9,10},{10,1... | collective-permute-start | bytes 786440 | tf_op jit(solution)/shard_map/ppermute | solution.py:404
  184.7 21.8 %collective-permute-start.21 = (f32[128,512]{1,0:T(8,128)S(1)}, f32[128,512]{1,0:T(8,128)S(1)}, u32[]{:S(2)}, u32[]{:S(2)}) collective-permute-start(f32[128,512]{1,0:T(8,128)S(1)} %get-tuple-element.116), channel_id=1, source_target_pairs={{0,2},{1,3},{2,0},{3,1},{4,6},{5,7},{6,4},{7,5},{8,10},{9,11},{10,... | collective-permute-start | bytes 786440 | tf_op jit(solution)/shard_map/ppermute | solution.py:404
  186.2 20.3 %collective-permute-start.22 = (f32[128,512]{1,0:T(8,128)S(1)}, f32[128,512]{1,0:T(8,128)S(1)}, u32[]{:S(2)}, u32[]{:S(2)}) collective-permute-start(f32[128,512]{1,0:T(8,128)S(1)} %get-tuple-element.117), channel_id=1, source_target_pairs={{0,3},{1,0},{2,1},{3,2},{4,7},{5,4},{6,5},{7,6},{8,11},{9,8},{10,9... | collective-permute-start | bytes 786440 | tf_op jit(solution)/shard_map/ppermute | solution.py:404
  194.2 6.8 %collective-permute-start.23 = (f32[128,128]{1,0:T(8,128)S(1)}, f32[128,128]{1,0:T(8,128)S(1)}, u32[]{:S(2)}, u32[]{:S(2)}) collective-permute-start(f32[128,128]{1,0:T(8,128)S(1)} %get-tuple-element.123), channel_id=1, source_target_pairs={{0,3},{1,0},{2,1},{3,2},{4,7},{5,4},{6,5},{7,6},{8,11},{9,8},{10,9... | collective-permute-start | bytes 196616 | tf_op jit(solution)/shard_map/ppermute | solution.py:404
  195.6 8.7 %collective-permute-start.24 = (f32[128,128]{1,0:T(8,128)S(1)}, f32[128,128]{1,0:T(8,128)S(1)}, u32[]{:S(2)}, u32[]{:S(2)}) collective-permute-start(f32[128,128]{1,0:T(8,128)S(1)} %get-tuple-element.124), channel_id=1, source_target_pairs={{0,2},{1,3},{2,0},{3,1},{4,6},{5,7},{6,4},{7,5},{8,10},{9,11},{10,... | collective-permute-start | bytes 196616 | tf_op jit(solution)/shard_map/ppermute | solution.py:404
  201.0 5.5 %collective-permute-start.25 = (f32[128,128]{1,0:T(8,128)S(1)}, f32[128,128]{1,0:T(8,128)S(1)}, u32[]{:S(2)}, u32[]{:S(2)}) collective-permute-start(f32[128,128]{1,0:T(8,128)S(1)} %get-tuple-element.125), channel_id=1, source_target_pairs={{0,1},{1,2},{2,3},{3,0},{4,5},{5,6},{6,7},{7,4},{8,9},{9,10},{10,1... | collective-permute-start | bytes 196616 | tf_op jit(solution)/shard_map/ppermute | solution.py:404
  210.8 13.0 %copy-start = (f32[32,16,128]{2,1,0:T(8,128)}, f32[32,16,128]{2,1,0:T(8,128)S(1)}, u32[]{:S(2)}) copy-start(f32[32,16,128]{2,1,0:T(8,128)S(1)} %all-to-all-done.3.scale) | copy-start | bytes 786436
  210.8 13.0 %all-to-all-start.4 = ((f32[32,16,128]{2,1,0:T(8,128)}), f32[32,16,128]{2,1,0:T(8,128)S(1)}, u32[]{:S(2)}, u32[]{:S(2)}) async-start(f32[32,16,128]{2,1,0:T(8,128)} %get-tuple-element.128), calls=%async_computation.4 | async-start | bytes 524288 | tf_op jit(solution)/shard_map/all_to_all | solution.py:418
  216.0 14.5 %collective-permute-start.26 = (f32[128,512]{1,0:T(8,128)S(1)}, f32[128,512]{1,0:T(8,128)S(1)}, u32[]{:S(2)}, u32[]{:S(2)}) collective-permute-start(f32[128,512]{1,0:T(8,128)S(1)} %get-tuple-element.130), channel_id=1, source_target_pairs={{4,0},{8,4},{12,8},{16,12},{20,16},{24,20},{28,24},{32,28},{36,32}... | collective-permute-start | bytes 786440 | tf_op jit(solution)/shard_map/ppermute | solution.py:413
  225.5 12.8 %all-to-all-start.5 = ((f32[32,16,128]{2,1,0:T(8,128)}), f32[32,16,128]{2,1,0:T(8,128)S(1)}, u32[]{:S(2)}, u32[]{:S(2)}) async-start(f32[32,16,128]{2,1,0:T(8,128)} %shard_map.116), calls=%async_computation.5 | async-start | bytes 524288 | tf_op jit(solution)/shard_map/all_to_all | solution.py:418
  230.6 7.8 %copy-start.3 = (f32[128,512]{1,0:T(8,128)}, f32[128,512]{1,0:T(8,128)S(1)}, u32[]{:S(2)}) copy-start(f32[128,512]{1,0:T(8,128)S(1)} %collective-permute-done.26.following) | copy-start | bytes 786436
Sparse Core Ops, SparseCore 0:
  10.9 45.6 all-gather.4
  58.8 42.9 all-gather.2

commit v3 on v2

--- a/solution.py
+++ b/solution.py
@@ -110,15 +110,20 @@
         to_chunks(scale, g, product)
 
 
-def laplace_kernel(place, current, before, after, term):
+def weights_kernel(
+    place, current, before, after, decay, inflow, term, weights, base, force_weight
+):
     stations, height, width = current.shape
+    first = place[1] == 1
     above = jnp.where(place[2] == 1, 0.0, before[height : height + EDGE])
     below = jnp.where(place[3] == 1, 0.0, after[height : height + EDGE])
     lane = lax.broadcasted_iota(jnp.int32, (SUB, width), 1)
-    for s in range(stations):
-        for g, rows in groups(height):
+    for g, rows in groups(height):
+        lo, hi = SUB * g, SUB * g + SUB
+        total = jnp.zeros((SUB, width), F32)
+        factor = None
+        for s in reversed(range(stations)):
             here = current[s, rows]
-            lo, hi = SUB * g, SUB * g + SUB
             if g == 0:
                 up = jnp.concatenate([above[s : s + 1], current[s, 0 : SUB - 1]], axis=0)
             else:
@@ -129,13 +134,25 @@
                 down = current[s, lo + 1 : hi + 1]
             left = jnp.where(lane == 0, 0.0, pltpu.roll(here, 1, 1))
             right = jnp.where(lane == width - 1, 0.0, pltpu.roll(here, width - 1, 1))
-            term[s, rows] = VISCOSITY * (up + down + left + right - 4.0 * here)
-
-
-def solve_kernel(
-    place, x0, x1, x2, x3, high_far, low_far, inverse_far, p0, p1, p2, p3,
-    plane, high, low, inverse, arrivals,
-):
+            t = VISCOSITY * (up + down + left + right - 4.0 * here)
+            term[s, rows] = t
+            d = decay[s, rows]
+            if factor is None:
+                total, weight, factor = t, 1.0 - d, d
+            else:
+                if s == 0:
+                    force_weight[rows] = factor
+                total, weight, factor = total + factor * t, factor * (1.0 - d), factor * d
+            if s == 0:
+                entry = jnp.where(first, factor, 0.0)
+                weight = weight + entry
+                total = total + entry * inflow[rows]
+            weights[s, rows] = weight
+        base[rows] = total
+
+
+def solve_kernel(place, x0, x1, x2, x3, high_far, low_far, inverse_far, *rest):
+    *forces, p0, p1, p2, p3, plane, high, low, inverse, arrivals = rest
     c = place[0]
     copies = [
         pltpu.make_async_copy(far_ref, ref, arrivals.at[i])
@@ -147,7 +164,7 @@
         copy.start()
     inputs, outputs = (x0, x1, x2, x3), (p0, p1, p2, p3)
     count = len(inputs)
-    height = p0.shape[0]
+    height = x0.shape[0]
     for r, ref in enumerate(inputs):
         b = lax.rem(c - r + count, count)
         plane[pl.ds(pl.multiple_of(b * height, height), height), :] = ref[0:height]
@@ -175,10 +192,18 @@
     plane[...] = right(left(modes))
     for r, ref in enumerate(outputs):
         b = lax.rem(c + r, count)
-        ref[...] = plane[pl.ds(pl.multiple_of(b * height, height), height), :]
-
-
-def disc_kernel(d0, d1, d2, d3, owners, blade_a, blade_b, f0, f1, f2, f3, plane, total):
+        ref[0:height] = plane[pl.ds(pl.multiple_of(b * height, height), height), :]
+    if forces:
+        extra = p0.shape[0] - height
+        for r, ref in enumerate(outputs):
+            for q in range(height // extra):
+                ref[height : height + extra, LANE * q : LANE * (q + 1)] = forces[-r][
+                    extra * q : extra * (q + 1)
+                ]
+
+
+def disc_kernel(d0, d1, d2, d3, owners, *rest):
+    *blades, f0, f1, f2, f3, plane, total = rest
     step = pl.program_id(0)
     height = d0.shape[0]
 
@@ -188,12 +213,12 @@
             plane[height * r : height * (r + 1)] = ref[...]
         total[...] = jnp.zeros_like(total)
 
-    per_step = blade_a.shape[0]
+    per_step = blades[0].shape[0]
     for i in range(0, per_step, 2):
         pair = jnp.concatenate(
             [
-                jnp.concatenate([blade_a[i], blade_b[i]], axis=0),
-                jnp.concatenate([blade_a[i + 1], blade_b[i + 1]], axis=0),
+                jnp.concatenate([blade[j] for blade in blades], axis=0)
+                for j in (i, i + 1)
             ],
             axis=1,
         )
@@ -208,31 +233,54 @@
             ref[...] = jnp.tanh(total[height * r : height * (r + 1)])
 
 
-def offset_kernel(
-    place, p0, p1, p2, p3, f0, f1, f2, f3, decay, term, inflow, pressure, lead, force, offset
-):
+def offset_kernel(place, *rest):
     c = place[0]
-    first = place[1]
-    pieces, forces = (p0, p1, p2, p3), (f0, f1, f2, f3)
-    count = len(pieces)
-    width = inflow.shape[1] // count
+    pieces = rest[:4]
+    *forces, weights, base, force_weight, lead, lead_far, force, offset = rest[4:]
+    count, height, full = weights.shape
+    width = full // count
     for r in range(count):
-        s = lax.rem(c - r + count, count)
-        pressure[s] = pieces[r][...]
-        b = lax.rem(c + r, count)
-        force[:, pl.ds(pl.multiple_of(b * width, width), width)] = forces[r][...]
-    for g, rows in groups(inflow.shape[0]):
-        start = pressure[0, rows]
-        lead[rows] = start
-        state = jnp.where(first == 1, inflow[rows] + start, 0.0)
+        b = lax.rem(c + r if forces else c - r + count, count)
+        lanes = pl.ds(pl.multiple_of(b * width, width), width)
+        if forces:
+            force[:, lanes] = forces[r][...]
+        else:
+            extra = pieces[r].shape[0] - height
+            for q in range(height // extra):
+                force[extra * q : extra * (q + 1), lanes] = pieces[r][
+                    height : height + extra, width * q : width * (q + 1)
+                ]
+
+    for r in range(count):
+        @pl.when(c == r)
+        def _():
+            lead[...] = pieces[r][0:height]
+            lead_far[...] = pieces[r][0:height]
+
+    for g, rows in groups(height):
+        state = base[rows] + force_weight[rows] * force[rows]
+        for r in range(count):
+            s = lax.rem(c - r + count, count)
+            state = state + weights[s, rows] * pieces[r][rows]
+        to_chunks(offset, g, state)
+
+
+def change_kernel(place, p0, p1, p2, p3, term, force, change, pressure):
+    c = place[0]
+    pieces = (p0, p1, p2, p3)
+    count, height, _ = term.shape
+    for r in range(count):
+        pressure[lax.rem(c - r + count, count)] = pieces[r][...]
+    for _, rows in groups(height):
+        here = pressure[0, rows]
         for s in range(count):
-            p = pressure[s, rows]
-            t = term[s, rows]
+            value = term[s, rows] + here
             if s == 0:
-                t = t + force[rows]
-            d = decay[s, rows]
-            state = d * state + (t + (1.0 - d) * p)
-        to_chunks(offset, g, state)
+                value = value + force[rows]
+            if s < count - 1:
+                here = pressure[s + 1, rows]
+                value = value - here
+            change[s, rows] = value
 
 
 def scan_kernel(scale, offset, entering):
@@ -243,32 +291,27 @@
         state = scale[m] * state + offset[m]
 
 
-def march_rows(first, g, rows, entering, pressure, following, decay, term, force, inflow):
+def march_rows(first, g, rows, entering, change, following, decay, lead, inflow):
     stations = decay.shape[0]
-    ahead = pressure[0, rows]
-    state = jnp.where(first == 1, inflow[rows], from_chunks(entering, g) - ahead)
+    state = jnp.where(first == 1, inflow[rows], from_chunks(entering, g) - lead[rows])
     states = [state]
     for s in range(stations):
-        here = ahead
-        ahead = following[rows] if s == stations - 1 else pressure[s + 1, rows]
-        t = term[s, rows]
-        if s == 0:
-            t = t + force[rows]
-        state = decay[s, rows] * state + (t - (ahead - here))
+        step = change[s, rows]
+        if s == stations - 1:
+            step = step - following[rows]
+        state = decay[s, rows] * state + step
         states.append(state)
     return states
 
 
 def middle_kernel(
-    place, entering, pressure, following, decay, term, force, inflow, damping,
+    place, entering, change, following, decay, lead, inflow, damping,
     current, decay_new, scale, disc, x0, x1, x2, x3, source,
 ):
     first = place[1]
     stations, height, _ = current.shape
     for g, rows in groups(height):
-        states = march_rows(
-            first, g, rows, entering, pressure, following, decay, term, force, inflow
-        )
+        states = march_rows(first, g, rows, entering, change, following, decay, lead, inflow)
         product = None
         for s in range(stations):
             value = states[s + 1]
@@ -284,14 +327,10 @@
     disc[...] = current[0].astype(BF16)
 
 
-def last_kernel(
-    place, entering, pressure, following, decay, term, force, inflow, current
-):
+def last_kernel(place, entering, change, following, decay, lead, inflow, current):
     first = place[1]
     for g, rows in groups(current.shape[1]):
-        states = march_rows(
-            first, g, rows, entering, pressure, following, decay, term, force, inflow
-        )
+        states = march_rows(first, g, rows, entering, change, following, decay, lead, inflow)
         for s in range(current.shape[0]):
             current[s, rows] = states[s + 1]
 
@@ -355,16 +394,17 @@
 def disc_forces(rows, owners, blades):
     height, width = rows[0].shape
     count = len(rows)
-    number, half, _ = blades[0].shape
-    per_step = 4
+    number = blades.shape[0]
+    per_step, streams = 8, 4
     fixed = lambda shape: pl.BlockSpec(shape, lambda i: (0,) * len(shape))
-    table = pl.BlockSpec((per_step, half, LANE), lambda i: (i, 0, 0))
-    blades = [stay(b) for b in blades]
+    table = lambda k: pl.BlockSpec((per_step, width // streams, LANE), lambda i: (i, k, 0))
     return pl.pallas_call(
         disc_kernel,
         grid=(number // per_step,),
         out_shape=[near((height, LANE))] * count,
-        in_specs=[fixed((height, width))] * count + [fixed(owners.shape), table, table],
+        in_specs=[fixed((height, width))] * count
+        + [fixed(owners.shape)]
+        + [table(k) for k in range(streams)],
         out_specs=[fixed((height, LANE))] * count,
         scratch_shapes=[
             pltpu.VMEM((count * height, width), BF16),
@@ -372,7 +412,7 @@
         ],
         compiler_params=pltpu.CompilerParams(vmem_limit_bytes=16 * MIB),
         cost_estimate=cost(2 * number * width * width * LANE, 5 * MIB),
-    )(*rows, stay(owners), *blades)
+    )(*rows, stay(owners), *[stay(blades)] * streams)
 
 
 def local(velocity_guess, damping, inflow, disc_rows, owner, blade):
@@ -417,11 +457,7 @@
     def across_march(value):
         return lax.all_to_all(value, "march", split_axis=0, concat_axis=0, tiled=True)
 
-    half = width // 2
-    blades = [
-        lax.all_gather(blade[:, half * i : half * (i + 1)], "march", axis=0, tiled=True)
-        for i in range(2)
-    ]
+    blades = lax.all_gather(blade, "march", axis=0, tiled=True)
     blocks = (cross_index - jnp.arange(cross_size, dtype=jnp.int32) + cross_size) % cross_size
     ids = (blocks[:, None] * height + jnp.arange(height, dtype=jnp.int32)[None, :]).reshape(-1)
     owners = jnp.max(
@@ -457,51 +493,72 @@
         cost(4e6, 3 * MIB),
     )
     for sweep_index in range(SWEEPS):
+        merged = sweep_index > 0
+        final = sweep_index == SWEEPS - 1
+        if merged:
+            rows = turns([disc] * cross_size)
         arrived = turns(source)
-        scales = across_march(scale)
-        if sweep_index > 0:
-            disc, *arrived = lax.optimization_barrier((disc, *arrived))
-            rows = turns([disc] * cross_size)
+        extra = []
+        piece = plane
+        if not merged:
+            scales = across_march(scale)
+        if merged:
+            extra = disc_forces(rows, owners, blades)
+            piece = (height + height * LANE // width, width)
         solved = pl.pallas_call(
             solve_kernel,
-            out_shape=[near(plane)] * cross_size,
-            in_specs=[SMEM] + [VMEM] * cross_size + [pl.BlockSpec(memory_space=pltpu.HBM)] * 3,
+            out_shape=[near(piece)] * cross_size,
+            in_specs=[SMEM]
+            + [VMEM] * cross_size
+            + [pl.BlockSpec(memory_space=pltpu.HBM)] * 3
+            + [VMEM] * len(extra),
             out_specs=[VMEM] * cross_size,
             scratch_shapes=[pltpu.VMEM((width, width), F32)]
             + [pltpu.VMEM((width, width), BF16)] * 2
             + [pltpu.VMEM((width, width), F32), pltpu.SemaphoreType.DMA((3,))],
             compiler_params=pltpu.CompilerParams(vmem_limit_bytes=20 * MIB),
             cost_estimate=cost(3 * 8 * width**3, 5 * MIB),
-        )(place, *arrived, *tabled)
-        rows, solved = lax.optimization_barrier((rows, solved))
+        )(place, *arrived, *tabled, *extra)
+        forces = []
+        if merged:
+            scales = across_march(scale)
+        else:
+            rows, scales, solved = lax.optimization_barrier((rows, scales, solved))
+            forces = turns(disc_forces(rows, owners, blades), -1)
         pieces = turns(solved)
-        forces = turns(disc_forces(rows, owners, blades), -1)
-        (term,) = call(
-            laplace_kernel,
-            [far(slab)],
-            (place, current, arrived[1], arrived[-1]),
-            cost(4e6, 2 * MIB),
+        decay = stay(decay)
+        term, weights, base, force_weight = call(
+            weights_kernel,
+            [far(slab), near(slab), near(plane), near(plane)],
+            (place, current, arrived[1], arrived[-1], decay, near_inflow),
+            cost(8e6, 4 * MIB),
             scalars=1,
-        )
-        decay, term = stay(decay), stay(term)
-        pressure, lead, force, offset = by_rows(
+            limit=12,
+        )
+        lead, lead_far, force, offset = call(
             offset_kernel,
+            [near(plane), far(plane), far(plane), far(chunks)],
+            (place, *pieces, *forces, weights, base, force_weight),
+            cost(2e6, 3 * MIB),
+            scalars=1,
+            limit=12,
+        )
+        following = along_march(lead, -1)
+        offset, force, *pieces = lax.optimization_barrier((offset, force, *pieces))
+        change, pressure = by_rows(
+            change_kernel,
             height,
-            [far(slab), near(plane), far(plane), far(chunks)],
+            [far(slab), far(slab)],
             place,
-            (*pieces, *forces, decay, term, near_inflow),
-            cost(4e6, 5 * MIB),
-        )
-        following = along_march(lead, -1)
+            (*pieces, stay(term), stay(force)),
+            cost(4e6, 4 * MIB),
+        )
         (entering,) = call(
-            scan_kernel,
-            [far(chunks)],
-            (stay(scales), across_march(offset)),
-            cost(1e5, MIB),
+            scan_kernel, [far(chunks)], (scales, across_march(offset)), cost(1e5, MIB)
         )
         entering = across_march(entering)
-        common = (entering, stay(pressure), stay(following), decay, term, stay(force), near_inflow)
-        if sweep_index == SWEEPS - 1:
+        common = (entering, stay(change), stay(following), decay, stay(lead_far), near_inflow)
+        if final:
             (current,) = by_rows(
                 last_kernel, height, [far(slab)], place, common, cost(4e6, 5 * MIB)
             )

time: 253 us -> 196 us (0.77)
  waiting for transfers between devices: 91.6 us -> 40.9 us
  starting transfers between devices: 79.8 us -> 74.4 us
    all_gather x2 -> x1, waiting for transfers between devices: 41.1 us -> 7.12 us  [local(): blades = lax.all_gather(blade, 'march', axis=0, tiled=True)]
    ppermute x24 -> x21, waiting for transfers between devices: 24.7 us -> 16.1 us  [turn(): lax.ppermute(value, 'cross', [(i, (i + steps) % cross_size) for i in rang...]
    all_to_all x6, waiting for transfers between devices: 22.4 us -> 14.3 us  [across_march(): lax.all_to_all(value, 'march', split_axis=0, concat_axis=0, tiled=True)]
    ppermute x24 -> x21, starting transfers between devices: 36 us -> 32.1 us  [turn(): lax.ppermute(value, 'cross', [(i, (i + steps) % cross_size) for i in rang...]
    pallas_call x2, Pallas kernels: 13.4 us -> 9.72 us  [disc_forces(): pl.pallas_call(disc_kernel, grid=(number // per_step,), out_shape=[near((...]
    pallas_call x4 -> x6, Pallas kernels: 9.47 us -> 12 us  [call(): pl.pallas_call(kernel, out_shape=outs, in_specs=[SMEM] * scalars + [VMEM]...]
  transfers between devices with their start and end apart: 35 -> 31, of which waited for: 16 -> 16; matrix products, arithmetic and copies ran while one was open for 1% -> 2% of each run, Pallas kernels for 20% -> 21%
where the time goes in v3:
time: 196 us; the launch traced here: 192 us
  starting transfers between devices  74.4 us (38%)
  Pallas kernels  57.2 us (29%)
  waiting for transfers between devices  40.9 us (21%)
  between operations  14.2 us (7%)
  local copies, waits for them, and re-layouts  4.44 us (2%)
    ppermute x21, starting transfers between devices, turn(): lax.ppermute(value, 'cross', [(i, (i + steps) % cross_size) for i in rang...  32.1 us
    all_to_all x6, starting transfers between devices, across_march(): lax.all_to_all(value, 'march', split_axis=0, concat_axis=0, tiled=True)  31.6 us
    pallas_call x6, Pallas kernels, by_rows(): pl.pallas_call(kernel, grid_spec=pltpu.PrefetchScalarGridSpec(num_scalar_...  24.4 us
    ppermute x21, waiting for transfers between devices, turn(): lax.ppermute(value, 'cross', [(i, (i + steps) % cross_size) for i in rang...  16.1 us
    all_to_all x6, waiting for transfers between devices, across_march(): lax.all_to_all(value, 'march', split_axis=0, concat_axis=0, tiled=True)  14.3 us
    pallas_call x6, Pallas kernels, call(): pl.pallas_call(kernel, out_shape=outs, in_specs=[SMEM] * scalars + [VMEM]...  12 us
    pallas_call x2, Pallas kernels, local(): pl.pallas_call(solve_kernel, out_shape=[near(piece)] * cross_size, in_spe...  11.1 us
    ppermute x3, starting transfers between devices, along_march(): lax.ppermute(value, 'march', [(i, i + steps) for i in range(count) if 0 <...  10.6 us
  transfers between devices with their start and end apart: 31, of which 16 were waited for; matrix products, arithmetic and copies ran while one was open for 2% of the time, Pallas kernels for 21%

profile of v3, /device:TPU:2, one launch (start us, length us, event | category | flops | bytes accessed | tf_op | source)
XLA Modules:
  0.0 192.2 jit_solution(16360431099900879346)
XLA Ops:
  7.9 1.0 slice_bitcast_fusion
  8.9 1.9 collective-permute-start.3
  10.8 1.0 fusion.d0
  11.8 4.1 %collective-permute-start.2 = (bf16[128,512]{1,0:T(8,128)(2,1)S(1)}, bf16[128,512]{1,0:T(8,128)(2,1)S(1)}, u32[]{:S(2)}, u32[]{:S(2)}) collective-permute-start(bf16[128,512]{1,0:T(8,128)(2,1)S(1)} %fusion.d0), channel_id=1, source_target_pairs={{0,3},{1,0},{2,1},{3,2},{4,7},{5,4},{6,5},{7,6},{8,11},{9,8},{10,9... | collective-permute-start | bytes 393224 | tf_op jit(solution)/shard_map/ppermute | solution.py:444
  16.0 2.7 %collective-permute-done.3.upstream = f32[128,512]{1,0:T(8,128)S(1)} collective-permute-done((f32[128,512]{1,0:T(8,128)S(1)}, f32[128,512]{1,0:T(8,128)S(1)}, u32[]{:S(2)}, u32[]{:S(2)}) %collective-permute-start.3) | collective-permute-done | bytes 262176 | tf_op jit(solution)/shard_map/ppermute | solution.py:453
  18.7 2.7 %shard_map.104 = (f32[128,512]{1,0:T(8,128)S(1)}, f32[136,512]{1,0:T(8,128)S(1)}, f32[128,512]{1,0:T(8,128)S(1)}, f32[136,512]{1,0:T(8,128)S(1)}) custom-call(s32[4]{0:T(128)S(1)} %pad_add_fusion.place, f32[4,128,512]{2,1,0:T(8,128)} %current.4, f32[128,512]{1,0:T(8,128)S(1)} %collective-permute-done.3.upstream, f32[128,512]{1,0:T(8,128)} %inflow.9), custom_call_target="tpu_custom_call" | custom-call | flops 1000000 | bytes 2097152 | tf_op jit(solution)/shard_map/pallas_call | solution.py:379
  21.4 4.0 %collective-permute-start.5 = (f32[128,512]{1,0:T(8,128)S(1)}, f32[128,512]{1,0:T(8,128)S(1)}, u32[]{:S(2)}, u32[]{:S(2)}) collective-permute-start(f32[128,512]{1,0:T(8,128)S(1)} %get-tuple-element.87), channel_id=1, source_target_pairs={{0,2},{1,3},{2,0},{3,1},{4,6},{5,7},{6,4},{7,5},{8,10},{9,11},{10,... | collective-permute-start | bytes 786440 | tf_op jit(solution)/shard_map/ppermute | solution.py:444
  25.4 1.0 collective-permute-start.4
  26.4 2.2 %collective-permute-start.6 = (f32[136,512]{1,0:T(8,128)S(1)}, f32[136,512]{1,0:T(8,128)S(1)}, u32[]{:S(2)}, u32[]{:S(2)}) collective-permute-start(f32[136,512]{1,0:T(8,128)S(1)} %get-tuple-element.88), channel_id=1, source_target_pairs={{0,3},{1,0},{2,1},{3,2},{4,7},{5,4},{6,5},{7,6},{8,11},{9,8},{10,9... | collective-permute-start | bytes 835592 | tf_op jit(solution)/shard_map/ppermute | solution.py:444
  29.6 4.2 %shard_map.105 = (f32[4,128,512]{2,1,0:T(8,128)}, f32[32,16,128]{2,1,0:T(8,128)}) custom-call(s32[4]{0:T(128)S(1)} %pad_add_fusion.place, f32[4,128,512]{2,1,0:T(8,128)} %current.4, f32[4,128,512]{2,1,0:T(8,128)} %damping.2), custom_call_target="tpu_custom_call" | custom-call | flops 4000000 | bytes 3145728 | tf_op jit(solution)/shard_map/pallas_call | solution.py:379
  33.8 5.5 %all-to-all-start = ((f32[32,16,128]{2,1,0:T(8,128)}), f32[32,16,128]{2,1,0:T(8,128)S(1)}, u32[]{:S(2)}, u32[]{:S(2)}) async-start(f32[32,16,128]{2,1,0:T(8,128)} %get-tuple-element.84), calls=%async_computation | async-start | bytes 524288 | tf_op jit(solution)/shard_map/all_to_all | solution.py:458
  41.0 5.6 %shard_map.106 = (f32[128,512]{1,0:T(8,128)S(1)}, f32[128,512]{1,0:T(8,128)S(1)}, f32[128,512]{1,0:T(8,128)S(1)}, f32[128,512]{1,0:T(8,128)S(1)}) custom-call(s32[4]{0:T(128)S(1)} %pad_add_fusion.place, f32[128,512]{1,0:T(8,128)S(1)} %get-tuple-element.85.x0, f32[136,512]{1,0:T(8,128)S(1)} %collective-permute-done.4.x1.before, f32[128,512]{1,0:T(8,128)S(1)} %copy-done.1, ...), custom_call_target="tpu_custom_call" | custom-call | flops 3221225472 | bytes 5242880 | tf_op jit(solution)/shard_map/pallas_call | solution.py:508
  47.1 4.4 %collective-permute-start.8 = (f32[128,512]{1,0:T(8,128)S(1)}, f32[128,512]{1,0:T(8,128)S(1)}, u32[]{:S(2)}, u32[]{:S(2)}) collective-permute-start(f32[128,512]{1,0:T(8,128)S(1)} %get-tuple-element.96), channel_id=1, source_target_pairs={{0,2},{1,3},{2,0},{3,1},{4,6},{5,7},{6,4},{7,5},{8,10},{9,11},{10,... | collective-permute-start | bytes 786440 | tf_op jit(solution)/shard_map/ppermute | solution.py:444
  51.5 7.1 %all-gather.2.cloned.1.call-done.rest_0_.rest_1_.rest_2_.rest_3_ = bf16[32,512,128]{2,1,0:T(8,128)(2,1)} async-done(((bf16[1,512,128]{2,1,0:T(8,128)(2,1)}), bf16[32,512,128]{2,1,0:T(8,128)(2,1)}) %all-gather.2.cloned.1.call-update) | async-done | bytes 4194320 | tf_op jit(solution)/shard_map/all_gather | solution.py:460
  59.5 4.9 %shard_map.107 = (f32[128,128]{1,0:T(8,128)S(1)}, f32[128,128]{1,0:T(8,128)S(1)}, f32[128,128]{1,0:T(8,128)S(1)}, f32[128,128]{1,0:T(8,128)S(1)}) custom-call(bf16[128,512]{1,0:T(8,128)(2,1)S(1)} %fusion.d0, bf16[128,512]{1,0:T(8,128)(2,1)S(1)} %collective-permute-done.d1, bf16[128,512]{1,0:T(8,128)(2,1)S(1)} %collective-permute-done.1.d2, ...), custom_call_target="tpu_custom_call" | custom-call | flops 2147483648 | bytes 5242880 | tf_op jit(solution)/shard_map/pallas_call | solution.py:401
  64.3 2.7 %collective-permute-start.10 = (f32[128,128]{1,0:T(8,128)S(1)}, f32[128,128]{1,0:T(8,128)S(1)}, u32[]{:S(2)}, u32[]{:S(2)}) collective-permute-start(f32[128,128]{1,0:T(8,128)S(1)} %get-tuple-element.103), channel_id=1, source_target_pairs={{0,3},{1,0},{2,1},{3,2},{4,7},{5,4},{6,5},{7,6},{8,11},{9,8},{10,9... | collective-permute-start | bytes 196616 | tf_op jit(solution)/shard_map/ppermute | solution.py:444
  67.7 1.0 collective-permute-start.12
  68.6 3.6 %shard_map.108 = (f32[4,128,512]{2,1,0:T(8,128)}, f32[4,128,512]{2,1,0:T(8,128)S(1)}, f32[128,512]{1,0:T(8,128)S(1)}, f32[128,512]{1,0:T(8,128)S(1)}) custom-call(s32[4]{0:T(128)S(1)} %pad_add_fusion.place, f32[4,128,512]{2,1,0:T(8,128)} %current.4, f32[136,512]{1,0:T(8,128)S(1)} %collective-permute-done.4.x1.before, ...), custom_call_target="tpu_custom_call" | custom-call | flops 8000000 | bytes 4194304 | tf_op jit(solution)/shard_map/pallas_call | solution.py:355
  72.2 1.0 collective-permute-done.11.rest_6_
  73.9 1.6 shard_map.109
  75.5 5.9 %all-to-all-start.1 = ((f32[32,16,128]{2,1,0:T(8,128)}), f32[32,16,128]{2,1,0:T(8,128)S(1)}, u32[]{:S(2)}, u32[]{:S(2)}) async-start(f32[32,16,128]{2,1,0:T(8,128)} %get-tuple-element.112), calls=%async_computation.1 | async-start | bytes 524288 | tf_op jit(solution)/shard_map/all_to_all | solution.py:458
  81.4 4.3 %collective-permute-start.13 = (f32[128,512]{1,0:T(8,128)S(1)}, f32[128,512]{1,0:T(8,128)S(1)}, u32[]{:S(2)}, u32[]{:S(2)}) collective-permute-start(f32[128,512]{1,0:T(8,128)S(1)} %get-tuple-element.120), channel_id=1, source_target_pairs={{4,0},{8,4},{12,8},{16,12},{20,16},{24,20},{28,24},{32,28},{36,32}... | collective-permute-start | bytes 786440 | tf_op jit(solution)/shard_map/ppermute | solution.py:453
  85.8 3.4 %all-to-all-done.1.offset = f32[32,16,128]{2,1,0:T(8,128)S(1)} async-done(((f32[32,16,128]{2,1,0:T(8,128)}), f32[32,16,128]{2,1,0:T(8,128)S(1)}, u32[]{:S(2)}, u32[]{:S(2)}) %all-to-all-start.1) | async-done | bytes 262176 | tf_op jit(solution)/shard_map/all_to_all | solution.py:458
  89.9 5.0 %all-to-all-start.2 = ((f32[32,16,128]{2,1,0:T(8,128)}), f32[32,16,128]{2,1,0:T(8,128)S(1)}, u32[]{:S(2)}, u32[]{:S(2)}) async-start(f32[32,16,128]{2,1,0:T(8,128)} %shard_map.110), calls=%async_computation.2 | async-start | bytes 524288 | tf_op jit(solution)/shard_map/all_to_all | solution.py:458
  94.9 4.2 %shard_map.111 = (f32[4,128,512]{2,1,0:T(8,128)}, f32[4,128,512]{2,1,0:T(8,128)}) custom-call(s32[4]{0:T(128)S(1)} %pad_add_fusion.place, f32[128,512]{1,0:T(8,128)S(1)} %get-tuple-element.113.rest_0_.p0, f32[128,512]{1,0:T(8,128)S(1)} %collective-permute-done.7.rest_1_.p1, f32[128,512]{1,0:T(8,128)S(1)} %collective-permute-done.8.rest_2_.p2, ...), custom_call_target="tpu_custom_call" | custom-call | flops 4000000 | bytes 4194304 | tf_op jit(solution)/shard_map/pallas_call | solution.py:379
  99.1 3.6 %all-to-all-done.2.entering = f32[32,16,128]{2,1,0:T(8,128)S(1)} async-done(((f32[32,16,128]{2,1,0:T(8,128)}), f32[32,16,128]{2,1,0:T(8,128)S(1)}, u32[]{:S(2)}, u32[]{:S(2)}) %all-to-all-start.2) | async-done | bytes 262176 | tf_op jit(solution)/shard_map/all_to_all | solution.py:458
  102.7 4.8 %shard_map.112 = (f32[4,128,512]{2,1,0:T(8,128)}, f32[4,128,512]{2,1,0:T(8,128)}, f32[32,16,128]{2,1,0:T(8,128)}, bf16[128,512]{1,0:T(8,128)(2,1)S(1)}, f32[128,...) custom-call(s32[4]{0:T(128)S(1)} %pad_add_fusion.place, ...), custom_call_target="tpu_custom_call" | custom-call | flops 8000000 | bytes 8388608 | tf_op jit(solution)/shard_map/pallas_call | solution.py:379
  108.4 1.6 collective-permute-start.18
  110.2 1.7 collective-permute-start.14
  111.9 1.5 collective-permute-start.16
  114.1 1.9 collective-permute-start.15
  116.3 2.1 %collective-permute-done.17.d1 = bf16[128,512]{1,0:T(8,128)(2,1)S(1)} collective-permute-done((bf16[128,512]{1,0:T(8,128)(2,1)S(1)}, bf16[128,512]{1,0:T(8,128)(2,1)S(1)}, u32[]{:S(2)}, u32[]{:S(2)}) %collective-permute-start.17) | collective-permute-done | bytes 131104 | tf_op jit(solution)/shard_map/ppermute | solution.py:444
  118.4 4.9 %shard_map.113 = (f32[128,128]{1,0:T(8,128)S(1)}, f32[128,128]{1,0:T(8,128)S(1)}, f32[128,128]{1,0:T(8,128)S(1)}, f32[128,128]{1,0:T(8,128)S(1)}) custom-call(bf16[128,512]{1,0:T(8,128)(2,1)S(1)} %get-tuple-element.127.d0, bf16[128,512]{1,0:T(8,128)(2,1)S(1)} %collective-permute-done.17.d1, bf16[128,512]{1,0:T(8,128)(2,1)S(1)} %collective-permute-done.18.d2, ...), custom_call_target="tpu_custom_call" | custom-call | flops 2147483648 | bytes 5242880 | tf_op jit(solution)/shard_map/pallas_call | solution.py:401
  123.3 6.5 %collective-permute-done.15.x2 = f32[128,512]{1,0:T(8,128)S(1)} collective-permute-done((f32[128,512]{1,0:T(8,128)S(1)}, f32[128,512]{1,0:T(8,128)S(1)}, u32[]{:S(2)}, u32[]{:S(2)}) %collective-permute-start.15) | collective-permute-done | bytes 262176 | tf_op jit(solution)/shard_map/ppermute | solution.py:444
  129.8 5.6 %shard_map.114 = (f32[160,512]{1,0:T(8,128)S(1)}, f32[160,512]{1,0:T(8,128)S(1)}, f32[160,512]{1,0:T(8,128)S(1)}, f32[160,512]{1,0:T(8,128)S(1)}) custom-call(s32[4]{0:T(128)S(1)} %pad_add_fusion.place, f32[128,512]{1,0:T(8,128)S(1)} %get-tuple-element.123.x0, f32[136,512]{1,0:T(8,128)S(1)} %collective-permute-done.14.x1.before, ...), custom_call_target="tpu_custom_call" | custom-call | flops 3221225472 | bytes 5242880 | tf_op jit(solution)/shard_map/pallas_call | solution.py:508
  135.4 2.3 %collective-permute-start.21 = (f32[160,512]{1,0:T(8,128)S(1)}, f32[160,512]{1,0:T(8,128)S(1)}, u32[]{:S(2)}, u32[]{:S(2)}) collective-permute-start(f32[160,512]{1,0:T(8,128)S(1)} %get-tuple-element.134), channel_id=1, source_target_pairs={{0,2},{1,3},{2,0},{3,1},{4,6},{5,7},{6,4},{7,5},{8,10},{9,11},{10,... | collective-permute-start | bytes 983048 | tf_op jit(solution)/shard_map/ppermute | solution.py:444
  137.7 2.0 %collective-permute-start.22 = (f32[160,512]{1,0:T(8,128)S(1)}, f32[160,512]{1,0:T(8,128)S(1)}, u32[]{:S(2)}, u32[]{:S(2)}) collective-permute-start(f32[160,512]{1,0:T(8,128)S(1)} %get-tuple-element.135), channel_id=1, source_target_pairs={{0,3},{1,0},{2,1},{3,2},{4,7},{5,4},{6,5},{7,6},{8,11},{9,8},{10,9... | collective-permute-start | bytes 983048 | tf_op jit(solution)/shard_map/ppermute | solution.py:444
  139.7 5.1 %all-to-all-start.3 = ((f32[32,16,128]{2,1,0:T(8,128)}), f32[32,16,128]{2,1,0:T(8,128)S(1)}, u32[]{:S(2)}, u32[]{:S(2)}) async-start(f32[32,16,128]{2,1,0:T(8,128)} %get-tuple-element.122), calls=%async_computation.3 | async-start | bytes 524288 | tf_op jit(solution)/shard_map/all_to_all | solution.py:458
  144.8 3.6 %shard_map.115 = (f32[4,128,512]{2,1,0:T(8,128)}, f32[4,128,512]{2,1,0:T(8,128)S(1)}, f32[128,512]{1,0:T(8,128)S(1)}, f32[128,512]{1,0:T(8,128)S(1)}) custom-call(s32[4]{0:T(128)S(1)} %pad_add_fusion.place, f32[4,128,512]{2,1,0:T(8,128)} %get-tuple-element.136.current, f32[136,512]{1,0:T(8,128)S(1)} %collective-permute-done.14.x1.before, ...), custom_call_target="tpu_custom_call" | custom-call | flops 8000000 | bytes 4194304 | tf_op jit(solution)/shard_map/pallas_call | solution.py:355
  148.4 4.0 %collective-permute-done.20.rest_1_.p1 = f32[160,512]{1,0:T(8,128)S(1)} collective-permute-done((f32[160,512]{1,0:T(8,128)S(1)}, f32[160,512]{1,0:T(8,128)S(1)}, u32[]{:S(2)}, u32[]{:S(2)}) %collective-permute-start.20) | collective-permute-done | bytes 327712 | tf_op jit(solution)/shard_map/ppermute | solution.py:444
  153.0 1.6 shard_map.116
  154.6 5.1 %all-to-all-start.4 = ((f32[32,16,128]{2,1,0:T(8,128)}), f32[32,16,128]{2,1,0:T(8,128)S(1)}, u32[]{:S(2)}, u32[]{:S(2)}) async-start(f32[32,16,128]{2,1,0:T(8,128)} %get-tuple-element.143), calls=%async_computation.4 | async-start | bytes 524288 | tf_op jit(solution)/shard_map/all_to_all | solution.py:458
  159.8 4.3 %collective-permute-start.23 = (f32[128,512]{1,0:T(8,128)S(1)}, f32[128,512]{1,0:T(8,128)S(1)}, u32[]{:S(2)}, u32[]{:S(2)}) collective-permute-start(f32[128,512]{1,0:T(8,128)S(1)} %get-tuple-element.151), channel_id=1, source_target_pairs={{4,0},{8,4},{12,8},{16,12},{20,16},{24,20},{28,24},{32,28},{36,32}... | collective-permute-start | bytes 786440 | tf_op jit(solution)/shard_map/ppermute | solution.py:453
  164.1 3.5 %all-to-all-done.4.offset = f32[32,16,128]{2,1,0:T(8,128)S(1)} async-done(((f32[32,16,128]{2,1,0:T(8,128)}), f32[32,16,128]{2,1,0:T(8,128)S(1)}, u32[]{:S(2)}, u32[]{:S(2)}) %all-to-all-start.4) | async-done | bytes 262176 | tf_op jit(solution)/shard_map/all_to_all | solution.py:458
  168.3 5.0 %all-to-all-start.5 = ((f32[32,16,128]{2,1,0:T(8,128)}), f32[32,16,128]{2,1,0:T(8,128)S(1)}, u32[]{:S(2)}, u32[]{:S(2)}) async-start(f32[32,16,128]{2,1,0:T(8,128)} %shard_map.117), calls=%async_computation.5 | async-start | bytes 524288 | tf_op jit(solution)/shard_map/all_to_all | solution.py:458
  173.3 4.2 %shard_map.118 = (f32[4,128,512]{2,1,0:T(8,128)}, f32[4,128,512]{2,1,0:T(8,128)}) custom-call(s32[4]{0:T(128)S(1)} %pad_add_fusion.place, f32[160,512]{1,0:T(8,128)S(1)} %get-tuple-element.144.rest_0_.p0, f32[160,512]{1,0:T(8,128)S(1)} %collective-permute-done.20.rest_1_.p1, f32[160,512]{1,0:T(8,128)S(1)} %collective-permute-done.21.rest_2_.p2, ...), custom_call_target="tpu_custom_call" | custom-call | flops 4000000 | bytes 4194304 | tf_op jit(solution)/shard_map/pallas_call | solution.py:379
  177.5 3.6 %all-to-all-done.5.entering = f32[32,16,128]{2,1,0:T(8,128)S(1)} async-done(((f32[32,16,128]{2,1,0:T(8,128)}), f32[32,16,128]{2,1,0:T(8,128)S(1)}, u32[]{:S(2)}, u32[]{:S(2)}) %all-to-all-start.5) | async-done | bytes 262176 | tf_op jit(solution)/shard_map/all_to_all | solution.py:458
  181.1 4.2 %shard_map.119 = f32[4,128,512]{2,1,0:T(8,128)} custom-call(s32[4]{0:T(128)S(1)} %pad_add_fusion.place, f32[32,16,128]{2,1,0:T(8,128)S(1)} %all-to-all-done.5.entering, f32[4,128,512]{2,1,0:T(8,128)} %get-tuple-element.150.change, f32[128,512]{1,0:T(8,128)} %copy-done.3, f32[4,128,512]{2,1,0:T(8,128)} %get-tuple-element.137.decay, ...), custom_call_target="tpu_custom_call" | custom-call | flops 4000000 | bytes 5242880 | tf_op jit(solution)/shard_map/pallas_call | solution.py:379
  (47 shorter events, 10.4 us)
Async XLA Ops:
  7.2 51.5 %all-gather.2.cloned.1.call-start = ((), (), s32[]{:S(2)}) async-start(), calls=%async_computation.6 | async-start | bytes 4325376 | tf_op jit(solution)/shard_map/all_gather | solution.py:460
  8.9 9.8 %collective-permute-start.3 = (f32[128,512]{1,0:T(8,128)S(1)}, f32[128,512]{1,0:T(8,128)S(1)}, u32[]{:S(2)}, u32[]{:S(2)}) collective-permute-start(f32[128,512]{1,0:T(8,128)S(1)} %slice_bitcast_fusion), channel_id=1, source_target_pairs={{0,4},{4,8},{8,12},{12,16},{16,20},{20,24},{24,28},{28,32},{32,36}... | collective-permute-start | bytes 786440 | tf_op jit(solution)/shard_map/ppermute | solution.py:453
  11.8 34.8 %collective-permute-start.2 = (bf16[128,512]{1,0:T(8,128)(2,1)S(1)}, bf16[128,512]{1,0:T(8,128)(2,1)S(1)}, u32[]{:S(2)}, u32[]{:S(2)}) collective-permute-start(bf16[128,512]{1,0:T(8,128)(2,1)S(1)} %fusion.d0), channel_id=1, source_target_pairs={{0,3},{1,0},{2,1},{3,2},{4,7},{5,4},{6,5},{7,6},{8,11},{9,8},{10,9... | collective-permute-start | bytes 393224 | tf_op jit(solution)/shard_map/ppermute | solution.py:444
  15.9 30.7 %collective-permute-start.1 = (bf16[128,512]{1,0:T(8,128)(2,1)S(1)}, bf16[128,512]{1,0:T(8,128)(2,1)S(1)}, u32[]{:S(2)}, u32[]{:S(2)}) collective-permute-start(bf16[128,512]{1,0:T(8,128)(2,1)S(1)} %fusion.d0), channel_id=1, source_target_pairs={{0,2},{1,3},{2,0},{3,1},{4,6},{5,7},{6,4},{7,5},{8,10},{9,11},{10,... | collective-permute-start | bytes 393224 | tf_op jit(solution)/shard_map/ppermute | solution.py:444
  21.4 17.9 %collective-permute-start.5 = (f32[128,512]{1,0:T(8,128)S(1)}, f32[128,512]{1,0:T(8,128)S(1)}, u32[]{:S(2)}, u32[]{:S(2)}) collective-permute-start(f32[128,512]{1,0:T(8,128)S(1)} %get-tuple-element.87), channel_id=1, source_target_pairs={{0,2},{1,3},{2,0},{3,1},{4,6},{5,7},{6,4},{7,5},{8,10},{9,11},{10,... | collective-permute-start | bytes 786440 | tf_op jit(solution)/shard_map/ppermute | solution.py:444
  25.4 14.7 %collective-permute-start.4 = (f32[136,512]{1,0:T(8,128)S(1)}, f32[136,512]{1,0:T(8,128)S(1)}, u32[]{:S(2)}, u32[]{:S(2)}) collective-permute-start(f32[136,512]{1,0:T(8,128)S(1)} %get-tuple-element.86), channel_id=1, source_target_pairs={{0,1},{1,2},{2,3},{3,0},{4,5},{5,6},{6,7},{7,4},{8,9},{9,10},{10,1... | collective-permute-start | bytes 835592 | tf_op jit(solution)/shard_map/ppermute | solution.py:444
  26.4 13.7 %collective-permute-start.6 = (f32[136,512]{1,0:T(8,128)S(1)}, f32[136,512]{1,0:T(8,128)S(1)}, u32[]{:S(2)}, u32[]{:S(2)}) collective-permute-start(f32[136,512]{1,0:T(8,128)S(1)} %get-tuple-element.88), channel_id=1, source_target_pairs={{0,3},{1,0},{2,1},{3,2},{4,7},{5,4},{6,5},{7,6},{8,11},{9,8},{10,9... | collective-permute-start | bytes 835592 | tf_op jit(solution)/shard_map/ppermute | solution.py:444
  33.8 13.3 %all-to-all-start = ((f32[32,16,128]{2,1,0:T(8,128)}), f32[32,16,128]{2,1,0:T(8,128)S(1)}, u32[]{:S(2)}, u32[]{:S(2)}) async-start(f32[32,16,128]{2,1,0:T(8,128)} %get-tuple-element.84), calls=%async_computation | async-start | bytes 524288 | tf_op jit(solution)/shard_map/all_to_all | solution.py:458
  39.3 0.7 copy-start
  40.1 6.8 %collective-permute-start = (bf16[128,512]{1,0:T(8,128)(2,1)S(1)}, bf16[128,512]{1,0:T(8,128)(2,1)S(1)}, u32[]{:S(2)}, u32[]{:S(2)}) collective-permute-start(bf16[128,512]{1,0:T(8,128)(2,1)S(1)} %fusion.d0), channel_id=1, source_target_pairs={{0,1},{1,2},{2,3},{3,0},{4,5},{5,6},{6,7},{7,4},{8,9},{9,10},{10,1... | collective-permute-start | bytes 393224 | tf_op jit(solution)/shard_map/ppermute | solution.py:444
  40.1 1.0 copy-start.1
  47.1 20.6 %collective-permute-start.7 = (f32[128,512]{1,0:T(8,128)S(1)}, f32[128,512]{1,0:T(8,128)S(1)}, u32[]{:S(2)}, u32[]{:S(2)}) collective-permute-start(f32[128,512]{1,0:T(8,128)S(1)} %get-tuple-element.95), channel_id=1, source_target_pairs={{0,1},{1,2},{2,3},{3,0},{4,5},{5,6},{6,7},{7,4},{8,9},{9,10},{10,1... | collective-permute-start | bytes 786440 | tf_op jit(solution)/shard_map/ppermute | solution.py:444
  47.1 25.1 %collective-permute-start.8 = (f32[128,512]{1,0:T(8,128)S(1)}, f32[128,512]{1,0:T(8,128)S(1)}, u32[]{:S(2)}, u32[]{:S(2)}) collective-permute-start(f32[128,512]{1,0:T(8,128)S(1)} %get-tuple-element.96), channel_id=1, source_target_pairs={{0,2},{1,3},{2,0},{3,1},{4,6},{5,7},{6,4},{7,5},{8,10},{9,11},{10,... | collective-permute-start | bytes 786440 | tf_op jit(solution)/shard_map/ppermute | solution.py:444
  51.5 20.7 %collective-permute-start.9 = (f32[128,512]{1,0:T(8,128)S(1)}, f32[128,512]{1,0:T(8,128)S(1)}, u32[]{:S(2)}, u32[]{:S(2)}) collective-permute-start(f32[128,512]{1,0:T(8,128)S(1)} %get-tuple-element.97), channel_id=1, source_target_pairs={{0,3},{1,0},{2,1},{3,2},{4,7},{5,4},{6,5},{7,6},{8,11},{9,8},{10,9... | collective-permute-start | bytes 786440 | tf_op jit(solution)/shard_map/ppermute | solution.py:444
  64.3 7.9 %collective-permute-start.10 = (f32[128,128]{1,0:T(8,128)S(1)}, f32[128,128]{1,0:T(8,128)S(1)}, u32[]{:S(2)}, u32[]{:S(2)}) collective-permute-start(f32[128,128]{1,0:T(8,128)S(1)} %get-tuple-element.103), channel_id=1, source_target_pairs={{0,3},{1,0},{2,1},{3,2},{4,7},{5,4},{6,5},{7,6},{8,11},{9,8},{10,9... | collective-permute-start | bytes 196616 | tf_op jit(solution)/shard_map/ppermute | solution.py:444
  67.0 6.2 %collective-permute-start.11 = (f32[128,128]{1,0:T(8,128)S(1)}, f32[128,128]{1,0:T(8,128)S(1)}, u32[]{:S(2)}, u32[]{:S(2)}) collective-permute-start(f32[128,128]{1,0:T(8,128)S(1)} %get-tuple-element.104), channel_id=1, source_target_pairs={{0,2},{1,3},{2,0},{3,1},{4,6},{5,7},{6,4},{7,5},{8,10},{9,11},{10,... | collective-permute-start | bytes 196616 | tf_op jit(solution)/shard_map/ppermute | solution.py:444
  67.7 6.2 %collective-permute-start.12 = (f32[128,128]{1,0:T(8,128)S(1)}, f32[128,128]{1,0:T(8,128)S(1)}, u32[]{:S(2)}, u32[]{:S(2)}) collective-permute-start(f32[128,128]{1,0:T(8,128)S(1)} %get-tuple-element.105), channel_id=1, source_target_pairs={{0,1},{1,2},{2,3},{3,0},{4,5},{5,6},{6,7},{7,4},{8,9},{9,10},{10,1... | collective-permute-start | bytes 196616 | tf_op jit(solution)/shard_map/ppermute | solution.py:444
  75.5 13.6 %all-to-all-start.1 = ((f32[32,16,128]{2,1,0:T(8,128)}), f32[32,16,128]{2,1,0:T(8,128)S(1)}, u32[]{:S(2)}, u32[]{:S(2)}) async-start(f32[32,16,128]{2,1,0:T(8,128)} %get-tuple-element.112), calls=%async_computation.1 | async-start | bytes 524288 | tf_op jit(solution)/shard_map/all_to_all | solution.py:458
  81.4 17.7 %collective-permute-start.13 = (f32[128,512]{1,0:T(8,128)S(1)}, f32[128,512]{1,0:T(8,128)S(1)}, u32[]{:S(2)}, u32[]{:S(2)}) collective-permute-start(f32[128,512]{1,0:T(8,128)S(1)} %get-tuple-element.120), channel_id=1, source_target_pairs={{4,0},{8,4},{12,8},{16,12},{20,16},{24,20},{28,24},{32,28},{36,32}... | collective-permute-start | bytes 786440 | tf_op jit(solution)/shard_map/ppermute | solution.py:453
  89.9 12.8 %all-to-all-start.2 = ((f32[32,16,128]{2,1,0:T(8,128)}), f32[32,16,128]{2,1,0:T(8,128)S(1)}, u32[]{:S(2)}, u32[]{:S(2)}) async-start(f32[32,16,128]{2,1,0:T(8,128)} %shard_map.110), calls=%async_computation.2 | async-start | bytes 524288 | tf_op jit(solution)/shard_map/all_to_all | solution.py:458
  99.1 3.6 %copy-start.2 = (f32[128,512]{1,0:T(8,128)}, f32[128,512]{1,0:T(8,128)S(1)}, u32[]{:S(2)}) copy-start(f32[128,512]{1,0:T(8,128)S(1)} %collective-permute-done.13.following) | copy-start | bytes 786436
  107.6 6.5 %collective-permute-start.19 = (bf16[128,512]{1,0:T(8,128)(2,1)S(1)}, bf16[128,512]{1,0:T(8,128)(2,1)S(1)}, u32[]{:S(2)}, u32[]{:S(2)}) collective-permute-start(bf16[128,512]{1,0:T(8,128)(2,1)S(1)} %get-tuple-element.127.d0), channel_id=1, source_target_pairs={{0,3},{1,0},{2,1},{3,2},{4,7},{5,4},{6,5},{7,6},{8,11},{9,8},{10,9... | collective-permute-start | bytes 393224 | tf_op jit(solution)/shard_map/ppermute | solution.py:444
  108.4 7.9 %collective-permute-start.18 = (bf16[128,512]{1,0:T(8,128)(2,1)S(1)}, bf16[128,512]{1,0:T(8,128)(2,1)S(1)}, u32[]{:S(2)}, u32[]{:S(2)}) collective-permute-start(bf16[128,512]{1,0:T(8,128)(2,1)S(1)} %get-tuple-element.127.d0), channel_id=1, source_target_pairs={{0,2},{1,3},{2,0},{3,1},{4,6},{5,7},{6,4},{7,5},{8,10},{9,11},{10,... | collective-permute-start | bytes 393224 | tf_op jit(solution)/shard_map/ppermute | solution.py:444
  110.1 8.3 %collective-permute-start.17 = (bf16[128,512]{1,0:T(8,128)(2,1)S(1)}, bf16[128,512]{1,0:T(8,128)(2,1)S(1)}, u32[]{:S(2)}, u32[]{:S(2)}) collective-permute-start(bf16[128,512]{1,0:T(8,128)(2,1)S(1)} %get-tuple-element.127.d0), channel_id=1, source_target_pairs={{0,1},{1,2},{2,3},{3,0},{4,5},{5,6},{6,7},{7,4},{8,9},{9,10},{10,1... | collective-permute-start | bytes 393224 | tf_op jit(solution)/shard_map/ppermute | solution.py:444
  110.2 19.5 %collective-permute-start.14 = (f32[136,512]{1,0:T(8,128)S(1)}, f32[136,512]{1,0:T(8,128)S(1)}, u32[]{:S(2)}, u32[]{:S(2)}) collective-permute-start(f32[136,512]{1,0:T(8,128)S(1)} %get-tuple-element.124), channel_id=1, source_target_pairs={{0,1},{1,2},{2,3},{3,0},{4,5},{5,6},{6,7},{7,4},{8,9},{9,10},{10,1... | collective-permute-start | bytes 835592 | tf_op jit(solution)/shard_map/ppermute | solution.py:444
  111.9 17.8 %collective-permute-start.16 = (f32[136,512]{1,0:T(8,128)S(1)}, f32[136,512]{1,0:T(8,128)S(1)}, u32[]{:S(2)}, u32[]{:S(2)}) collective-permute-start(f32[136,512]{1,0:T(8,128)S(1)} %get-tuple-element.126), channel_id=1, source_target_pairs={{0,3},{1,0},{2,1},{3,2},{4,7},{5,4},{6,5},{7,6},{8,11},{9,8},{10,9... | collective-permute-start | bytes 835592 | tf_op jit(solution)/shard_map/ppermute | solution.py:444
  114.1 15.6 %collective-permute-start.15 = (f32[128,512]{1,0:T(8,128)S(1)}, f32[128,512]{1,0:T(8,128)S(1)}, u32[]{:S(2)}, u32[]{:S(2)}) collective-permute-start(f32[128,512]{1,0:T(8,128)S(1)} %get-tuple-element.125), channel_id=1, source_target_pairs={{0,2},{1,3},{2,0},{3,1},{4,6},{5,7},{6,4},{7,5},{8,10},{9,11},{10,... | collective-permute-start | bytes 786440 | tf_op jit(solution)/shard_map/ppermute | solution.py:444
  135.3 17.1 %collective-permute-start.20 = (f32[160,512]{1,0:T(8,128)S(1)}, f32[160,512]{1,0:T(8,128)S(1)}, u32[]{:S(2)}, u32[]{:S(2)}) collective-permute-start(f32[160,512]{1,0:T(8,128)S(1)} %get-tuple-element.133), channel_id=1, source_target_pairs={{0,1},{1,2},{2,3},{3,0},{4,5},{5,6},{6,7},{7,4},{8,9},{9,10},{10,1... | collective-permute-start | bytes 983048 | tf_op jit(solution)/shard_map/ppermute | solution.py:444
  135.4 17.0 %collective-permute-start.21 = (f32[160,512]{1,0:T(8,128)S(1)}, f32[160,512]{1,0:T(8,128)S(1)}, u32[]{:S(2)}, u32[]{:S(2)}) collective-permute-start(f32[160,512]{1,0:T(8,128)S(1)} %get-tuple-element.134), channel_id=1, source_target_pairs={{0,2},{1,3},{2,0},{3,1},{4,6},{5,7},{6,4},{7,5},{8,10},{9,11},{10,... | collective-permute-start | bytes 983048 | tf_op jit(solution)/shard_map/ppermute | solution.py:444
  137.7 15.3 %collective-permute-start.22 = (f32[160,512]{1,0:T(8,128)S(1)}, f32[160,512]{1,0:T(8,128)S(1)}, u32[]{:S(2)}, u32[]{:S(2)}) collective-permute-start(f32[160,512]{1,0:T(8,128)S(1)} %get-tuple-element.135), channel_id=1, source_target_pairs={{0,3},{1,0},{2,1},{3,2},{4,7},{5,4},{6,5},{7,6},{8,11},{9,8},{10,9... | collective-permute-start | bytes 983048 | tf_op jit(solution)/shard_map/ppermute | solution.py:444
  139.7 14.9 %all-to-all-start.3 = ((f32[32,16,128]{2,1,0:T(8,128)}), f32[32,16,128]{2,1,0:T(8,128)S(1)}, u32[]{:S(2)}, u32[]{:S(2)}) async-start(f32[32,16,128]{2,1,0:T(8,128)} %get-tuple-element.122), calls=%async_computation.3 | async-start | bytes 524288 | tf_op jit(solution)/shard_map/all_to_all | solution.py:458
  154.6 12.9 %all-to-all-start.4 = ((f32[32,16,128]{2,1,0:T(8,128)}), f32[32,16,128]{2,1,0:T(8,128)S(1)}, u32[]{:S(2)}, u32[]{:S(2)}) async-start(f32[32,16,128]{2,1,0:T(8,128)} %get-tuple-element.143), calls=%async_computation.4 | async-start | bytes 524288 | tf_op jit(solution)/shard_map/all_to_all | solution.py:458
  159.8 17.8 %collective-permute-start.23 = (f32[128,512]{1,0:T(8,128)S(1)}, f32[128,512]{1,0:T(8,128)S(1)}, u32[]{:S(2)}, u32[]{:S(2)}) collective-permute-start(f32[128,512]{1,0:T(8,128)S(1)} %get-tuple-element.151), channel_id=1, source_target_pairs={{4,0},{8,4},{12,8},{16,12},{20,16},{24,20},{28,24},{32,28},{36,32}... | collective-permute-start | bytes 786440 | tf_op jit(solution)/shard_map/ppermute | solution.py:453
  168.3 12.8 %all-to-all-start.5 = ((f32[32,16,128]{2,1,0:T(8,128)}), f32[32,16,128]{2,1,0:T(8,128)S(1)}, u32[]{:S(2)}, u32[]{:S(2)}) async-start(f32[32,16,128]{2,1,0:T(8,128)} %shard_map.117), calls=%async_computation.5 | async-start | bytes 524288 | tf_op jit(solution)/shard_map/all_to_all | solution.py:458
  177.5 3.6 %copy-start.3 = (f32[128,512]{1,0:T(8,128)}, f32[128,512]{1,0:T(8,128)S(1)}, u32[]{:S(2)}) copy-start(f32[128,512]{1,0:T(8,128)S(1)} %collective-permute-done.23.following) | copy-start | bytes 786436
Sparse Core Ops, SparseCore 0:
  10.3 48.3 all-gather.1

commit v4 on v3

--- a/solution.py
+++ b/solution.py
@@ -5,7 +5,7 @@
 from jax import lax
 from jax.experimental import pallas as pl
 from jax.experimental.pallas import tpu as pltpu
-from jax.sharding import PartitionSpec as P
+from jax.sharding import Mesh, PartitionSpec as P
 
 SWEEPS = 2
 SOURCE_GAIN = 0.04
@@ -13,6 +13,7 @@
 VISCOSITY = 0.1
 DRAG_RATE = 0.01
 
+MARCH = ("chip", "core")
 F32 = jnp.float32
 BF16 = jnp.bfloat16
 SUB = 8
@@ -44,11 +45,11 @@
     return [(g, slice(SUB * g, SUB * g + SUB)) for g in range(rows // SUB)]
 
 
-def to_chunks(ref, g, value):
+def to_chunks(ref, g, value, base=0):
     for h in range(2):
         for q in range(2):
             at = (2 * h + q) * LANE
-            ref[2 * g + h, SUB * q : SUB * q + SUB, :] = value[:, at : at + LANE]
+            ref[2 * g + h, base + SUB * q : base + SUB * q + SUB, :] = value[:, at : at + LANE]
 
 
 def from_chunks(ref, g):
@@ -100,18 +101,9 @@
     send_edges(current, outs)
 
 
-def decay_kernel(place, current, damping, decay, scale):
-    for g, rows in groups(current.shape[1]):
-        product = None
-        for s in range(current.shape[0]):
-            d = decay_of(current[s, rows], damping[s, rows])
-            decay[s, rows] = d
-            product = d if product is None else product * d
-        to_chunks(scale, g, product)
-
-
 def weights_kernel(
-    place, current, before, after, decay, inflow, term, weights, base, force_weight
+    place, current, before, after, damping, inflow,
+    term, decay, weights, base, force_weight, scale,
 ):
     stations, height, width = current.shape
     first = place[1] == 1
@@ -136,7 +128,8 @@
             right = jnp.where(lane == width - 1, 0.0, pltpu.roll(here, width - 1, 1))
             t = VISCOSITY * (up + down + left + right - 4.0 * here)
             term[s, rows] = t
-            d = decay[s, rows]
+            d = decay_of(here, damping[s, rows])
+            decay[s, rows] = d
             if factor is None:
                 total, weight, factor = t, 1.0 - d, d
             else:
@@ -149,10 +142,13 @@
                 total = total + entry * inflow[rows]
             weights[s, rows] = weight
         base[rows] = total
-
-
-def solve_kernel(place, x0, x1, x2, x3, high_far, low_far, inverse_far, *rest):
-    *forces, p0, p1, p2, p3, plane, high, low, inverse, arrivals = rest
+        scale[rows] = factor
+
+
+def solve_kernel(
+    place, x0, x1, x2, x3, high_far, low_far, inverse_far, p0, p1, p2, p3,
+    plane, high, low, inverse, arrivals,
+):
     c = place[0]
     copies = [
         pltpu.make_async_copy(far_ref, ref, arrivals.at[i])
@@ -192,18 +188,11 @@
     plane[...] = right(left(modes))
     for r, ref in enumerate(outputs):
         b = lax.rem(c + r, count)
-        ref[0:height] = plane[pl.ds(pl.multiple_of(b * height, height), height), :]
-    if forces:
-        extra = p0.shape[0] - height
-        for r, ref in enumerate(outputs):
-            for q in range(height // extra):
-                ref[height : height + extra, LANE * q : LANE * (q + 1)] = forces[-r][
-                    extra * q : extra * (q + 1)
-                ]
+        ref[...] = plane[pl.ds(pl.multiple_of(b * height, height), height), :]
 
 
 def disc_kernel(d0, d1, d2, d3, owners, *rest):
-    *blades, f0, f1, f2, f3, plane, total = rest
+    *blades, forces, plane, total = rest
     step = pl.program_id(0)
     height = d0.shape[0]
 
@@ -229,40 +218,46 @@
 
     @pl.when(step == pl.num_programs(0) - 1)
     def _():
-        for r, ref in enumerate((f0, f1, f2, f3)):
-            ref[...] = jnp.tanh(total[height * r : height * (r + 1)])
-
-
-def offset_kernel(place, *rest):
+        forces[...] = jnp.tanh(total[...])
+
+
+def share_kernel(place, own, other, f0, f1, f2, f3):
+    height = f0.shape[0]
+    for r, ref in enumerate((f0, f1, f2, f3)):
+        rows = slice(height * r, height * (r + 1))
+        ref[...] = jnp.where(place[4] == 1, own[rows] + other[rows], 0.0)
+
+
+def partial_kernel(place, p0, p1, p2, p3, weights, base, lead, lead_far, state):
     c = place[0]
-    pieces = rest[:4]
-    *forces, weights, base, force_weight, lead, lead_far, force, offset = rest[4:]
-    count, height, full = weights.shape
-    width = full // count
-    for r in range(count):
-        b = lax.rem(c + r if forces else c - r + count, count)
-        lanes = pl.ds(pl.multiple_of(b * width, width), width)
-        if forces:
-            force[:, lanes] = forces[r][...]
-        else:
-            extra = pieces[r].shape[0] - height
-            for q in range(height // extra):
-                force[extra * q : extra * (q + 1), lanes] = pieces[r][
-                    height : height + extra, width * q : width * (q + 1)
-                ]
-
+    pieces = (p0, p1, p2, p3)
+    count, height, _ = weights.shape
     for r in range(count):
         @pl.when(c == r)
         def _():
-            lead[...] = pieces[r][0:height]
-            lead_far[...] = pieces[r][0:height]
-
-    for g, rows in groups(height):
-        state = base[rows] + force_weight[rows] * force[rows]
+            lead[...] = pieces[r][...]
+            lead_far[...] = pieces[r][...]
+
+    for _, rows in groups(height):
+        total = base[rows]
         for r in range(count):
             s = lax.rem(c - r + count, count)
-            state = state + weights[s, rows] * pieces[r][rows]
-        to_chunks(offset, g, state)
+            total = total + weights[s, rows] * pieces[r][rows]
+        state[rows] = total
+
+
+def offset_kernel(place, f0, f1, f2, f3, state, force_weight, scale, force, chunks):
+    c = place[0]
+    forces = (f0, f1, f2, f3)
+    count = len(forces)
+    height, full = state.shape
+    width = full // count
+    for r in range(count):
+        b = lax.rem(c + r, count)
+        force[:, pl.ds(pl.multiple_of(b * width, width), width)] = forces[r][...]
+    for g, rows in groups(height):
+        to_chunks(chunks, g, state[rows] + force_weight[rows] * force[rows])
+        to_chunks(chunks, g, scale[rows], chunks.shape[1] // 2)
 
 
 def change_kernel(place, p0, p1, p2, p3, term, force, change, pressure):
@@ -283,12 +278,13 @@
             change[s, rows] = value
 
 
-def scan_kernel(scale, offset, entering):
+def scan_kernel(chunks, entering):
+    half = entering.shape[1]
     entering[0] = jnp.zeros_like(entering[0])
-    state = offset[0]
-    for m in range(1, scale.shape[0]):
+    state = chunks[0, 0:half]
+    for m in range(1, chunks.shape[0]):
         entering[m] = state
-        state = scale[m] * state + offset[m]
+        state = chunks[m, half : 2 * half] * state + chunks[m, 0:half]
 
 
 def march_rows(first, g, rows, entering, change, following, decay, lead, inflow):
@@ -305,22 +301,16 @@
 
 
 def middle_kernel(
-    place, entering, change, following, decay, lead, inflow, damping,
-    current, decay_new, scale, disc, x0, x1, x2, x3, source,
+    place, entering, change, following, decay, lead, inflow,
+    current, disc, x0, x1, x2, x3, source,
 ):
     first = place[1]
     stations, height, _ = current.shape
     for g, rows in groups(height):
         states = march_rows(first, g, rows, entering, change, following, decay, lead, inflow)
-        product = None
         for s in range(stations):
-            value = states[s + 1]
-            current[s, rows] = value
-            source[s, rows] = SOURCE_GAIN * (value - states[s])
-            d = decay_of(value, damping[s, rows])
-            decay_new[s, rows] = d
-            product = d if product is None else product * d
-        to_chunks(scale, g, product)
+            current[s, rows] = states[s + 1]
+            source[s, rows] = SOURCE_GAIN * (states[s + 1] - states[s])
     outs = (x0, x1, x2, x3)
     send_order(place, pl.program_id(0), source, outs)
     send_edges(current, outs)
@@ -401,25 +391,28 @@
     return pl.pallas_call(
         disc_kernel,
         grid=(number // per_step,),
-        out_shape=[near((height, LANE))] * count,
+        out_shape=near((count * height, LANE)),
         in_specs=[fixed((height, width))] * count
         + [fixed(owners.shape)]
         + [table(k) for k in range(streams)],
-        out_specs=[fixed((height, LANE))] * count,
+        out_specs=fixed((count * height, LANE)),
         scratch_shapes=[
             pltpu.VMEM((count * height, width), BF16),
             pltpu.VMEM((count * height, LANE), F32),
         ],
         compiler_params=pltpu.CompilerParams(vmem_limit_bytes=16 * MIB),
-        cost_estimate=cost(2 * number * width * width * LANE, 5 * MIB),
+        cost_estimate=cost(1, 1),
     )(*rows, stay(owners), *[stay(blades)] * streams)
 
 
 def local(velocity_guess, damping, inflow, disc_rows, owner, blade):
     stations, height, width = velocity_guess.shape
-    march_size = lax.axis_size("march")
+    cores = lax.axis_size("core")
+    march_size = lax.axis_size("chip") * cores
     cross_size = lax.axis_size("cross")
-    march_index = lax.axis_index("march")
+    chip_index = lax.axis_index("chip")
+    core_index = lax.axis_index("core")
+    march_index = chip_index * cores + core_index
     cross_index = lax.axis_index("cross")
     disc_slab = stations * march_size // 2 // stations
     at_disc = march_index == disc_slab
@@ -430,6 +423,7 @@
             first.astype(jnp.int32),
             (cross_index == 0).astype(jnp.int32),
             (cross_index == cross_size - 1).astype(jnp.int32),
+            at_disc.astype(jnp.int32),
         ]
     )
     tabled = [stay(jnp.asarray(t)) for t in tables(width)]
@@ -451,28 +445,35 @@
     def along_march(value, steps):
         count = march_size
         return lax.ppermute(
-            value, "march", [(i, i + steps) for i in range(count) if 0 <= i + steps < count]
+            value, MARCH, [(i, i + steps) for i in range(count) if 0 <= i + steps < count]
         )
 
     def across_march(value):
-        return lax.all_to_all(value, "march", split_axis=0, concat_axis=0, tiled=True)
-
-    blades = lax.all_gather(blade, "march", axis=0, tiled=True)
+        return lax.all_to_all(value, MARCH, split_axis=0, concat_axis=0, tiled=True)
+
+    def swap(value):
+        return lax.ppermute(value, "core", [(i, (i + 1) % cores) for i in range(cores)])
+
+    def share(value):
+        return jnp.where(core_index == disc_slab % cores, value, swap(value))
+
+    blades = lax.all_gather(blade, "chip", axis=0, tiled=True)
     blocks = (cross_index - jnp.arange(cross_size, dtype=jnp.int32) + cross_size) % cross_size
     ids = (blocks[:, None] * height + jnp.arange(height, dtype=jnp.int32)[None, :]).reshape(-1)
     owners = jnp.max(
         jnp.where(ids[:, None] == disc_rows[None, :], owner[None, :], -1), axis=1
     )
-    owners = jnp.where(at_disc, owners, -1)
+    here = (chip_index == disc_slab // cores) & (owners % cores == core_index)
+    owners = jnp.where(here & (owners >= 0), owners // cores, -1)
     owners = jnp.broadcast_to(owners[:, None], (cross_size * height, LANE))
 
     step = (stations, height // STEPS, width)
-    turned = range(4, 8)
+    turned = range(2, 6)
     near_inflow = stay(inflow)
     upstream = along_march(velocity_guess[-1], 1)
     current = stay(velocity_guess)
     disc = velocity_guess[0].astype(BF16)
-    rows = turns([disc] * cross_size)
+    rows = turns([share(disc)] * cross_size)
     source = by_rows(
         source_kernel,
         height,
@@ -483,63 +484,54 @@
         whole=range(4),
         scratch=[pltpu.VMEM(step, F32)],
     )
-    guess, damp, *source = lax.optimization_barrier((velocity_guess, damping, *source))
-    decay, scale = by_rows(
-        decay_kernel,
-        height,
-        [far(slab), far(chunks)],
-        place,
-        (stay(guess), stay(damp)),
-        cost(4e6, 3 * MIB),
-    )
     for sweep_index in range(SWEEPS):
-        merged = sweep_index > 0
         final = sweep_index == SWEEPS - 1
-        if merged:
-            rows = turns([disc] * cross_size)
         arrived = turns(source)
-        extra = []
-        piece = plane
-        if not merged:
-            scales = across_march(scale)
-        if merged:
-            extra = disc_forces(rows, owners, blades)
-            piece = (height + height * LANE // width, width)
+        if sweep_index > 0:
+            rows = turns([share(disc)] * cross_size)
         solved = pl.pallas_call(
             solve_kernel,
-            out_shape=[near(piece)] * cross_size,
-            in_specs=[SMEM]
-            + [VMEM] * cross_size
-            + [pl.BlockSpec(memory_space=pltpu.HBM)] * 3
-            + [VMEM] * len(extra),
+            out_shape=[near(plane)] * cross_size,
+            in_specs=[SMEM] + [VMEM] * cross_size + [pl.BlockSpec(memory_space=pltpu.HBM)] * 3,
             out_specs=[VMEM] * cross_size,
             scratch_shapes=[pltpu.VMEM((width, width), F32)]
             + [pltpu.VMEM((width, width), BF16)] * 2
             + [pltpu.VMEM((width, width), F32), pltpu.SemaphoreType.DMA((3,))],
             compiler_params=pltpu.CompilerParams(vmem_limit_bytes=20 * MIB),
             cost_estimate=cost(3 * 8 * width**3, 5 * MIB),
-        )(place, *arrived, *tabled, *extra)
-        forces = []
-        if merged:
-            scales = across_march(scale)
-        else:
-            rows, scales, solved = lax.optimization_barrier((rows, scales, solved))
-            forces = turns(disc_forces(rows, owners, blades), -1)
+        )(place, *arrived, *tabled)
+        rows, solved = lax.optimization_barrier((rows, solved))
         pieces = turns(solved)
-        decay = stay(decay)
-        term, weights, base, force_weight = call(
+        part = disc_forces(rows, owners, blades)
+        forces = call(
+            share_kernel,
+            [near((height, LANE))] * cross_size,
+            (place, part, swap(part)),
+            cost(1, 1),
+            scalars=1,
+        )
+        forces = turns(forces, -1)
+        term, decay, weights, base, force_weight, scale = call(
             weights_kernel,
-            [far(slab), near(slab), near(plane), near(plane)],
-            (place, current, arrived[1], arrived[-1], decay, near_inflow),
-            cost(8e6, 4 * MIB),
+            [far(slab), far(slab), near(slab), near(plane), near(plane), near(plane)],
+            (place, current, arrived[1], arrived[-1], stay(damping), near_inflow),
+            cost(1, 1),
             scalars=1,
             limit=12,
         )
-        lead, lead_far, force, offset = call(
+        lead, lead_far, state = call(
+            partial_kernel,
+            [near(plane), far(plane), near(plane)],
+            (place, *pieces, weights, base),
+            cost(2e6, 2 * MIB),
+            scalars=1,
+            limit=12,
+        )
+        force, offset = call(
             offset_kernel,
-            [near(plane), far(plane), far(plane), far(chunks)],
-            (place, *pieces, *forces, weights, base, force_weight),
-            cost(2e6, 3 * MIB),
+            [far(plane), far((march_size, 2 * chunks[1], LANE))],
+            (place, *forces, state, force_weight, scale),
+            cost(2e6, MIB),
             scalars=1,
             limit=12,
         )
@@ -554,22 +546,29 @@
             cost(4e6, 4 * MIB),
         )
         (entering,) = call(
-            scan_kernel, [far(chunks)], (scales, across_march(offset)), cost(1e5, MIB)
+            scan_kernel, [far(chunks)], (across_march(offset),), cost(1e5, MIB)
         )
         entering = across_march(entering)
-        common = (entering, stay(change), stay(following), decay, stay(lead_far), near_inflow)
+        common = (
+            entering,
+            stay(change),
+            stay(following),
+            stay(decay),
+            stay(lead_far),
+            near_inflow,
+        )
         if final:
             (current,) = by_rows(
                 last_kernel, height, [far(slab)], place, common, cost(4e6, 5 * MIB)
             )
             return (current, pressure)
-        current, decay, scale, disc, *source = by_rows(
+        current, disc, *source = by_rows(
             middle_kernel,
             height,
-            [far(slab), far(slab), far(chunks), near(plane, BF16)] + sources,
+            [far(slab), near(plane, BF16)] + sources,
             place,
-            common + (stay(damping),),
-            cost(8e6, 8 * MIB),
+            common,
+            cost(6e6, 5 * MIB),
             whole=turned,
             scratch=[pltpu.VMEM(step, F32)],
         )
@@ -577,13 +576,16 @@
 
 
 def solution(mesh):
+    march_size, cross_size = (mesh.shape[name] for name in ("march", "cross"))
+    devices = mesh.devices.reshape(march_size // 2, 2, cross_size)
+    mesh = Mesh(devices, (*MARCH, "cross"))
     in_specs = (
-        P("march", "cross", None),
-        P("march", "cross", None),
+        P(MARCH, "cross", None),
+        P(MARCH, "cross", None),
         P("cross", None),
         P(),
         P(),
-        P("march", None, "cross"),
+        P(MARCH, None, "cross"),
     )
-    out_specs = (P("march", "cross", None), P("march", "cross", None))
+    out_specs = (P(MARCH, "cross", None), P(MARCH, "cross", None))
     return jax.shard_map(local, mesh=mesh, in_specs=in_specs, out_specs=out_specs, check_vma=False)

time: 196 us -> 209 us (1.066)
  waiting for transfers between devices: 40.9 us -> 57.7 us
  Pallas kernels: 57.2 us -> 52.9 us
    ppermute x21 -> x24, starting transfers between devices: 32.1 us -> 42.5 us  [turn(): lax.ppermute(value, 'cross', [(i, (i + steps) % cross_size) for i in rang...]
    all_to_all x6 -> x4, starting transfers between devices: 31.6 us -> 22 us  [across_march(): return lax.all_to_all(value, MARCH, split_axis=0, concat_axis=0, tiled=True)]
    ppermute x21 -> x24, waiting for transfers between devices: 16.1 us -> 21 us  [turn(): lax.ppermute(value, 'cross', [(i, (i + steps) % cross_size) for i in rang...]
    all_gather x1, waiting for transfers between devices: 7.12 us -> 11.9 us  [local(): blades = lax.all_gather(blade, 'chip', axis=0, tiled=True)]
    pallas_call x6 -> x5, Pallas kernels: 24.4 us -> 19.6 us  [by_rows(): pl.pallas_call(kernel, grid_spec=pltpu.PrefetchScalarGridSpec(num_scalar_...]
    pallas_call x6 -> x10, Pallas kernels: 12 us -> 16.5 us  [call(): pl.pallas_call(kernel, out_shape=outs, in_specs=[SMEM] * scalars + [VMEM]...]
    pallas_call x4, Pallas kernels: 20.8 us -> 16.8 us  [the longest x2 11.1 us: local(): pl.pallas_call(solve_kernel, out_shape=[near(plane)] * cross_size, in_spe...]
    ppermute x3 -> x7, waiting for transfers between devices: 2.7 us -> 6.28 us  [the longest x3 6.27 us: along_march(): lax.ppermute(value, MARCH, [(i, i + steps) for i in range(count) if 0 <=...]
  transfers between devices with their start and end apart: 31 -> 36, of which waited for: 16 -> 14; matrix products, arithmetic and copies ran while one was open for 2% -> 2% of each run, Pallas kernels for 21% -> 17%
where the time goes in v4:
time: 209 us; the launch traced here: 206 us
  starting transfers between devices  76.1 us (36%)
  waiting for transfers between devices  57.7 us (28%)
  Pallas kernels  52.9 us (25%)
  between operations  14.3 us (7%)
  local copies, waits for them, and re-layouts  2.87 us (1%)
    ppermute x24, starting transfers between devices, turn(): lax.ppermute(value, 'cross', [(i, (i + steps) % cross_size) for i in rang...  42.5 us
    all_to_all x4, starting transfers between devices, across_march(): return lax.all_to_all(value, MARCH, split_axis=0, concat_axis=0, tiled=True)  22 us
    ppermute x24, waiting for transfers between devices, turn(): lax.ppermute(value, 'cross', [(i, (i + steps) % cross_size) for i in rang...  21 us
    pallas_call x5, Pallas kernels, by_rows(): pl.pallas_call(kernel, grid_spec=pltpu.PrefetchScalarGridSpec(num_scalar_...  19.6 us
    all_to_all x4, waiting for transfers between devices, across_march(): return lax.all_to_all(value, MARCH, split_axis=0, concat_axis=0, tiled=True)  17.8 us
    pallas_call x10, Pallas kernels, call(): pl.pallas_call(kernel, out_shape=outs, in_specs=[SMEM] * scalars + [VMEM]...  16.5 us
    all_gather x1, waiting for transfers between devices, local(): blades = lax.all_gather(blade, 'chip', axis=0, tiled=True)  11.9 us
    pallas_call x2, Pallas kernels, local(): pl.pallas_call(solve_kernel, out_shape=[near(plane)] * cross_size, in_spe...  11.1 us
  transfers between devices with their start and end apart: 36, of which 14 were waited for; matrix products, arithmetic and copies ran while one was open for 2% of the time, Pallas kernels for 17%

profile of v4, /device:TPU:2, one launch (start us, length us, event | category | flops | bytes accessed | tf_op | source)
XLA Modules:
  0.0 205.9 jit_solution(3108553628218127696)
XLA Ops:
  9.9 2.4 %collective-permute-start.4 = (f32[128,512]{1,0:T(8,128)S(1)}, f32[128,512]{1,0:T(8,128)S(1)}, u32[]{:S(2)}, u32[]{:S(2)}) collective-permute-start(f32[128,512]{1,0:T(8,128)S(1)} %slice_bitcast_fusion), channel_id=1, source_target_pairs={{0,4},{4,8},{8,12},{12,16},{16,20},{20,24},{24,28},{28,32},{32,36}... | collective-permute-start | bytes 786440 | tf_op jit(solution)/shard_map/ppermute | solution.py:447
  13.5 6.3 %collective-permute-done.4.upstream = f32[128,512]{1,0:T(8,128)S(1)} collective-permute-done((f32[128,512]{1,0:T(8,128)S(1)}, f32[128,512]{1,0:T(8,128)S(1)}, u32[]{:S(2)}, u32[]{:S(2)}) %collective-permute-start.4) | collective-permute-done | bytes 262176 | tf_op jit(solution)/shard_map/ppermute | solution.py:447
  19.7 2.8 %shard_map.104 = (f32[128,512]{1,0:T(8,128)S(1)}, f32[136,512]{1,0:T(8,128)S(1)}, f32[128,512]{1,0:T(8,128)S(1)}, f32[136,512]{1,0:T(8,128)S(1)}) custom-call(s32[5]{0:T(128)S(1)} %stack.39.place, f32[4,128,512]{2,1,0:T(8,128)} %current.3, f32[128,512]{1,0:T(8,128)S(1)} %collective-permute-done.4.upstream, f32[128,512]{1,0:T(8,128)} %inflow.9), custom_call_target="tpu_custom_call" | custom-call | flops 1000000 | bytes 2097152 | tf_op jit(solution)/shard_map/pallas_call | solution.py:369
  22.5 4.0 %collective-permute-start.6 = (f32[128,512]{1,0:T(8,128)S(1)}, f32[128,512]{1,0:T(8,128)S(1)}, u32[]{:S(2)}, u32[]{:S(2)}) collective-permute-start(f32[128,512]{1,0:T(8,128)S(1)} %get-tuple-element.83), channel_id=1, source_target_pairs={{0,2},{1,3},{2,0},{3,1},{4,6},{5,7},{6,4},{7,5},{8,10},{9,11},{10,... | collective-permute-start | bytes 786440 | tf_op jit(solution)/shard_map/ppermute | solution.py:438
  27.5 2.2 %collective-permute-start.7 = (f32[136,512]{1,0:T(8,128)S(1)}, f32[136,512]{1,0:T(8,128)S(1)}, u32[]{:S(2)}, u32[]{:S(2)}) collective-permute-start(f32[136,512]{1,0:T(8,128)S(1)} %get-tuple-element.84), channel_id=1, source_target_pairs={{0,3},{1,0},{2,1},{3,2},{4,7},{5,4},{6,5},{7,6},{8,11},{9,8},{10,9... | collective-permute-start | bytes 835592 | tf_op jit(solution)/shard_map/ppermute | solution.py:438
  30.8 1.9 collective-permute-start.2
  33.8 1.5 collective-permute-start.1
  35.3 3.5 %collective-permute-done.5.x1.before = f32[136,512]{1,0:T(8,128)S(1)} collective-permute-done((f32[136,512]{1,0:T(8,128)S(1)}, f32[136,512]{1,0:T(8,128)S(1)}, u32[]{:S(2)}, u32[]{:S(2)}) %collective-permute-start.5) | collective-permute-done | bytes 278560 | tf_op jit(solution)/shard_map/ppermute | solution.py:438
  39.5 5.6 %shard_map.105 = (f32[128,512]{1,0:T(8,128)S(1)}, f32[128,512]{1,0:T(8,128)S(1)}, f32[128,512]{1,0:T(8,128)S(1)}, f32[128,512]{1,0:T(8,128)S(1)}) custom-call(s32[5]{0:T(128)S(1)} %stack.39.place, f32[128,512]{1,0:T(8,128)S(1)} %get-tuple-element.81.x0, f32[136,512]{1,0:T(8,128)S(1)} %collective-permute-done.5.x1.before, ...), custom_call_target="tpu_custom_call" | custom-call | flops 3221225472 | bytes 5242880 | tf_op jit(solution)/shard_map/pallas_call | solution.py:492
  45.1 11.9 %all-gather.2.cloned.1.call-done.rest_0_.rest_1_.rest_2_.rest_3_ = bf16[16,512,128]{2,1,0:T(8,128)(2,1)} async-done(((bf16[1,512,128]{2,1,0:T(8,128)(2,1)}), bf16[16,512,128]{2,1,0:T(8,128)(2,1)}) %all-gather.2.cloned.1.call-update) | async-done | bytes 2097168 | tf_op jit(solution)/shard_map/all_gather | solution.py:460
  57.8 2.8 %shard_map.106.own = f32[512,128]{1,0:T(8,128)S(1)} custom-call(bf16[128,512]{1,0:T(8,128)(2,1)S(1)} %broadcast_select_fusion.1.d0, bf16[128,512]{1,0:T(8,128)(2,1)S(1)} %collective-permute-done.1.d1, bf16[128,512]{1,0:T(8,128)(2,1)S(1)} %collective-permute-done.2.d2, bf16[128,512]{1,0:T(8,128)(2,1)S(1)} %collective-permute-done.3.d3, ...), custom_call_target="tpu_custom_call" | custom-call | flops 1 | bytes 1 | tf_op jit(solution)/shard_map/pallas_call | solution.py:391
  60.8 1.6 collective-permute-start.12
  62.4 2.9 %collective-permute-start.13 = (f32[128,512]{1,0:T(8,128)S(1)}, f32[128,512]{1,0:T(8,128)S(1)}, u32[]{:S(2)}, u32[]{:S(2)}) collective-permute-start(f32[128,512]{1,0:T(8,128)S(1)} %get-tuple-element.99), channel_id=1, source_target_pairs={{0,2},{1,3},{2,0},{3,1},{4,6},{5,7},{6,4},{7,5},{8,10},{9,11},{10,... | collective-permute-start | bytes 786440 | tf_op jit(solution)/shard_map/ppermute | solution.py:438
  65.3 1.4 collective-permute-start.14
  67.3 2.7 %collective-permute-start.10 = (f32[128,128]{1,0:T(8,128)S(1)}, f32[128,128]{1,0:T(8,128)S(1)}, u32[]{:S(2)}, u32[]{:S(2)}) collective-permute-start(f32[128,128]{1,0:T(8,128)S(1)} %get-tuple-element.95), channel_id=1, source_target_pairs={{0,2},{1,3},{2,0},{3,1},{4,6},{5,7},{6,4},{7,5},{8,10},{9,11},{10,... | collective-permute-start | bytes 196616 | tf_op jit(solution)/shard_map/ppermute | solution.py:438
  71.5 3.9 %shard_map.108 = (f32[4,128,512]{2,1,0:T(8,128)}, f32[4,128,512]{2,1,0:T(8,128)}, f32[4,128,512]{2,1,0:T(8,128)S(1)}, f32[128,512]{1,0:T(8,128)S(1)}, f32[128,512]{1,0:T(8,128)S(1)}, /*index=5*/f32[128,512]{1,0:T(8,128)S(1)}) custom-call(s32[5]{0:T(128)S(1)} %stack.39.place, f32[4,128,512]{2,1,0:T(8,128)} %current.3, ...), custom_call_target="tpu_custom_call" | custom-call | flops 1 | bytes 1 | tf_op jit(solution)/shard_map/pallas_call | solution.py:345
  75.5 2.6 %collective-permute-done.13.p2 = f32[128,512]{1,0:T(8,128)S(1)} collective-permute-done((f32[128,512]{1,0:T(8,128)S(1)}, f32[128,512]{1,0:T(8,128)S(1)}, u32[]{:S(2)}, u32[]{:S(2)}) %collective-permute-start.13) | collective-permute-done | bytes 262176 | tf_op jit(solution)/shard_map/ppermute | solution.py:438
  78.1 1.5 shard_map.109
  80.3 1.5 shard_map.110
  81.8 5.9 %all-to-all-start = ((f32[32,32,128]{2,1,0:T(8,128)}), f32[32,32,128]{2,1,0:T(8,128)S(1)}, u32[]{:S(2)}, u32[]{:S(2)}) async-start(f32[32,32,128]{2,1,0:T(8,128)} %get-tuple-element.108), calls=%async_computation | async-start | bytes 1048576 | tf_op jit(solution)/shard_map/all_to_all | solution.py:452
  87.7 4.3 %collective-permute-start.15 = (f32[128,512]{1,0:T(8,128)S(1)}, f32[128,512]{1,0:T(8,128)S(1)}, u32[]{:S(2)}, u32[]{:S(2)}) collective-permute-start(f32[128,512]{1,0:T(8,128)S(1)} %get-tuple-element.116), channel_id=1, source_target_pairs={{4,0},{8,4},{12,8},{16,12},{20,16},{24,20},{28,24},{32,28},{36,32}... | collective-permute-start | bytes 786440 | tf_op jit(solution)/shard_map/ppermute | solution.py:447
  92.0 5.3 %all-to-all-done.chunks = f32[32,32,128]{2,1,0:T(8,128)S(1)} async-done(((f32[32,32,128]{2,1,0:T(8,128)}), f32[32,32,128]{2,1,0:T(8,128)S(1)}, u32[]{:S(2)}, u32[]{:S(2)}) %all-to-all-start) | async-done | bytes 524320 | tf_op jit(solution)/shard_map/all_to_all | solution.py:452
  98.1 5.6 %all-to-all-start.1 = ((f32[32,16,128]{2,1,0:T(8,128)}), f32[32,16,128]{2,1,0:T(8,128)S(1)}, u32[]{:S(2)}, u32[]{:S(2)}) async-start(f32[32,16,128]{2,1,0:T(8,128)} %shard_map.111), calls=%async_computation.1 | async-start | bytes 524288 | tf_op jit(solution)/shard_map/all_to_all | solution.py:452
  103.7 4.2 %shard_map.112 = (f32[4,128,512]{2,1,0:T(8,128)}, f32[4,128,512]{2,1,0:T(8,128)}) custom-call(s32[5]{0:T(128)S(1)} %stack.39.place, f32[128,512]{1,0:T(8,128)S(1)} %get-tuple-element.109.p0, f32[128,512]{1,0:T(8,128)S(1)} %collective-permute-done.12.p1, f32[128,512]{1,0:T(8,128)S(1)} %collective-permute-done.13.p2, ...), custom_call_target="tpu_custom_call" | custom-call | flops 4000000 | bytes 4194304 | tf_op jit(solution)/shard_map/pallas_call | solution.py:369
  107.9 3.5 %all-to-all-done.1.entering = f32[32,16,128]{2,1,0:T(8,128)S(1)} async-done(((f32[32,16,128]{2,1,0:T(8,128)}), f32[32,16,128]{2,1,0:T(8,128)S(1)}, u32[]{:S(2)}, u32[]{:S(2)}) %all-to-all-start.1) | async-done | bytes 262176 | tf_op jit(solution)/shard_map/all_to_all | solution.py:452
  111.4 4.3 %shard_map.113 = (f32[4,128,512]{2,1,0:T(8,128)}, bf16[128,512]{1,0:T(8,128)(2,1)S(1)}, f32[128,512]{1,0:T(8,128)S(1)}, f32[136,512]{1,0:T(8,128)S(1)}, f32[128,512]{1,0:T(8,128)S(1)}, /*index=5*/f32[136,512]{1,0:T(8,128)S(1)}) custom-call(s32[5]{0:T(128)S(1)} %stack.39.place, f32[32,16,128]{2,1,0:T(8,128)S(1)} %all-to-all-done.1.entering, ...), custom_call_target="tpu_custom_call" | custom-call | flops 6000000 | bytes 5242880 | tf_op jit(solution)/shard_map/pallas_call | solution.py:369
  116.0 2.0 collective-permute-start.20
  118.0 1.2 collective-permute-start.22
  120.1 2.7 %collective-permute-start.19 = (bf16[128,512]{1,0:T(8,128)(2,1)S(1)}, bf16[128,512]{1,0:T(8,128)(2,1)S(1)}, u32[]{:S(2)}, u32[]{:S(2)}) collective-permute-start(bf16[128,512]{1,0:T(8,128)(2,1)S(1)} %broadcast_select_fusion.d0), channel_id=1, source_target_pairs={{0,3},{1,0},{2,1},{3,2},{4,7},{5,4},{6,5},{7,6},{8,11},{9,8},{10,9... | collective-permute-start | bytes 393224 | tf_op jit(solution)/shard_map/ppermute | solution.py:438
  123.2 9.5 %collective-permute-done.21.x2 = f32[128,512]{1,0:T(8,128)S(1)} collective-permute-done((f32[128,512]{1,0:T(8,128)S(1)}, f32[128,512]{1,0:T(8,128)S(1)}, u32[]{:S(2)}, u32[]{:S(2)}) %collective-permute-start.21) | collective-permute-done | bytes 262176 | tf_op jit(solution)/shard_map/ppermute | solution.py:438
  132.7 1.5 collective-permute-start.17
  134.2 5.6 %shard_map.114 = (f32[128,512]{1,0:T(8,128)S(1)}, f32[128,512]{1,0:T(8,128)S(1)}, f32[128,512]{1,0:T(8,128)S(1)}, f32[128,512]{1,0:T(8,128)S(1)}) custom-call(s32[5]{0:T(128)S(1)} %stack.39.place, f32[128,512]{1,0:T(8,128)S(1)} %get-tuple-element.120.x0, f32[136,512]{1,0:T(8,128)S(1)} %collective-permute-done.20.x1.before, ...), custom_call_target="tpu_custom_call" | custom-call | flops 3221225472 | bytes 5242880 | tf_op jit(solution)/shard_map/pallas_call | solution.py:492
  139.8 2.9 %shard_map.115.own = f32[512,128]{1,0:T(8,128)S(1)} custom-call(bf16[128,512]{1,0:T(8,128)(2,1)S(1)} %broadcast_select_fusion.d0, bf16[128,512]{1,0:T(8,128)(2,1)S(1)} %collective-permute-done.17.d1, bf16[128,512]{1,0:T(8,128)(2,1)S(1)} %collective-permute-done.18.d2, bf16[128,512]{1,0:T(8,128)(2,1)S(1)} %collective-permute-done.19.d3, ...), custom_call_target="tpu_custom_call" | custom-call | flops 1 | bytes 1 | tf_op jit(solution)/shard_map/pallas_call | solution.py:391
  143.2 2.9 %collective-permute-start.28 = (f32[128,512]{1,0:T(8,128)S(1)}, f32[128,512]{1,0:T(8,128)S(1)}, u32[]{:S(2)}, u32[]{:S(2)}) collective-permute-start(f32[128,512]{1,0:T(8,128)S(1)} %get-tuple-element.138), channel_id=1, source_target_pairs={{0,2},{1,3},{2,0},{3,1},{4,6},{5,7},{6,4},{7,5},{8,10},{9,11},{10,... | collective-permute-start | bytes 786440 | tf_op jit(solution)/shard_map/ppermute | solution.py:438
  146.1 2.5 %collective-permute-start.29 = (f32[128,512]{1,0:T(8,128)S(1)}, f32[128,512]{1,0:T(8,128)S(1)}, u32[]{:S(2)}, u32[]{:S(2)}) collective-permute-start(f32[128,512]{1,0:T(8,128)S(1)} %get-tuple-element.139), channel_id=1, source_target_pairs={{0,3},{1,0},{2,1},{3,2},{4,7},{5,4},{6,5},{7,6},{8,11},{9,8},{10,9... | collective-permute-start | bytes 786440 | tf_op jit(solution)/shard_map/ppermute | solution.py:438
  149.3 1.5 collective-permute-start.25
  150.8 2.0 collective-permute-done.27.p1
  152.8 6.3 %collective-permute-start.26 = (f32[128,128]{1,0:T(8,128)S(1)}, f32[128,128]{1,0:T(8,128)S(1)}, u32[]{:S(2)}, u32[]{:S(2)}) collective-permute-start(f32[128,128]{1,0:T(8,128)S(1)} %get-tuple-element.135), channel_id=1, source_target_pairs={{0,1},{1,2},{2,3},{3,0},{4,5},{5,6},{6,7},{7,4},{8,9},{9,10},{10,1... | collective-permute-start | bytes 196616 | tf_op jit(solution)/shard_map/ppermute | solution.py:438
  159.1 3.9 %shard_map.117 = (f32[4,128,512]{2,1,0:T(8,128)}, f32[4,128,512]{2,1,0:T(8,128)}, f32[4,128,512]{2,1,0:T(8,128)S(1)}, f32[128,512]{1,0:T(8,128)S(1)}, f32[128,512]{1,0:T(8,128)S(1)}, /*index=5*/f32[128,512]{1,0:T(8,128)S(1)}) custom-call(s32[5]{0:T(128)S(1)} %stack.39.place, f32[4,128,512]{2,1,0:T(8,128)} %get-tuple-element.140.current, ...), custom_call_target="tpu_custom_call" | custom-call | flops 1 | bytes 1 | tf_op jit(solution)/shard_map/pallas_call | solution.py:345
  163.0 1.5 shard_map.118
  164.5 1.5 shard_map.119
  166.0 5.1 %all-to-all-start.2 = ((f32[32,32,128]{2,1,0:T(8,128)}), f32[32,32,128]{2,1,0:T(8,128)S(1)}, u32[]{:S(2)}, u32[]{:S(2)}) async-start(f32[32,32,128]{2,1,0:T(8,128)} %get-tuple-element.148), calls=%async_computation.2 | async-start | bytes 1048576 | tf_op jit(solution)/shard_map/all_to_all | solution.py:452
  171.1 4.3 %collective-permute-start.30 = (f32[128,512]{1,0:T(8,128)S(1)}, f32[128,512]{1,0:T(8,128)S(1)}, u32[]{:S(2)}, u32[]{:S(2)}) collective-permute-start(f32[128,512]{1,0:T(8,128)S(1)} %get-tuple-element.156), channel_id=1, source_target_pairs={{4,0},{8,4},{12,8},{16,12},{20,16},{24,20},{28,24},{32,28},{36,32}... | collective-permute-start | bytes 786440 | tf_op jit(solution)/shard_map/ppermute | solution.py:447
  175.4 5.4 %all-to-all-done.2.chunks = f32[32,32,128]{2,1,0:T(8,128)S(1)} async-done(((f32[32,32,128]{2,1,0:T(8,128)}), f32[32,32,128]{2,1,0:T(8,128)S(1)}, u32[]{:S(2)}, u32[]{:S(2)}) %all-to-all-start.2) | async-done | bytes 524320 | tf_op jit(solution)/shard_map/all_to_all | solution.py:452
  181.6 5.5 %all-to-all-start.3 = ((f32[32,16,128]{2,1,0:T(8,128)}), f32[32,16,128]{2,1,0:T(8,128)S(1)}, u32[]{:S(2)}, u32[]{:S(2)}) async-start(f32[32,16,128]{2,1,0:T(8,128)} %shard_map.120), calls=%async_computation.3 | async-start | bytes 524288 | tf_op jit(solution)/shard_map/all_to_all | solution.py:452
  187.2 4.2 %shard_map.121 = (f32[4,128,512]{2,1,0:T(8,128)}, f32[4,128,512]{2,1,0:T(8,128)}) custom-call(s32[5]{0:T(128)S(1)} %stack.39.place, f32[128,512]{1,0:T(8,128)S(1)} %get-tuple-element.149.p0, f32[128,512]{1,0:T(8,128)S(1)} %collective-permute-done.27.p1, f32[128,512]{1,0:T(8,128)S(1)} %collective-permute-done.28.p2, ...), custom_call_target="tpu_custom_call" | custom-call | flops 4000000 | bytes 4194304 | tf_op jit(solution)/shard_map/pallas_call | solution.py:369
  191.3 3.5 %all-to-all-done.3.entering = f32[32,16,128]{2,1,0:T(8,128)S(1)} async-done(((f32[32,16,128]{2,1,0:T(8,128)}), f32[32,16,128]{2,1,0:T(8,128)S(1)}, u32[]{:S(2)}, u32[]{:S(2)}) %all-to-all-start.3) | async-done | bytes 262176 | tf_op jit(solution)/shard_map/all_to_all | solution.py:452
  194.9 4.2 %shard_map.122 = f32[4,128,512]{2,1,0:T(8,128)} custom-call(s32[5]{0:T(128)S(1)} %stack.39.place, f32[32,16,128]{2,1,0:T(8,128)S(1)} %all-to-all-done.3.entering, f32[4,128,512]{2,1,0:T(8,128)} %get-tuple-element.155.change, f32[128,512]{1,0:T(8,128)} %copy-done, f32[4,128,512]{2,1,0:T(8,128)} %get-tuple-element.157.decay, ...), custom_call_target="tpu_custom_call" | custom-call | flops 4000000 | bytes 5242880 | tf_op jit(solution)/shard_map/pallas_call | solution.py:369
  (58 shorter events, 15.9 us)
Async XLA Ops:
  7.2 49.8 %all-gather.2.cloned.1.call-start = ((), (), s32[]{:S(2)}) async-start(), calls=%async_computation.4 | async-start | bytes 2228224 | tf_op jit(solution)/shard_map/all_gather | solution.py:460
  8.9 20.9 %collective-permute-start = (bf16[128,512]{1,0:T(8,128)(2,1)S(1)}, bf16[128,512]{1,0:T(8,128)(2,1)S(1)}, u32[]{:S(2)}, u32[]{:S(2)}) collective-permute-start(bf16[128,512]{1,0:T(8,128)(2,1)S(1)} %fusion), channel_id=1, source_target_pairs={{0,4},{4,0},{1,5},{5,1},{2,6},{6,2},{3,7},{7,3},{8,12},{12,8},{9,1... | collective-permute-start | bytes 393224 | tf_op jit(solution)/shard_map/ppermute | solution.py:455
  9.9 9.8 %collective-permute-start.4 = (f32[128,512]{1,0:T(8,128)S(1)}, f32[128,512]{1,0:T(8,128)S(1)}, u32[]{:S(2)}, u32[]{:S(2)}) collective-permute-start(f32[128,512]{1,0:T(8,128)S(1)} %slice_bitcast_fusion), channel_id=1, source_target_pairs={{0,4},{4,8},{8,12},{12,16},{16,20},{20,24},{24,28},{28,32},{32,36}... | collective-permute-start | bytes 786440 | tf_op jit(solution)/shard_map/ppermute | solution.py:447
  22.5 11.2 %collective-permute-start.6 = (f32[128,512]{1,0:T(8,128)S(1)}, f32[128,512]{1,0:T(8,128)S(1)}, u32[]{:S(2)}, u32[]{:S(2)}) collective-permute-start(f32[128,512]{1,0:T(8,128)S(1)} %get-tuple-element.83), channel_id=1, source_target_pairs={{0,2},{1,3},{2,0},{3,1},{4,6},{5,7},{6,4},{7,5},{8,10},{9,11},{10,... | collective-permute-start | bytes 786440 | tf_op jit(solution)/shard_map/ppermute | solution.py:438
  26.5 12.3 %collective-permute-start.5 = (f32[136,512]{1,0:T(8,128)S(1)}, f32[136,512]{1,0:T(8,128)S(1)}, u32[]{:S(2)}, u32[]{:S(2)}) collective-permute-start(f32[136,512]{1,0:T(8,128)S(1)} %get-tuple-element.82), channel_id=1, source_target_pairs={{0,1},{1,2},{2,3},{3,0},{4,5},{5,6},{6,7},{7,4},{8,9},{9,10},{10,1... | collective-permute-start | bytes 835592 | tf_op jit(solution)/shard_map/ppermute | solution.py:438
  27.5 12.0 %collective-permute-start.7 = (f32[136,512]{1,0:T(8,128)S(1)}, f32[136,512]{1,0:T(8,128)S(1)}, u32[]{:S(2)}, u32[]{:S(2)}) collective-permute-start(f32[136,512]{1,0:T(8,128)S(1)} %get-tuple-element.84), channel_id=1, source_target_pairs={{0,3},{1,0},{2,1},{3,2},{4,7},{5,4},{6,5},{7,6},{8,11},{9,8},{10,9... | collective-permute-start | bytes 835592 | tf_op jit(solution)/shard_map/ppermute | solution.py:438
  30.7 14.4 %collective-permute-start.3 = (bf16[128,512]{1,0:T(8,128)(2,1)S(1)}, bf16[128,512]{1,0:T(8,128)(2,1)S(1)}, u32[]{:S(2)}, u32[]{:S(2)}) collective-permute-start(bf16[128,512]{1,0:T(8,128)(2,1)S(1)} %broadcast_select_fusion.1.d0), channel_id=1, source_target_pairs={{0,3},{1,0},{2,1},{3,2},{4,7},{5,4},{6,5},{7,6},{8,11},{9,8},{10,9... | collective-permute-start | bytes 393224 | tf_op jit(solution)/shard_map/ppermute | solution.py:438
  30.8 14.3 %collective-permute-start.2 = (bf16[128,512]{1,0:T(8,128)(2,1)S(1)}, bf16[128,512]{1,0:T(8,128)(2,1)S(1)}, u32[]{:S(2)}, u32[]{:S(2)}) collective-permute-start(bf16[128,512]{1,0:T(8,128)(2,1)S(1)} %broadcast_select_fusion.1.d0), channel_id=1, source_target_pairs={{0,2},{1,3},{2,0},{3,1},{4,6},{5,7},{6,4},{7,5},{8,10},{9,11},{10,... | collective-permute-start | bytes 393224 | tf_op jit(solution)/shard_map/ppermute | solution.py:438
  33.8 11.4 %collective-permute-start.1 = (bf16[128,512]{1,0:T(8,128)(2,1)S(1)}, bf16[128,512]{1,0:T(8,128)(2,1)S(1)}, u32[]{:S(2)}, u32[]{:S(2)}) collective-permute-start(bf16[128,512]{1,0:T(8,128)(2,1)S(1)} %broadcast_select_fusion.1.d0), channel_id=1, source_target_pairs={{0,1},{1,2},{2,3},{3,0},{4,5},{5,6},{6,7},{7,4},{8,9},{9,10},{10,1... | collective-permute-start | bytes 393224 | tf_op jit(solution)/shard_map/ppermute | solution.py:438
  60.7 5.9 %collective-permute-start.8 = (f32[512,128]{1,0:T(8,128)S(1)}, f32[512,128]{1,0:T(8,128)S(1)}, u32[]{:S(2)}, u32[]{:S(2)}) collective-permute-start(f32[512,128]{1,0:T(8,128)S(1)} %shard_map.106.own), channel_id=1, source_target_pairs={{0,4},{4,0},{1,5},{5,1},{2,6},{6,2},{3,7},{7,3},{8,12},{12,8},{9,1... | collective-permute-start | bytes 786440 | tf_op jit(solution)/shard_map/ppermute | solution.py:455
  60.8 9.9 %collective-permute-start.12 = (f32[128,512]{1,0:T(8,128)S(1)}, f32[128,512]{1,0:T(8,128)S(1)}, u32[]{:S(2)}, u32[]{:S(2)}) collective-permute-start(f32[128,512]{1,0:T(8,128)S(1)} %get-tuple-element.98), channel_id=1, source_target_pairs={{0,1},{1,2},{2,3},{3,0},{4,5},{5,6},{6,7},{7,4},{8,9},{9,10},{10,1... | collective-permute-start | bytes 786440 | tf_op jit(solution)/shard_map/ppermute | solution.py:438
  62.4 15.7 %collective-permute-start.13 = (f32[128,512]{1,0:T(8,128)S(1)}, f32[128,512]{1,0:T(8,128)S(1)}, u32[]{:S(2)}, u32[]{:S(2)}) collective-permute-start(f32[128,512]{1,0:T(8,128)S(1)} %get-tuple-element.99), channel_id=1, source_target_pairs={{0,2},{1,3},{2,0},{3,1},{4,6},{5,7},{6,4},{7,5},{8,10},{9,11},{10,... | collective-permute-start | bytes 786440 | tf_op jit(solution)/shard_map/ppermute | solution.py:438
  65.3 12.8 %collective-permute-start.14 = (f32[128,512]{1,0:T(8,128)S(1)}, f32[128,512]{1,0:T(8,128)S(1)}, u32[]{:S(2)}, u32[]{:S(2)}) collective-permute-start(f32[128,512]{1,0:T(8,128)S(1)} %get-tuple-element.100), channel_id=1, source_target_pairs={{0,3},{1,0},{2,1},{3,2},{4,7},{5,4},{6,5},{7,6},{8,11},{9,8},{10,9... | collective-permute-start | bytes 786440 | tf_op jit(solution)/shard_map/ppermute | solution.py:438
  67.2 12.3 %collective-permute-start.9 = (f32[128,128]{1,0:T(8,128)S(1)}, f32[128,128]{1,0:T(8,128)S(1)}, u32[]{:S(2)}, u32[]{:S(2)}) collective-permute-start(f32[128,128]{1,0:T(8,128)S(1)} %get-tuple-element.94), channel_id=1, source_target_pairs={{0,3},{1,0},{2,1},{3,2},{4,7},{5,4},{6,5},{7,6},{8,11},{9,8},{10,9... | collective-permute-start | bytes 196616 | tf_op jit(solution)/shard_map/ppermute | solution.py:438
  67.3 12.3 %collective-permute-start.10 = (f32[128,128]{1,0:T(8,128)S(1)}, f32[128,128]{1,0:T(8,128)S(1)}, u32[]{:S(2)}, u32[]{:S(2)}) collective-permute-start(f32[128,128]{1,0:T(8,128)S(1)} %get-tuple-element.95), channel_id=1, source_target_pairs={{0,2},{1,3},{2,0},{3,1},{4,6},{5,7},{6,4},{7,5},{8,10},{9,11},{10,... | collective-permute-start | bytes 196616 | tf_op jit(solution)/shard_map/ppermute | solution.py:438
  70.7 9.6 %collective-permute-start.11 = (f32[128,128]{1,0:T(8,128)S(1)}, f32[128,128]{1,0:T(8,128)S(1)}, u32[]{:S(2)}, u32[]{:S(2)}) collective-permute-start(f32[128,128]{1,0:T(8,128)S(1)} %get-tuple-element.96), channel_id=1, source_target_pairs={{0,1},{1,2},{2,3},{3,0},{4,5},{5,6},{6,7},{7,4},{8,9},{9,10},{10,1... | collective-permute-start | bytes 196616 | tf_op jit(solution)/shard_map/ppermute | solution.py:438
  81.8 15.6 %all-to-all-start = ((f32[32,32,128]{2,1,0:T(8,128)}), f32[32,32,128]{2,1,0:T(8,128)S(1)}, u32[]{:S(2)}, u32[]{:S(2)}) async-start(f32[32,32,128]{2,1,0:T(8,128)} %get-tuple-element.108), calls=%async_computation | async-start | bytes 1048576 | tf_op jit(solution)/shard_map/all_to_all | solution.py:452
  87.7 20.2 %collective-permute-start.15 = (f32[128,512]{1,0:T(8,128)S(1)}, f32[128,512]{1,0:T(8,128)S(1)}, u32[]{:S(2)}, u32[]{:S(2)}) collective-permute-start(f32[128,512]{1,0:T(8,128)S(1)} %get-tuple-element.116), channel_id=1, source_target_pairs={{4,0},{8,4},{12,8},{16,12},{20,16},{24,20},{28,24},{32,28},{36,32}... | collective-permute-start | bytes 786440 | tf_op jit(solution)/shard_map/ppermute | solution.py:447
  98.1 13.3 %all-to-all-start.1 = ((f32[32,16,128]{2,1,0:T(8,128)}), f32[32,16,128]{2,1,0:T(8,128)S(1)}, u32[]{:S(2)}, u32[]{:S(2)}) async-start(f32[32,16,128]{2,1,0:T(8,128)} %shard_map.111), calls=%async_computation.1 | async-start | bytes 524288 | tf_op jit(solution)/shard_map/all_to_all | solution.py:452
  107.9 3.5 %copy-start.1 = (f32[128,512]{1,0:T(8,128)}, f32[128,512]{1,0:T(8,128)S(1)}, u32[]{:S(2)}) copy-start(f32[128,512]{1,0:T(8,128)S(1)} %collective-permute-done.15.following) | copy-start | bytes 786436
  115.7 4.4 %collective-permute-start.16 = (bf16[128,512]{1,0:T(8,128)(2,1)S(1)}, bf16[128,512]{1,0:T(8,128)(2,1)S(1)}, u32[]{:S(2)}, u32[]{:S(2)}) collective-permute-start(bf16[128,512]{1,0:T(8,128)(2,1)S(1)} %get-tuple-element.119), channel_id=1, source_target_pairs={{0,4},{4,0},{1,5},{5,1},{2,6},{6,2},{3,7},{7,3},{8,12},{12,8},{9,1... | collective-permute-start | bytes 393224 | tf_op jit(solution)/shard_map/ppermute | solution.py:455
  116.0 18.2 %collective-permute-start.20 = (f32[136,512]{1,0:T(8,128)S(1)}, f32[136,512]{1,0:T(8,128)S(1)}, u32[]{:S(2)}, u32[]{:S(2)}) collective-permute-start(f32[136,512]{1,0:T(8,128)S(1)} %get-tuple-element.121), channel_id=1, source_target_pairs={{0,1},{1,2},{2,3},{3,0},{4,5},{5,6},{6,7},{7,4},{8,9},{9,10},{10,1... | collective-permute-start | bytes 835592 | tf_op jit(solution)/shard_map/ppermute | solution.py:438
  118.0 16.2 %collective-permute-start.22 = (f32[136,512]{1,0:T(8,128)S(1)}, f32[136,512]{1,0:T(8,128)S(1)}, u32[]{:S(2)}, u32[]{:S(2)}) collective-permute-start(f32[136,512]{1,0:T(8,128)S(1)} %get-tuple-element.123), channel_id=1, source_target_pairs={{0,3},{1,0},{2,1},{3,2},{4,7},{5,4},{6,5},{7,6},{8,11},{9,8},{10,9... | collective-permute-start | bytes 835592 | tf_op jit(solution)/shard_map/ppermute | solution.py:438
  119.2 13.4 %collective-permute-start.21 = (f32[128,512]{1,0:T(8,128)S(1)}, f32[128,512]{1,0:T(8,128)S(1)}, u32[]{:S(2)}, u32[]{:S(2)}) collective-permute-start(f32[128,512]{1,0:T(8,128)S(1)} %get-tuple-element.122), channel_id=1, source_target_pairs={{0,2},{1,3},{2,0},{3,1},{4,6},{5,7},{6,4},{7,5},{8,10},{9,11},{10,... | collective-permute-start | bytes 786440 | tf_op jit(solution)/shard_map/ppermute | solution.py:438
  120.1 19.6 %collective-permute-start.19 = (bf16[128,512]{1,0:T(8,128)(2,1)S(1)}, bf16[128,512]{1,0:T(8,128)(2,1)S(1)}, u32[]{:S(2)}, u32[]{:S(2)}) collective-permute-start(bf16[128,512]{1,0:T(8,128)(2,1)S(1)} %broadcast_select_fusion.d0), channel_id=1, source_target_pairs={{0,3},{1,0},{2,1},{3,2},{4,7},{5,4},{6,5},{7,6},{8,11},{9,8},{10,9... | collective-permute-start | bytes 393224 | tf_op jit(solution)/shard_map/ppermute | solution.py:438
  122.8 17.0 %collective-permute-start.18 = (bf16[128,512]{1,0:T(8,128)(2,1)S(1)}, bf16[128,512]{1,0:T(8,128)(2,1)S(1)}, u32[]{:S(2)}, u32[]{:S(2)}) collective-permute-start(bf16[128,512]{1,0:T(8,128)(2,1)S(1)} %broadcast_select_fusion.d0), channel_id=1, source_target_pairs={{0,2},{1,3},{2,0},{3,1},{4,6},{5,7},{6,4},{7,5},{8,10},{9,11},{10,... | collective-permute-start | bytes 393224 | tf_op jit(solution)/shard_map/ppermute | solution.py:438
  132.7 7.1 %collective-permute-start.17 = (bf16[128,512]{1,0:T(8,128)(2,1)S(1)}, bf16[128,512]{1,0:T(8,128)(2,1)S(1)}, u32[]{:S(2)}, u32[]{:S(2)}) collective-permute-start(bf16[128,512]{1,0:T(8,128)(2,1)S(1)} %broadcast_select_fusion.d0), channel_id=1, source_target_pairs={{0,1},{1,2},{2,3},{3,0},{4,5},{5,6},{6,7},{7,4},{8,9},{9,10},{10,1... | collective-permute-start | bytes 393224 | tf_op jit(solution)/shard_map/ppermute | solution.py:438
  142.6 5.9 %collective-permute-start.23 = (f32[512,128]{1,0:T(8,128)S(1)}, f32[512,128]{1,0:T(8,128)S(1)}, u32[]{:S(2)}, u32[]{:S(2)}) collective-permute-start(f32[512,128]{1,0:T(8,128)S(1)} %shard_map.115.own), channel_id=1, source_target_pairs={{0,4},{4,0},{1,5},{5,1},{2,6},{6,2},{3,7},{7,3},{8,12},{12,8},{9,1... | collective-permute-start | bytes 786440 | tf_op jit(solution)/shard_map/ppermute | solution.py:455
  142.7 10.1 %collective-permute-start.27 = (f32[128,512]{1,0:T(8,128)S(1)}, f32[128,512]{1,0:T(8,128)S(1)}, u32[]{:S(2)}, u32[]{:S(2)}) collective-permute-start(f32[128,512]{1,0:T(8,128)S(1)} %get-tuple-element.137), channel_id=1, source_target_pairs={{0,1},{1,2},{2,3},{3,0},{4,5},{5,6},{6,7},{7,4},{8,9},{9,10},{10,1... | collective-permute-start | bytes 786440 | tf_op jit(solution)/shard_map/ppermute | solution.py:438
  143.2 19.8 %collective-permute-start.28 = (f32[128,512]{1,0:T(8,128)S(1)}, f32[128,512]{1,0:T(8,128)S(1)}, u32[]{:S(2)}, u32[]{:S(2)}) collective-permute-start(f32[128,512]{1,0:T(8,128)S(1)} %get-tuple-element.138), channel_id=1, source_target_pairs={{0,2},{1,3},{2,0},{3,1},{4,6},{5,7},{6,4},{7,5},{8,10},{9,11},{10,... | collective-permute-start | bytes 786440 | tf_op jit(solution)/shard_map/ppermute | solution.py:438
  146.1 17.0 %collective-permute-start.29 = (f32[128,512]{1,0:T(8,128)S(1)}, f32[128,512]{1,0:T(8,128)S(1)}, u32[]{:S(2)}, u32[]{:S(2)}) collective-permute-start(f32[128,512]{1,0:T(8,128)S(1)} %get-tuple-element.139), channel_id=1, source_target_pairs={{0,3},{1,0},{2,1},{3,2},{4,7},{5,4},{6,5},{7,6},{8,11},{9,8},{10,9... | collective-permute-start | bytes 786440 | tf_op jit(solution)/shard_map/ppermute | solution.py:438
  149.2 15.4 %collective-permute-start.24 = (f32[128,128]{1,0:T(8,128)S(1)}, f32[128,128]{1,0:T(8,128)S(1)}, u32[]{:S(2)}, u32[]{:S(2)}) collective-permute-start(f32[128,128]{1,0:T(8,128)S(1)} %get-tuple-element.133), channel_id=1, source_target_pairs={{0,3},{1,0},{2,1},{3,2},{4,7},{5,4},{6,5},{7,6},{8,11},{9,8},{10,9... | collective-permute-start | bytes 196616 | tf_op jit(solution)/shard_map/ppermute | solution.py:438
  149.3 15.3 %collective-permute-start.25 = (f32[128,128]{1,0:T(8,128)S(1)}, f32[128,128]{1,0:T(8,128)S(1)}, u32[]{:S(2)}, u32[]{:S(2)}) collective-permute-start(f32[128,128]{1,0:T(8,128)S(1)} %get-tuple-element.134), channel_id=1, source_target_pairs={{0,2},{1,3},{2,0},{3,1},{4,6},{5,7},{6,4},{7,5},{8,10},{9,11},{10,... | collective-permute-start | bytes 196616 | tf_op jit(solution)/shard_map/ppermute | solution.py:438
  152.8 11.7 %collective-permute-start.26 = (f32[128,128]{1,0:T(8,128)S(1)}, f32[128,128]{1,0:T(8,128)S(1)}, u32[]{:S(2)}, u32[]{:S(2)}) collective-permute-start(f32[128,128]{1,0:T(8,128)S(1)} %get-tuple-element.135), channel_id=1, source_target_pairs={{0,1},{1,2},{2,3},{3,0},{4,5},{5,6},{6,7},{7,4},{8,9},{9,10},{10,1... | collective-permute-start | bytes 196616 | tf_op jit(solution)/shard_map/ppermute | solution.py:438
  166.0 14.9 %all-to-all-start.2 = ((f32[32,32,128]{2,1,0:T(8,128)}), f32[32,32,128]{2,1,0:T(8,128)S(1)}, u32[]{:S(2)}, u32[]{:S(2)}) async-start(f32[32,32,128]{2,1,0:T(8,128)} %get-tuple-element.148), calls=%async_computation.2 | async-start | bytes 1048576 | tf_op jit(solution)/shard_map/all_to_all | solution.py:452
  171.1 20.2 %collective-permute-start.30 = (f32[128,512]{1,0:T(8,128)S(1)}, f32[128,512]{1,0:T(8,128)S(1)}, u32[]{:S(2)}, u32[]{:S(2)}) collective-permute-start(f32[128,512]{1,0:T(8,128)S(1)} %get-tuple-element.156), channel_id=1, source_target_pairs={{4,0},{8,4},{12,8},{16,12},{20,16},{24,20},{28,24},{32,28},{36,32}... | collective-permute-start | bytes 786440 | tf_op jit(solution)/shard_map/ppermute | solution.py:447
  181.6 13.2 %all-to-all-start.3 = ((f32[32,16,128]{2,1,0:T(8,128)}), f32[32,16,128]{2,1,0:T(8,128)S(1)}, u32[]{:S(2)}, u32[]{:S(2)}) async-start(f32[32,16,128]{2,1,0:T(8,128)} %shard_map.120), calls=%async_computation.3 | async-start | bytes 524288 | tf_op jit(solution)/shard_map/all_to_all | solution.py:452
  191.3 3.6 %copy-start = (f32[128,512]{1,0:T(8,128)}, f32[128,512]{1,0:T(8,128)S(1)}, u32[]{:S(2)}) copy-start(f32[128,512]{1,0:T(8,128)S(1)} %collective-permute-done.30.following) | copy-start | bytes 786436
Sparse Core Ops, SparseCore 0:
  10.1 46.8 all-gather.1

commit v5 on v3

--- a/solution.py
+++ b/solution.py
@@ -151,25 +151,38 @@
         base[rows] = total
 
 
-def solve_kernel(place, x0, x1, x2, x3, high_far, low_far, inverse_far, *rest):
-    *forces, p0, p1, p2, p3, plane, high, low, inverse, arrivals = rest
-    c = place[0]
+def far_solve_kernel(
+    place, x0, x1, x2, x3, high_far, low_far, inverse_far, p0, p1, p2, p3,
+    plane, high, low, inverse, arrivals,
+):
     copies = [
         pltpu.make_async_copy(far_ref, ref, arrivals.at[i])
         for i, (far_ref, ref) in enumerate(
             ((high_far, high), (low_far, low), (inverse_far, inverse))
         )
     ]
+    solve(place, (x0, x1, x2, x3), (high, low, inverse), (), (p0, p1, p2, p3), plane, copies)
+
+
+def near_solve_kernel(
+    place, x0, x1, x2, x3, high, low, inverse, f0, f1, f2, f3, p0, p1, p2, p3, plane
+):
+    forces = (f0, f1, f2, f3)
+    solve(place, (x0, x1, x2, x3), (high, low, inverse), forces, (p0, p1, p2, p3), plane)
+
+
+def solve(place, inputs, tables_near, forces, outputs, plane, copies=()):
+    c = place[0]
+    high, low, inverse = tables_near
     for copy in copies:
         copy.start()
-    inputs, outputs = (x0, x1, x2, x3), (p0, p1, p2, p3)
     count = len(inputs)
-    height = x0.shape[0]
+    height = inputs[0].shape[0]
     for r, ref in enumerate(inputs):
         b = lax.rem(c - r + count, count)
         plane[pl.ds(pl.multiple_of(b * height, height), height), :] = ref[0:height]
-    copies[0].wait()
-    copies[1].wait()
+    for copy in copies[:2]:
+        copy.wait()
     sh, sl = high[...], low[...]
     by_left = jnp.concatenate([sh, sh, sl], axis=1)
     by_right = jnp.concatenate([sh, sl, sh], axis=0)
@@ -187,14 +200,15 @@
         )
 
     modes = left(right(plane[...]))
-    copies[2].wait()
+    for copy in copies[2:]:
+        copy.wait()
     modes = modes * inverse[...]
     plane[...] = right(left(modes))
     for r, ref in enumerate(outputs):
         b = lax.rem(c + r, count)
         ref[0:height] = plane[pl.ds(pl.multiple_of(b * height, height), height), :]
     if forces:
-        extra = p0.shape[0] - height
+        extra = outputs[0].shape[0] - height
         for r, ref in enumerate(outputs):
             for q in range(height // extra):
                 ref[height : height + extra, LANE * q : LANE * (q + 1)] = forces[-r][
@@ -202,15 +216,35 @@
                 ]
 
 
-def disc_kernel(d0, d1, d2, d3, owners, *rest):
-    *blades, f0, f1, f2, f3, plane, total = rest
+def disc_kernel(d0, d1, d2, d3, places, place_row, owners, *rest):
+    streams, tabled = 4, (len(rest) - 11) // 2
+    blades, tables_far = rest[:streams], rest[streams : streams + tabled]
+    f0, f1, f2, f3 = rest[streams + tabled : streams + tabled + 4]
+    tables_near = rest[streams + tabled + 4 : streams + 2 * tabled + 4]
+    picked, total = rest[streams + 2 * tabled + 4 : streams + 2 * tabled + 6]
     step = pl.program_id(0)
-    height = d0.shape[0]
+    last = pl.num_programs(0) - 1
+    height, width = d0.shape
+    number = picked.shape[0]
+    copies = [
+        pltpu.make_async_copy(source, target, rest[-1].at[i])
+        for i, (source, target) in enumerate(zip(tables_far, tables_near))
+    ]
 
     @pl.when(step == 0)
     def _():
-        for r, ref in enumerate((d0, d1, d2, d3)):
-            plane[height * r : height * (r + 1)] = ref[...]
+        for copy in copies:
+            copy.start()
+        plane = jnp.concatenate([d[...] for d in (d0, d1, d2, d3)], axis=0)
+        lane = lax.broadcasted_iota(jnp.int32, (number, LANE), 1)
+        chosen = [
+            jnp.where(places[...] == lane + LANE * q, 1.0, 0.0).astype(BF16)
+            for q in range(width // LANE)
+        ]
+        rows = jnp.dot(
+            jnp.concatenate(chosen, axis=1), plane, preferred_element_type=F32
+        )
+        picked[...] = rows.astype(BF16)
         total[...] = jnp.zeros_like(total)
 
     per_step = blades[0].shape[0]
@@ -222,15 +256,27 @@
             ],
             axis=1,
         )
-        response = jnp.dot(plane[...], pair, preferred_element_type=F32)
+        response = jnp.dot(picked[...], pair, preferred_element_type=F32)
         first = step * per_step + i
         kept = jnp.where(owners[...] == first, response[:, :LANE], total[...])
         total[...] = jnp.where(owners[...] == first + 1, response[:, LANE:], kept)
 
-    @pl.when(step == pl.num_programs(0) - 1)
+    @pl.when(step == last)
     def _():
+        rest_of, parts = jnp.tanh(total[...]), []
+        for _ in range(3):
+            parts.append(rest_of.astype(BF16))
+            rest_of = rest_of - parts[-1].astype(F32)
+        forces = jnp.concatenate(parts, axis=0)
+        at = place_row[0:1]
         for r, ref in enumerate((f0, f1, f2, f3)):
-            ref[...] = jnp.tanh(total[height * r : height * (r + 1)])
+            row = lax.broadcasted_iota(jnp.int32, (height, number), 0) + height * r
+            back = jnp.where(row == at, 1.0, 0.0).astype(BF16)
+            ref[...] = jnp.dot(
+                jnp.concatenate([back] * 3, axis=1), forces, preferred_element_type=F32
+            )
+        for copy in copies:
+            copy.wait()
 
 
 def offset_kernel(place, *rest):
@@ -391,28 +437,32 @@
     )(place, *args)
 
 
-def disc_forces(rows, owners, blades):
+def disc_forces(rows, where, blades, tabled=()):
     height, width = rows[0].shape
     count = len(rows)
     number = blades.shape[0]
     per_step, streams = 8, 4
     fixed = lambda shape: pl.BlockSpec(shape, lambda i: (0,) * len(shape))
     table = lambda k: pl.BlockSpec((per_step, width // streams, LANE), lambda i: (i, k, 0))
+    discs = where[0].shape[0]
     return pl.pallas_call(
         disc_kernel,
         grid=(number // per_step,),
-        out_shape=[near((height, LANE))] * count,
+        out_shape=[near((height, LANE))] * count + [near(t.shape, t.dtype) for t in tabled],
         in_specs=[fixed((height, width))] * count
-        + [fixed(owners.shape)]
-        + [table(k) for k in range(streams)],
-        out_specs=[fixed((height, LANE))] * count,
+        + [fixed(w.shape) for w in where]
+        + [table(k) for k in range(streams)]
+        + [pl.BlockSpec(memory_space=pltpu.HBM)] * len(tabled),
+        out_specs=[fixed((height, LANE))] * count
+        + [pl.BlockSpec(memory_space=pltpu.VMEM)] * len(tabled),
         scratch_shapes=[
-            pltpu.VMEM((count * height, width), BF16),
-            pltpu.VMEM((count * height, LANE), F32),
+            pltpu.VMEM((discs, width), BF16),
+            pltpu.VMEM((discs, LANE), F32),
+            pltpu.SemaphoreType.DMA((3,)),
         ],
         compiler_params=pltpu.CompilerParams(vmem_limit_bytes=16 * MIB),
         cost_estimate=cost(2 * number * width * width * LANE, 5 * MIB),
-    )(*rows, stay(owners), *[stay(blades)] * streams)
+    )(*rows, *map(stay, where), *[stay(blades)] * streams, *tabled)
 
 
 def local(velocity_guess, damping, inflow, disc_rows, owner, blade):
@@ -458,18 +508,20 @@
         return lax.all_to_all(value, "march", split_axis=0, concat_axis=0, tiled=True)
 
     blades = lax.all_gather(blade, "march", axis=0, tiled=True)
-    blocks = (cross_index - jnp.arange(cross_size, dtype=jnp.int32) + cross_size) % cross_size
-    ids = (blocks[:, None] * height + jnp.arange(height, dtype=jnp.int32)[None, :]).reshape(-1)
-    owners = jnp.max(
-        jnp.where(ids[:, None] == disc_rows[None, :], owner[None, :], -1), axis=1
+    turn_of = (cross_index - disc_rows // height + cross_size) % cross_size
+    places = turn_of * height + disc_rows % height
+    count = disc_rows.shape[0]
+    where = (
+        jnp.broadcast_to(places[:, None], (count, LANE)),
+        jnp.broadcast_to(places[None, :], (SUB, count)),
+        jnp.broadcast_to(jnp.where(at_disc, owner, -1)[:, None], (count, LANE)),
     )
-    owners = jnp.where(at_disc, owners, -1)
-    owners = jnp.broadcast_to(owners[:, None], (cross_size * height, LANE))
 
     step = (stations, height // STEPS, width)
     turned = range(4, 8)
     near_inflow = stay(inflow)
     upstream = along_march(velocity_guess[-1], 1)
+    upstream, *where = lax.optimization_barrier((upstream, *where))
     current = stay(velocity_guess)
     disc = velocity_guess[0].astype(BF16)
     rows = turns([disc] * cross_size)
@@ -498,33 +550,35 @@
         if merged:
             rows = turns([disc] * cross_size)
         arrived = turns(source)
-        extra = []
-        piece = plane
-        if not merged:
+        solve_cost = cost(3 * 8 * width**3, 5 * MIB)
+        if merged:
+            made = disc_forces(rows, where, blades, tabled)
+            forces, near_tables = made[:cross_size], made[cross_size:]
+            solved = call(
+                near_solve_kernel,
+                [near((height + height * LANE // width, width))] * cross_size,
+                (place, *arrived, *near_tables, *forces),
+                solve_cost,
+                scalars=1,
+                limit=16,
+                scratch=[pltpu.VMEM((width, width), F32)],
+            )
             scales = across_march(scale)
-        if merged:
-            extra = disc_forces(rows, owners, blades)
-            piece = (height + height * LANE // width, width)
-        solved = pl.pallas_call(
-            solve_kernel,
-            out_shape=[near(piece)] * cross_size,
-            in_specs=[SMEM]
-            + [VMEM] * cross_size
-            + [pl.BlockSpec(memory_space=pltpu.HBM)] * 3
-            + [VMEM] * len(extra),
-            out_specs=[VMEM] * cross_size,
-            scratch_shapes=[pltpu.VMEM((width, width), F32)]
-            + [pltpu.VMEM((width, width), BF16)] * 2
-            + [pltpu.VMEM((width, width), F32), pltpu.SemaphoreType.DMA((3,))],
-            compiler_params=pltpu.CompilerParams(vmem_limit_bytes=20 * MIB),
-            cost_estimate=cost(3 * 8 * width**3, 5 * MIB),
-        )(place, *arrived, *tabled, *extra)
-        forces = []
-        if merged:
+            forces = []
+        else:
             scales = across_march(scale)
-        else:
+            solved = pl.pallas_call(
+                far_solve_kernel,
+                out_shape=[near(plane)] * cross_size,
+                in_specs=[SMEM] + [VMEM] * cross_size + [pl.BlockSpec(memory_space=pltpu.HBM)] * 3,
+                out_specs=[VMEM] * cross_size,
+                scratch_shapes=[pltpu.VMEM((width, width), F32)]
+                + [pltpu.VMEM((width, width), BF16)] * 2
+                + [pltpu.VMEM((width, width), F32), pltpu.SemaphoreType.DMA((3,))],
+                compiler_params=pltpu.CompilerParams(vmem_limit_bytes=20 * MIB),
+                cost_estimate=solve_cost,
+            )(place, *arrived, *tabled)
             rows, scales, solved = lax.optimization_barrier((rows, scales, solved))
-            forces = turns(disc_forces(rows, owners, blades), -1)
         pieces = turns(solved)
         decay = stay(decay)
         term, weights, base, force_weight = call(
@@ -535,6 +589,9 @@
             scalars=1,
             limit=12,
         )
+        if not merged:
+            rows, base = lax.optimization_barrier((rows, base))
+            forces = turns(disc_forces(rows, where, blades), -1)
         lead, lead_far, force, offset = call(
             offset_kernel,
             [near(plane), far(plane), far(plane), far(chunks)],

time: 196 us -> 199 us (1.015)
  local copies, waits for them, and re-layouts: 4.44 us -> 8.65 us
  starting transfers between devices: 74.4 us -> 71.5 us
  waiting for transfers between devices: 40.9 us -> 43.7 us
    all_gather x1, waiting for transfers between devices: 7.12 us -> 0.01 us  [local(): blades = lax.all_gather(blade, 'march', axis=0, tiled=True)]
    pallas_call x2 -> x1, Pallas kernels: 11.1 us -> 6.44 us  [local(): pl.pallas_call(far_solve_kernel, out_shape=[near(plane)] * cross_size, in...]
    ppermute x3, waiting for transfers between devices: 2.7 us -> 7.07 us  [along_march(): lax.ppermute(value, 'march', [(i, i + steps) for i in range(count) if 0 <...]
    pallas_call x6 -> x7, Pallas kernels: 12 us -> 16.3 us  [call(): pl.pallas_call(kernel, out_shape=outs, in_specs=[SMEM] * scalars + [VMEM]...]
    ppermute x21, waiting for transfers between devices: 16.1 us -> 20.3 us  [turn(): lax.ppermute(value, 'cross', [(i, (i + steps) % cross_size) for i in rang...]
    ppermute x21, starting transfers between devices: 32.1 us -> 28.8 us  [turn(): lax.ppermute(value, 'cross', [(i, (i + steps) % cross_size) for i in rang...]
    unnamed x8 -> x18, local copies, waits for them, and re-layouts: 1.65 us -> 4.59 us
  transfers between devices with their start and end apart: 31 -> 31, of which waited for: 16 -> 14; matrix products, arithmetic and copies ran while one was open for 2% -> 2% of each run, Pallas kernels for 21% -> 21%
where the time goes in v5:
time: 199 us; the launch traced here: 196 us
  starting transfers between devices  71.5 us (36%)
  Pallas kernels  56.6 us (28%)
  waiting for transfers between devices  43.7 us (22%)
  between operations  14.2 us (7%)
  local copies, waits for them, and re-layouts  8.65 us (4%)
    all_to_all x6, starting transfers between devices, across_march(): lax.all_to_all(value, 'march', split_axis=0, concat_axis=0, tiled=True)  32.1 us
    ppermute x21, starting transfers between devices, turn(): lax.ppermute(value, 'cross', [(i, (i + steps) % cross_size) for i in rang...  28.8 us
    pallas_call x6, Pallas kernels, by_rows(): pl.pallas_call(kernel, grid_spec=pltpu.PrefetchScalarGridSpec(num_scalar_...  24.5 us
    ppermute x21, waiting for transfers between devices, turn(): lax.ppermute(value, 'cross', [(i, (i + steps) % cross_size) for i in rang...  20.3 us
    pallas_call x7, Pallas kernels, call(): pl.pallas_call(kernel, out_shape=outs, in_specs=[SMEM] * scalars + [VMEM]...  16.3 us
    all_to_all x6, waiting for transfers between devices, across_march(): lax.all_to_all(value, 'march', split_axis=0, concat_axis=0, tiled=True)  15.7 us
    ppermute x3, starting transfers between devices, along_march(): lax.ppermute(value, 'march', [(i, i + steps) for i in range(count) if 0 <...  10.6 us
    pallas_call x2, Pallas kernels, disc_forces(): pl.pallas_call(disc_kernel, grid=(number // per_step,), out_shape=[near((...  9.47 us
  transfers between devices with their start and end apart: 31, of which 14 were waited for; matrix products, arithmetic and copies ran while one was open for 2% of the time, Pallas kernels for 21%

profile of v5, /device:TPU:2, one launch (start us, length us, event | category | flops | bytes accessed | tf_op | source)
XLA Modules:
  0.0 195.5 jit_solution(17107108146747115126)
XLA Ops:
  7.9 1.0 slice_bitcast_fusion
  8.9 1.9 collective-permute-start.3
  11.6 7.1 %collective-permute-done.3.upstream = f32[128,512]{1,0:T(8,128)S(1)} collective-permute-done((f32[128,512]{1,0:T(8,128)S(1)}, f32[128,512]{1,0:T(8,128)S(1)}, u32[]{:S(2)}, u32[]{:S(2)}) %collective-permute-start.3) | collective-permute-done | bytes 262176 | tf_op jit(solution)/shard_map/ppermute | solution.py:503
  20.8 2.8 %shard_map.104 = (f32[128,512]{1,0:T(8,128)S(1)}, f32[136,512]{1,0:T(8,128)S(1)}, f32[128,512]{1,0:T(8,128)S(1)}, f32[136,512]{1,0:T(8,128)S(1)}) custom-call(s32[4]{0:T(128)S(1)} %pad_add_fusion.place, f32[4,128,512]{2,1,0:T(8,128)} %current.4, f32[128,512]{1,0:T(8,128)S(1)} %collective-permute-done.3.upstream, f32[128,512]{1,0:T(8,128)} %inflow.9), custom_call_target="tpu_custom_call" | custom-call | flops 1000000 | bytes 2097152 | tf_op jit(solution)/shard_map/pallas_call | solution.py:425
  23.6 2.0 %collective-permute-start.4 = (f32[136,512]{1,0:T(8,128)S(1)}, f32[136,512]{1,0:T(8,128)S(1)}, u32[]{:S(2)}, u32[]{:S(2)}) collective-permute-start(f32[136,512]{1,0:T(8,128)S(1)} %get-tuple-element.99), channel_id=1, source_target_pairs={{0,1},{1,2},{2,3},{3,0},{4,5},{5,6},{6,7},{7,4},{8,9},{9,10},{10,1... | collective-permute-start | bytes 835592 | tf_op jit(solution)/shard_map/ppermute | solution.py:494
  25.6 2.2 %collective-permute-start.6 = (f32[136,512]{1,0:T(8,128)S(1)}, f32[136,512]{1,0:T(8,128)S(1)}, u32[]{:S(2)}, u32[]{:S(2)}) collective-permute-start(f32[136,512]{1,0:T(8,128)S(1)} %get-tuple-element.101), channel_id=1, source_target_pairs={{0,3},{1,0},{2,1},{3,2},{4,7},{5,4},{6,5},{7,6},{8,11},{9,8},{10,9... | collective-permute-start | bytes 835592 | tf_op jit(solution)/shard_map/ppermute | solution.py:494
  27.7 1.8 collective-permute-start.5
  31.3 2.4 %collective-permute-start.1 = (bf16[128,512]{1,0:T(8,128)(2,1)S(1)}, bf16[128,512]{1,0:T(8,128)(2,1)S(1)}, u32[]{:S(2)}, u32[]{:S(2)}) collective-permute-start(bf16[128,512]{1,0:T(8,128)(2,1)S(1)} %fusion.d0), channel_id=1, source_target_pairs={{0,2},{1,3},{2,0},{3,1},{4,6},{5,7},{6,4},{7,5},{8,10},{9,11},{10,... | collective-permute-start | bytes 393224 | tf_op jit(solution)/shard_map/ppermute | solution.py:494
  33.6 4.2 %shard_map.105 = (f32[4,128,512]{2,1,0:T(8,128)}, f32[32,16,128]{2,1,0:T(8,128)}) custom-call(s32[4]{0:T(128)S(1)} %pad_add_fusion.place, f32[4,128,512]{2,1,0:T(8,128)} %current.4, f32[4,128,512]{2,1,0:T(8,128)} %damping.2), custom_call_target="tpu_custom_call" | custom-call | flops 4000000 | bytes 3145728 | tf_op jit(solution)/shard_map/pallas_call | solution.py:425
  37.8 5.5 %all-to-all-start = ((f32[32,16,128]{2,1,0:T(8,128)}), f32[32,16,128]{2,1,0:T(8,128)S(1)}, u32[]{:S(2)}, u32[]{:S(2)}) async-start(f32[32,16,128]{2,1,0:T(8,128)} %get-tuple-element.97), calls=%async_computation | async-start | bytes 524288 | tf_op jit(solution)/shard_map/all_to_all | solution.py:508
  43.5 6.4 %shard_map.106 = (f32[128,512]{1,0:T(8,128)S(1)}, f32[128,512]{1,0:T(8,128)}, f32[128,512]{1,0:T(8,128)}, f32[128,512]{1,0:T(8,128)}) custom-call(s32[4]{0:T(128)S(1)} %pad_add_fusion.place, f32[128,512]{1,0:T(8,128)S(1)} %get-tuple-element.98.x0, f32[136,512]{1,0:T(8,128)S(1)} %collective-permute-done.4.x1.before, ...), custom_call_target="tpu_custom_call" | custom-call | flops 3221225472 | bytes 5242880 | tf_op jit(solution)/shard_map/pallas_call | solution.py:570
  51.3 1.7 all-to-all-done.scale
  53.0 2.9 %collective-permute-start.8 = (f32[128,512]{1,0:T(8,128)}, f32[128,512]{1,0:T(8,128)S(1)}, u32[]{:S(2)}, u32[]{:S(2)}) collective-permute-start(f32[128,512]{1,0:T(8,128)} %get-tuple-element.109), channel_id=1, source_target_pairs={{0,2},{1,3},{2,0},{3,1},{4,6},{5,7},{6,4},{7,5},{8,10},{9,11},{10,... | collective-permute-start | bytes 786440 | tf_op jit(solution)/shard_map/ppermute | solution.py:494
  55.9 1.0 collective-permute-start.9
  57.0 3.6 %shard_map.107 = (f32[4,128,512]{2,1,0:T(8,128)}, f32[4,128,512]{2,1,0:T(8,128)S(1)}, f32[128,512]{1,0:T(8,128)S(1)}, f32[128,512]{1,0:T(8,128)S(1)}) custom-call(s32[4]{0:T(128)S(1)} %pad_add_fusion.place, f32[4,128,512]{2,1,0:T(8,128)} %current.4, f32[136,512]{1,0:T(8,128)S(1)} %collective-permute-done.4.x1.before, ...), custom_call_target="tpu_custom_call" | custom-call | flops 8000000 | bytes 4194304 | tf_op jit(solution)/shard_map/pallas_call | solution.py:401
  63.2 4.7 %shard_map.108 = (f32[128,128]{1,0:T(8,128)S(1)}, f32[128,128]{1,0:T(8,128)S(1)}, f32[128,128]{1,0:T(8,128)S(1)}, f32[128,128]{1,0:T(8,128)S(1)}) custom-call(bf16[128,512]{1,0:T(8,128)(2,1)S(1)} %fusion.d0, bf16[128,512]{1,0:T(8,128)(2,1)S(1)} %copy-done.5, bf16[128,512]{1,0:T(8,128)(2,1)S(1)} %copy-done.3, bf16[128,512]{1,0:T(8,128)(2,1)S(1)} %collective-permute-done.2.d3, ...), custom_call_target="tpu_custom_call" | custom-call | flops 2147483648 | bytes 5242880 | tf_op jit(solution)/shard_map/pallas_call | solution.py:448
  67.9 2.8 %collective-permute-start.10 = (f32[128,128]{1,0:T(8,128)S(1)}, f32[128,128]{1,0:T(8,128)S(1)}, u32[]{:S(2)}, u32[]{:S(2)}) collective-permute-start(f32[128,128]{1,0:T(8,128)S(1)} %get-tuple-element.125), channel_id=1, source_target_pairs={{0,3},{1,0},{2,1},{3,2},{4,7},{5,4},{6,5},{7,6},{8,11},{9,8},{10,9... | collective-permute-start | bytes 196616 | tf_op jit(solution)/shard_map/ppermute | solution.py:494
  71.8 2.0 %collective-permute-done.10.rest_5_ = f32[128,128]{1,0:T(8,128)S(1)} collective-permute-done((f32[128,128]{1,0:T(8,128)S(1)}, f32[128,128]{1,0:T(8,128)S(1)}, u32[]{:S(2)}, u32[]{:S(2)}) %collective-permute-start.10) | collective-permute-done | bytes 65568 | tf_op jit(solution)/shard_map/ppermute | solution.py:494
  73.8 3.0 %collective-permute-done.11.rest_6_ = f32[128,128]{1,0:T(8,128)S(1)} collective-permute-done((f32[128,128]{1,0:T(8,128)S(1)}, f32[128,128]{1,0:T(8,128)S(1)}, u32[]{:S(2)}, u32[]{:S(2)}) %collective-permute-start.11) | collective-permute-done | bytes 65568 | tf_op jit(solution)/shard_map/ppermute | solution.py:494
  77.4 1.6 shard_map.109
  79.8 6.5 %all-to-all-start.1 = ((f32[32,16,128]{2,1,0:T(8,128)}), f32[32,16,128]{2,1,0:T(8,128)S(1)}, u32[]{:S(2)}, u32[]{:S(2)}) async-start(f32[32,16,128]{2,1,0:T(8,128)} %get-tuple-element.133), calls=%async_computation.1 | async-start | bytes 524288 | tf_op jit(solution)/shard_map/all_to_all | solution.py:508
  86.2 4.3 %collective-permute-start.13 = (f32[128,512]{1,0:T(8,128)}, f32[128,512]{1,0:T(8,128)S(1)}, u32[]{:S(2)}, u32[]{:S(2)}) collective-permute-start(f32[128,512]{1,0:T(8,128)} %copy-done.6), channel_id=1, source_target_pairs={{4,0},{8,4},{12,8},{16,12},{20,16},{24,20},{28,24},{32,28},{36,32}... | collective-permute-start | bytes 786440 | tf_op jit(solution)/shard_map/ppermute | solution.py:503
  90.6 3.4 %all-to-all-done.1.offset = f32[32,16,128]{2,1,0:T(8,128)S(1)} async-done(((f32[32,16,128]{2,1,0:T(8,128)}), f32[32,16,128]{2,1,0:T(8,128)S(1)}, u32[]{:S(2)}, u32[]{:S(2)}) %all-to-all-start.1) | async-done | bytes 262176 | tf_op jit(solution)/shard_map/all_to_all | solution.py:508
  94.7 5.0 %all-to-all-start.2 = ((f32[32,16,128]{2,1,0:T(8,128)}), f32[32,16,128]{2,1,0:T(8,128)S(1)}, u32[]{:S(2)}, u32[]{:S(2)}) async-start(f32[32,16,128]{2,1,0:T(8,128)} %shard_map.110), calls=%async_computation.2 | async-start | bytes 524288 | tf_op jit(solution)/shard_map/all_to_all | solution.py:508
  99.8 4.3 %shard_map.111 = (f32[4,128,512]{2,1,0:T(8,128)}, f32[4,128,512]{2,1,0:T(8,128)}) custom-call(s32[4]{0:T(128)S(1)} %pad_add_fusion.place, f32[128,512]{1,0:T(8,128)S(1)} %get-tuple-element.134.rest_0_.p0, f32[128,512]{1,0:T(8,128)S(1)} %collective-permute-done.7.rest_1_.p1, f32[128,512]{1,0:T(8,128)S(1)} %collective-permute-done.8.rest_2_.p2, ...), custom_call_target="tpu_custom_call" | custom-call | flops 4000000 | bytes 4194304 | tf_op jit(solution)/shard_map/pallas_call | solution.py:425
  104.0 3.5 %all-to-all-done.2.entering = f32[32,16,128]{2,1,0:T(8,128)S(1)} async-done(((f32[32,16,128]{2,1,0:T(8,128)}), f32[32,16,128]{2,1,0:T(8,128)S(1)}, u32[]{:S(2)}, u32[]{:S(2)}) %all-to-all-start.2) | async-done | bytes 262176 | tf_op jit(solution)/shard_map/all_to_all | solution.py:508
  107.6 4.9 %shard_map.112 = (f32[4,128,512]{2,1,0:T(8,128)}, f32[4,128,512]{2,1,0:T(8,128)}, f32[32,16,128]{2,1,0:T(8,128)}, bf16[128,512]{1,0:T(8,128)(2,1)S(1)}, f32[128,...) custom-call(s32[4]{0:T(128)S(1)} %pad_add_fusion.place, ...), custom_call_target="tpu_custom_call" | custom-call | flops 8000000 | bytes 8388608 | tf_op jit(solution)/shard_map/pallas_call | solution.py:425
  113.0 1.2 collective-permute-start.18
  115.0 1.4 collective-permute-start.14
  116.5 1.8 collective-permute-start.16
  118.9 1.9 collective-permute-start.15
  120.8 2.0 %collective-permute-done.17.d1 = bf16[128,512]{1,0:T(8,128)(2,1)S(1)} collective-permute-done((bf16[128,512]{1,0:T(8,128)(2,1)S(1)}, bf16[128,512]{1,0:T(8,128)(2,1)S(1)}, u32[]{:S(2)}, u32[]{:S(2)}) %collective-permute-start.17) | collective-permute-done | bytes 131104 | tf_op jit(solution)/shard_map/ppermute | solution.py:494
  122.8 4.8 %shard_map.113 = (f32[128,128]{1,0:T(8,128)S(1)}, f32[128,128]{1,0:T(8,128)S(1)}, f32[128,128]{1,0:T(8,128)S(1)}, f32[128,128]{1,0:T(8,128)S(1)}, bf16[512,512]{...) custom-call(bf16[128,512]{1,0:T(8,128)(2,1)S(1)} %get-tuple-element.148.d0, ...), custom_call_target="tpu_custom_call" | custom-call | flops 2147483648 | bytes 5242880 | tf_op jit(solution)/shard_map/pallas_call | solution.py:448
  127.6 6.7 %collective-permute-done.15.x2 = f32[128,512]{1,0:T(8,128)S(1)} collective-permute-done((f32[128,512]{1,0:T(8,128)S(1)}, f32[128,512]{1,0:T(8,128)S(1)}, u32[]{:S(2)}, u32[]{:S(2)}) %collective-permute-start.15) | collective-permute-done | bytes 262176 | tf_op jit(solution)/shard_map/ppermute | solution.py:494
  134.3 4.3 %shard_map.114 = (f32[160,512]{1,0:T(8,128)S(1)}, f32[160,512]{1,0:T(8,128)S(1)}, f32[160,512]{1,0:T(8,128)S(1)}, f32[160,512]{1,0:T(8,128)S(1)}) custom-call(s32[4]{0:T(128)S(1)} %pad_add_fusion.place, f32[128,512]{1,0:T(8,128)S(1)} %get-tuple-element.144.x0, f32[136,512]{1,0:T(8,128)S(1)} %collective-permute-done.14.x1.before, ...), custom_call_target="tpu_custom_call" | custom-call | flops 3221225472 | bytes 5242880 | tf_op jit(solution)/shard_map/pallas_call | solution.py:401
  138.7 2.6 %collective-permute-start.21 = (f32[160,512]{1,0:T(8,128)S(1)}, f32[160,512]{1,0:T(8,128)S(1)}, u32[]{:S(2)}, u32[]{:S(2)}) collective-permute-start(f32[160,512]{1,0:T(8,128)S(1)} %get-tuple-element.158), channel_id=1, source_target_pairs={{0,2},{1,3},{2,0},{3,1},{4,6},{5,7},{6,4},{7,5},{8,10},{9,11},{10,... | collective-permute-start | bytes 983048 | tf_op jit(solution)/shard_map/ppermute | solution.py:494
  141.2 1.2 collective-permute-start.22
  142.5 5.1 %all-to-all-start.3 = ((f32[32,16,128]{2,1,0:T(8,128)}), f32[32,16,128]{2,1,0:T(8,128)S(1)}, u32[]{:S(2)}, u32[]{:S(2)}) async-start(f32[32,16,128]{2,1,0:T(8,128)} %get-tuple-element.143), calls=%async_computation.3 | async-start | bytes 524288 | tf_op jit(solution)/shard_map/all_to_all | solution.py:508
  147.6 3.6 %shard_map.115 = (f32[4,128,512]{2,1,0:T(8,128)}, f32[4,128,512]{2,1,0:T(8,128)S(1)}, f32[128,512]{1,0:T(8,128)S(1)}, f32[128,512]{1,0:T(8,128)S(1)}) custom-call(s32[4]{0:T(128)S(1)} %pad_add_fusion.place, f32[4,128,512]{2,1,0:T(8,128)} %get-tuple-element.160.current, f32[136,512]{1,0:T(8,128)S(1)} %collective-permute-done.14.x1.before, ...), custom_call_target="tpu_custom_call" | custom-call | flops 8000000 | bytes 4194304 | tf_op jit(solution)/shard_map/pallas_call | solution.py:401
  151.2 4.6 %collective-permute-done.20.rest_1_.p1 = f32[160,512]{1,0:T(8,128)S(1)} collective-permute-done((f32[160,512]{1,0:T(8,128)S(1)}, f32[160,512]{1,0:T(8,128)S(1)}, u32[]{:S(2)}, u32[]{:S(2)}) %collective-permute-start.20) | collective-permute-done | bytes 327712 | tf_op jit(solution)/shard_map/ppermute | solution.py:494
  156.4 1.6 shard_map.116
  158.0 5.1 %all-to-all-start.4 = ((f32[32,16,128]{2,1,0:T(8,128)}), f32[32,16,128]{2,1,0:T(8,128)S(1)}, u32[]{:S(2)}, u32[]{:S(2)}) async-start(f32[32,16,128]{2,1,0:T(8,128)} %get-tuple-element.167), calls=%async_computation.4 | async-start | bytes 524288 | tf_op jit(solution)/shard_map/all_to_all | solution.py:508
  163.1 4.3 %collective-permute-start.23 = (f32[128,512]{1,0:T(8,128)S(1)}, f32[128,512]{1,0:T(8,128)S(1)}, u32[]{:S(2)}, u32[]{:S(2)}) collective-permute-start(f32[128,512]{1,0:T(8,128)S(1)} %get-tuple-element.175), channel_id=1, source_target_pairs={{4,0},{8,4},{12,8},{16,12},{20,16},{24,20},{28,24},{32,28},{36,32}... | collective-permute-start | bytes 786440 | tf_op jit(solution)/shard_map/ppermute | solution.py:503
  167.4 3.5 %all-to-all-done.4.offset = f32[32,16,128]{2,1,0:T(8,128)S(1)} async-done(((f32[32,16,128]{2,1,0:T(8,128)}), f32[32,16,128]{2,1,0:T(8,128)S(1)}, u32[]{:S(2)}, u32[]{:S(2)}) %all-to-all-start.4) | async-done | bytes 262176 | tf_op jit(solution)/shard_map/all_to_all | solution.py:508
  171.7 5.0 %all-to-all-start.5 = ((f32[32,16,128]{2,1,0:T(8,128)}), f32[32,16,128]{2,1,0:T(8,128)S(1)}, u32[]{:S(2)}, u32[]{:S(2)}) async-start(f32[32,16,128]{2,1,0:T(8,128)} %shard_map.117), calls=%async_computation.5 | async-start | bytes 524288 | tf_op jit(solution)/shard_map/all_to_all | solution.py:508
  176.7 4.2 %shard_map.118 = (f32[4,128,512]{2,1,0:T(8,128)}, f32[4,128,512]{2,1,0:T(8,128)}) custom-call(s32[4]{0:T(128)S(1)} %pad_add_fusion.place, f32[160,512]{1,0:T(8,128)S(1)} %get-tuple-element.168.rest_0_.p0, f32[160,512]{1,0:T(8,128)S(1)} %collective-permute-done.20.rest_1_.p1, f32[160,512]{1,0:T(8,128)S(1)} %collective-permute-done.21.rest_2_.p2, ...), custom_call_target="tpu_custom_call" | custom-call | flops 4000000 | bytes 4194304 | tf_op jit(solution)/shard_map/pallas_call | solution.py:425
  180.8 3.6 %all-to-all-done.5.entering = f32[32,16,128]{2,1,0:T(8,128)S(1)} async-done(((f32[32,16,128]{2,1,0:T(8,128)}), f32[32,16,128]{2,1,0:T(8,128)S(1)}, u32[]{:S(2)}, u32[]{:S(2)}) %all-to-all-start.5) | async-done | bytes 262176 | tf_op jit(solution)/shard_map/all_to_all | solution.py:508
  184.5 4.2 %shard_map.119 = f32[4,128,512]{2,1,0:T(8,128)} custom-call(s32[4]{0:T(128)S(1)} %pad_add_fusion.place, f32[32,16,128]{2,1,0:T(8,128)S(1)} %all-to-all-done.5.entering, f32[4,128,512]{2,1,0:T(8,128)} %get-tuple-element.174.change, f32[128,512]{1,0:T(8,128)} %copy-done.8, f32[4,128,512]{2,1,0:T(8,128)} %get-tuple-element.161.decay, ...), custom_call_target="tpu_custom_call" | custom-call | flops 4000000 | bytes 5242880 | tf_op jit(solution)/shard_map/pallas_call | solution.py:425
  (57 shorter events, 16.2 us)
Async XLA Ops:
  7.2 54.1 %all-gather.2.cloned.1.call-start = ((), (), s32[]{:S(2)}) async-start(), calls=%async_computation.6 | async-start | bytes 4325376 | tf_op jit(solution)/shard_map/all_gather | solution.py:510
  8.9 9.8 %collective-permute-start.3 = (f32[128,512]{1,0:T(8,128)S(1)}, f32[128,512]{1,0:T(8,128)S(1)}, u32[]{:S(2)}, u32[]{:S(2)}) collective-permute-start(f32[128,512]{1,0:T(8,128)S(1)} %slice_bitcast_fusion), channel_id=1, source_target_pairs={{0,4},{4,8},{8,12},{12,16},{16,20},{20,24},{24,28},{28,32},{32,36}... | collective-permute-start | bytes 786440 | tf_op jit(solution)/shard_map/ppermute | solution.py:503
  23.6 20.0 %collective-permute-start.4 = (f32[136,512]{1,0:T(8,128)S(1)}, f32[136,512]{1,0:T(8,128)S(1)}, u32[]{:S(2)}, u32[]{:S(2)}) collective-permute-start(f32[136,512]{1,0:T(8,128)S(1)} %get-tuple-element.99), channel_id=1, source_target_pairs={{0,1},{1,2},{2,3},{3,0},{4,5},{5,6},{6,7},{7,4},{8,9},{9,10},{10,1... | collective-permute-start | bytes 835592 | tf_op jit(solution)/shard_map/ppermute | solution.py:494
  25.6 18.0 %collective-permute-start.6 = (f32[136,512]{1,0:T(8,128)S(1)}, f32[136,512]{1,0:T(8,128)S(1)}, u32[]{:S(2)}, u32[]{:S(2)}) collective-permute-start(f32[136,512]{1,0:T(8,128)S(1)} %get-tuple-element.101), channel_id=1, source_target_pairs={{0,3},{1,0},{2,1},{3,2},{4,7},{5,4},{6,5},{7,6},{8,11},{9,8},{10,9... | collective-permute-start | bytes 835592 | tf_op jit(solution)/shard_map/ppermute | solution.py:494
  27.7 15.6 %collective-permute-start.5 = (f32[128,512]{1,0:T(8,128)S(1)}, f32[128,512]{1,0:T(8,128)S(1)}, u32[]{:S(2)}, u32[]{:S(2)}) collective-permute-start(f32[128,512]{1,0:T(8,128)S(1)} %get-tuple-element.100), channel_id=1, source_target_pairs={{0,2},{1,3},{2,0},{3,1},{4,6},{5,7},{6,4},{7,5},{8,10},{9,11},{10,... | collective-permute-start | bytes 786440 | tf_op jit(solution)/shard_map/ppermute | solution.py:494
  30.5 19.5 %collective-permute-start.2 = (bf16[128,512]{1,0:T(8,128)(2,1)S(1)}, bf16[128,512]{1,0:T(8,128)(2,1)S(1)}, u32[]{:S(2)}, u32[]{:S(2)}) collective-permute-start(bf16[128,512]{1,0:T(8,128)(2,1)S(1)} %fusion.d0), channel_id=1, source_target_pairs={{0,3},{1,0},{2,1},{3,2},{4,7},{5,4},{6,5},{7,6},{8,11},{9,8},{10,9... | collective-permute-start | bytes 393224 | tf_op jit(solution)/shard_map/ppermute | solution.py:494
  31.3 18.7 %collective-permute-start.1 = (bf16[128,512]{1,0:T(8,128)(2,1)S(1)}, bf16[128,512]{1,0:T(8,128)(2,1)S(1)}, u32[]{:S(2)}, u32[]{:S(2)}) collective-permute-start(bf16[128,512]{1,0:T(8,128)(2,1)S(1)} %fusion.d0), channel_id=1, source_target_pairs={{0,2},{1,3},{2,0},{3,1},{4,6},{5,7},{6,4},{7,5},{8,10},{9,11},{10,... | collective-permute-start | bytes 393224 | tf_op jit(solution)/shard_map/ppermute | solution.py:494
  37.8 15.2 %all-to-all-start = ((f32[32,16,128]{2,1,0:T(8,128)}), f32[32,16,128]{2,1,0:T(8,128)S(1)}, u32[]{:S(2)}, u32[]{:S(2)}) async-start(f32[32,16,128]{2,1,0:T(8,128)} %get-tuple-element.97), calls=%async_computation | async-start | bytes 524288 | tf_op jit(solution)/shard_map/all_to_all | solution.py:508
  43.4 7.3 %collective-permute-start = (bf16[128,512]{1,0:T(8,128)(2,1)S(1)}, bf16[128,512]{1,0:T(8,128)(2,1)S(1)}, u32[]{:S(2)}, u32[]{:S(2)}) collective-permute-start(bf16[128,512]{1,0:T(8,128)(2,1)S(1)} %fusion.d0), channel_id=1, source_target_pairs={{0,1},{1,2},{2,3},{3,0},{4,5},{5,6},{6,7},{7,4},{8,9},{9,10},{10,1... | collective-permute-start | bytes 393224 | tf_op jit(solution)/shard_map/ppermute | solution.py:494
  50.0 0.7 copy-start.2
  50.7 0.7 copy-start.4
  53.0 18.1 %collective-permute-start.7 = (f32[128,512]{1,0:T(8,128)}, f32[128,512]{1,0:T(8,128)S(1)}, u32[]{:S(2)}, u32[]{:S(2)}) collective-permute-start(f32[128,512]{1,0:T(8,128)} %get-tuple-element.108), channel_id=1, source_target_pairs={{0,1},{1,2},{2,3},{3,0},{4,5},{5,6},{6,7},{7,4},{8,9},{9,10},{10,1... | collective-permute-start | bytes 786440 | tf_op jit(solution)/shard_map/ppermute | solution.py:494
  53.0 18.8 %collective-permute-start.8 = (f32[128,512]{1,0:T(8,128)}, f32[128,512]{1,0:T(8,128)S(1)}, u32[]{:S(2)}, u32[]{:S(2)}) collective-permute-start(f32[128,512]{1,0:T(8,128)} %get-tuple-element.109), channel_id=1, source_target_pairs={{0,2},{1,3},{2,0},{3,1},{4,6},{5,7},{6,4},{7,5},{8,10},{9,11},{10,... | collective-permute-start | bytes 786440 | tf_op jit(solution)/shard_map/ppermute | solution.py:494
  55.9 15.8 %collective-permute-start.9 = (f32[128,512]{1,0:T(8,128)}, f32[128,512]{1,0:T(8,128)S(1)}, u32[]{:S(2)}, u32[]{:S(2)}) collective-permute-start(f32[128,512]{1,0:T(8,128)} %get-tuple-element.110), channel_id=1, source_target_pairs={{0,3},{1,0},{2,1},{3,2},{4,7},{5,4},{6,5},{7,6},{8,11},{9,8},{10,9... | collective-permute-start | bytes 786440 | tf_op jit(solution)/shard_map/ppermute | solution.py:494
  60.6 0.7 copy-start
  61.3 16.1 %copy-start.1 = (f32[128,512]{1,0:T(8,128)S(1)}, f32[128,512]{1,0:T(8,128)}, u32[]{:S(2)}) copy-start(f32[128,512]{1,0:T(8,128)} %copy-done) | copy-start | bytes 786436
  61.3 0.9 copy-start.3
  62.2 0.9 copy-start.5
  67.9 6.0 %collective-permute-start.10 = (f32[128,128]{1,0:T(8,128)S(1)}, f32[128,128]{1,0:T(8,128)S(1)}, u32[]{:S(2)}, u32[]{:S(2)}) collective-permute-start(f32[128,128]{1,0:T(8,128)S(1)} %get-tuple-element.125), channel_id=1, source_target_pairs={{0,3},{1,0},{2,1},{3,2},{4,7},{5,4},{6,5},{7,6},{8,11},{9,8},{10,9... | collective-permute-start | bytes 196616 | tf_op jit(solution)/shard_map/ppermute | solution.py:494
  70.6 6.2 %collective-permute-start.11 = (f32[128,128]{1,0:T(8,128)S(1)}, f32[128,128]{1,0:T(8,128)S(1)}, u32[]{:S(2)}, u32[]{:S(2)}) collective-permute-start(f32[128,128]{1,0:T(8,128)S(1)} %get-tuple-element.126), channel_id=1, source_target_pairs={{0,2},{1,3},{2,0},{3,1},{4,6},{5,7},{6,4},{7,5},{8,10},{9,11},{10,... | collective-permute-start | bytes 196616 | tf_op jit(solution)/shard_map/ppermute | solution.py:494
  71.1 6.3 %collective-permute-start.12 = (f32[128,128]{1,0:T(8,128)S(1)}, f32[128,128]{1,0:T(8,128)S(1)}, u32[]{:S(2)}, u32[]{:S(2)}) collective-permute-start(f32[128,128]{1,0:T(8,128)S(1)} %get-tuple-element.127), channel_id=1, source_target_pairs={{0,1},{1,2},{2,3},{3,0},{4,5},{5,6},{6,7},{7,4},{8,9},{9,10},{10,1... | collective-permute-start | bytes 196616 | tf_op jit(solution)/shard_map/ppermute | solution.py:494
  79.1 0.7 copy-start.6
  79.8 14.2 %all-to-all-start.1 = ((f32[32,16,128]{2,1,0:T(8,128)}), f32[32,16,128]{2,1,0:T(8,128)S(1)}, u32[]{:S(2)}, u32[]{:S(2)}) async-start(f32[32,16,128]{2,1,0:T(8,128)} %get-tuple-element.133), calls=%async_computation.1 | async-start | bytes 524288 | tf_op jit(solution)/shard_map/all_to_all | solution.py:508
  86.2 17.8 %collective-permute-start.13 = (f32[128,512]{1,0:T(8,128)}, f32[128,512]{1,0:T(8,128)S(1)}, u32[]{:S(2)}, u32[]{:S(2)}) collective-permute-start(f32[128,512]{1,0:T(8,128)} %copy-done.6), channel_id=1, source_target_pairs={{4,0},{8,4},{12,8},{16,12},{20,16},{24,20},{28,24},{32,28},{36,32}... | collective-permute-start | bytes 786440 | tf_op jit(solution)/shard_map/ppermute | solution.py:503
  94.7 12.8 %all-to-all-start.2 = ((f32[32,16,128]{2,1,0:T(8,128)}), f32[32,16,128]{2,1,0:T(8,128)S(1)}, u32[]{:S(2)}, u32[]{:S(2)}) async-start(f32[32,16,128]{2,1,0:T(8,128)} %shard_map.110), calls=%async_computation.2 | async-start | bytes 524288 | tf_op jit(solution)/shard_map/all_to_all | solution.py:508
  104.0 3.5 %copy-start.7 = (f32[128,512]{1,0:T(8,128)}, f32[128,512]{1,0:T(8,128)S(1)}, u32[]{:S(2)}) copy-start(f32[128,512]{1,0:T(8,128)S(1)} %collective-permute-done.13.following) | copy-start | bytes 786436
  112.4 6.5 %collective-permute-start.19 = (bf16[128,512]{1,0:T(8,128)(2,1)S(1)}, bf16[128,512]{1,0:T(8,128)(2,1)S(1)}, u32[]{:S(2)}, u32[]{:S(2)}) collective-permute-start(bf16[128,512]{1,0:T(8,128)(2,1)S(1)} %get-tuple-element.148.d0), channel_id=1, source_target_pairs={{0,3},{1,0},{2,1},{3,2},{4,7},{5,4},{6,5},{7,6},{8,11},{9,8},{10,9... | collective-permute-start | bytes 393224 | tf_op jit(solution)/shard_map/ppermute | solution.py:494
  113.0 7.8 %collective-permute-start.18 = (bf16[128,512]{1,0:T(8,128)(2,1)S(1)}, bf16[128,512]{1,0:T(8,128)(2,1)S(1)}, u32[]{:S(2)}, u32[]{:S(2)}) collective-permute-start(bf16[128,512]{1,0:T(8,128)(2,1)S(1)} %get-tuple-element.148.d0), channel_id=1, source_target_pairs={{0,2},{1,3},{2,0},{3,1},{4,6},{5,7},{6,4},{7,5},{8,10},{9,11},{10,... | collective-permute-start | bytes 393224 | tf_op jit(solution)/shard_map/ppermute | solution.py:494
  114.2 8.6 %collective-permute-start.17 = (bf16[128,512]{1,0:T(8,128)(2,1)S(1)}, bf16[128,512]{1,0:T(8,128)(2,1)S(1)}, u32[]{:S(2)}, u32[]{:S(2)}) collective-permute-start(bf16[128,512]{1,0:T(8,128)(2,1)S(1)} %get-tuple-element.148.d0), channel_id=1, source_target_pairs={{0,1},{1,2},{2,3},{3,0},{4,5},{5,6},{6,7},{7,4},{8,9},{9,10},{10,1... | collective-permute-start | bytes 393224 | tf_op jit(solution)/shard_map/ppermute | solution.py:494
  115.0 19.3 %collective-permute-start.14 = (f32[136,512]{1,0:T(8,128)S(1)}, f32[136,512]{1,0:T(8,128)S(1)}, u32[]{:S(2)}, u32[]{:S(2)}) collective-permute-start(f32[136,512]{1,0:T(8,128)S(1)} %get-tuple-element.145), channel_id=1, source_target_pairs={{0,1},{1,2},{2,3},{3,0},{4,5},{5,6},{6,7},{7,4},{8,9},{9,10},{10,1... | collective-permute-start | bytes 835592 | tf_op jit(solution)/shard_map/ppermute | solution.py:494
  116.5 17.8 %collective-permute-start.16 = (f32[136,512]{1,0:T(8,128)S(1)}, f32[136,512]{1,0:T(8,128)S(1)}, u32[]{:S(2)}, u32[]{:S(2)}) collective-permute-start(f32[136,512]{1,0:T(8,128)S(1)} %get-tuple-element.147), channel_id=1, source_target_pairs={{0,3},{1,0},{2,1},{3,2},{4,7},{5,4},{6,5},{7,6},{8,11},{9,8},{10,9... | collective-permute-start | bytes 835592 | tf_op jit(solution)/shard_map/ppermute | solution.py:494
  118.9 15.3 %collective-permute-start.15 = (f32[128,512]{1,0:T(8,128)S(1)}, f32[128,512]{1,0:T(8,128)S(1)}, u32[]{:S(2)}, u32[]{:S(2)}) collective-permute-start(f32[128,512]{1,0:T(8,128)S(1)} %get-tuple-element.146), channel_id=1, source_target_pairs={{0,2},{1,3},{2,0},{3,1},{4,6},{5,7},{6,4},{7,5},{8,10},{9,11},{10,... | collective-permute-start | bytes 786440 | tf_op jit(solution)/shard_map/ppermute | solution.py:494
  138.6 17.2 %collective-permute-start.20 = (f32[160,512]{1,0:T(8,128)S(1)}, f32[160,512]{1,0:T(8,128)S(1)}, u32[]{:S(2)}, u32[]{:S(2)}) collective-permute-start(f32[160,512]{1,0:T(8,128)S(1)} %get-tuple-element.157), channel_id=1, source_target_pairs={{0,1},{1,2},{2,3},{3,0},{4,5},{5,6},{6,7},{7,4},{8,9},{9,10},{10,1... | collective-permute-start | bytes 983048 | tf_op jit(solution)/shard_map/ppermute | solution.py:494
  138.7 17.1 %collective-permute-start.21 = (f32[160,512]{1,0:T(8,128)S(1)}, f32[160,512]{1,0:T(8,128)S(1)}, u32[]{:S(2)}, u32[]{:S(2)}) collective-permute-start(f32[160,512]{1,0:T(8,128)S(1)} %get-tuple-element.158), channel_id=1, source_target_pairs={{0,2},{1,3},{2,0},{3,1},{4,6},{5,7},{6,4},{7,5},{8,10},{9,11},{10,... | collective-permute-start | bytes 983048 | tf_op jit(solution)/shard_map/ppermute | solution.py:494
  141.2 15.2 %collective-permute-start.22 = (f32[160,512]{1,0:T(8,128)S(1)}, f32[160,512]{1,0:T(8,128)S(1)}, u32[]{:S(2)}, u32[]{:S(2)}) collective-permute-start(f32[160,512]{1,0:T(8,128)S(1)} %get-tuple-element.159), channel_id=1, source_target_pairs={{0,3},{1,0},{2,1},{3,2},{4,7},{5,4},{6,5},{7,6},{8,11},{9,8},{10,9... | collective-permute-start | bytes 983048 | tf_op jit(solution)/shard_map/ppermute | solution.py:494
  142.5 15.6 %all-to-all-start.3 = ((f32[32,16,128]{2,1,0:T(8,128)}), f32[32,16,128]{2,1,0:T(8,128)S(1)}, u32[]{:S(2)}, u32[]{:S(2)}) async-start(f32[32,16,128]{2,1,0:T(8,128)} %get-tuple-element.143), calls=%async_computation.3 | async-start | bytes 524288 | tf_op jit(solution)/shard_map/all_to_all | solution.py:508
  158.0 12.9 %all-to-all-start.4 = ((f32[32,16,128]{2,1,0:T(8,128)}), f32[32,16,128]{2,1,0:T(8,128)S(1)}, u32[]{:S(2)}, u32[]{:S(2)}) async-start(f32[32,16,128]{2,1,0:T(8,128)} %get-tuple-element.167), calls=%async_computation.4 | async-start | bytes 524288 | tf_op jit(solution)/shard_map/all_to_all | solution.py:508
  163.1 17.7 %collective-permute-start.23 = (f32[128,512]{1,0:T(8,128)S(1)}, f32[128,512]{1,0:T(8,128)S(1)}, u32[]{:S(2)}, u32[]{:S(2)}) collective-permute-start(f32[128,512]{1,0:T(8,128)S(1)} %get-tuple-element.175), channel_id=1, source_target_pairs={{4,0},{8,4},{12,8},{16,12},{20,16},{24,20},{28,24},{32,28},{36,32}... | collective-permute-start | bytes 786440 | tf_op jit(solution)/shard_map/ppermute | solution.py:503
  171.7 12.8 %all-to-all-start.5 = ((f32[32,16,128]{2,1,0:T(8,128)}), f32[32,16,128]{2,1,0:T(8,128)S(1)}, u32[]{:S(2)}, u32[]{:S(2)}) async-start(f32[32,16,128]{2,1,0:T(8,128)} %shard_map.117), calls=%async_computation.5 | async-start | bytes 524288 | tf_op jit(solution)/shard_map/all_to_all | solution.py:508
  180.8 3.6 %copy-start.8 = (f32[128,512]{1,0:T(8,128)}, f32[128,512]{1,0:T(8,128)S(1)}, u32[]{:S(2)}) copy-start(f32[128,512]{1,0:T(8,128)S(1)} %collective-permute-done.23.following) | copy-start | bytes 786436
Sparse Core Ops, SparseCore 0:
  10.3 50.3 all-gather.1

commit v6 on v5

--- a/solution.py
+++ b/solution.py
@@ -63,25 +63,24 @@
     return 1.0 - (damping + DRAG_RATE * jnp.abs(value))
 
 
-def send_order(place, i, source, outs):
+def send_order(place, source, outs, i=None):
     count, height, _ = source.shape
-    at = pl.multiple_of(i * height, height)
+    rows = slice(0, height) if i is None else pl.ds(pl.multiple_of(i * height, height), height)
     for r, ref in enumerate(outs):
-        ref[pl.ds(at, height), :] = source[lax.rem(place[0] + r, count)]
-
-
-def send_edges(current, outs):
+        ref[rows, :] = source[lax.rem(place[0] + r, count)]
+
+
+def send_edges(current, outs, first=True, last=True):
     stations, height, width = current.shape
-    i = pl.program_id(0)
     total = outs[1].shape[0]
     empty = jnp.zeros((EDGE - stations, width), F32)
 
-    @pl.when(i == pl.num_programs(0) - 1)
+    @pl.when(last)
     def _():
         rows = [current[s, height - 1 : height] for s in range(stations)]
         outs[1][total - EDGE : total] = jnp.concatenate(rows + [empty], axis=0)
 
-    @pl.when(i == 0)
+    @pl.when(first)
     def _():
         rows = [current[s, 0:1] for s in range(stations)]
         outs[-1][total - EDGE : total] = jnp.concatenate(rows + [empty], axis=0)
@@ -96,8 +95,9 @@
             source[s, rows] = SOURCE_GAIN * (here - previous)
             previous = here
     outs = (x0, x1, x2, x3)
-    send_order(place, pl.program_id(0), source, outs)
-    send_edges(current, outs)
+    i = pl.program_id(0)
+    send_order(place, source, outs, i)
+    send_edges(current, outs, i == 0, i == pl.num_programs(0) - 1)
 
 
 def decay_kernel(place, current, damping, decay, scale):
@@ -282,7 +282,7 @@
 def offset_kernel(place, *rest):
     c = place[0]
     pieces = rest[:4]
-    *forces, weights, base, force_weight, lead, lead_far, force, offset = rest[4:]
+    *forces, weights, base, force_weight, lead, force, offset = rest[4:]
     count, height, full = weights.shape
     width = full // count
     for r in range(count):
@@ -301,7 +301,6 @@
         @pl.when(c == r)
         def _():
             lead[...] = pieces[r][0:height]
-            lead_far[...] = pieces[r][0:height]
 
     for g, rows in groups(height):
         state = base[rows] + force_weight[rows] * force[rows]
@@ -311,7 +310,10 @@
         to_chunks(offset, g, state)
 
 
-def change_kernel(place, p0, p1, p2, p3, term, force, change, pressure):
+def change_kernel(
+    place, p0, p1, p2, p3, term, force, decay, inflow,
+    change, pressure, decay_near, entry,
+):
     c = place[0]
     pieces = (p0, p1, p2, p3)
     count, height, _ = term.shape
@@ -319,6 +321,7 @@
         pressure[lax.rem(c - r + count, count)] = pieces[r][...]
     for _, rows in groups(height):
         here = pressure[0, rows]
+        entry[rows] = jnp.where(place[1] == 1, inflow[rows], -here)
         for s in range(count):
             value = term[s, rows] + here
             if s == 0:
@@ -327,6 +330,7 @@
                 here = pressure[s + 1, rows]
                 value = value - here
             change[s, rows] = value
+            decay_near[s, rows] = decay[s, rows]
 
 
 def scan_kernel(scale, offset, entering):
@@ -337,9 +341,9 @@
         state = scale[m] * state + offset[m]
 
 
-def march_rows(first, g, rows, entering, change, following, decay, lead, inflow):
+def march_rows(g, rows, entering, change, following, decay, entry):
     stations = decay.shape[0]
-    state = jnp.where(first == 1, inflow[rows], from_chunks(entering, g) - lead[rows])
+    state = from_chunks(entering, g) + entry[rows]
     states = [state]
     for s in range(stations):
         step = change[s, rows]
@@ -351,32 +355,23 @@
 
 
 def middle_kernel(
-    place, entering, change, following, decay, lead, inflow, damping,
-    current, decay_new, scale, disc, x0, x1, x2, x3, source,
+    place, entering, change, following, decay, entry, current, disc, x0, x1, x2, x3, source
 ):
-    first = place[1]
     stations, height, _ = current.shape
     for g, rows in groups(height):
-        states = march_rows(first, g, rows, entering, change, following, decay, lead, inflow)
-        product = None
+        states = march_rows(g, rows, entering, change, following, decay, entry)
         for s in range(stations):
-            value = states[s + 1]
-            current[s, rows] = value
-            source[s, rows] = SOURCE_GAIN * (value - states[s])
-            d = decay_of(value, damping[s, rows])
-            decay_new[s, rows] = d
-            product = d if product is None else product * d
-        to_chunks(scale, g, product)
+            current[s, rows] = states[s + 1]
+            source[s, rows] = SOURCE_GAIN * (states[s + 1] - states[s])
     outs = (x0, x1, x2, x3)
-    send_order(place, pl.program_id(0), source, outs)
+    send_order(place, source, outs)
     send_edges(current, outs)
     disc[...] = current[0].astype(BF16)
 
 
-def last_kernel(place, entering, change, following, decay, lead, inflow, current):
-    first = place[1]
+def last_kernel(entering, change, following, decay, entry, current):
     for g, rows in groups(current.shape[1]):
-        states = march_rows(first, g, rows, entering, change, following, decay, lead, inflow)
+        states = march_rows(g, rows, entering, change, following, decay, entry)
         for s in range(current.shape[0]):
             current[s, rows] = states[s + 1]
 
@@ -518,7 +513,6 @@
     )
 
     step = (stations, height // STEPS, width)
-    turned = range(4, 8)
     near_inflow = stay(inflow)
     upstream = along_march(velocity_guess[-1], 1)
     upstream, *where = lax.optimization_barrier((upstream, *where))
@@ -535,23 +529,24 @@
         whole=range(4),
         scratch=[pltpu.VMEM(step, F32)],
     )
-    guess, damp, *source = lax.optimization_barrier((velocity_guess, damping, *source))
-    decay, scale = by_rows(
-        decay_kernel,
-        height,
-        [far(slab), far(chunks)],
-        place,
-        (stay(guess), stay(damp)),
-        cost(4e6, 3 * MIB),
-    )
     for sweep_index in range(SWEEPS):
         merged = sweep_index > 0
         final = sweep_index == SWEEPS - 1
         if merged:
             rows = turns([disc] * cross_size)
+        guess, damp, *source = lax.optimization_barrier((current, damping, *source))
         arrived = turns(source)
+        decay, scale = by_rows(
+            decay_kernel,
+            height,
+            [far(slab), far(chunks)],
+            place,
+            (guess if merged else stay(guess), stay(damp)),
+            cost(4e6, 3 * MIB),
+        )
         solve_cost = cost(3 * 8 * width**3, 5 * MIB)
         if merged:
+            scale, *arrived = lax.optimization_barrier((scale, *arrived))
             made = disc_forces(rows, where, blades, tabled)
             forces, near_tables = made[:cross_size], made[cross_size:]
             solved = call(
@@ -579,6 +574,7 @@
                 cost_estimate=solve_cost,
             )(place, *arrived, *tabled)
             rows, scales, solved = lax.optimization_barrier((rows, scales, solved))
+            forces = turns(disc_forces(rows, where, blades), -1)
         pieces = turns(solved)
         decay = stay(decay)
         term, weights, base, force_weight = call(
@@ -589,12 +585,9 @@
             scalars=1,
             limit=12,
         )
-        if not merged:
-            rows, base = lax.optimization_barrier((rows, base))
-            forces = turns(disc_forces(rows, where, blades), -1)
-        lead, lead_far, force, offset = call(
+        lead, force, offset = call(
             offset_kernel,
-            [near(plane), far(plane), far(plane), far(chunks)],
+            [near(plane), far(plane), far(chunks)],
             (place, *pieces, *forces, weights, base, force_weight),
             cost(2e6, 3 * MIB),
             scalars=1,
@@ -602,35 +595,33 @@
         )
         following = along_march(lead, -1)
         offset, force, *pieces = lax.optimization_barrier((offset, force, *pieces))
-        change, pressure = by_rows(
+        change, pressure, decay, entry = by_rows(
             change_kernel,
             height,
-            [far(slab), far(slab)],
+            [near(slab), far(slab), near(slab), near(plane)],
             place,
-            (*pieces, stay(term), stay(force)),
+            (*pieces, stay(term), stay(force), decay, near_inflow),
             cost(4e6, 4 * MIB),
         )
         (entering,) = call(
             scan_kernel, [far(chunks)], (scales, across_march(offset)), cost(1e5, MIB)
         )
         entering = across_march(entering)
-        common = (entering, stay(change), stay(following), decay, stay(lead_far), near_inflow)
+        common = (entering, change, following, decay, entry)
         if final:
-            (current,) = by_rows(
-                last_kernel, height, [far(slab)], place, common, cost(4e6, 5 * MIB)
+            (current,) = call(
+                last_kernel, [far(slab)], common, cost(4e6, 5 * MIB), limit=12
             )
             return (current, pressure)
-        current, decay, scale, disc, *source = by_rows(
+        current, disc, *source = call(
             middle_kernel,
-            height,
-            [far(slab), far(slab), far(chunks), near(plane, BF16)] + sources,
-            place,
-            common + (stay(damping),),
-            cost(8e6, 8 * MIB),
-            whole=turned,
-            scratch=[pltpu.VMEM(step, F32)],
-        )
-        current = stay(current)
+            [near(slab), near(plane, BF16)] + sources,
+            (place, *common),
+            cost(6e6, 5 * MIB),
+            scalars=1,
+            limit=12,
+            scratch=[pltpu.VMEM(slab, F32)],
+        )
 
 
 def solution(mesh):

time: 199 us -> 195 us (0.980)
  waiting for transfers between devices: 43.7 us -> 37.2 us
  starting transfers between devices: 71.5 us -> 75.3 us
    ppermute x21, waiting for transfers between devices: 20.3 us -> 12.2 us  [turn(): lax.ppermute(value, 'cross', [(i, (i + steps) % cross_size) for i in rang...]
    pallas_call x6 -> x5, Pallas kernels: 24.5 us -> 19.6 us  [by_rows(): pl.pallas_call(kernel, grid_spec=pltpu.PrefetchScalarGridSpec(num_scalar_...]
    pallas_call x7 -> x9, Pallas kernels: 16.3 us -> 20.4 us  [call(): pl.pallas_call(kernel, out_shape=outs, in_specs=[SMEM] * scalars + [VMEM]...]
    all_gather x1, waiting for transfers between devices: 0.01 us -> 4.06 us  [local(): blades = lax.all_gather(blade, 'march', axis=0, tiled=True)]
    all_to_all x6, starting transfers between devices: 32.1 us -> 35 us  [across_march(): lax.all_to_all(value, 'march', split_axis=0, concat_axis=0, tiled=True)]
    all_to_all x6, waiting for transfers between devices: 15.7 us -> 13.2 us  [across_march(): lax.all_to_all(value, 'march', split_axis=0, concat_axis=0, tiled=True)]
    unnamed x18 -> x16, local copies, waits for them, and re-layouts: 4.59 us -> 5.2 us
  transfers between devices with their start and end apart: 31 -> 31, of which waited for: 14 -> 14; matrix products, arithmetic and copies ran while one was open for 2% -> 3% of each run, Pallas kernels for 21% -> 23%
where the time goes in v6:
time: 195 us; the launch traced here: 192 us
  starting transfers between devices  75.3 us (39%)
  Pallas kernels  55 us (28%)
  waiting for transfers between devices  37.2 us (19%)
  between operations  14.3 us (7%)
  local copies, waits for them, and re-layouts  9.24 us (5%)
    all_to_all x6, starting transfers between devices, across_march(): lax.all_to_all(value, 'march', split_axis=0, concat_axis=0, tiled=True)  35 us
    ppermute x21, starting transfers between devices, turn(): lax.ppermute(value, 'cross', [(i, (i + steps) % cross_size) for i in rang...  29.7 us
    pallas_call x9, Pallas kernels, call(): pl.pallas_call(kernel, out_shape=outs, in_specs=[SMEM] * scalars + [VMEM]...  20.4 us
    pallas_call x5, Pallas kernels, by_rows(): pl.pallas_call(kernel, grid_spec=pltpu.PrefetchScalarGridSpec(num_scalar_...  19.6 us
    all_to_all x6, waiting for transfers between devices, across_march(): lax.all_to_all(value, 'march', split_axis=0, concat_axis=0, tiled=True)  13.2 us
    ppermute x21, waiting for transfers between devices, turn(): lax.ppermute(value, 'cross', [(i, (i + steps) % cross_size) for i in rang...  12.2 us
    ppermute x3, starting transfers between devices, along_march(): lax.ppermute(value, 'march', [(i, i + steps) for i in range(count) if 0 <...  10.6 us
    pallas_call x2, Pallas kernels, disc_forces(): pl.pallas_call(disc_kernel, grid=(number // per_step,), out_shape=[near((...  9.51 us
  transfers between devices with their start and end apart: 31, of which 14 were waited for; matrix products, arithmetic and copies ran while one was open for 3% of the time, Pallas kernels for 23%

profile of v6, /device:TPU:2, one launch (start us, length us, event | category | flops | bytes accessed | tf_op | source)
XLA Modules:
  0.0 191.8 jit_solution(17432787356102142246)
XLA Ops:
  7.9 1.0 slice_bitcast_fusion
  8.9 1.9 %collective-permute-start.3 = (f32[128,512]{1,0:T(8,128)S(1)}, f32[128,512]{1,0:T(8,128)S(1)}, u32[]{:S(2)}, u32[]{:S(2)}) collective-permute-start(f32[128,512]{1,0:T(8,128)S(1)} %slice_bitcast_fusion), channel_id=1, source_target_pairs={{0,4},{4,8},{8,12},{12,16},{16,20},{20,24},{24,28},{28,32},{32,36}... | collective-permute-start | bytes 786440 | tf_op jit(solution)/shard_map/ppermute | solution.py:498
  11.6 7.1 %collective-permute-done.3.upstream = f32[128,512]{1,0:T(8,128)S(1)} collective-permute-done((f32[128,512]{1,0:T(8,128)S(1)}, f32[128,512]{1,0:T(8,128)S(1)}, u32[]{:S(2)}, u32[]{:S(2)}) %collective-permute-start.3) | collective-permute-done | bytes 262176 | tf_op jit(solution)/shard_map/ppermute | solution.py:498
  20.8 2.8 %shard_map.104 = (f32[128,512]{1,0:T(8,128)S(1)}, f32[136,512]{1,0:T(8,128)S(1)}, f32[128,512]{1,0:T(8,128)S(1)}, f32[136,512]{1,0:T(8,128)S(1)}) custom-call(s32[4]{0:T(128)S(1)} %pad_add_fusion.place, f32[4,128,512]{2,1,0:T(8,128)} %current.4, f32[128,512]{1,0:T(8,128)S(1)} %collective-permute-done.3.upstream, f32[128,512]{1,0:T(8,128)} %inflow.9), custom_call_target="tpu_custom_call" | custom-call | flops 1000000 | bytes 2097152 | tf_op jit(solution)/shard_map/pallas_call | solution.py:420
  23.5 2.0 %collective-permute-start.4 = (f32[136,512]{1,0:T(8,128)S(1)}, f32[136,512]{1,0:T(8,128)S(1)}, u32[]{:S(2)}, u32[]{:S(2)}) collective-permute-start(f32[136,512]{1,0:T(8,128)S(1)} %get-tuple-element.107), channel_id=1, source_target_pairs={{0,1},{1,2},{2,3},{3,0},{4,5},{5,6},{6,7},{7,4},{8,9},{9,10},{10,1... | collective-permute-start | bytes 835592 | tf_op jit(solution)/shard_map/ppermute | solution.py:489
  25.5 2.2 %collective-permute-start.6 = (f32[136,512]{1,0:T(8,128)S(1)}, f32[136,512]{1,0:T(8,128)S(1)}, u32[]{:S(2)}, u32[]{:S(2)}) collective-permute-start(f32[136,512]{1,0:T(8,128)S(1)} %get-tuple-element.109), channel_id=1, source_target_pairs={{0,3},{1,0},{2,1},{3,2},{4,7},{5,4},{6,5},{7,6},{8,11},{9,8},{10,9... | collective-permute-start | bytes 835592 | tf_op jit(solution)/shard_map/ppermute | solution.py:489
  27.7 1.8 collective-permute-start.5
  29.5 1.0 fusion.d0
  31.3 2.4 %collective-permute-start.1 = (bf16[128,512]{1,0:T(8,128)(2,1)S(1)}, bf16[128,512]{1,0:T(8,128)(2,1)S(1)}, u32[]{:S(2)}, u32[]{:S(2)}) collective-permute-start(bf16[128,512]{1,0:T(8,128)(2,1)S(1)} %fusion.d0), channel_id=1, source_target_pairs={{0,2},{1,3},{2,0},{3,1},{4,6},{5,7},{6,4},{7,5},{8,10},{9,11},{10,... | collective-permute-start | bytes 393224 | tf_op jit(solution)/shard_map/ppermute | solution.py:489
  33.6 4.2 %shard_map.105 = (f32[4,128,512]{2,1,0:T(8,128)}, f32[32,16,128]{2,1,0:T(8,128)}) custom-call(s32[4]{0:T(128)S(1)} %pad_add_fusion.place, f32[4,128,512]{2,1,0:T(8,128)} %current.4, f32[4,128,512]{2,1,0:T(8,128)} %damping.1), custom_call_target="tpu_custom_call" | custom-call | flops 4000000 | bytes 3145728 | tf_op jit(solution)/shard_map/pallas_call | solution.py:420
  37.8 5.5 %all-to-all-start = ((f32[32,16,128]{2,1,0:T(8,128)}), f32[32,16,128]{2,1,0:T(8,128)S(1)}, u32[]{:S(2)}, u32[]{:S(2)}) async-start(f32[32,16,128]{2,1,0:T(8,128)} %get-tuple-element.105), calls=%async_computation | async-start | bytes 524288 | tf_op jit(solution)/shard_map/all_to_all | solution.py:503
  43.5 5.6 %shard_map.106 = (f32[128,512]{1,0:T(8,128)S(1)}, f32[128,512]{1,0:T(8,128)S(1)}, f32[128,512]{1,0:T(8,128)S(1)}, f32[128,512]{1,0:T(8,128)S(1)}) custom-call(s32[4]{0:T(128)S(1)} %pad_add_fusion.place, f32[128,512]{1,0:T(8,128)S(1)} %get-tuple-element.106.x0, f32[136,512]{1,0:T(8,128)S(1)} %collective-permute-done.4.x1.before, ...), custom_call_target="tpu_custom_call" | custom-call | flops 3221225472 | bytes 5242880 | tf_op jit(solution)/shard_map/pallas_call | solution.py:565
  49.1 1.1 collective-permute-done.d1
  50.2 2.8 %all-to-all-done.scale = f32[32,16,128]{2,1,0:T(8,128)S(1)} async-done(((f32[32,16,128]{2,1,0:T(8,128)}), f32[32,16,128]{2,1,0:T(8,128)S(1)}, u32[]{:S(2)}, u32[]{:S(2)}) %all-to-all-start) | async-done | bytes 262176 | tf_op jit(solution)/shard_map/all_to_all | solution.py:503
  53.0 2.7 %collective-permute-start.8 = (f32[128,512]{1,0:T(8,128)S(1)}, f32[128,512]{1,0:T(8,128)S(1)}, u32[]{:S(2)}, u32[]{:S(2)}) collective-permute-start(f32[128,512]{1,0:T(8,128)S(1)} %get-tuple-element.117), channel_id=1, source_target_pairs={{0,2},{1,3},{2,0},{3,1},{4,6},{5,7},{6,4},{7,5},{8,10},{9,11},{10,... | collective-permute-start | bytes 786440 | tf_op jit(solution)/shard_map/ppermute | solution.py:489
  56.6 4.1 %all-gather.2.cloned.1.call-done.rest_0_.rest_1_.rest_2_.rest_3_ = bf16[32,512,128]{2,1,0:T(8,128)(2,1)} async-done(((bf16[1,512,128]{2,1,0:T(8,128)(2,1)}), bf16[32,512,128]{2,1,0:T(8,128)(2,1)}) %all-gather.2.cloned.1.call-update) | async-done | bytes 4194320 | tf_op jit(solution)/shard_map/all_gather | solution.py:505
  60.7 4.7 %shard_map.107 = (f32[128,128]{1,0:T(8,128)S(1)}, f32[128,128]{1,0:T(8,128)S(1)}, f32[128,128]{1,0:T(8,128)S(1)}, f32[128,128]{1,0:T(8,128)S(1)}) custom-call(bf16[128,512]{1,0:T(8,128)(2,1)S(1)} %fusion.d0, bf16[128,512]{1,0:T(8,128)(2,1)S(1)} %collective-permute-done.d1, bf16[128,512]{1,0:T(8,128)(2,1)S(1)} %collective-permute-done.1.d2, ...), custom_call_target="tpu_custom_call" | custom-call | flops 2147483648 | bytes 5242880 | tf_op jit(solution)/shard_map/pallas_call | solution.py:443
  65.4 3.5 %collective-permute-start.10 = (f32[128,128]{1,0:T(8,128)S(1)}, f32[128,128]{1,0:T(8,128)S(1)}, u32[]{:S(2)}, u32[]{:S(2)}) collective-permute-start(f32[128,128]{1,0:T(8,128)S(1)} %get-tuple-element.127), channel_id=1, source_target_pairs={{0,3},{1,0},{2,1},{3,2},{4,7},{5,4},{6,5},{7,6},{8,11},{9,8},{10,9... | collective-permute-start | bytes 196616 | tf_op jit(solution)/shard_map/ppermute | solution.py:489
  69.9 3.6 %shard_map.108 = (f32[4,128,512]{2,1,0:T(8,128)}, f32[4,128,512]{2,1,0:T(8,128)S(1)}, f32[128,512]{1,0:T(8,128)S(1)}, f32[128,512]{1,0:T(8,128)S(1)}) custom-call(s32[4]{0:T(128)S(1)} %pad_add_fusion.place, f32[4,128,512]{2,1,0:T(8,128)} %current.4, f32[136,512]{1,0:T(8,128)S(1)} %collective-permute-done.4.x1.before, ...), custom_call_target="tpu_custom_call" | custom-call | flops 8000000 | bytes 4194304 | tf_op jit(solution)/shard_map/pallas_call | solution.py:396
  73.6 1.5 collective-permute-done.11.rest_6_
  75.6 1.6 shard_map.109
  77.2 5.9 %all-to-all-start.1 = ((f32[32,16,128]{2,1,0:T(8,128)}), f32[32,16,128]{2,1,0:T(8,128)S(1)}, u32[]{:S(2)}, u32[]{:S(2)}) async-start(f32[32,16,128]{2,1,0:T(8,128)} %get-tuple-element.136), calls=%async_computation.1 | async-start | bytes 524288 | tf_op jit(solution)/shard_map/all_to_all | solution.py:503
  83.1 4.3 %collective-permute-start.13 = (f32[128,512]{1,0:T(8,128)}, f32[128,512]{1,0:T(8,128)}, u32[]{:S(2)}, u32[]{:S(2)}) collective-permute-start(f32[128,512]{1,0:T(8,128)} %get-tuple-element.144), channel_id=1, source_target_pairs={{4,0},{8,4},{12,8},{16,12},{20,16},{24,20},{28,24},{32,28},{36,32}... | collective-permute-start | bytes 786440 | tf_op jit(solution)/shard_map/ppermute | solution.py:498
  87.5 3.4 %all-to-all-done.1.offset = f32[32,16,128]{2,1,0:T(8,128)S(1)} async-done(((f32[32,16,128]{2,1,0:T(8,128)}), f32[32,16,128]{2,1,0:T(8,128)S(1)}, u32[]{:S(2)}, u32[]{:S(2)}) %all-to-all-start.1) | async-done | bytes 262176 | tf_op jit(solution)/shard_map/all_to_all | solution.py:503
  91.6 5.0 %all-to-all-start.2 = ((f32[32,16,128]{2,1,0:T(8,128)}), f32[32,16,128]{2,1,0:T(8,128)S(1)}, u32[]{:S(2)}, u32[]{:S(2)}) async-start(f32[32,16,128]{2,1,0:T(8,128)} %shard_map.110), calls=%async_computation.2 | async-start | bytes 524288 | tf_op jit(solution)/shard_map/all_to_all | solution.py:503
  98.6 4.3 %shard_map.111 = (f32[4,128,512]{2,1,0:T(8,128)S(1)}, f32[4,128,512]{2,1,0:T(8,128)}, f32[4,128,512]{2,1,0:T(8,128)S(1)}, f32[128,512]{1,0:T(8,128)S(1)}) custom-call(s32[4]{0:T(128)S(1)} %pad_add_fusion.place, f32[128,512]{1,0:T(8,128)S(1)} %get-tuple-element.137.rest_0_.p0, f32[128,512]{1,0:T(8,128)S(1)} %collective-permute-done.7.rest_1_.p1, ...), custom_call_target="tpu_custom_call" | custom-call | flops 4000000 | bytes 4194304 | tf_op jit(solution)/shard_map/pallas_call | solution.py:420
  105.4 1.2 shard_map.112
  107.5 1.8 collective-permute-start.18
  109.3 1.7 collective-permute-start.14
  111.0 1.6 collective-permute-start.16
  113.2 1.9 collective-permute-start.15
  115.1 4.0 %shard_map.113 = (f32[4,128,512]{2,1,0:T(8,128)}, f32[32,16,128]{2,1,0:T(8,128)}) custom-call(s32[4]{0:T(128)S(1)} %pad_add_fusion.place, f32[4,128,512]{2,1,0:T(8,128)S(1)} %get-tuple-element.152.current, f32[4,128,512]{2,1,0:T(8,128)} %damping.1), custom_call_target="tpu_custom_call" | custom-call | flops 4000000 | bytes 3145728 | tf_op jit(solution)/shard_map/pallas_call | solution.py:420
  119.1 4.8 %shard_map.114 = (f32[128,128]{1,0:T(8,128)S(1)}, f32[128,128]{1,0:T(8,128)S(1)}, f32[128,128]{1,0:T(8,128)S(1)}, f32[128,128]{1,0:T(8,128)S(1)}, bf16[512,512]{...) custom-call(bf16[128,512]{1,0:T(8,128)(2,1)S(1)} %get-tuple-element.164.d0, ...), custom_call_target="tpu_custom_call" | custom-call | flops 2147483648 | bytes 5242880 | tf_op jit(solution)/shard_map/pallas_call | solution.py:443
  124.0 4.8 %collective-permute-done.15.x2 = f32[128,512]{1,0:T(8,128)S(1)} collective-permute-done((f32[128,512]{1,0:T(8,128)S(1)}, f32[128,512]{1,0:T(8,128)S(1)}, u32[]{:S(2)}, u32[]{:S(2)}) %collective-permute-start.15) | collective-permute-done | bytes 262176 | tf_op jit(solution)/shard_map/ppermute | solution.py:489
  128.8 5.2 %shard_map.115 = (f32[160,512]{1,0:T(8,128)S(1)}, f32[160,512]{1,0:T(8,128)}, f32[160,512]{1,0:T(8,128)}, f32[160,512]{1,0:T(8,128)}) custom-call(s32[4]{0:T(128)S(1)} %pad_add_fusion.place, f32[128,512]{1,0:T(8,128)S(1)} %get-tuple-element.160.x0, f32[136,512]{1,0:T(8,128)S(1)} %collective-permute-done.14.x1.before, ...), custom_call_target="tpu_custom_call" | custom-call | flops 3221225472 | bytes 5242880 | tf_op jit(solution)/shard_map/pallas_call | solution.py:396
  134.0 2.4 %collective-permute-start.21 = (f32[160,512]{1,0:T(8,128)}, f32[160,512]{1,0:T(8,128)S(1)}, u32[]{:S(2)}, u32[]{:S(2)}) collective-permute-start(f32[160,512]{1,0:T(8,128)} %get-tuple-element.174), channel_id=1, source_target_pairs={{0,2},{1,3},{2,0},{3,1},{4,6},{5,7},{6,4},{7,5},{8,10},{9,11},{10,... | collective-permute-start | bytes 983048 | tf_op jit(solution)/shard_map/ppermute | solution.py:489
  136.4 2.1 %collective-permute-start.22 = (f32[160,512]{1,0:T(8,128)}, f32[160,512]{1,0:T(8,128)S(1)}, u32[]{:S(2)}, u32[]{:S(2)}) collective-permute-start(f32[160,512]{1,0:T(8,128)} %get-tuple-element.175), channel_id=1, source_target_pairs={{0,3},{1,0},{2,1},{3,2},{4,7},{5,4},{6,5},{7,6},{8,11},{9,8},{10,9... | collective-permute-start | bytes 983048 | tf_op jit(solution)/shard_map/ppermute | solution.py:489
  138.5 6.5 %all-to-all-start.3 = ((f32[32,16,128]{2,1,0:T(8,128)}), f32[32,16,128]{2,1,0:T(8,128)S(1)}, u32[]{:S(2)}, u32[]{:S(2)}) async-start(f32[32,16,128]{2,1,0:T(8,128)} %get-tuple-element.159), calls=%async_computation.3 | async-start | bytes 524288 | tf_op jit(solution)/shard_map/all_to_all | solution.py:503
  145.0 3.3 %shard_map.116 = (f32[4,128,512]{2,1,0:T(8,128)}, f32[4,128,512]{2,1,0:T(8,128)S(1)}, f32[128,512]{1,0:T(8,128)S(1)}, f32[128,512]{1,0:T(8,128)S(1)}) custom-call(s32[4]{0:T(128)S(1)} %pad_add_fusion.place, f32[4,128,512]{2,1,0:T(8,128)S(1)} %get-tuple-element.152.current, f32[136,512]{1,0:T(8,128)S(1)} %collective-permute-done.14.x1.before, ...), custom_call_target="tpu_custom_call" | custom-call | flops 8000000 | bytes 4194304 | tf_op jit(solution)/shard_map/pallas_call | solution.py:396
  148.3 2.9 %collective-permute-done.20.rest_1_.p1 = f32[160,512]{1,0:T(8,128)S(1)} collective-permute-done((f32[160,512]{1,0:T(8,128)}, f32[160,512]{1,0:T(8,128)S(1)}, u32[]{:S(2)}, u32[]{:S(2)}) %collective-permute-start.20) | collective-permute-done | bytes 327712 | tf_op jit(solution)/shard_map/ppermute | solution.py:489
  151.9 1.6 shard_map.117
  153.5 6.4 %all-to-all-start.4 = ((f32[32,16,128]{2,1,0:T(8,128)}), f32[32,16,128]{2,1,0:T(8,128)S(1)}, u32[]{:S(2)}, u32[]{:S(2)}) async-start(f32[32,16,128]{2,1,0:T(8,128)} %get-tuple-element.182), calls=%async_computation.4 | async-start | bytes 524288 | tf_op jit(solution)/shard_map/all_to_all | solution.py:503
  159.8 4.3 %collective-permute-start.23 = (f32[128,512]{1,0:T(8,128)}, f32[128,512]{1,0:T(8,128)}, u32[]{:S(2)}, u32[]{:S(2)}) collective-permute-start(f32[128,512]{1,0:T(8,128)} %get-tuple-element.190), channel_id=1, source_target_pairs={{4,0},{8,4},{12,8},{16,12},{20,16},{24,20},{28,24},{32,28},{36,32}... | collective-permute-start | bytes 786440 | tf_op jit(solution)/shard_map/ppermute | solution.py:498
  164.2 3.4 %all-to-all-done.4.offset = f32[32,16,128]{2,1,0:T(8,128)S(1)} async-done(((f32[32,16,128]{2,1,0:T(8,128)}), f32[32,16,128]{2,1,0:T(8,128)S(1)}, u32[]{:S(2)}, u32[]{:S(2)}) %all-to-all-start.4) | async-done | bytes 262176 | tf_op jit(solution)/shard_map/all_to_all | solution.py:503
  168.4 5.7 %all-to-all-start.5 = ((f32[32,16,128]{2,1,0:T(8,128)}), f32[32,16,128]{2,1,0:T(8,128)}, u32[]{:S(2)}, u32[]{:S(2)}) async-start(f32[32,16,128]{2,1,0:T(8,128)} %shard_map.118), calls=%async_computation.5 | async-start | bytes 524288 | tf_op jit(solution)/shard_map/all_to_all | solution.py:503
  174.0 4.3 %shard_map.119 = (f32[4,128,512]{2,1,0:T(8,128)S(1)}, f32[4,128,512]{2,1,0:T(8,128)}, f32[4,128,512]{2,1,0:T(8,128)S(1)}, f32[128,512]{1,0:T(8,128)S(1)}) custom-call(s32[4]{0:T(128)S(1)} %pad_add_fusion.place, f32[160,512]{1,0:T(8,128)S(1)} %get-tuple-element.183.rest_0_.p0, f32[160,512]{1,0:T(8,128)S(1)} %collective-permute-done.20.rest_1_.p1, ...), custom_call_target="tpu_custom_call" | custom-call | flops 4000000 | bytes 4194304 | tf_op jit(solution)/shard_map/pallas_call | solution.py:420
  179.1 2.8 %all-to-all-done.5.entering = f32[32,16,128]{2,1,0:T(8,128)} async-done(((f32[32,16,128]{2,1,0:T(8,128)}), f32[32,16,128]{2,1,0:T(8,128)}, u32[]{:S(2)}, u32[]{:S(2)}) %all-to-all-start.5) | async-done | bytes 262176 | tf_op jit(solution)/shard_map/all_to_all | solution.py:503
  182.8 2.1 %shard_map.120 = f32[4,128,512]{2,1,0:T(8,128)} custom-call(f32[32,16,128]{2,1,0:T(8,128)} %all-to-all-done.5.entering, f32[4,128,512]{2,1,0:T(8,128)S(1)} %get-tuple-element.189.change, f32[128,512]{1,0:T(8,128)} %collective-permute-done.23.following, f32[4,128,512]{2,1,0:T(8,128)S(1)} %get-tuple-element.191.decay, f32[128,512]{1,0:T(8,128)S(1)} %copy-done.7), custom_call_target="tpu_custom_call" | custom-call | flops 4000000 | bytes 5242880 | tf_op jit(solution)/shard_map/pallas_call | solution.py:396
  (56 shorter events, 16.9 us)
Async XLA Ops:
  7.2 53.5 %all-gather.2.cloned.1.call-start = ((), (), s32[]{:S(2)}) async-start(), calls=%async_computation.6 | async-start | bytes 4325376 | tf_op jit(solution)/shard_map/all_gather | solution.py:505
  8.9 9.8 %collective-permute-start.3 = (f32[128,512]{1,0:T(8,128)S(1)}, f32[128,512]{1,0:T(8,128)S(1)}, u32[]{:S(2)}, u32[]{:S(2)}) collective-permute-start(f32[128,512]{1,0:T(8,128)S(1)} %slice_bitcast_fusion), channel_id=1, source_target_pairs={{0,4},{4,8},{8,12},{12,16},{16,20},{20,24},{24,28},{28,32},{32,36}... | collective-permute-start | bytes 786440 | tf_op jit(solution)/shard_map/ppermute | solution.py:498
  23.5 20.0 %collective-permute-start.4 = (f32[136,512]{1,0:T(8,128)S(1)}, f32[136,512]{1,0:T(8,128)S(1)}, u32[]{:S(2)}, u32[]{:S(2)}) collective-permute-start(f32[136,512]{1,0:T(8,128)S(1)} %get-tuple-element.107), channel_id=1, source_target_pairs={{0,1},{1,2},{2,3},{3,0},{4,5},{5,6},{6,7},{7,4},{8,9},{9,10},{10,1... | collective-permute-start | bytes 835592 | tf_op jit(solution)/shard_map/ppermute | solution.py:489
  25.5 18.0 %collective-permute-start.6 = (f32[136,512]{1,0:T(8,128)S(1)}, f32[136,512]{1,0:T(8,128)S(1)}, u32[]{:S(2)}, u32[]{:S(2)}) collective-permute-start(f32[136,512]{1,0:T(8,128)S(1)} %get-tuple-element.109), channel_id=1, source_target_pairs={{0,3},{1,0},{2,1},{3,2},{4,7},{5,4},{6,5},{7,6},{8,11},{9,8},{10,9... | collective-permute-start | bytes 835592 | tf_op jit(solution)/shard_map/ppermute | solution.py:489
  27.7 15.6 %collective-permute-start.5 = (f32[128,512]{1,0:T(8,128)S(1)}, f32[128,512]{1,0:T(8,128)S(1)}, u32[]{:S(2)}, u32[]{:S(2)}) collective-permute-start(f32[128,512]{1,0:T(8,128)S(1)} %get-tuple-element.108), channel_id=1, source_target_pairs={{0,2},{1,3},{2,0},{3,1},{4,6},{5,7},{6,4},{7,5},{8,10},{9,11},{10,... | collective-permute-start | bytes 786440 | tf_op jit(solution)/shard_map/ppermute | solution.py:489
  30.5 18.6 %collective-permute-start.2 = (bf16[128,512]{1,0:T(8,128)(2,1)S(1)}, bf16[128,512]{1,0:T(8,128)(2,1)S(1)}, u32[]{:S(2)}, u32[]{:S(2)}) collective-permute-start(bf16[128,512]{1,0:T(8,128)(2,1)S(1)} %fusion.d0), channel_id=1, source_target_pairs={{0,3},{1,0},{2,1},{3,2},{4,7},{5,4},{6,5},{7,6},{8,11},{9,8},{10,9... | collective-permute-start | bytes 393224 | tf_op jit(solution)/shard_map/ppermute | solution.py:489
  31.3 17.8 %collective-permute-start.1 = (bf16[128,512]{1,0:T(8,128)(2,1)S(1)}, bf16[128,512]{1,0:T(8,128)(2,1)S(1)}, u32[]{:S(2)}, u32[]{:S(2)}) collective-permute-start(bf16[128,512]{1,0:T(8,128)(2,1)S(1)} %fusion.d0), channel_id=1, source_target_pairs={{0,2},{1,3},{2,0},{3,1},{4,6},{5,7},{6,4},{7,5},{8,10},{9,11},{10,... | collective-permute-start | bytes 393224 | tf_op jit(solution)/shard_map/ppermute | solution.py:489
  37.8 15.2 %all-to-all-start = ((f32[32,16,128]{2,1,0:T(8,128)}), f32[32,16,128]{2,1,0:T(8,128)S(1)}, u32[]{:S(2)}, u32[]{:S(2)}) async-start(f32[32,16,128]{2,1,0:T(8,128)} %get-tuple-element.105), calls=%async_computation | async-start | bytes 524288 | tf_op jit(solution)/shard_map/all_to_all | solution.py:503
  43.3 6.8 %collective-permute-start = (bf16[128,512]{1,0:T(8,128)(2,1)S(1)}, bf16[128,512]{1,0:T(8,128)(2,1)S(1)}, u32[]{:S(2)}, u32[]{:S(2)}) collective-permute-start(bf16[128,512]{1,0:T(8,128)(2,1)S(1)} %fusion.d0), channel_id=1, source_target_pairs={{0,1},{1,2},{2,3},{3,0},{4,5},{5,6},{6,7},{7,4},{8,9},{9,10},{10,1... | collective-permute-start | bytes 393224 | tf_op jit(solution)/shard_map/ppermute | solution.py:489
  53.0 16.3 %collective-permute-start.7 = (f32[128,512]{1,0:T(8,128)S(1)}, f32[128,512]{1,0:T(8,128)S(1)}, u32[]{:S(2)}, u32[]{:S(2)}) collective-permute-start(f32[128,512]{1,0:T(8,128)S(1)} %get-tuple-element.116), channel_id=1, source_target_pairs={{0,1},{1,2},{2,3},{3,0},{4,5},{5,6},{6,7},{7,4},{8,9},{9,10},{10,1... | collective-permute-start | bytes 786440 | tf_op jit(solution)/shard_map/ppermute | solution.py:489
  53.0 20.6 %collective-permute-start.8 = (f32[128,512]{1,0:T(8,128)S(1)}, f32[128,512]{1,0:T(8,128)S(1)}, u32[]{:S(2)}, u32[]{:S(2)}) collective-permute-start(f32[128,512]{1,0:T(8,128)S(1)} %get-tuple-element.117), channel_id=1, source_target_pairs={{0,2},{1,3},{2,0},{3,1},{4,6},{5,7},{6,4},{7,5},{8,10},{9,11},{10,... | collective-permute-start | bytes 786440 | tf_op jit(solution)/shard_map/ppermute | solution.py:489
  55.7 17.8 %collective-permute-start.9 = (f32[128,512]{1,0:T(8,128)S(1)}, f32[128,512]{1,0:T(8,128)S(1)}, u32[]{:S(2)}, u32[]{:S(2)}) collective-permute-start(f32[128,512]{1,0:T(8,128)S(1)} %get-tuple-element.118), channel_id=1, source_target_pairs={{0,3},{1,0},{2,1},{3,2},{4,7},{5,4},{6,5},{7,6},{8,11},{9,8},{10,9... | collective-permute-start | bytes 786440 | tf_op jit(solution)/shard_map/ppermute | solution.py:489
  65.4 8.2 %collective-permute-start.10 = (f32[128,128]{1,0:T(8,128)S(1)}, f32[128,128]{1,0:T(8,128)S(1)}, u32[]{:S(2)}, u32[]{:S(2)}) collective-permute-start(f32[128,128]{1,0:T(8,128)S(1)} %get-tuple-element.127), channel_id=1, source_target_pairs={{0,3},{1,0},{2,1},{3,2},{4,7},{5,4},{6,5},{7,6},{8,11},{9,8},{10,9... | collective-permute-start | bytes 196616 | tf_op jit(solution)/shard_map/ppermute | solution.py:489
  68.8 6.2 %collective-permute-start.11 = (f32[128,128]{1,0:T(8,128)S(1)}, f32[128,128]{1,0:T(8,128)S(1)}, u32[]{:S(2)}, u32[]{:S(2)}) collective-permute-start(f32[128,128]{1,0:T(8,128)S(1)} %get-tuple-element.128), channel_id=1, source_target_pairs={{0,2},{1,3},{2,0},{3,1},{4,6},{5,7},{6,4},{7,5},{8,10},{9,11},{10,... | collective-permute-start | bytes 196616 | tf_op jit(solution)/shard_map/ppermute | solution.py:489
  69.3 6.3 %collective-permute-start.12 = (f32[128,128]{1,0:T(8,128)S(1)}, f32[128,128]{1,0:T(8,128)S(1)}, u32[]{:S(2)}, u32[]{:S(2)}) collective-permute-start(f32[128,128]{1,0:T(8,128)S(1)} %get-tuple-element.129), channel_id=1, source_target_pairs={{0,1},{1,2},{2,3},{3,0},{4,5},{5,6},{6,7},{7,4},{8,9},{9,10},{10,1... | collective-permute-start | bytes 196616 | tf_op jit(solution)/shard_map/ppermute | solution.py:489
  73.5 3.7 %copy-start = (f32[128,512]{1,0:T(8,128)}, f32[128,512]{1,0:T(8,128)S(1)}, u32[]{:S(2)}) copy-start(f32[128,512]{1,0:T(8,128)S(1)} %collective-permute-done.8.rest_2_.p2) | copy-start | bytes 786436
  73.5 23.1 %copy-start.2 = (f32[128,512]{1,0:T(8,128)}, f32[128,512]{1,0:T(8,128)S(1)}, u32[]{:S(2)}) copy-start(f32[128,512]{1,0:T(8,128)S(1)} %collective-permute-done.9.rest_3_.p3) | copy-start | bytes 786436
  77.2 13.6 %all-to-all-start.1 = ((f32[32,16,128]{2,1,0:T(8,128)}), f32[32,16,128]{2,1,0:T(8,128)S(1)}, u32[]{:S(2)}, u32[]{:S(2)}) async-start(f32[32,16,128]{2,1,0:T(8,128)} %get-tuple-element.136), calls=%async_computation.1 | async-start | bytes 524288 | tf_op jit(solution)/shard_map/all_to_all | solution.py:503
  83.1 20.5 %collective-permute-start.13 = (f32[128,512]{1,0:T(8,128)}, f32[128,512]{1,0:T(8,128)}, u32[]{:S(2)}, u32[]{:S(2)}) collective-permute-start(f32[128,512]{1,0:T(8,128)} %get-tuple-element.144), channel_id=1, source_target_pairs={{4,0},{8,4},{12,8},{16,12},{20,16},{24,20},{28,24},{32,28},{36,32}... | collective-permute-start | bytes 786440 | tf_op jit(solution)/shard_map/ppermute | solution.py:498
  91.6 12.8 %all-to-all-start.2 = ((f32[32,16,128]{2,1,0:T(8,128)}), f32[32,16,128]{2,1,0:T(8,128)S(1)}, u32[]{:S(2)}, u32[]{:S(2)}) async-start(f32[32,16,128]{2,1,0:T(8,128)} %shard_map.110), calls=%async_computation.2 | async-start | bytes 524288 | tf_op jit(solution)/shard_map/all_to_all | solution.py:503
  96.7 1.0 copy-start.1
  97.6 0.9 copy-start.3
  102.9 0.7 copy-start.4
  104.5 1.0 copy-start.5
  106.7 6.6 %collective-permute-start.19 = (bf16[128,512]{1,0:T(8,128)(2,1)S(1)}, bf16[128,512]{1,0:T(8,128)(2,1)S(1)}, u32[]{:S(2)}, u32[]{:S(2)}) collective-permute-start(bf16[128,512]{1,0:T(8,128)(2,1)S(1)} %get-tuple-element.164.d0), channel_id=1, source_target_pairs={{0,3},{1,0},{2,1},{3,2},{4,7},{5,4},{6,5},{7,6},{8,11},{9,8},{10,9... | collective-permute-start | bytes 393224 | tf_op jit(solution)/shard_map/ppermute | solution.py:489
  107.5 11.6 %collective-permute-start.18 = (bf16[128,512]{1,0:T(8,128)(2,1)S(1)}, bf16[128,512]{1,0:T(8,128)(2,1)S(1)}, u32[]{:S(2)}, u32[]{:S(2)}) collective-permute-start(bf16[128,512]{1,0:T(8,128)(2,1)S(1)} %get-tuple-element.164.d0), channel_id=1, source_target_pairs={{0,2},{1,3},{2,0},{3,1},{4,6},{5,7},{6,4},{7,5},{8,10},{9,11},{10,... | collective-permute-start | bytes 393224 | tf_op jit(solution)/shard_map/ppermute | solution.py:489
  109.3 9.9 %collective-permute-start.17 = (bf16[128,512]{1,0:T(8,128)(2,1)S(1)}, bf16[128,512]{1,0:T(8,128)(2,1)S(1)}, u32[]{:S(2)}, u32[]{:S(2)}) collective-permute-start(bf16[128,512]{1,0:T(8,128)(2,1)S(1)} %get-tuple-element.164.d0), channel_id=1, source_target_pairs={{0,1},{1,2},{2,3},{3,0},{4,5},{5,6},{6,7},{7,4},{8,9},{9,10},{10,1... | collective-permute-start | bytes 393224 | tf_op jit(solution)/shard_map/ppermute | solution.py:489
  109.3 19.5 %collective-permute-start.14 = (f32[136,512]{1,0:T(8,128)S(1)}, f32[136,512]{1,0:T(8,128)S(1)}, u32[]{:S(2)}, u32[]{:S(2)}) collective-permute-start(f32[136,512]{1,0:T(8,128)S(1)} %get-tuple-element.156), channel_id=1, source_target_pairs={{0,1},{1,2},{2,3},{3,0},{4,5},{5,6},{6,7},{7,4},{8,9},{9,10},{10,1... | collective-permute-start | bytes 835592 | tf_op jit(solution)/shard_map/ppermute | solution.py:489
  111.0 17.8 %collective-permute-start.16 = (f32[136,512]{1,0:T(8,128)S(1)}, f32[136,512]{1,0:T(8,128)S(1)}, u32[]{:S(2)}, u32[]{:S(2)}) collective-permute-start(f32[136,512]{1,0:T(8,128)S(1)} %get-tuple-element.158), channel_id=1, source_target_pairs={{0,3},{1,0},{2,1},{3,2},{4,7},{5,4},{6,5},{7,6},{8,11},{9,8},{10,9... | collective-permute-start | bytes 835592 | tf_op jit(solution)/shard_map/ppermute | solution.py:489
  113.2 15.6 %collective-permute-start.15 = (f32[128,512]{1,0:T(8,128)S(1)}, f32[128,512]{1,0:T(8,128)S(1)}, u32[]{:S(2)}, u32[]{:S(2)}) collective-permute-start(f32[128,512]{1,0:T(8,128)S(1)} %get-tuple-element.157), channel_id=1, source_target_pairs={{0,2},{1,3},{2,0},{3,1},{4,6},{5,7},{6,4},{7,5},{8,10},{9,11},{10,... | collective-permute-start | bytes 786440 | tf_op jit(solution)/shard_map/ppermute | solution.py:489
  134.0 17.2 %collective-permute-start.20 = (f32[160,512]{1,0:T(8,128)}, f32[160,512]{1,0:T(8,128)S(1)}, u32[]{:S(2)}, u32[]{:S(2)}) collective-permute-start(f32[160,512]{1,0:T(8,128)} %get-tuple-element.173), channel_id=1, source_target_pairs={{0,1},{1,2},{2,3},{3,0},{4,5},{5,6},{6,7},{7,4},{8,9},{9,10},{10,1... | collective-permute-start | bytes 983048 | tf_op jit(solution)/shard_map/ppermute | solution.py:489
  134.0 17.2 %collective-permute-start.21 = (f32[160,512]{1,0:T(8,128)}, f32[160,512]{1,0:T(8,128)S(1)}, u32[]{:S(2)}, u32[]{:S(2)}) collective-permute-start(f32[160,512]{1,0:T(8,128)} %get-tuple-element.174), channel_id=1, source_target_pairs={{0,2},{1,3},{2,0},{3,1},{4,6},{5,7},{6,4},{7,5},{8,10},{9,11},{10,... | collective-permute-start | bytes 983048 | tf_op jit(solution)/shard_map/ppermute | solution.py:489
  136.4 15.5 %collective-permute-start.22 = (f32[160,512]{1,0:T(8,128)}, f32[160,512]{1,0:T(8,128)S(1)}, u32[]{:S(2)}, u32[]{:S(2)}) collective-permute-start(f32[160,512]{1,0:T(8,128)} %get-tuple-element.175), channel_id=1, source_target_pairs={{0,3},{1,0},{2,1},{3,2},{4,7},{5,4},{6,5},{7,6},{8,11},{9,8},{10,9... | collective-permute-start | bytes 983048 | tf_op jit(solution)/shard_map/ppermute | solution.py:489
  138.5 15.0 %all-to-all-start.3 = ((f32[32,16,128]{2,1,0:T(8,128)}), f32[32,16,128]{2,1,0:T(8,128)S(1)}, u32[]{:S(2)}, u32[]{:S(2)}) async-start(f32[32,16,128]{2,1,0:T(8,128)} %get-tuple-element.159), calls=%async_computation.3 | async-start | bytes 524288 | tf_op jit(solution)/shard_map/all_to_all | solution.py:503
  153.5 14.1 %all-to-all-start.4 = ((f32[32,16,128]{2,1,0:T(8,128)}), f32[32,16,128]{2,1,0:T(8,128)S(1)}, u32[]{:S(2)}, u32[]{:S(2)}) async-start(f32[32,16,128]{2,1,0:T(8,128)} %get-tuple-element.182), calls=%async_computation.4 | async-start | bytes 524288 | tf_op jit(solution)/shard_map/all_to_all | solution.py:503
  159.8 19.2 %collective-permute-start.23 = (f32[128,512]{1,0:T(8,128)}, f32[128,512]{1,0:T(8,128)}, u32[]{:S(2)}, u32[]{:S(2)}) collective-permute-start(f32[128,512]{1,0:T(8,128)} %get-tuple-element.190), channel_id=1, source_target_pairs={{4,0},{8,4},{12,8},{16,12},{20,16},{24,20},{28,24},{32,28},{36,32}... | collective-permute-start | bytes 786440 | tf_op jit(solution)/shard_map/ppermute | solution.py:498
  168.4 13.5 %all-to-all-start.5 = ((f32[32,16,128]{2,1,0:T(8,128)}), f32[32,16,128]{2,1,0:T(8,128)}, u32[]{:S(2)}, u32[]{:S(2)}) async-start(f32[32,16,128]{2,1,0:T(8,128)} %shard_map.118), calls=%async_computation.5 | async-start | bytes 524288 | tf_op jit(solution)/shard_map/all_to_all | solution.py:503
  178.4 0.7 copy-start.6
  181.9 1.0 copy-start.7
Sparse Core Ops, SparseCore 0:
  10.3 50.3 all-gather.1

commit v7 on v6

--- a/solution.py
+++ b/solution.py
@@ -100,11 +100,14 @@
     send_edges(current, outs, i == 0, i == pl.num_programs(0) - 1)
 
 
-def decay_kernel(place, current, damping, decay, scale):
+def decay_kernel(place, current, damping, decay, scale, *copy):
     for g, rows in groups(current.shape[1]):
         product = None
         for s in range(current.shape[0]):
-            d = decay_of(current[s, rows], damping[s, rows])
+            here = current[s, rows]
+            for ref in copy:
+                ref[s, rows] = here
+            d = decay_of(here, damping[s, rows])
             decay[s, rows] = d
             product = d if product is None else product * d
         to_chunks(scale, g, product)
@@ -216,67 +219,63 @@
                 ]
 
 
-def disc_kernel(d0, d1, d2, d3, places, place_row, owners, *rest):
-    streams, tabled = 4, (len(rest) - 11) // 2
-    blades, tables_far = rest[:streams], rest[streams : streams + tabled]
-    f0, f1, f2, f3 = rest[streams + tabled : streams + tabled + 4]
-    tables_near = rest[streams + tabled + 4 : streams + 2 * tabled + 4]
-    picked, total = rest[streams + 2 * tabled + 4 : streams + 2 * tabled + 6]
-    step = pl.program_id(0)
-    last = pl.num_programs(0) - 1
+def disc_kernel(d0, d1, d2, d3, *rest):
+    tabled = (len(rest) - 14) // 2
+    where_far, blades_far, tables_far = rest[:3], rest[3], rest[4 : 4 + tabled]
+    f0, f1, f2, f3 = rest[4 + tabled : 8 + tabled]
+    tables_near = rest[8 + tabled : 8 + 2 * tabled]
+    *where, blades, total, sems = rest[8 + 2 * tabled :]
+    places, place_row, owners = where
     height, width = d0.shape
-    number = picked.shape[0]
+    number = places.shape[0]
+    pairs = blades.shape[0] // 2
+    sources = list(where_far) + list(tables_far)
+    targets = where + list(tables_near)
     copies = [
-        pltpu.make_async_copy(source, target, rest[-1].at[i])
-        for i, (source, target) in enumerate(zip(tables_far, tables_near))
+        pltpu.make_async_copy(source, target, sems.at[pairs + i])
+        for i, (source, target) in enumerate(zip(sources, targets))
     ]
-
-    @pl.when(step == 0)
-    def _():
-        for copy in copies:
-            copy.start()
-        plane = jnp.concatenate([d[...] for d in (d0, d1, d2, d3)], axis=0)
-        lane = lax.broadcasted_iota(jnp.int32, (number, LANE), 1)
-        chosen = [
-            jnp.where(places[...] == lane + LANE * q, 1.0, 0.0).astype(BF16)
-            for q in range(width // LANE)
-        ]
-        rows = jnp.dot(
-            jnp.concatenate(chosen, axis=1), plane, preferred_element_type=F32
-        )
-        picked[...] = rows.astype(BF16)
-        total[...] = jnp.zeros_like(total)
-
-    per_step = blades[0].shape[0]
-    for i in range(0, per_step, 2):
-        pair = jnp.concatenate(
-            [
-                jnp.concatenate([blade[j] for blade in blades], axis=0)
-                for j in (i, i + 1)
-            ],
-            axis=1,
-        )
-        response = jnp.dot(picked[...], pair, preferred_element_type=F32)
-        first = step * per_step + i
-        kept = jnp.where(owners[...] == first, response[:, :LANE], total[...])
-        total[...] = jnp.where(owners[...] == first + 1, response[:, LANE:], kept)
-
-    @pl.when(step == last)
-    def _():
-        rest_of, parts = jnp.tanh(total[...]), []
-        for _ in range(3):
-            parts.append(rest_of.astype(BF16))
-            rest_of = rest_of - parts[-1].astype(F32)
-        forces = jnp.concatenate(parts, axis=0)
-        at = place_row[0:1]
-        for r, ref in enumerate((f0, f1, f2, f3)):
-            row = lax.broadcasted_iota(jnp.int32, (height, number), 0) + height * r
-            back = jnp.where(row == at, 1.0, 0.0).astype(BF16)
-            ref[...] = jnp.dot(
-                jnp.concatenate([back] * 3, axis=1), forces, preferred_element_type=F32
-            )
-        for copy in copies:
-            copy.wait()
+    fetches = [
+        pltpu.make_async_copy(
+            blades_far.at[pl.ds(2 * i, 2)], blades.at[pl.ds(2 * i, 2)], sems.at[i]
+        )
+        for i in range(pairs)
+    ]
+    for copy in copies[:3] + fetches + copies[3:]:
+        copy.start()
+    plane = jnp.concatenate([d[...] for d in (d0, d1, d2, d3)], axis=0)
+    for copy in copies[:3]:
+        copy.wait()
+    lane = lax.broadcasted_iota(jnp.int32, (number, LANE), 1)
+    chosen = [
+        jnp.where(places[...] == lane + LANE * q, 1.0, 0.0).astype(BF16)
+        for q in range(width // LANE)
+    ]
+    picked = jnp.dot(
+        jnp.concatenate(chosen, axis=1), plane, preferred_element_type=F32
+    ).astype(BF16)
+    total[...] = jnp.zeros_like(total)
+    for i in range(pairs):
+        fetches[i].wait()
+        pair = jnp.concatenate([blades[2 * i], blades[2 * i + 1]], axis=1)
+        response = jnp.dot(picked, pair, preferred_element_type=F32)
+        kept = jnp.where(owners[...] == 2 * i, response[:, :LANE], total[...])
+        total[...] = jnp.where(owners[...] == 2 * i + 1, response[:, LANE:], kept)
+
+    rest_of, parts = jnp.tanh(total[...]), []
+    for _ in range(3):
+        parts.append(rest_of.astype(BF16))
+        rest_of = rest_of - parts[-1].astype(F32)
+    forces = jnp.concatenate(parts, axis=0)
+    at = place_row[0:1]
+    for r, ref in enumerate((f0, f1, f2, f3)):
+        row = lax.broadcasted_iota(jnp.int32, (height, number), 0) + height * r
+        back = jnp.where(row == at, 1.0, 0.0).astype(BF16)
+        ref[...] = jnp.dot(
+            jnp.concatenate([back] * 3, axis=1), forces, preferred_element_type=F32
+        )
+    for copy in copies[3:]:
+        copy.wait()
 
 
 def offset_kernel(place, *rest):
@@ -433,31 +432,27 @@
 
 
 def disc_forces(rows, where, blades, tabled=()):
-    height, width = rows[0].shape
+    height = rows[0].shape[0]
     count = len(rows)
     number = blades.shape[0]
-    per_step, streams = 8, 4
-    fixed = lambda shape: pl.BlockSpec(shape, lambda i: (0,) * len(shape))
-    table = lambda k: pl.BlockSpec((per_step, width // streams, LANE), lambda i: (i, k, 0))
-    discs = where[0].shape[0]
+    brought = [*where, blades, *tabled]
     return pl.pallas_call(
         disc_kernel,
-        grid=(number // per_step,),
         out_shape=[near((height, LANE))] * count + [near(t.shape, t.dtype) for t in tabled],
-        in_specs=[fixed((height, width))] * count
-        + [fixed(w.shape) for w in where]
-        + [table(k) for k in range(streams)]
-        + [pl.BlockSpec(memory_space=pltpu.HBM)] * len(tabled),
-        out_specs=[fixed((height, LANE))] * count
-        + [pl.BlockSpec(memory_space=pltpu.VMEM)] * len(tabled),
-        scratch_shapes=[
-            pltpu.VMEM((discs, width), BF16),
-            pltpu.VMEM((discs, LANE), F32),
-            pltpu.SemaphoreType.DMA((3,)),
+        in_specs=[VMEM] * count + [pl.BlockSpec(memory_space=pltpu.HBM)] * len(brought),
+        out_specs=[VMEM] * (count + len(tabled)),
+        scratch_shapes=[pltpu.VMEM(a.shape, a.dtype) for a in (*where, blades)]
+        + [
+            pltpu.VMEM((where[0].shape[0], LANE), F32),
+            pltpu.SemaphoreType.DMA((number // 2 + 3 + len(tabled),)),
         ],
         compiler_params=pltpu.CompilerParams(vmem_limit_bytes=16 * MIB),
-        cost_estimate=cost(2 * number * width * width * LANE, 5 * MIB),
-    )(*rows, *map(stay, where), *[stay(blades)] * streams, *tabled)
+        cost_estimate=cost(2 * number * blade_work(blades), 5 * MIB),
+    )(*rows, *map(stay, brought))
+
+
+def blade_work(blades):
+    return blades.shape[1] ** 2 * blades.shape[2]
 
 
 def local(velocity_guess, damping, inflow, disc_rows, owner, blade):
@@ -515,7 +510,6 @@
     step = (stations, height // STEPS, width)
     near_inflow = stay(inflow)
     upstream = along_march(velocity_guess[-1], 1)
-    upstream, *where = lax.optimization_barrier((upstream, *where))
     current = stay(velocity_guess)
     disc = velocity_guess[0].astype(BF16)
     rows = turns([disc] * cross_size)
@@ -536,10 +530,10 @@
             rows = turns([disc] * cross_size)
         guess, damp, *source = lax.optimization_barrier((current, damping, *source))
         arrived = turns(source)
-        decay, scale = by_rows(
+        decay, scale, *kept = by_rows(
             decay_kernel,
             height,
-            [far(slab), far(chunks)],
+            [far(slab), far(chunks)] + [far(slab)] * merged,
             place,
             (guess if merged else stay(guess), stay(damp)),
             cost(4e6, 3 * MIB),
@@ -573,10 +567,12 @@
                 compiler_params=pltpu.CompilerParams(vmem_limit_bytes=20 * MIB),
                 cost_estimate=solve_cost,
             )(place, *arrived, *tabled)
-            rows, scales, solved = lax.optimization_barrier((rows, scales, solved))
+            rows, scales, solved, where = lax.optimization_barrier((rows, scales, solved, where))
             forces = turns(disc_forces(rows, where, blades), -1)
         pieces = turns(solved)
         decay = stay(decay)
+        if merged:
+            current = stay(kept[0])
         term, weights, base, force_weight = call(
             weights_kernel,
             [far(slab), near(slab), near(plane), near(plane)],
@@ -603,9 +599,10 @@
             (*pieces, stay(term), stay(force), decay, near_inflow),
             cost(4e6, 4 * MIB),
         )
-        (entering,) = call(
-            scan_kernel, [far(chunks)], (scales, across_march(offset)), cost(1e5, MIB)
-        )
+        offset = across_march(offset)
+        if not merged:
+            offset, change = lax.optimization_barrier((offset, change))
+        (entering,) = call(scan_kernel, [far(chunks)], (scales, offset), cost(1e5, MIB))
         entering = across_march(entering)
         common = (entering, change, following, decay, entry)
         if final:

time: 195 us -> 195 us (level)
  Pallas kernels: 55 us -> 57.8 us
    ppermute x3, waiting for transfers between devices: 7.07 us -> 2.72 us  [along_march(): lax.ppermute(value, 'march', [(i, i + steps) for i in range(count) if 0 <...]
    pallas_call x2, Pallas kernels: 9.51 us -> 12.8 us  [disc_forces(): pl.pallas_call(disc_kernel, out_shape=[near((height, LANE))] * count + [n...]
    all_gather x1, waiting for transfers between devices: 4.06 us -> 6.23 us  [local(): blades = lax.all_gather(blade, 'march', axis=0, tiled=True)]
    all_to_all x6, starting transfers between devices: 35 us -> 32.8 us  [across_march(): lax.all_to_all(value, 'march', split_axis=0, concat_axis=0, tiled=True)]
    unnamed x16 -> x12, local copies, waits for them, and re-layouts: 5.2 us -> 4.25 us
  transfers between devices with their start and end apart: 31 -> 31, of which waited for: 14 -> 13; matrix products, arithmetic and copies ran while one was open for 3% -> 3% of each run, Pallas kernels for 23% -> 25%
where the time goes in v7:
time: 195 us; the launch traced here: 191 us
  starting transfers between devices  74.4 us (38%)
  Pallas kernels  57.8 us (30%)
  waiting for transfers between devices  35.7 us (18%)
  between operations  14.3 us (7%)
  local copies, waits for them, and re-layouts  8.3 us (4%)
    all_to_all x6, starting transfers between devices, across_march(): lax.all_to_all(value, 'march', split_axis=0, concat_axis=0, tiled=True)  32.8 us
    ppermute x21, starting transfers between devices, turn(): lax.ppermute(value, 'cross', [(i, (i + steps) % cross_size) for i in rang...  31 us
    pallas_call x5, Pallas kernels, by_rows(): pl.pallas_call(kernel, grid_spec=pltpu.PrefetchScalarGridSpec(num_scalar_...  19.8 us
    pallas_call x9, Pallas kernels, call(): pl.pallas_call(kernel, out_shape=outs, in_specs=[SMEM] * scalars + [VMEM]...  19.7 us
    all_to_all x6, waiting for transfers between devices, across_march(): lax.all_to_all(value, 'march', split_axis=0, concat_axis=0, tiled=True)  14.9 us
    pallas_call x2, Pallas kernels, disc_forces(): pl.pallas_call(disc_kernel, out_shape=[near((height, LANE))] * count + [n...  12.8 us
    ppermute x21, waiting for transfers between devices, turn(): lax.ppermute(value, 'cross', [(i, (i + steps) % cross_size) for i in rang...  11.2 us
    ppermute x3, starting transfers between devices, along_march(): lax.ppermute(value, 'march', [(i, i + steps) for i in range(count) if 0 <...  10.6 us
  transfers between devices with their start and end apart: 31, of which 13 were waited for; matrix products, arithmetic and copies ran while one was open for 3% of the time, Pallas kernels for 25%

profile of v7, /device:TPU:2, one launch (start us, length us, event | category | flops | bytes accessed | tf_op | source)
XLA Modules:
  0.0 191.3 jit_solution(10355111751968475695)
XLA Ops:
  7.9 1.0 slice_bitcast_fusion
  8.9 1.9 %collective-permute-start.3 = (f32[128,512]{1,0:T(8,128)S(1)}, f32[128,512]{1,0:T(8,128)S(1)}, u32[]{:S(2)}, u32[]{:S(2)}) collective-permute-start(f32[128,512]{1,0:T(8,128)S(1)} %slice_bitcast_fusion), channel_id=1, source_target_pairs={{0,4},{4,8},{8,12},{12,16},{16,20},{20,24},{24,28},{28,32},{32,36}... | collective-permute-start | bytes 786440 | tf_op jit(solution)/shard_map/ppermute | solution.py:493
  10.8 1.0 fusion.d0
  11.8 4.1 %collective-permute-start.2 = (bf16[128,512]{1,0:T(8,128)(2,1)S(1)}, bf16[128,512]{1,0:T(8,128)(2,1)S(1)}, u32[]{:S(2)}, u32[]{:S(2)}) collective-permute-start(bf16[128,512]{1,0:T(8,128)(2,1)S(1)} %fusion.d0), channel_id=1, source_target_pairs={{0,3},{1,0},{2,1},{3,2},{4,7},{5,4},{6,5},{7,6},{8,11},{9,8},{10,9... | collective-permute-start | bytes 393224 | tf_op jit(solution)/shard_map/ppermute | solution.py:484
  16.0 2.7 %collective-permute-done.3.upstream = f32[128,512]{1,0:T(8,128)S(1)} collective-permute-done((f32[128,512]{1,0:T(8,128)S(1)}, f32[128,512]{1,0:T(8,128)S(1)}, u32[]{:S(2)}, u32[]{:S(2)}) %collective-permute-start.3) | collective-permute-done | bytes 262176 | tf_op jit(solution)/shard_map/ppermute | solution.py:493
  18.7 2.7 %shard_map.104 = (f32[128,512]{1,0:T(8,128)S(1)}, f32[136,512]{1,0:T(8,128)S(1)}, f32[128,512]{1,0:T(8,128)S(1)}, f32[136,512]{1,0:T(8,128)S(1)}) custom-call(s32[4]{0:T(128)S(1)} %pad_add_fusion.place, f32[4,128,512]{2,1,0:T(8,128)} %current.4, f32[128,512]{1,0:T(8,128)S(1)} %collective-permute-done.3.upstream, f32[128,512]{1,0:T(8,128)} %inflow.9), custom_call_target="tpu_custom_call" | custom-call | flops 1000000 | bytes 2097152 | tf_op jit(solution)/shard_map/pallas_call | solution.py:419
  21.4 4.0 %collective-permute-start.5 = (f32[128,512]{1,0:T(8,128)S(1)}, f32[128,512]{1,0:T(8,128)S(1)}, u32[]{:S(2)}, u32[]{:S(2)}) collective-permute-start(f32[128,512]{1,0:T(8,128)S(1)} %get-tuple-element.109), channel_id=1, source_target_pairs={{0,2},{1,3},{2,0},{3,1},{4,6},{5,7},{6,4},{7,5},{8,10},{9,11},{10,... | collective-permute-start | bytes 786440 | tf_op jit(solution)/shard_map/ppermute | solution.py:484
  25.4 1.0 collective-permute-start.4
  26.4 2.2 %collective-permute-start.6 = (f32[136,512]{1,0:T(8,128)S(1)}, f32[136,512]{1,0:T(8,128)S(1)}, u32[]{:S(2)}, u32[]{:S(2)}) collective-permute-start(f32[136,512]{1,0:T(8,128)S(1)} %get-tuple-element.110), channel_id=1, source_target_pairs={{0,3},{1,0},{2,1},{3,2},{4,7},{5,4},{6,5},{7,6},{8,11},{9,8},{10,9... | collective-permute-start | bytes 835592 | tf_op jit(solution)/shard_map/ppermute | solution.py:484
  29.3 4.2 %shard_map.105 = (f32[4,128,512]{2,1,0:T(8,128)}, f32[32,16,128]{2,1,0:T(8,128)}) custom-call(s32[4]{0:T(128)S(1)} %pad_add_fusion.place, f32[4,128,512]{2,1,0:T(8,128)} %current.4, f32[4,128,512]{2,1,0:T(8,128)} %damping.1), custom_call_target="tpu_custom_call" | custom-call | flops 4000000 | bytes 3145728 | tf_op jit(solution)/shard_map/pallas_call | solution.py:419
  33.5 5.7 %all-to-all-start = ((f32[32,16,128]{2,1,0:T(8,128)}), f32[32,16,128]{2,1,0:T(8,128)S(1)}, u32[]{:S(2)}, u32[]{:S(2)}) async-start(f32[32,16,128]{2,1,0:T(8,128)} %get-tuple-element.106), calls=%async_computation | async-start | bytes 524288 | tf_op jit(solution)/shard_map/all_to_all | solution.py:498
  39.3 5.6 %shard_map.106 = (f32[128,512]{1,0:T(8,128)S(1)}, f32[128,512]{1,0:T(8,128)S(1)}, f32[128,512]{1,0:T(8,128)S(1)}, f32[128,512]{1,0:T(8,128)S(1)}) custom-call(s32[4]{0:T(128)S(1)} %pad_add_fusion.place, f32[128,512]{1,0:T(8,128)S(1)} %get-tuple-element.107.x0, f32[136,512]{1,0:T(8,128)S(1)} %collective-permute-done.4.x1.before, ...), custom_call_target="tpu_custom_call" | custom-call | flops 3221225472 | bytes 5242880 | tf_op jit(solution)/shard_map/pallas_call | solution.py:559
  44.9 1.1 collective-permute-done.d1
  49.1 2.6 %collective-permute-start.8 = (f32[128,512]{1,0:T(8,128)S(1)}, f32[128,512]{1,0:T(8,128)S(1)}, u32[]{:S(2)}, u32[]{:S(2)}) collective-permute-start(f32[128,512]{1,0:T(8,128)S(1)} %get-tuple-element.118), channel_id=1, source_target_pairs={{0,2},{1,3},{2,0},{3,1},{4,6},{5,7},{6,4},{7,5},{8,10},{9,11},{10,... | collective-permute-start | bytes 786440 | tf_op jit(solution)/shard_map/ppermute | solution.py:484
  52.3 6.2 %all-gather.2.cloned.1.call-done.rest_3_ = bf16[32,512,128]{2,1,0:T(8,128)(2,1)} async-done(((bf16[1,512,128]{2,1,0:T(8,128)(2,1)}), bf16[32,512,128]{2,1,0:T(8,128)(2,1)}) %all-gather.2.cloned.1.call-update) | async-done | bytes 4194320 | tf_op jit(solution)/shard_map/all_gather | solution.py:500
  58.6 6.4 %shard_map.107 = (f32[128,128]{1,0:T(8,128)S(1)}, f32[128,128]{1,0:T(8,128)S(1)}, f32[128,128]{1,0:T(8,128)S(1)}, f32[128,128]{1,0:T(8,128)S(1)}) custom-call(bf16[128,512]{1,0:T(8,128)(2,1)S(1)} %fusion.d0, bf16[128,512]{1,0:T(8,128)(2,1)S(1)} %collective-permute-done.d1, bf16[128,512]{1,0:T(8,128)(2,1)S(1)} %collective-permute-done.1.d2, ...), custom_call_target="tpu_custom_call" | custom-call | flops 2147483648 | bytes 5242880 | tf_op jit(solution)/shard_map/pallas_call | solution.py:439
  64.9 2.7 %collective-permute-start.10 = (f32[128,128]{1,0:T(8,128)S(1)}, f32[128,128]{1,0:T(8,128)S(1)}, u32[]{:S(2)}, u32[]{:S(2)}) collective-permute-start(f32[128,128]{1,0:T(8,128)S(1)} %get-tuple-element.128), channel_id=1, source_target_pairs={{0,3},{1,0},{2,1},{3,2},{4,7},{5,4},{6,5},{7,6},{8,11},{9,8},{10,9... | collective-permute-start | bytes 196616 | tf_op jit(solution)/shard_map/ppermute | solution.py:484
  68.3 1.0 collective-permute-start.12
  69.3 3.6 %shard_map.108 = (f32[4,128,512]{2,1,0:T(8,128)}, f32[4,128,512]{2,1,0:T(8,128)S(1)}, f32[128,512]{1,0:T(8,128)S(1)}, f32[128,512]{1,0:T(8,128)S(1)}) custom-call(s32[4]{0:T(128)S(1)} %pad_add_fusion.place, f32[4,128,512]{2,1,0:T(8,128)} %current.4, f32[136,512]{1,0:T(8,128)S(1)} %collective-permute-done.4.x1.before, ...), custom_call_target="tpu_custom_call" | custom-call | flops 8000000 | bytes 4194304 | tf_op jit(solution)/shard_map/pallas_call | solution.py:395
  72.9 1.0 collective-permute-done.11.rest_6_
  74.5 1.6 shard_map.109
  76.2 6.1 %all-to-all-start.1 = ((f32[32,16,128]{2,1,0:T(8,128)}), f32[32,16,128]{2,1,0:T(8,128)S(1)}, u32[]{:S(2)}, u32[]{:S(2)}) async-start(f32[32,16,128]{2,1,0:T(8,128)} %get-tuple-element.137), calls=%async_computation.1 | async-start | bytes 524288 | tf_op jit(solution)/shard_map/all_to_all | solution.py:498
  82.3 4.3 %collective-permute-start.13 = (f32[128,512]{1,0:T(8,128)}, f32[128,512]{1,0:T(8,128)}, u32[]{:S(2)}, u32[]{:S(2)}) collective-permute-start(f32[128,512]{1,0:T(8,128)} %get-tuple-element.147), channel_id=1, source_target_pairs={{4,0},{8,4},{12,8},{16,12},{20,16},{24,20},{28,24},{32,28},{36,32}... | collective-permute-start | bytes 786440 | tf_op jit(solution)/shard_map/ppermute | solution.py:493
  87.6 4.3 %shard_map.110 = (f32[4,128,512]{2,1,0:T(8,128)S(1)}, f32[4,128,512]{2,1,0:T(8,128)}, f32[4,128,512]{2,1,0:T(8,128)S(1)}, f32[128,512]{1,0:T(8,128)S(1)}) custom-call(s32[4]{0:T(128)S(1)} %pad_add_fusion.place, f32[128,512]{1,0:T(8,128)S(1)} %get-tuple-element.138.rest_0_.p0, f32[128,512]{1,0:T(8,128)S(1)} %collective-permute-done.7.rest_1_.p1, ...), custom_call_target="tpu_custom_call" | custom-call | flops 4000000 | bytes 4194304 | tf_op jit(solution)/shard_map/pallas_call | solution.py:419
  93.4 5.3 %all-to-all-start.2 = ((f32[32,16,128]{2,1,0:T(8,128)}), f32[32,16,128]{2,1,0:T(8,128)S(1)}, u32[]{:S(2)}, u32[]{:S(2)}) async-start(f32[32,16,128]{2,1,0:T(8,128)} %shard_map.111), calls=%async_computation.2 | async-start | bytes 524288 | tf_op jit(solution)/shard_map/all_to_all | solution.py:498
  98.7 7.7 %all-to-all-done.2.entering = f32[32,16,128]{2,1,0:T(8,128)S(1)} async-done(((f32[32,16,128]{2,1,0:T(8,128)}), f32[32,16,128]{2,1,0:T(8,128)S(1)}, u32[]{:S(2)}, u32[]{:S(2)}) %all-to-all-start.2) | async-done | bytes 262176 | tf_op jit(solution)/shard_map/all_to_all | solution.py:498
  107.3 1.2 shard_map.112
  109.3 1.6 collective-permute-start.18
  111.1 1.7 collective-permute-start.14
  112.8 1.5 collective-permute-start.16
  115.0 1.9 collective-permute-start.15
  116.8 4.2 %shard_map.113 = (f32[4,128,512]{2,1,0:T(8,128)}, f32[32,16,128]{2,1,0:T(8,128)}, f32[4,128,512]{2,1,0:T(8,128)}) custom-call(s32[4]{0:T(128)S(1)} %pad_add_fusion.place, f32[4,128,512]{2,1,0:T(8,128)S(1)} %get-tuple-element.155.current, f32[4,128,512]{2,1,0:T(8,128)} %damping.1), custom_call_target="tpu_custom_call" | custom-call | flops 4000000 | bytes 3145728 | tf_op jit(solution)/shard_map/pallas_call | solution.py:419
  121.1 6.4 %shard_map.114 = (f32[128,128]{1,0:T(8,128)S(1)}, f32[128,128]{1,0:T(8,128)S(1)}, f32[128,128]{1,0:T(8,128)S(1)}, f32[128,128]{1,0:T(8,128)S(1)}, bf16[512,512]{...) custom-call(bf16[128,512]{1,0:T(8,128)(2,1)S(1)} %get-tuple-element.167.d0, ...), custom_call_target="tpu_custom_call" | custom-call | flops 2147483648 | bytes 5242880 | tf_op jit(solution)/shard_map/pallas_call | solution.py:439
  127.5 3.1 %collective-permute-done.15.x2 = f32[128,512]{1,0:T(8,128)S(1)} collective-permute-done((f32[128,512]{1,0:T(8,128)S(1)}, f32[128,512]{1,0:T(8,128)S(1)}, u32[]{:S(2)}, u32[]{:S(2)}) %collective-permute-start.15) | collective-permute-done | bytes 262176 | tf_op jit(solution)/shard_map/ppermute | solution.py:484
  130.6 4.2 %shard_map.115 = (f32[160,512]{1,0:T(8,128)S(1)}, f32[160,512]{1,0:T(8,128)S(1)}, f32[160,512]{1,0:T(8,128)S(1)}, f32[160,512]{1,0:T(8,128)S(1)}) custom-call(s32[4]{0:T(128)S(1)} %pad_add_fusion.place, f32[128,512]{1,0:T(8,128)S(1)} %get-tuple-element.163.x0, f32[136,512]{1,0:T(8,128)S(1)} %collective-permute-done.14.x1.before, ...), custom_call_target="tpu_custom_call" | custom-call | flops 3221225472 | bytes 5242880 | tf_op jit(solution)/shard_map/pallas_call | solution.py:395
  135.0 2.3 %collective-permute-start.21 = (f32[160,512]{1,0:T(8,128)S(1)}, f32[160,512]{1,0:T(8,128)S(1)}, u32[]{:S(2)}, u32[]{:S(2)}) collective-permute-start(f32[160,512]{1,0:T(8,128)S(1)} %get-tuple-element.177), channel_id=1, source_target_pairs={{0,2},{1,3},{2,0},{3,1},{4,6},{5,7},{6,4},{7,5},{8,10},{9,11},{10,... | collective-permute-start | bytes 983048 | tf_op jit(solution)/shard_map/ppermute | solution.py:484
  137.2 2.0 %collective-permute-start.22 = (f32[160,512]{1,0:T(8,128)S(1)}, f32[160,512]{1,0:T(8,128)S(1)}, u32[]{:S(2)}, u32[]{:S(2)}) collective-permute-start(f32[160,512]{1,0:T(8,128)S(1)} %get-tuple-element.178), channel_id=1, source_target_pairs={{0,3},{1,0},{2,1},{3,2},{4,7},{5,4},{6,5},{7,6},{8,11},{9,8},{10,9... | collective-permute-start | bytes 983048 | tf_op jit(solution)/shard_map/ppermute | solution.py:484
  139.3 5.1 %all-to-all-start.3 = ((f32[32,16,128]{2,1,0:T(8,128)}), f32[32,16,128]{2,1,0:T(8,128)S(1)}, u32[]{:S(2)}, u32[]{:S(2)}) async-start(f32[32,16,128]{2,1,0:T(8,128)} %get-tuple-element.162), calls=%async_computation.3 | async-start | bytes 524288 | tf_op jit(solution)/shard_map/all_to_all | solution.py:498
  144.3 3.7 %shard_map.116 = (f32[4,128,512]{2,1,0:T(8,128)}, f32[4,128,512]{2,1,0:T(8,128)S(1)}, f32[128,512]{1,0:T(8,128)S(1)}, f32[128,512]{1,0:T(8,128)S(1)}) custom-call(s32[4]{0:T(128)S(1)} %pad_add_fusion.place, f32[4,128,512]{2,1,0:T(8,128)} %get-tuple-element.179.current, f32[136,512]{1,0:T(8,128)S(1)} %collective-permute-done.14.x1.before, ...), custom_call_target="tpu_custom_call" | custom-call | flops 8000000 | bytes 4194304 | tf_op jit(solution)/shard_map/pallas_call | solution.py:395
  148.0 4.0 %collective-permute-done.20.rest_1_.p1 = f32[160,512]{1,0:T(8,128)S(1)} collective-permute-done((f32[160,512]{1,0:T(8,128)S(1)}, f32[160,512]{1,0:T(8,128)S(1)}, u32[]{:S(2)}, u32[]{:S(2)}) %collective-permute-start.20) | collective-permute-done | bytes 327712 | tf_op jit(solution)/shard_map/ppermute | solution.py:484
  152.6 1.6 shard_map.117
  154.2 5.1 %all-to-all-start.4 = ((f32[32,16,128]{2,1,0:T(8,128)}), f32[32,16,128]{2,1,0:T(8,128)S(1)}, u32[]{:S(2)}, u32[]{:S(2)}) async-start(f32[32,16,128]{2,1,0:T(8,128)} %get-tuple-element.186), calls=%async_computation.4 | async-start | bytes 524288 | tf_op jit(solution)/shard_map/all_to_all | solution.py:498
  159.3 4.3 %collective-permute-start.23 = (f32[128,512]{1,0:T(8,128)}, f32[128,512]{1,0:T(8,128)}, u32[]{:S(2)}, u32[]{:S(2)}) collective-permute-start(f32[128,512]{1,0:T(8,128)} %get-tuple-element.194), channel_id=1, source_target_pairs={{4,0},{8,4},{12,8},{16,12},{20,16},{24,20},{28,24},{32,28},{36,32}... | collective-permute-start | bytes 786440 | tf_op jit(solution)/shard_map/ppermute | solution.py:493
  163.6 3.5 %all-to-all-done.4.offset = f32[32,16,128]{2,1,0:T(8,128)S(1)} async-done(((f32[32,16,128]{2,1,0:T(8,128)}), f32[32,16,128]{2,1,0:T(8,128)S(1)}, u32[]{:S(2)}, u32[]{:S(2)}) %all-to-all-start.4) | async-done | bytes 262176 | tf_op jit(solution)/shard_map/all_to_all | solution.py:498
  167.9 5.7 %all-to-all-start.5 = ((f32[32,16,128]{2,1,0:T(8,128)}), f32[32,16,128]{2,1,0:T(8,128)}, u32[]{:S(2)}, u32[]{:S(2)}) async-start(f32[32,16,128]{2,1,0:T(8,128)} %shard_map.118), calls=%async_computation.5 | async-start | bytes 524288 | tf_op jit(solution)/shard_map/all_to_all | solution.py:498
  173.5 4.3 %shard_map.119 = (f32[4,128,512]{2,1,0:T(8,128)S(1)}, f32[4,128,512]{2,1,0:T(8,128)}, f32[4,128,512]{2,1,0:T(8,128)S(1)}, f32[128,512]{1,0:T(8,128)S(1)}) custom-call(s32[4]{0:T(128)S(1)} %pad_add_fusion.place, f32[160,512]{1,0:T(8,128)S(1)} %get-tuple-element.187.rest_0_.p0, f32[160,512]{1,0:T(8,128)S(1)} %collective-permute-done.20.rest_1_.p1, ...), custom_call_target="tpu_custom_call" | custom-call | flops 4000000 | bytes 4194304 | tf_op jit(solution)/shard_map/pallas_call | solution.py:419
  178.5 2.8 %all-to-all-done.5.entering = f32[32,16,128]{2,1,0:T(8,128)} async-done(((f32[32,16,128]{2,1,0:T(8,128)}), f32[32,16,128]{2,1,0:T(8,128)}, u32[]{:S(2)}, u32[]{:S(2)}) %all-to-all-start.5) | async-done | bytes 262176 | tf_op jit(solution)/shard_map/all_to_all | solution.py:498
  182.3 2.1 %shard_map.120 = f32[4,128,512]{2,1,0:T(8,128)} custom-call(f32[32,16,128]{2,1,0:T(8,128)} %all-to-all-done.5.entering, f32[4,128,512]{2,1,0:T(8,128)S(1)} %get-tuple-element.193.change, f32[128,512]{1,0:T(8,128)} %collective-permute-done.23.following, f32[4,128,512]{2,1,0:T(8,128)S(1)} %get-tuple-element.195.decay, f32[128,512]{1,0:T(8,128)S(1)} %copy-done.5), custom_call_target="tpu_custom_call" | custom-call | flops 4000000 | bytes 5242880 | tf_op jit(solution)/shard_map/pallas_call | solution.py:395
  (52 shorter events, 14.6 us)
Async XLA Ops:
  7.2 51.4 %all-gather.2.cloned.1.call-start = ((), (), s32[]{:S(2)}) async-start(), calls=%async_computation.6 | async-start | bytes 4325376 | tf_op jit(solution)/shard_map/all_gather | solution.py:500
  8.9 9.8 %collective-permute-start.3 = (f32[128,512]{1,0:T(8,128)S(1)}, f32[128,512]{1,0:T(8,128)S(1)}, u32[]{:S(2)}, u32[]{:S(2)}) collective-permute-start(f32[128,512]{1,0:T(8,128)S(1)} %slice_bitcast_fusion), channel_id=1, source_target_pairs={{0,4},{4,8},{8,12},{12,16},{16,20},{20,24},{24,28},{28,32},{32,36}... | collective-permute-start | bytes 786440 | tf_op jit(solution)/shard_map/ppermute | solution.py:493
  11.8 33.1 %collective-permute-start.2 = (bf16[128,512]{1,0:T(8,128)(2,1)S(1)}, bf16[128,512]{1,0:T(8,128)(2,1)S(1)}, u32[]{:S(2)}, u32[]{:S(2)}) collective-permute-start(bf16[128,512]{1,0:T(8,128)(2,1)S(1)} %fusion.d0), channel_id=1, source_target_pairs={{0,3},{1,0},{2,1},{3,2},{4,7},{5,4},{6,5},{7,6},{8,11},{9,8},{10,9... | collective-permute-start | bytes 393224 | tf_op jit(solution)/shard_map/ppermute | solution.py:484
  15.9 29.0 %collective-permute-start.1 = (bf16[128,512]{1,0:T(8,128)(2,1)S(1)}, bf16[128,512]{1,0:T(8,128)(2,1)S(1)}, u32[]{:S(2)}, u32[]{:S(2)}) collective-permute-start(bf16[128,512]{1,0:T(8,128)(2,1)S(1)} %fusion.d0), channel_id=1, source_target_pairs={{0,2},{1,3},{2,0},{3,1},{4,6},{5,7},{6,4},{7,5},{8,10},{9,11},{10,... | collective-permute-start | bytes 393224 | tf_op jit(solution)/shard_map/ppermute | solution.py:484
  21.4 17.8 %collective-permute-start.5 = (f32[128,512]{1,0:T(8,128)S(1)}, f32[128,512]{1,0:T(8,128)S(1)}, u32[]{:S(2)}, u32[]{:S(2)}) collective-permute-start(f32[128,512]{1,0:T(8,128)S(1)} %get-tuple-element.109), channel_id=1, source_target_pairs={{0,2},{1,3},{2,0},{3,1},{4,6},{5,7},{6,4},{7,5},{8,10},{9,11},{10,... | collective-permute-start | bytes 786440 | tf_op jit(solution)/shard_map/ppermute | solution.py:484
  25.4 13.9 %collective-permute-start.4 = (f32[136,512]{1,0:T(8,128)S(1)}, f32[136,512]{1,0:T(8,128)S(1)}, u32[]{:S(2)}, u32[]{:S(2)}) collective-permute-start(f32[136,512]{1,0:T(8,128)S(1)} %get-tuple-element.108), channel_id=1, source_target_pairs={{0,1},{1,2},{2,3},{3,0},{4,5},{5,6},{6,7},{7,4},{8,9},{9,10},{10,1... | collective-permute-start | bytes 835592 | tf_op jit(solution)/shard_map/ppermute | solution.py:484
  26.4 12.9 %collective-permute-start.6 = (f32[136,512]{1,0:T(8,128)S(1)}, f32[136,512]{1,0:T(8,128)S(1)}, u32[]{:S(2)}, u32[]{:S(2)}) collective-permute-start(f32[136,512]{1,0:T(8,128)S(1)} %get-tuple-element.110), channel_id=1, source_target_pairs={{0,3},{1,0},{2,1},{3,2},{4,7},{5,4},{6,5},{7,6},{8,11},{9,8},{10,9... | collective-permute-start | bytes 835592 | tf_op jit(solution)/shard_map/ppermute | solution.py:484
  33.5 13.4 %all-to-all-start = ((f32[32,16,128]{2,1,0:T(8,128)}), f32[32,16,128]{2,1,0:T(8,128)S(1)}, u32[]{:S(2)}, u32[]{:S(2)}) async-start(f32[32,16,128]{2,1,0:T(8,128)} %get-tuple-element.106), calls=%async_computation | async-start | bytes 524288 | tf_op jit(solution)/shard_map/all_to_all | solution.py:498
  39.2 6.8 %collective-permute-start = (bf16[128,512]{1,0:T(8,128)(2,1)S(1)}, bf16[128,512]{1,0:T(8,128)(2,1)S(1)}, u32[]{:S(2)}, u32[]{:S(2)}) collective-permute-start(bf16[128,512]{1,0:T(8,128)(2,1)S(1)} %fusion.d0), channel_id=1, source_target_pairs={{0,1},{1,2},{2,3},{3,0},{4,5},{5,6},{6,7},{7,4},{8,9},{9,10},{10,1... | collective-permute-start | bytes 393224 | tf_op jit(solution)/shard_map/ppermute | solution.py:484
  49.1 19.3 %collective-permute-start.7 = (f32[128,512]{1,0:T(8,128)S(1)}, f32[128,512]{1,0:T(8,128)S(1)}, u32[]{:S(2)}, u32[]{:S(2)}) collective-permute-start(f32[128,512]{1,0:T(8,128)S(1)} %get-tuple-element.117), channel_id=1, source_target_pairs={{0,1},{1,2},{2,3},{3,0},{4,5},{5,6},{6,7},{7,4},{8,9},{9,10},{10,1... | collective-permute-start | bytes 786440 | tf_op jit(solution)/shard_map/ppermute | solution.py:484
  49.1 23.8 %collective-permute-start.8 = (f32[128,512]{1,0:T(8,128)S(1)}, f32[128,512]{1,0:T(8,128)S(1)}, u32[]{:S(2)}, u32[]{:S(2)}) collective-permute-start(f32[128,512]{1,0:T(8,128)S(1)} %get-tuple-element.118), channel_id=1, source_target_pairs={{0,2},{1,3},{2,0},{3,1},{4,6},{5,7},{6,4},{7,5},{8,10},{9,11},{10,... | collective-permute-start | bytes 786440 | tf_op jit(solution)/shard_map/ppermute | solution.py:484
  51.7 21.2 %collective-permute-start.9 = (f32[128,512]{1,0:T(8,128)S(1)}, f32[128,512]{1,0:T(8,128)S(1)}, u32[]{:S(2)}, u32[]{:S(2)}) collective-permute-start(f32[128,512]{1,0:T(8,128)S(1)} %get-tuple-element.119), channel_id=1, source_target_pairs={{0,3},{1,0},{2,1},{3,2},{4,7},{5,4},{6,5},{7,6},{8,11},{9,8},{10,9... | collective-permute-start | bytes 786440 | tf_op jit(solution)/shard_map/ppermute | solution.py:484
  64.9 8.0 %collective-permute-start.10 = (f32[128,128]{1,0:T(8,128)S(1)}, f32[128,128]{1,0:T(8,128)S(1)}, u32[]{:S(2)}, u32[]{:S(2)}) collective-permute-start(f32[128,128]{1,0:T(8,128)S(1)} %get-tuple-element.128), channel_id=1, source_target_pairs={{0,3},{1,0},{2,1},{3,2},{4,7},{5,4},{6,5},{7,6},{8,11},{9,8},{10,9... | collective-permute-start | bytes 196616 | tf_op jit(solution)/shard_map/ppermute | solution.py:484
  67.7 6.2 %collective-permute-start.11 = (f32[128,128]{1,0:T(8,128)S(1)}, f32[128,128]{1,0:T(8,128)S(1)}, u32[]{:S(2)}, u32[]{:S(2)}) collective-permute-start(f32[128,128]{1,0:T(8,128)S(1)} %get-tuple-element.129), channel_id=1, source_target_pairs={{0,2},{1,3},{2,0},{3,1},{4,6},{5,7},{6,4},{7,5},{8,10},{9,11},{10,... | collective-permute-start | bytes 196616 | tf_op jit(solution)/shard_map/ppermute | solution.py:484
  68.3 6.2 %collective-permute-start.12 = (f32[128,128]{1,0:T(8,128)S(1)}, f32[128,128]{1,0:T(8,128)S(1)}, u32[]{:S(2)}, u32[]{:S(2)}) collective-permute-start(f32[128,128]{1,0:T(8,128)S(1)} %get-tuple-element.130), channel_id=1, source_target_pairs={{0,1},{1,2},{2,3},{3,0},{4,5},{5,6},{6,7},{7,4},{8,9},{9,10},{10,1... | collective-permute-start | bytes 196616 | tf_op jit(solution)/shard_map/ppermute | solution.py:484
  72.9 3.3 %copy-start = (f32[128,512]{1,0:T(8,128)}, f32[128,512]{1,0:T(8,128)S(1)}, u32[]{:S(2)}) copy-start(f32[128,512]{1,0:T(8,128)S(1)} %collective-permute-done.9.rest_3_.p3) | copy-start | bytes 786436
  76.2 16.4 %all-to-all-start.1 = ((f32[32,16,128]{2,1,0:T(8,128)}), f32[32,16,128]{2,1,0:T(8,128)S(1)}, u32[]{:S(2)}, u32[]{:S(2)}) async-start(f32[32,16,128]{2,1,0:T(8,128)} %get-tuple-element.137), calls=%async_computation.1 | async-start | bytes 524288 | tf_op jit(solution)/shard_map/all_to_all | solution.py:498
  82.3 16.4 %collective-permute-start.13 = (f32[128,512]{1,0:T(8,128)}, f32[128,512]{1,0:T(8,128)}, u32[]{:S(2)}, u32[]{:S(2)}) collective-permute-start(f32[128,512]{1,0:T(8,128)} %get-tuple-element.147), channel_id=1, source_target_pairs={{4,0},{8,4},{12,8},{16,12},{20,16},{24,20},{28,24},{32,28},{36,32}... | collective-permute-start | bytes 786440 | tf_op jit(solution)/shard_map/ppermute | solution.py:493
  86.6 1.0 copy-start.1
  91.9 0.7 copy-start.2
  93.4 13.0 %all-to-all-start.2 = ((f32[32,16,128]{2,1,0:T(8,128)}), f32[32,16,128]{2,1,0:T(8,128)S(1)}, u32[]{:S(2)}, u32[]{:S(2)}) async-start(f32[32,16,128]{2,1,0:T(8,128)} %shard_map.111), calls=%async_computation.2 | async-start | bytes 524288 | tf_op jit(solution)/shard_map/all_to_all | solution.py:498
  106.4 1.0 copy-start.3
  108.6 6.4 %collective-permute-start.19 = (bf16[128,512]{1,0:T(8,128)(2,1)S(1)}, bf16[128,512]{1,0:T(8,128)(2,1)S(1)}, u32[]{:S(2)}, u32[]{:S(2)}) collective-permute-start(bf16[128,512]{1,0:T(8,128)(2,1)S(1)} %get-tuple-element.167.d0), channel_id=1, source_target_pairs={{0,3},{1,0},{2,1},{3,2},{4,7},{5,4},{6,5},{7,6},{8,11},{9,8},{10,9... | collective-permute-start | bytes 393224 | tf_op jit(solution)/shard_map/ppermute | solution.py:484
  109.3 11.8 %collective-permute-start.18 = (bf16[128,512]{1,0:T(8,128)(2,1)S(1)}, bf16[128,512]{1,0:T(8,128)(2,1)S(1)}, u32[]{:S(2)}, u32[]{:S(2)}) collective-permute-start(bf16[128,512]{1,0:T(8,128)(2,1)S(1)} %get-tuple-element.167.d0), channel_id=1, source_target_pairs={{0,2},{1,3},{2,0},{3,1},{4,6},{5,7},{6,4},{7,5},{8,10},{9,11},{10,... | collective-permute-start | bytes 393224 | tf_op jit(solution)/shard_map/ppermute | solution.py:484
  111.0 10.1 %collective-permute-start.17 = (bf16[128,512]{1,0:T(8,128)(2,1)S(1)}, bf16[128,512]{1,0:T(8,128)(2,1)S(1)}, u32[]{:S(2)}, u32[]{:S(2)}) collective-permute-start(bf16[128,512]{1,0:T(8,128)(2,1)S(1)} %get-tuple-element.167.d0), channel_id=1, source_target_pairs={{0,1},{1,2},{2,3},{3,0},{4,5},{5,6},{6,7},{7,4},{8,9},{9,10},{10,1... | collective-permute-start | bytes 393224 | tf_op jit(solution)/shard_map/ppermute | solution.py:484
  111.1 19.5 %collective-permute-start.14 = (f32[136,512]{1,0:T(8,128)S(1)}, f32[136,512]{1,0:T(8,128)S(1)}, u32[]{:S(2)}, u32[]{:S(2)}) collective-permute-start(f32[136,512]{1,0:T(8,128)S(1)} %get-tuple-element.159), channel_id=1, source_target_pairs={{0,1},{1,2},{2,3},{3,0},{4,5},{5,6},{6,7},{7,4},{8,9},{9,10},{10,1... | collective-permute-start | bytes 835592 | tf_op jit(solution)/shard_map/ppermute | solution.py:484
  112.8 17.8 %collective-permute-start.16 = (f32[136,512]{1,0:T(8,128)S(1)}, f32[136,512]{1,0:T(8,128)S(1)}, u32[]{:S(2)}, u32[]{:S(2)}) collective-permute-start(f32[136,512]{1,0:T(8,128)S(1)} %get-tuple-element.161), channel_id=1, source_target_pairs={{0,3},{1,0},{2,1},{3,2},{4,7},{5,4},{6,5},{7,6},{8,11},{9,8},{10,9... | collective-permute-start | bytes 835592 | tf_op jit(solution)/shard_map/ppermute | solution.py:484
  115.0 15.6 %collective-permute-start.15 = (f32[128,512]{1,0:T(8,128)S(1)}, f32[128,512]{1,0:T(8,128)S(1)}, u32[]{:S(2)}, u32[]{:S(2)}) collective-permute-start(f32[128,512]{1,0:T(8,128)S(1)} %get-tuple-element.160), channel_id=1, source_target_pairs={{0,2},{1,3},{2,0},{3,1},{4,6},{5,7},{6,4},{7,5},{8,10},{9,11},{10,... | collective-permute-start | bytes 786440 | tf_op jit(solution)/shard_map/ppermute | solution.py:484
  134.9 17.1 %collective-permute-start.20 = (f32[160,512]{1,0:T(8,128)S(1)}, f32[160,512]{1,0:T(8,128)S(1)}, u32[]{:S(2)}, u32[]{:S(2)}) collective-permute-start(f32[160,512]{1,0:T(8,128)S(1)} %get-tuple-element.176), channel_id=1, source_target_pairs={{0,1},{1,2},{2,3},{3,0},{4,5},{5,6},{6,7},{7,4},{8,9},{9,10},{10,1... | collective-permute-start | bytes 983048 | tf_op jit(solution)/shard_map/ppermute | solution.py:484
  135.0 17.0 %collective-permute-start.21 = (f32[160,512]{1,0:T(8,128)S(1)}, f32[160,512]{1,0:T(8,128)S(1)}, u32[]{:S(2)}, u32[]{:S(2)}) collective-permute-start(f32[160,512]{1,0:T(8,128)S(1)} %get-tuple-element.177), channel_id=1, source_target_pairs={{0,2},{1,3},{2,0},{3,1},{4,6},{5,7},{6,4},{7,5},{8,10},{9,11},{10,... | collective-permute-start | bytes 983048 | tf_op jit(solution)/shard_map/ppermute | solution.py:484
  137.2 15.3 %collective-permute-start.22 = (f32[160,512]{1,0:T(8,128)S(1)}, f32[160,512]{1,0:T(8,128)S(1)}, u32[]{:S(2)}, u32[]{:S(2)}) collective-permute-start(f32[160,512]{1,0:T(8,128)S(1)} %get-tuple-element.178), channel_id=1, source_target_pairs={{0,3},{1,0},{2,1},{3,2},{4,7},{5,4},{6,5},{7,6},{8,11},{9,8},{10,9... | collective-permute-start | bytes 983048 | tf_op jit(solution)/shard_map/ppermute | solution.py:484
  139.3 14.9 %all-to-all-start.3 = ((f32[32,16,128]{2,1,0:T(8,128)}), f32[32,16,128]{2,1,0:T(8,128)S(1)}, u32[]{:S(2)}, u32[]{:S(2)}) async-start(f32[32,16,128]{2,1,0:T(8,128)} %get-tuple-element.162), calls=%async_computation.3 | async-start | bytes 524288 | tf_op jit(solution)/shard_map/all_to_all | solution.py:498
  154.2 12.9 %all-to-all-start.4 = ((f32[32,16,128]{2,1,0:T(8,128)}), f32[32,16,128]{2,1,0:T(8,128)S(1)}, u32[]{:S(2)}, u32[]{:S(2)}) async-start(f32[32,16,128]{2,1,0:T(8,128)} %get-tuple-element.186), calls=%async_computation.4 | async-start | bytes 524288 | tf_op jit(solution)/shard_map/all_to_all | solution.py:498
  159.3 19.2 %collective-permute-start.23 = (f32[128,512]{1,0:T(8,128)}, f32[128,512]{1,0:T(8,128)}, u32[]{:S(2)}, u32[]{:S(2)}) collective-permute-start(f32[128,512]{1,0:T(8,128)} %get-tuple-element.194), channel_id=1, source_target_pairs={{4,0},{8,4},{12,8},{16,12},{20,16},{24,20},{28,24},{32,28},{36,32}... | collective-permute-start | bytes 786440 | tf_op jit(solution)/shard_map/ppermute | solution.py:493
  167.9 13.5 %all-to-all-start.5 = ((f32[32,16,128]{2,1,0:T(8,128)}), f32[32,16,128]{2,1,0:T(8,128)}, u32[]{:S(2)}, u32[]{:S(2)}) async-start(f32[32,16,128]{2,1,0:T(8,128)} %shard_map.118), calls=%async_computation.5 | async-start | bytes 524288 | tf_op jit(solution)/shard_map/all_to_all | solution.py:498
  177.8 0.7 copy-start.4
  181.4 1.0 copy-start.5
Sparse Core Ops, SparseCore 0:
  10.3 48.2 all-gather.1

commit v8 on v6

--- a/solution.py
+++ b/solution.py
@@ -100,11 +100,14 @@
     send_edges(current, outs, i == 0, i == pl.num_programs(0) - 1)
 
 
-def decay_kernel(place, current, damping, decay, scale):
+def decay_kernel(place, current, damping, decay, scale, *copy):
     for g, rows in groups(current.shape[1]):
         product = None
         for s in range(current.shape[0]):
-            d = decay_of(current[s, rows], damping[s, rows])
+            here = current[s, rows]
+            for ref in copy:
+                ref[s, rows] = here
+            d = decay_of(here, damping[s, rows])
             decay[s, rows] = d
             product = d if product is None else product * d
         to_chunks(scale, g, product)
@@ -312,16 +315,18 @@
 
 def change_kernel(
     place, p0, p1, p2, p3, term, force, decay, inflow,
-    change, pressure, decay_near, entry,
+    change, decay_near, pressure,
 ):
     c = place[0]
     pieces = (p0, p1, p2, p3)
     count, height, _ = term.shape
     for r in range(count):
-        pressure[lax.rem(c - r + count, count)] = pieces[r][...]
+        pressure[lax.rem(c - r + count, count)] = pieces[r][0:height]
     for _, rows in groups(height):
         here = pressure[0, rows]
-        entry[rows] = jnp.where(place[1] == 1, inflow[rows], -here)
+        entry = jnp.where(place[1] == 1, inflow[rows], -here)
+        if change.shape[0] > count:
+            change[count, rows] = entry
         for s in range(count):
             value = term[s, rows] + here
             if s == 0:
@@ -329,8 +334,11 @@
             if s < count - 1:
                 here = pressure[s + 1, rows]
                 value = value - here
+            d = decay[s, rows]
+            decay_near[s, rows] = d
+            if s == 0 and change.shape[0] == count:
+                value = value + d * entry
             change[s, rows] = value
-            decay_near[s, rows] = decay[s, rows]
 
 
 def scan_kernel(scale, offset, entering):
@@ -341,9 +349,11 @@
         state = scale[m] * state + offset[m]
 
 
-def march_rows(g, rows, entering, change, following, decay, entry):
+def march_rows(g, rows, entering, change, following, decay):
     stations = decay.shape[0]
-    state = from_chunks(entering, g) + entry[rows]
+    state = from_chunks(entering, g)
+    if change.shape[0] > stations:
+        state = state + change[stations, rows]
     states = [state]
     for s in range(stations):
         step = change[s, rows]
@@ -355,11 +365,11 @@
 
 
 def middle_kernel(
-    place, entering, change, following, decay, entry, current, disc, x0, x1, x2, x3, source
+    place, entering, change, following, decay, current, disc, x0, x1, x2, x3, source
 ):
     stations, height, _ = current.shape
     for g, rows in groups(height):
-        states = march_rows(g, rows, entering, change, following, decay, entry)
+        states = march_rows(g, rows, entering, change, following, decay)
         for s in range(stations):
             current[s, rows] = states[s + 1]
             source[s, rows] = SOURCE_GAIN * (states[s + 1] - states[s])
@@ -369,9 +379,9 @@
     disc[...] = current[0].astype(BF16)
 
 
-def last_kernel(entering, change, following, decay, entry, current):
+def last_kernel(entering, change, following, decay, current):
     for g, rows in groups(current.shape[1]):
-        states = march_rows(g, rows, entering, change, following, decay, entry)
+        states = march_rows(g, rows, entering, change, following, decay)
         for s in range(current.shape[0]):
             current[s, rows] = states[s + 1]
 
@@ -515,7 +525,6 @@
     step = (stations, height // STEPS, width)
     near_inflow = stay(inflow)
     upstream = along_march(velocity_guess[-1], 1)
-    upstream, *where = lax.optimization_barrier((upstream, *where))
     current = stay(velocity_guess)
     disc = velocity_guess[0].astype(BF16)
     rows = turns([disc] * cross_size)
@@ -536,10 +545,10 @@
             rows = turns([disc] * cross_size)
         guess, damp, *source = lax.optimization_barrier((current, damping, *source))
         arrived = turns(source)
-        decay, scale = by_rows(
+        decay, scale, *kept = by_rows(
             decay_kernel,
             height,
-            [far(slab), far(chunks)],
+            [far(slab), far(chunks)] + [far(slab)] * merged,
             place,
             (guess if merged else stay(guess), stay(damp)),
             cost(4e6, 3 * MIB),
@@ -573,10 +582,12 @@
                 compiler_params=pltpu.CompilerParams(vmem_limit_bytes=20 * MIB),
                 cost_estimate=solve_cost,
             )(place, *arrived, *tabled)
-            rows, scales, solved = lax.optimization_barrier((rows, scales, solved))
+            rows, scales, solved, where = lax.optimization_barrier((rows, scales, solved, where))
             forces = turns(disc_forces(rows, where, blades), -1)
         pieces = turns(solved)
         decay = stay(decay)
+        if merged:
+            current = stay(kept[0])
         term, weights, base, force_weight = call(
             weights_kernel,
             [far(slab), near(slab), near(plane), near(plane)],
@@ -595,24 +606,24 @@
         )
         following = along_march(lead, -1)
         offset, force, *pieces = lax.optimization_barrier((offset, force, *pieces))
-        change, pressure, decay, entry = by_rows(
+        change, decay, *pressure = call(
             change_kernel,
-            height,
-            [near(slab), far(slab), near(slab), near(plane)],
-            place,
-            (*pieces, stay(term), stay(force), decay, near_inflow),
+            [near((stations + (not final), *plane)), near(slab)] + [far(slab)] * final,
+            (place, *pieces, stay(term), stay(force), decay, near_inflow),
             cost(4e6, 4 * MIB),
-        )
-        (entering,) = call(
-            scan_kernel, [far(chunks)], (scales, across_march(offset)), cost(1e5, MIB)
-        )
+            scalars=1,
+            limit=12,
+            scratch=[] if final else [pltpu.VMEM(slab, F32)],
+        )
+        offset = across_march(offset)
+        (entering,) = call(scan_kernel, [far(chunks)], (scales, offset), cost(1e5, MIB))
         entering = across_march(entering)
-        common = (entering, change, following, decay, entry)
+        common = (entering, change, following, decay)
         if final:
             (current,) = call(
                 last_kernel, [far(slab)], common, cost(4e6, 5 * MIB), limit=12
             )
-            return (current, pressure)
+            return (current, pressure[0])
         current, disc, *source = call(
             middle_kernel,
             [near(slab), near(plane, BF16)] + sources,

time: 195 us -> 188 us (0.964)
  Pallas kernels: 55 us -> 49.5 us
  local copies, waits for them, and re-layouts: 9.24 us -> 7.19 us
    pallas_call x5 -> x3, Pallas kernels: 19.6 us -> 11.2 us  [by_rows(): pl.pallas_call(kernel, grid_spec=pltpu.PrefetchScalarGridSpec(num_scalar_...]
    ppermute x3, waiting for transfers between devices: 7.07 us -> 2.72 us  [along_march(): lax.ppermute(value, 'march', [(i, i + steps) for i in range(count) if 0 <...]
    all_to_all x6, waiting for transfers between devices: 13.2 us -> 16.7 us  [across_march(): lax.all_to_all(value, 'march', split_axis=0, concat_axis=0, tiled=True)]
    all_to_all x6, starting transfers between devices: 35 us -> 31.8 us  [across_march(): lax.all_to_all(value, 'march', split_axis=0, concat_axis=0, tiled=True)]
    pallas_call x9 -> x11, Pallas kernels: 20.4 us -> 23.3 us  [call(): pl.pallas_call(kernel, out_shape=outs, in_specs=[SMEM] * scalars + [VMEM]...]
    all_gather x1, waiting for transfers between devices: 4.06 us -> 6.24 us  [local(): blades = lax.all_gather(blade, 'march', axis=0, tiled=True)]
    unnamed x16 -> x8, local copies, waits for them, and re-layouts: 5.2 us -> 3.14 us
  transfers between devices with their start and end apart: 31 -> 31, of which waited for: 14 -> 14; matrix products, arithmetic and copies ran while one was open for 3% -> 3% of each run, Pallas kernels for 23% -> 22%
where the time goes in v8:
time: 188 us; the launch traced here: 184 us
  starting transfers between devices  73.4 us (39%)
  Pallas kernels  49.5 us (26%)
  waiting for transfers between devices  39.1 us (21%)
  between operations  14.3 us (8%)
  local copies, waits for them, and re-layouts  7.19 us (4%)
    all_to_all x6, starting transfers between devices, across_march(): lax.all_to_all(value, 'march', split_axis=0, concat_axis=0, tiled=True)  31.8 us
    ppermute x21, starting transfers between devices, turn(): lax.ppermute(value, 'cross', [(i, (i + steps) % cross_size) for i in rang...  31 us
    pallas_call x11, Pallas kernels, call(): pl.pallas_call(kernel, out_shape=outs, in_specs=[SMEM] * scalars + [VMEM]...  23.3 us
    all_to_all x6, waiting for transfers between devices, across_march(): lax.all_to_all(value, 'march', split_axis=0, concat_axis=0, tiled=True)  16.7 us
    ppermute x21, waiting for transfers between devices, turn(): lax.ppermute(value, 'cross', [(i, (i + steps) % cross_size) for i in rang...  12.8 us
    pallas_call x3, Pallas kernels, by_rows(): pl.pallas_call(kernel, grid_spec=pltpu.PrefetchScalarGridSpec(num_scalar_...  11.2 us
    ppermute x3, starting transfers between devices, along_march(): lax.ppermute(value, 'march', [(i, i + steps) for i in range(count) if 0 <...  10.6 us
    pallas_call x2, Pallas kernels, disc_forces(): pl.pallas_call(disc_kernel, grid=(number // per_step,), out_shape=[near((...  9.51 us
  transfers between devices with their start and end apart: 31, of which 14 were waited for; matrix products, arithmetic and copies ran while one was open for 3% of the time, Pallas kernels for 22%

profile of v8, /device:TPU:2, one launch (start us, length us, event | category | flops | bytes accessed | tf_op | source)
XLA Modules:
  0.0 184.2 jit_solution(12119213546313653980)
XLA Ops:
  7.9 1.0 slice_bitcast_fusion
  8.9 1.9 %collective-permute-start.3 = (f32[128,512]{1,0:T(8,128)S(1)}, f32[128,512]{1,0:T(8,128)S(1)}, u32[]{:S(2)}, u32[]{:S(2)}) collective-permute-start(f32[128,512]{1,0:T(8,128)S(1)} %slice_bitcast_fusion), channel_id=1, source_target_pairs={{0,4},{4,8},{8,12},{12,16},{16,20},{20,24},{24,28},{28,32},{32,36}... | collective-permute-start | bytes 786440 | tf_op jit(solution)/shard_map/ppermute | solution.py:508
  10.8 1.0 fusion.d0
  11.8 4.1 %collective-permute-start.2 = (bf16[128,512]{1,0:T(8,128)(2,1)S(1)}, bf16[128,512]{1,0:T(8,128)(2,1)S(1)}, u32[]{:S(2)}, u32[]{:S(2)}) collective-permute-start(bf16[128,512]{1,0:T(8,128)(2,1)S(1)} %fusion.d0), channel_id=1, source_target_pairs={{0,3},{1,0},{2,1},{3,2},{4,7},{5,4},{6,5},{7,6},{8,11},{9,8},{10,9... | collective-permute-start | bytes 393224 | tf_op jit(solution)/shard_map/ppermute | solution.py:499
  16.0 2.7 %collective-permute-done.3.upstream = f32[128,512]{1,0:T(8,128)S(1)} collective-permute-done((f32[128,512]{1,0:T(8,128)S(1)}, f32[128,512]{1,0:T(8,128)S(1)}, u32[]{:S(2)}, u32[]{:S(2)}) %collective-permute-start.3) | collective-permute-done | bytes 262176 | tf_op jit(solution)/shard_map/ppermute | solution.py:508
  18.7 2.7 %shard_map.104 = (f32[128,512]{1,0:T(8,128)S(1)}, f32[136,512]{1,0:T(8,128)S(1)}, f32[128,512]{1,0:T(8,128)S(1)}, f32[136,512]{1,0:T(8,128)S(1)}) custom-call(s32[4]{0:T(128)S(1)} %pad_add_fusion.place, f32[4,128,512]{2,1,0:T(8,128)} %current.4, f32[128,512]{1,0:T(8,128)S(1)} %collective-permute-done.3.upstream, f32[128,512]{1,0:T(8,128)} %inflow.9), custom_call_target="tpu_custom_call" | custom-call | flops 1000000 | bytes 2097152 | tf_op jit(solution)/shard_map/pallas_call | solution.py:430
  21.4 4.0 %collective-permute-start.5 = (f32[128,512]{1,0:T(8,128)S(1)}, f32[128,512]{1,0:T(8,128)S(1)}, u32[]{:S(2)}, u32[]{:S(2)}) collective-permute-start(f32[128,512]{1,0:T(8,128)S(1)} %get-tuple-element.105), channel_id=1, source_target_pairs={{0,2},{1,3},{2,0},{3,1},{4,6},{5,7},{6,4},{7,5},{8,10},{9,11},{10,... | collective-permute-start | bytes 786440 | tf_op jit(solution)/shard_map/ppermute | solution.py:499
  25.4 1.0 collective-permute-start.4
  26.4 2.2 %collective-permute-start.6 = (f32[136,512]{1,0:T(8,128)S(1)}, f32[136,512]{1,0:T(8,128)S(1)}, u32[]{:S(2)}, u32[]{:S(2)}) collective-permute-start(f32[136,512]{1,0:T(8,128)S(1)} %get-tuple-element.106), channel_id=1, source_target_pairs={{0,3},{1,0},{2,1},{3,2},{4,7},{5,4},{6,5},{7,6},{8,11},{9,8},{10,9... | collective-permute-start | bytes 835592 | tf_op jit(solution)/shard_map/ppermute | solution.py:499
  29.3 4.2 %shard_map.105 = (f32[4,128,512]{2,1,0:T(8,128)}, f32[32,16,128]{2,1,0:T(8,128)}) custom-call(s32[4]{0:T(128)S(1)} %pad_add_fusion.place, f32[4,128,512]{2,1,0:T(8,128)} %current.4, f32[4,128,512]{2,1,0:T(8,128)} %damping.1), custom_call_target="tpu_custom_call" | custom-call | flops 4000000 | bytes 3145728 | tf_op jit(solution)/shard_map/pallas_call | solution.py:430
  33.5 5.7 %all-to-all-start = ((f32[32,16,128]{2,1,0:T(8,128)}), f32[32,16,128]{2,1,0:T(8,128)S(1)}, u32[]{:S(2)}, u32[]{:S(2)}) async-start(f32[32,16,128]{2,1,0:T(8,128)} %get-tuple-element.102), calls=%async_computation | async-start | bytes 524288 | tf_op jit(solution)/shard_map/all_to_all | solution.py:513
  39.3 5.6 %shard_map.106 = (f32[128,512]{1,0:T(8,128)S(1)}, f32[128,512]{1,0:T(8,128)S(1)}, f32[128,512]{1,0:T(8,128)S(1)}, f32[128,512]{1,0:T(8,128)S(1)}) custom-call(s32[4]{0:T(128)S(1)} %pad_add_fusion.place, f32[128,512]{1,0:T(8,128)S(1)} %get-tuple-element.103.x0, f32[136,512]{1,0:T(8,128)S(1)} %collective-permute-done.4.x1.before, ...), custom_call_target="tpu_custom_call" | custom-call | flops 3221225472 | bytes 5242880 | tf_op jit(solution)/shard_map/pallas_call | solution.py:574
  44.9 1.1 collective-permute-done.d1
  49.1 2.6 %collective-permute-start.8 = (f32[128,512]{1,0:T(8,128)S(1)}, f32[128,512]{1,0:T(8,128)S(1)}, u32[]{:S(2)}, u32[]{:S(2)}) collective-permute-start(f32[128,512]{1,0:T(8,128)S(1)} %get-tuple-element.114), channel_id=1, source_target_pairs={{0,2},{1,3},{2,0},{3,1},{4,6},{5,7},{6,4},{7,5},{8,10},{9,11},{10,... | collective-permute-start | bytes 786440 | tf_op jit(solution)/shard_map/ppermute | solution.py:499
  52.3 6.2 %all-gather.2.cloned.1.call-done.rest_0_.rest_1_.rest_2_.rest_3_ = bf16[32,512,128]{2,1,0:T(8,128)(2,1)} async-done(((bf16[1,512,128]{2,1,0:T(8,128)(2,1)}), bf16[32,512,128]{2,1,0:T(8,128)(2,1)}) %all-gather.2.cloned.1.call-update) | async-done | bytes 4194320 | tf_op jit(solution)/shard_map/all_gather | solution.py:515
  58.6 4.7 %shard_map.107 = (f32[128,128]{1,0:T(8,128)S(1)}, f32[128,128]{1,0:T(8,128)S(1)}, f32[128,128]{1,0:T(8,128)S(1)}, f32[128,128]{1,0:T(8,128)S(1)}) custom-call(bf16[128,512]{1,0:T(8,128)(2,1)S(1)} %fusion.d0, bf16[128,512]{1,0:T(8,128)(2,1)S(1)} %collective-permute-done.d1, bf16[128,512]{1,0:T(8,128)(2,1)S(1)} %collective-permute-done.1.d2, ...), custom_call_target="tpu_custom_call" | custom-call | flops 2147483648 | bytes 5242880 | tf_op jit(solution)/shard_map/pallas_call | solution.py:453
  63.3 2.7 %collective-permute-start.10 = (f32[128,128]{1,0:T(8,128)S(1)}, f32[128,128]{1,0:T(8,128)S(1)}, u32[]{:S(2)}, u32[]{:S(2)}) collective-permute-start(f32[128,128]{1,0:T(8,128)S(1)} %get-tuple-element.124), channel_id=1, source_target_pairs={{0,3},{1,0},{2,1},{3,2},{4,7},{5,4},{6,5},{7,6},{8,11},{9,8},{10,9... | collective-permute-start | bytes 196616 | tf_op jit(solution)/shard_map/ppermute | solution.py:499
  67.6 3.6 %shard_map.108 = (f32[4,128,512]{2,1,0:T(8,128)}, f32[4,128,512]{2,1,0:T(8,128)S(1)}, f32[128,512]{1,0:T(8,128)S(1)}, f32[128,512]{1,0:T(8,128)S(1)}) custom-call(s32[4]{0:T(128)S(1)} %pad_add_fusion.place, f32[4,128,512]{2,1,0:T(8,128)} %current.4, f32[136,512]{1,0:T(8,128)S(1)} %collective-permute-done.4.x1.before, ...), custom_call_target="tpu_custom_call" | custom-call | flops 8000000 | bytes 4194304 | tf_op jit(solution)/shard_map/pallas_call | solution.py:406
  72.9 1.7 shard_map.109
  74.5 5.9 %all-to-all-start.1 = ((f32[32,16,128]{2,1,0:T(8,128)}), f32[32,16,128]{2,1,0:T(8,128)S(1)}, u32[]{:S(2)}, u32[]{:S(2)}) async-start(f32[32,16,128]{2,1,0:T(8,128)} %get-tuple-element.133), calls=%async_computation.1 | async-start | bytes 524288 | tf_op jit(solution)/shard_map/all_to_all | solution.py:513
  80.4 4.3 %collective-permute-start.13 = (f32[128,512]{1,0:T(8,128)}, f32[128,512]{1,0:T(8,128)}, u32[]{:S(2)}, u32[]{:S(2)}) collective-permute-start(f32[128,512]{1,0:T(8,128)} %get-tuple-element.141), channel_id=1, source_target_pairs={{4,0},{8,4},{12,8},{16,12},{20,16},{24,20},{28,24},{32,28},{36,32}... | collective-permute-start | bytes 786440 | tf_op jit(solution)/shard_map/ppermute | solution.py:508
  84.8 3.4 %all-to-all-done.1.offset = f32[32,16,128]{2,1,0:T(8,128)S(1)} async-done(((f32[32,16,128]{2,1,0:T(8,128)}), f32[32,16,128]{2,1,0:T(8,128)S(1)}, u32[]{:S(2)}, u32[]{:S(2)}) %all-to-all-start.1) | async-done | bytes 262176 | tf_op jit(solution)/shard_map/all_to_all | solution.py:513
  88.9 5.0 %all-to-all-start.2 = ((f32[32,16,128]{2,1,0:T(8,128)}), f32[32,16,128]{2,1,0:T(8,128)S(1)}, u32[]{:S(2)}, u32[]{:S(2)}) async-start(f32[32,16,128]{2,1,0:T(8,128)} %shard_map.110), calls=%async_computation.2 | async-start | bytes 524288 | tf_op jit(solution)/shard_map/all_to_all | solution.py:513
  94.9 1.9 %shard_map.111 = (f32[5,128,512]{2,1,0:T(8,128)S(1)}, f32[4,128,512]{2,1,0:T(8,128)S(1)}) custom-call(s32[4]{0:T(128)S(1)} %pad_add_fusion.place, f32[128,512]{1,0:T(8,128)S(1)} %get-tuple-element.134.rest_0_.p0, f32[128,512]{1,0:T(8,128)S(1)} %collective-permute-done.7.rest_1_.p1, f32[128,512]{1,0:T(8,128)S(1)} %collective-permute-done.8.rest_2_.p2, ...), custom_call_target="tpu_custom_call" | custom-call | flops 4000000 | bytes 4194304 | tf_op jit(solution)/shard_map/pallas_call | solution.py:406
  96.9 4.9 %all-to-all-done.2.entering = f32[32,16,128]{2,1,0:T(8,128)S(1)} async-done(((f32[32,16,128]{2,1,0:T(8,128)}), f32[32,16,128]{2,1,0:T(8,128)S(1)}, u32[]{:S(2)}, u32[]{:S(2)}) %all-to-all-start.2) | async-done | bytes 262176 | tf_op jit(solution)/shard_map/all_to_all | solution.py:513
  101.7 1.2 shard_map.112
  103.7 1.6 collective-permute-start.18
  105.5 1.7 collective-permute-start.14
  107.2 1.5 collective-permute-start.16
  109.4 1.9 %collective-permute-start.15 = (f32[128,512]{1,0:T(8,128)S(1)}, f32[128,512]{1,0:T(8,128)S(1)}, u32[]{:S(2)}, u32[]{:S(2)}) collective-permute-start(f32[128,512]{1,0:T(8,128)S(1)} %get-tuple-element.153), channel_id=1, source_target_pairs={{0,2},{1,3},{2,0},{3,1},{4,6},{5,7},{6,4},{7,5},{8,10},{9,11},{10,... | collective-permute-start | bytes 786440 | tf_op jit(solution)/shard_map/ppermute | solution.py:499
  111.2 4.2 %shard_map.113 = (f32[4,128,512]{2,1,0:T(8,128)}, f32[32,16,128]{2,1,0:T(8,128)}, f32[4,128,512]{2,1,0:T(8,128)}) custom-call(s32[4]{0:T(128)S(1)} %pad_add_fusion.place, f32[4,128,512]{2,1,0:T(8,128)S(1)} %get-tuple-element.148.current, f32[4,128,512]{2,1,0:T(8,128)} %damping.1), custom_call_target="tpu_custom_call" | custom-call | flops 4000000 | bytes 3145728 | tf_op jit(solution)/shard_map/pallas_call | solution.py:430
  115.5 4.8 %shard_map.114 = (f32[128,128]{1,0:T(8,128)S(1)}, f32[128,128]{1,0:T(8,128)S(1)}, f32[128,128]{1,0:T(8,128)S(1)}, f32[128,128]{1,0:T(8,128)S(1)}, bf16[512,512]{...) custom-call(bf16[128,512]{1,0:T(8,128)(2,1)S(1)} %get-tuple-element.160.d0, ...), custom_call_target="tpu_custom_call" | custom-call | flops 2147483648 | bytes 5242880 | tf_op jit(solution)/shard_map/pallas_call | solution.py:453
  120.3 4.7 %collective-permute-done.15.x2 = f32[128,512]{1,0:T(8,128)S(1)} collective-permute-done((f32[128,512]{1,0:T(8,128)S(1)}, f32[128,512]{1,0:T(8,128)S(1)}, u32[]{:S(2)}, u32[]{:S(2)}) %collective-permute-start.15) | collective-permute-done | bytes 262176 | tf_op jit(solution)/shard_map/ppermute | solution.py:499
  125.0 4.3 %shard_map.115 = (f32[160,512]{1,0:T(8,128)S(1)}, f32[160,512]{1,0:T(8,128)S(1)}, f32[160,512]{1,0:T(8,128)S(1)}, f32[160,512]{1,0:T(8,128)S(1)}) custom-call(s32[4]{0:T(128)S(1)} %pad_add_fusion.place, f32[128,512]{1,0:T(8,128)S(1)} %get-tuple-element.156.x0, f32[136,512]{1,0:T(8,128)S(1)} %collective-permute-done.14.x1.before, ...), custom_call_target="tpu_custom_call" | custom-call | flops 3221225472 | bytes 5242880 | tf_op jit(solution)/shard_map/pallas_call | solution.py:406
  129.4 2.3 %collective-permute-start.21 = (f32[160,512]{1,0:T(8,128)S(1)}, f32[160,512]{1,0:T(8,128)S(1)}, u32[]{:S(2)}, u32[]{:S(2)}) collective-permute-start(f32[160,512]{1,0:T(8,128)S(1)} %get-tuple-element.170), channel_id=1, source_target_pairs={{0,2},{1,3},{2,0},{3,1},{4,6},{5,7},{6,4},{7,5},{8,10},{9,11},{10,... | collective-permute-start | bytes 983048 | tf_op jit(solution)/shard_map/ppermute | solution.py:499
  131.7 2.0 %collective-permute-start.22 = (f32[160,512]{1,0:T(8,128)S(1)}, f32[160,512]{1,0:T(8,128)S(1)}, u32[]{:S(2)}, u32[]{:S(2)}) collective-permute-start(f32[160,512]{1,0:T(8,128)S(1)} %get-tuple-element.171), channel_id=1, source_target_pairs={{0,3},{1,0},{2,1},{3,2},{4,7},{5,4},{6,5},{7,6},{8,11},{9,8},{10,9... | collective-permute-start | bytes 983048 | tf_op jit(solution)/shard_map/ppermute | solution.py:499
  133.7 5.1 %all-to-all-start.3 = ((f32[32,16,128]{2,1,0:T(8,128)}), f32[32,16,128]{2,1,0:T(8,128)S(1)}, u32[]{:S(2)}, u32[]{:S(2)}) async-start(f32[32,16,128]{2,1,0:T(8,128)} %get-tuple-element.155), calls=%async_computation.3 | async-start | bytes 524288 | tf_op jit(solution)/shard_map/all_to_all | solution.py:513
  138.8 3.6 %shard_map.116 = (f32[4,128,512]{2,1,0:T(8,128)}, f32[4,128,512]{2,1,0:T(8,128)S(1)}, f32[128,512]{1,0:T(8,128)S(1)}, f32[128,512]{1,0:T(8,128)S(1)}) custom-call(s32[4]{0:T(128)S(1)} %pad_add_fusion.place, f32[4,128,512]{2,1,0:T(8,128)} %get-tuple-element.172.current, f32[136,512]{1,0:T(8,128)S(1)} %collective-permute-done.14.x1.before, ...), custom_call_target="tpu_custom_call" | custom-call | flops 8000000 | bytes 4194304 | tf_op jit(solution)/shard_map/pallas_call | solution.py:406
  142.4 4.0 %collective-permute-done.20.rest_1_.p1 = f32[160,512]{1,0:T(8,128)S(1)} collective-permute-done((f32[160,512]{1,0:T(8,128)S(1)}, f32[160,512]{1,0:T(8,128)S(1)}, u32[]{:S(2)}, u32[]{:S(2)}) %collective-permute-start.20) | collective-permute-done | bytes 327712 | tf_op jit(solution)/shard_map/ppermute | solution.py:499
  147.0 1.5 shard_map.117
  148.5 5.1 %all-to-all-start.4 = ((f32[32,16,128]{2,1,0:T(8,128)}), f32[32,16,128]{2,1,0:T(8,128)S(1)}, u32[]{:S(2)}, u32[]{:S(2)}) async-start(f32[32,16,128]{2,1,0:T(8,128)} %get-tuple-element.179), calls=%async_computation.4 | async-start | bytes 524288 | tf_op jit(solution)/shard_map/all_to_all | solution.py:513
  153.7 4.3 %collective-permute-start.23 = (f32[128,512]{1,0:T(8,128)S(1)}, f32[128,512]{1,0:T(8,128)S(1)}, u32[]{:S(2)}, u32[]{:S(2)}) collective-permute-start(f32[128,512]{1,0:T(8,128)S(1)} %get-tuple-element.187), channel_id=1, source_target_pairs={{4,0},{8,4},{12,8},{16,12},{20,16},{24,20},{28,24},{32,28},{36,32}... | collective-permute-start | bytes 786440 | tf_op jit(solution)/shard_map/ppermute | solution.py:508
  158.0 3.5 %all-to-all-done.4.offset = f32[32,16,128]{2,1,0:T(8,128)S(1)} async-done(((f32[32,16,128]{2,1,0:T(8,128)}), f32[32,16,128]{2,1,0:T(8,128)S(1)}, u32[]{:S(2)}, u32[]{:S(2)}) %all-to-all-start.4) | async-done | bytes 262176 | tf_op jit(solution)/shard_map/all_to_all | solution.py:513
  162.2 5.0 %all-to-all-start.5 = ((f32[32,16,128]{2,1,0:T(8,128)}), f32[32,16,128]{2,1,0:T(8,128)S(1)}, u32[]{:S(2)}, u32[]{:S(2)}) async-start(f32[32,16,128]{2,1,0:T(8,128)} %shard_map.118), calls=%async_computation.5 | async-start | bytes 524288 | tf_op jit(solution)/shard_map/all_to_all | solution.py:513
  167.3 2.8 %shard_map.119 = (f32[4,128,512]{2,1,0:T(8,128)S(1)}, f32[4,128,512]{2,1,0:T(8,128)S(1)}, f32[4,128,512]{2,1,0:T(8,128)}) custom-call(s32[4]{0:T(128)S(1)} %pad_add_fusion.place, f32[160,512]{1,0:T(8,128)S(1)} %get-tuple-element.180.rest_0_.p0, f32[160,512]{1,0:T(8,128)S(1)} %collective-permute-done.20.rest_1_.p1, ...), custom_call_target="tpu_custom_call" | custom-call | flops 4000000 | bytes 4194304 | tf_op jit(solution)/shard_map/pallas_call | solution.py:406
  171.0 4.1 %all-to-all-done.5.entering = f32[32,16,128]{2,1,0:T(8,128)S(1)} async-done(((f32[32,16,128]{2,1,0:T(8,128)}), f32[32,16,128]{2,1,0:T(8,128)S(1)}, u32[]{:S(2)}, u32[]{:S(2)}) %all-to-all-start.5) | async-done | bytes 262176 | tf_op jit(solution)/shard_map/all_to_all | solution.py:513
  175.0 1.2 copy-done.1
  176.3 1.1 shard_map.120
  (48 shorter events, 14.2 us)
Async XLA Ops:
  7.2 51.4 %all-gather.2.cloned.1.call-start = ((), (), s32[]{:S(2)}) async-start(), calls=%async_computation.6 | async-start | bytes 4325376 | tf_op jit(solution)/shard_map/all_gather | solution.py:515
  8.9 9.8 %collective-permute-start.3 = (f32[128,512]{1,0:T(8,128)S(1)}, f32[128,512]{1,0:T(8,128)S(1)}, u32[]{:S(2)}, u32[]{:S(2)}) collective-permute-start(f32[128,512]{1,0:T(8,128)S(1)} %slice_bitcast_fusion), channel_id=1, source_target_pairs={{0,4},{4,8},{8,12},{12,16},{16,20},{20,24},{24,28},{28,32},{32,36}... | collective-permute-start | bytes 786440 | tf_op jit(solution)/shard_map/ppermute | solution.py:508
  11.8 33.1 %collective-permute-start.2 = (bf16[128,512]{1,0:T(8,128)(2,1)S(1)}, bf16[128,512]{1,0:T(8,128)(2,1)S(1)}, u32[]{:S(2)}, u32[]{:S(2)}) collective-permute-start(bf16[128,512]{1,0:T(8,128)(2,1)S(1)} %fusion.d0), channel_id=1, source_target_pairs={{0,3},{1,0},{2,1},{3,2},{4,7},{5,4},{6,5},{7,6},{8,11},{9,8},{10,9... | collective-permute-start | bytes 393224 | tf_op jit(solution)/shard_map/ppermute | solution.py:499
  15.9 29.0 %collective-permute-start.1 = (bf16[128,512]{1,0:T(8,128)(2,1)S(1)}, bf16[128,512]{1,0:T(8,128)(2,1)S(1)}, u32[]{:S(2)}, u32[]{:S(2)}) collective-permute-start(bf16[128,512]{1,0:T(8,128)(2,1)S(1)} %fusion.d0), channel_id=1, source_target_pairs={{0,2},{1,3},{2,0},{3,1},{4,6},{5,7},{6,4},{7,5},{8,10},{9,11},{10,... | collective-permute-start | bytes 393224 | tf_op jit(solution)/shard_map/ppermute | solution.py:499
  21.4 17.8 %collective-permute-start.5 = (f32[128,512]{1,0:T(8,128)S(1)}, f32[128,512]{1,0:T(8,128)S(1)}, u32[]{:S(2)}, u32[]{:S(2)}) collective-permute-start(f32[128,512]{1,0:T(8,128)S(1)} %get-tuple-element.105), channel_id=1, source_target_pairs={{0,2},{1,3},{2,0},{3,1},{4,6},{5,7},{6,4},{7,5},{8,10},{9,11},{10,... | collective-permute-start | bytes 786440 | tf_op jit(solution)/shard_map/ppermute | solution.py:499
  25.4 13.9 %collective-permute-start.4 = (f32[136,512]{1,0:T(8,128)S(1)}, f32[136,512]{1,0:T(8,128)S(1)}, u32[]{:S(2)}, u32[]{:S(2)}) collective-permute-start(f32[136,512]{1,0:T(8,128)S(1)} %get-tuple-element.104), channel_id=1, source_target_pairs={{0,1},{1,2},{2,3},{3,0},{4,5},{5,6},{6,7},{7,4},{8,9},{9,10},{10,1... | collective-permute-start | bytes 835592 | tf_op jit(solution)/shard_map/ppermute | solution.py:499
  26.4 12.9 %collective-permute-start.6 = (f32[136,512]{1,0:T(8,128)S(1)}, f32[136,512]{1,0:T(8,128)S(1)}, u32[]{:S(2)}, u32[]{:S(2)}) collective-permute-start(f32[136,512]{1,0:T(8,128)S(1)} %get-tuple-element.106), channel_id=1, source_target_pairs={{0,3},{1,0},{2,1},{3,2},{4,7},{5,4},{6,5},{7,6},{8,11},{9,8},{10,9... | collective-permute-start | bytes 835592 | tf_op jit(solution)/shard_map/ppermute | solution.py:499
  33.5 13.4 %all-to-all-start = ((f32[32,16,128]{2,1,0:T(8,128)}), f32[32,16,128]{2,1,0:T(8,128)S(1)}, u32[]{:S(2)}, u32[]{:S(2)}) async-start(f32[32,16,128]{2,1,0:T(8,128)} %get-tuple-element.102), calls=%async_computation | async-start | bytes 524288 | tf_op jit(solution)/shard_map/all_to_all | solution.py:513
  39.2 6.8 %collective-permute-start = (bf16[128,512]{1,0:T(8,128)(2,1)S(1)}, bf16[128,512]{1,0:T(8,128)(2,1)S(1)}, u32[]{:S(2)}, u32[]{:S(2)}) collective-permute-start(bf16[128,512]{1,0:T(8,128)(2,1)S(1)} %fusion.d0), channel_id=1, source_target_pairs={{0,1},{1,2},{2,3},{3,0},{4,5},{5,6},{6,7},{7,4},{8,9},{9,10},{10,1... | collective-permute-start | bytes 393224 | tf_op jit(solution)/shard_map/ppermute | solution.py:499
  49.1 17.6 %collective-permute-start.7 = (f32[128,512]{1,0:T(8,128)S(1)}, f32[128,512]{1,0:T(8,128)S(1)}, u32[]{:S(2)}, u32[]{:S(2)}) collective-permute-start(f32[128,512]{1,0:T(8,128)S(1)} %get-tuple-element.113), channel_id=1, source_target_pairs={{0,1},{1,2},{2,3},{3,0},{4,5},{5,6},{6,7},{7,4},{8,9},{9,10},{10,1... | collective-permute-start | bytes 786440 | tf_op jit(solution)/shard_map/ppermute | solution.py:499
  49.1 22.2 %collective-permute-start.8 = (f32[128,512]{1,0:T(8,128)S(1)}, f32[128,512]{1,0:T(8,128)S(1)}, u32[]{:S(2)}, u32[]{:S(2)}) collective-permute-start(f32[128,512]{1,0:T(8,128)S(1)} %get-tuple-element.114), channel_id=1, source_target_pairs={{0,2},{1,3},{2,0},{3,1},{4,6},{5,7},{6,4},{7,5},{8,10},{9,11},{10,... | collective-permute-start | bytes 786440 | tf_op jit(solution)/shard_map/ppermute | solution.py:499
  51.7 19.5 %collective-permute-start.9 = (f32[128,512]{1,0:T(8,128)S(1)}, f32[128,512]{1,0:T(8,128)S(1)}, u32[]{:S(2)}, u32[]{:S(2)}) collective-permute-start(f32[128,512]{1,0:T(8,128)S(1)} %get-tuple-element.115), channel_id=1, source_target_pairs={{0,3},{1,0},{2,1},{3,2},{4,7},{5,4},{6,5},{7,6},{8,11},{9,8},{10,9... | collective-permute-start | bytes 786440 | tf_op jit(solution)/shard_map/ppermute | solution.py:499
  63.3 8.0 %collective-permute-start.10 = (f32[128,128]{1,0:T(8,128)S(1)}, f32[128,128]{1,0:T(8,128)S(1)}, u32[]{:S(2)}, u32[]{:S(2)}) collective-permute-start(f32[128,128]{1,0:T(8,128)S(1)} %get-tuple-element.124), channel_id=1, source_target_pairs={{0,3},{1,0},{2,1},{3,2},{4,7},{5,4},{6,5},{7,6},{8,11},{9,8},{10,9... | collective-permute-start | bytes 196616 | tf_op jit(solution)/shard_map/ppermute | solution.py:499
  66.0 6.2 %collective-permute-start.11 = (f32[128,128]{1,0:T(8,128)S(1)}, f32[128,128]{1,0:T(8,128)S(1)}, u32[]{:S(2)}, u32[]{:S(2)}) collective-permute-start(f32[128,128]{1,0:T(8,128)S(1)} %get-tuple-element.125), channel_id=1, source_target_pairs={{0,2},{1,3},{2,0},{3,1},{4,6},{5,7},{6,4},{7,5},{8,10},{9,11},{10,... | collective-permute-start | bytes 196616 | tf_op jit(solution)/shard_map/ppermute | solution.py:499
  66.7 6.2 %collective-permute-start.12 = (f32[128,128]{1,0:T(8,128)S(1)}, f32[128,128]{1,0:T(8,128)S(1)}, u32[]{:S(2)}, u32[]{:S(2)}) collective-permute-start(f32[128,128]{1,0:T(8,128)S(1)} %get-tuple-element.126), channel_id=1, source_target_pairs={{0,1},{1,2},{2,3},{3,0},{4,5},{5,6},{6,7},{7,4},{8,9},{9,10},{10,1... | collective-permute-start | bytes 196616 | tf_op jit(solution)/shard_map/ppermute | solution.py:499
  71.2 3.3 %copy-start.2 = (f32[128,512]{1,0:T(8,128)}, f32[128,512]{1,0:T(8,128)S(1)}, u32[]{:S(2)}) copy-start(f32[128,512]{1,0:T(8,128)S(1)} %collective-permute-done.9.rest_3_.p3) | copy-start | bytes 786436
  74.5 13.6 %all-to-all-start.1 = ((f32[32,16,128]{2,1,0:T(8,128)}), f32[32,16,128]{2,1,0:T(8,128)S(1)}, u32[]{:S(2)}, u32[]{:S(2)}) async-start(f32[32,16,128]{2,1,0:T(8,128)} %get-tuple-element.133), calls=%async_computation.1 | async-start | bytes 524288 | tf_op jit(solution)/shard_map/all_to_all | solution.py:513
  80.4 16.4 %collective-permute-start.13 = (f32[128,512]{1,0:T(8,128)}, f32[128,512]{1,0:T(8,128)}, u32[]{:S(2)}, u32[]{:S(2)}) collective-permute-start(f32[128,512]{1,0:T(8,128)} %get-tuple-element.141), channel_id=1, source_target_pairs={{4,0},{8,4},{12,8},{16,12},{20,16},{24,20},{28,24},{32,28},{36,32}... | collective-permute-start | bytes 786440 | tf_op jit(solution)/shard_map/ppermute | solution.py:508
  88.9 12.8 %all-to-all-start.2 = ((f32[32,16,128]{2,1,0:T(8,128)}), f32[32,16,128]{2,1,0:T(8,128)S(1)}, u32[]{:S(2)}, u32[]{:S(2)}) async-start(f32[32,16,128]{2,1,0:T(8,128)} %shard_map.110), calls=%async_computation.2 | async-start | bytes 524288 | tf_op jit(solution)/shard_map/all_to_all | solution.py:513
  93.9 1.0 copy-start.3
  103.0 6.4 %collective-permute-start.19 = (bf16[128,512]{1,0:T(8,128)(2,1)S(1)}, bf16[128,512]{1,0:T(8,128)(2,1)S(1)}, u32[]{:S(2)}, u32[]{:S(2)}) collective-permute-start(bf16[128,512]{1,0:T(8,128)(2,1)S(1)} %get-tuple-element.160.d0), channel_id=1, source_target_pairs={{0,3},{1,0},{2,1},{3,2},{4,7},{5,4},{6,5},{7,6},{8,11},{9,8},{10,9... | collective-permute-start | bytes 393224 | tf_op jit(solution)/shard_map/ppermute | solution.py:499
  103.7 11.8 %collective-permute-start.18 = (bf16[128,512]{1,0:T(8,128)(2,1)S(1)}, bf16[128,512]{1,0:T(8,128)(2,1)S(1)}, u32[]{:S(2)}, u32[]{:S(2)}) collective-permute-start(bf16[128,512]{1,0:T(8,128)(2,1)S(1)} %get-tuple-element.160.d0), channel_id=1, source_target_pairs={{0,2},{1,3},{2,0},{3,1},{4,6},{5,7},{6,4},{7,5},{8,10},{9,11},{10,... | collective-permute-start | bytes 393224 | tf_op jit(solution)/shard_map/ppermute | solution.py:499
  105.4 10.1 %collective-permute-start.17 = (bf16[128,512]{1,0:T(8,128)(2,1)S(1)}, bf16[128,512]{1,0:T(8,128)(2,1)S(1)}, u32[]{:S(2)}, u32[]{:S(2)}) collective-permute-start(bf16[128,512]{1,0:T(8,128)(2,1)S(1)} %get-tuple-element.160.d0), channel_id=1, source_target_pairs={{0,1},{1,2},{2,3},{3,0},{4,5},{5,6},{6,7},{7,4},{8,9},{9,10},{10,1... | collective-permute-start | bytes 393224 | tf_op jit(solution)/shard_map/ppermute | solution.py:499
  105.5 19.5 %collective-permute-start.14 = (f32[136,512]{1,0:T(8,128)S(1)}, f32[136,512]{1,0:T(8,128)S(1)}, u32[]{:S(2)}, u32[]{:S(2)}) collective-permute-start(f32[136,512]{1,0:T(8,128)S(1)} %get-tuple-element.152), channel_id=1, source_target_pairs={{0,1},{1,2},{2,3},{3,0},{4,5},{5,6},{6,7},{7,4},{8,9},{9,10},{10,1... | collective-permute-start | bytes 835592 | tf_op jit(solution)/shard_map/ppermute | solution.py:499
  107.2 17.8 %collective-permute-start.16 = (f32[136,512]{1,0:T(8,128)S(1)}, f32[136,512]{1,0:T(8,128)S(1)}, u32[]{:S(2)}, u32[]{:S(2)}) collective-permute-start(f32[136,512]{1,0:T(8,128)S(1)} %get-tuple-element.154), channel_id=1, source_target_pairs={{0,3},{1,0},{2,1},{3,2},{4,7},{5,4},{6,5},{7,6},{8,11},{9,8},{10,9... | collective-permute-start | bytes 835592 | tf_op jit(solution)/shard_map/ppermute | solution.py:499
  109.4 15.6 %collective-permute-start.15 = (f32[128,512]{1,0:T(8,128)S(1)}, f32[128,512]{1,0:T(8,128)S(1)}, u32[]{:S(2)}, u32[]{:S(2)}) collective-permute-start(f32[128,512]{1,0:T(8,128)S(1)} %get-tuple-element.153), channel_id=1, source_target_pairs={{0,2},{1,3},{2,0},{3,1},{4,6},{5,7},{6,4},{7,5},{8,10},{9,11},{10,... | collective-permute-start | bytes 786440 | tf_op jit(solution)/shard_map/ppermute | solution.py:499
  129.3 17.1 %collective-permute-start.20 = (f32[160,512]{1,0:T(8,128)S(1)}, f32[160,512]{1,0:T(8,128)S(1)}, u32[]{:S(2)}, u32[]{:S(2)}) collective-permute-start(f32[160,512]{1,0:T(8,128)S(1)} %get-tuple-element.169), channel_id=1, source_target_pairs={{0,1},{1,2},{2,3},{3,0},{4,5},{5,6},{6,7},{7,4},{8,9},{9,10},{10,1... | collective-permute-start | bytes 983048 | tf_op jit(solution)/shard_map/ppermute | solution.py:499
  129.4 17.0 %collective-permute-start.21 = (f32[160,512]{1,0:T(8,128)S(1)}, f32[160,512]{1,0:T(8,128)S(1)}, u32[]{:S(2)}, u32[]{:S(2)}) collective-permute-start(f32[160,512]{1,0:T(8,128)S(1)} %get-tuple-element.170), channel_id=1, source_target_pairs={{0,2},{1,3},{2,0},{3,1},{4,6},{5,7},{6,4},{7,5},{8,10},{9,11},{10,... | collective-permute-start | bytes 983048 | tf_op jit(solution)/shard_map/ppermute | solution.py:499
  131.7 15.3 %collective-permute-start.22 = (f32[160,512]{1,0:T(8,128)S(1)}, f32[160,512]{1,0:T(8,128)S(1)}, u32[]{:S(2)}, u32[]{:S(2)}) collective-permute-start(f32[160,512]{1,0:T(8,128)S(1)} %get-tuple-element.171), channel_id=1, source_target_pairs={{0,3},{1,0},{2,1},{3,2},{4,7},{5,4},{6,5},{7,6},{8,11},{9,8},{10,9... | collective-permute-start | bytes 983048 | tf_op jit(solution)/shard_map/ppermute | solution.py:499
  133.7 14.8 %all-to-all-start.3 = ((f32[32,16,128]{2,1,0:T(8,128)}), f32[32,16,128]{2,1,0:T(8,128)S(1)}, u32[]{:S(2)}, u32[]{:S(2)}) async-start(f32[32,16,128]{2,1,0:T(8,128)} %get-tuple-element.155), calls=%async_computation.3 | async-start | bytes 524288 | tf_op jit(solution)/shard_map/all_to_all | solution.py:513
  148.5 12.9 %all-to-all-start.4 = ((f32[32,16,128]{2,1,0:T(8,128)}), f32[32,16,128]{2,1,0:T(8,128)S(1)}, u32[]{:S(2)}, u32[]{:S(2)}) async-start(f32[32,16,128]{2,1,0:T(8,128)} %get-tuple-element.179), calls=%async_computation.4 | async-start | bytes 524288 | tf_op jit(solution)/shard_map/all_to_all | solution.py:513
  153.7 17.3 %collective-permute-start.23 = (f32[128,512]{1,0:T(8,128)S(1)}, f32[128,512]{1,0:T(8,128)S(1)}, u32[]{:S(2)}, u32[]{:S(2)}) collective-permute-start(f32[128,512]{1,0:T(8,128)S(1)} %get-tuple-element.187), channel_id=1, source_target_pairs={{4,0},{8,4},{12,8},{16,12},{20,16},{24,20},{28,24},{32,28},{36,32}... | collective-permute-start | bytes 786440 | tf_op jit(solution)/shard_map/ppermute | solution.py:508
  162.2 12.8 %all-to-all-start.5 = ((f32[32,16,128]{2,1,0:T(8,128)}), f32[32,16,128]{2,1,0:T(8,128)S(1)}, u32[]{:S(2)}, u32[]{:S(2)}) async-start(f32[32,16,128]{2,1,0:T(8,128)} %shard_map.118), calls=%async_computation.5 | async-start | bytes 524288 | tf_op jit(solution)/shard_map/all_to_all | solution.py:513
  170.0 1.0 copy-start
  175.0 1.2 copy-start.1
Sparse Core Ops, SparseCore 0:
  10.3 48.2 all-gather.1

commit v9 on v8

--- a/solution.py
+++ b/solution.py
@@ -59,6 +59,10 @@
     return jnp.concatenate(parts, axis=1)
 
 
+def far_first(blocks):
+    return (blocks[0], blocks[2], blocks[1], blocks[3])
+
+
 def decay_of(value, damping):
     return 1.0 - (damping + DRAG_RATE * jnp.abs(value))
 
@@ -68,6 +72,8 @@
     rows = slice(0, height) if i is None else pl.ds(pl.multiple_of(i * height, height), height)
     for r, ref in enumerate(outs):
         ref[rows, :] = source[lax.rem(place[0] + r, count)]
+        if 1 < r < count - 1:
+            ref[ref.shape[0] - EDGE :, :] = jnp.zeros((EDGE, ref.shape[1]), F32)
 
 
 def send_edges(current, outs, first=True, last=True):
@@ -155,7 +161,7 @@
 
 
 def far_solve_kernel(
-    place, x0, x1, x2, x3, high_far, low_far, inverse_far, p0, p1, p2, p3,
+    place, x0, x2, x1, x3, high_far, low_far, inverse_far, p0, p1, p2, p3,
     plane, high, low, inverse, arrivals,
 ):
     copies = [
@@ -168,7 +174,7 @@
 
 
 def near_solve_kernel(
-    place, x0, x1, x2, x3, high, low, inverse, f0, f1, f2, f3, p0, p1, p2, p3, plane
+    place, x0, x2, x1, x3, high, low, inverse, f0, f1, f2, f3, p0, p1, p2, p3, plane
 ):
     forces = (f0, f1, f2, f3)
     solve(place, (x0, x1, x2, x3), (high, low, inverse), forces, (p0, p1, p2, p3), plane)
@@ -284,7 +290,7 @@
 
 def offset_kernel(place, *rest):
     c = place[0]
-    pieces = rest[:4]
+    pieces = far_first(rest[:4])
     *forces, weights, base, force_weight, lead, force, offset = rest[4:]
     count, height, full = weights.shape
     width = full // count
@@ -493,7 +499,7 @@
     plane = (height, width)
     edged = (height + EDGE, width)
     chunks = (march_size, height * width // march_size // LANE, LANE)
-    sources = [near(plane), near(edged), near(plane), near(edged)]
+    sources = [near(plane)] + [near(edged)] * (cross_size - 1)
 
     def turn(value, steps):
         return lax.ppermute(
@@ -555,13 +561,14 @@
         )
         solve_cost = cost(3 * 8 * width**3, 5 * MIB)
         if merged:
-            scale, *arrived = lax.optimization_barrier((scale, *arrived))
+            scale, *arrived = lax.optimization_barrier((scale, *far_first(arrived)))
+            arrived = far_first(arrived)
             made = disc_forces(rows, where, blades, tabled)
             forces, near_tables = made[:cross_size], made[cross_size:]
             solved = call(
                 near_solve_kernel,
                 [near((height + height * LANE // width, width))] * cross_size,
-                (place, *arrived, *near_tables, *forces),
+                (place, *far_first(arrived), *near_tables, *forces),
                 solve_cost,
                 scalars=1,
                 limit=16,
@@ -581,7 +588,7 @@
                 + [pltpu.VMEM((width, width), F32), pltpu.SemaphoreType.DMA((3,))],
                 compiler_params=pltpu.CompilerParams(vmem_limit_bytes=20 * MIB),
                 cost_estimate=solve_cost,
-            )(place, *arrived, *tabled)
+            )(place, *far_first(arrived), *tabled)
             rows, scales, solved, where = lax.optimization_barrier((rows, scales, solved, where))
             forces = turns(disc_forces(rows, where, blades), -1)
         pieces = turns(solved)
@@ -599,7 +606,7 @@
         lead, force, offset = call(
             offset_kernel,
             [near(plane), far(plane), far(chunks)],
-            (place, *pieces, *forces, weights, base, force_weight),
+            (place, *far_first(pieces), *forces, weights, base, force_weight),
             cost(2e6, 3 * MIB),
             scalars=1,
             limit=12,

time: 188 us -> 189 us (level)
  starting transfers between devices: 73.4 us -> 75.7 us
    ppermute x21, starting transfers between devices: 31 us -> 33.4 us  [turn(): lax.ppermute(value, 'cross', [(i, (i + steps) % cross_size) for i in rang...]
  transfers between devices with their start and end apart: 31 -> 31, of which waited for: 14 -> 13; matrix products, arithmetic and copies ran while one was open for 3% -> 3% of each run, Pallas kernels for 22% -> 22%
where the time goes in v9:
time: 189 us; the launch traced here: 186 us
  starting transfers between devices  75.7 us (40%)
  Pallas kernels  50.2 us (27%)
  waiting for transfers between devices  37.6 us (20%)
  between operations  14.3 us (8%)
  local copies, waits for them, and re-layouts  7.19 us (4%)
    ppermute x21, starting transfers between devices, turn(): lax.ppermute(value, 'cross', [(i, (i + steps) % cross_size) for i in rang...  33.4 us
    all_to_all x6, starting transfers between devices, across_march(): lax.all_to_all(value, 'march', split_axis=0, concat_axis=0, tiled=True)  31.8 us
    pallas_call x11, Pallas kernels, call(): pl.pallas_call(kernel, out_shape=outs, in_specs=[SMEM] * scalars + [VMEM]...  24 us
    all_to_all x6, waiting for transfers between devices, across_march(): lax.all_to_all(value, 'march', split_axis=0, concat_axis=0, tiled=True)  16.7 us
    ppermute x21, waiting for transfers between devices, turn(): lax.ppermute(value, 'cross', [(i, (i + steps) % cross_size) for i in rang...  11.3 us
    pallas_call x3, Pallas kernels, by_rows(): pl.pallas_call(kernel, grid_spec=pltpu.PrefetchScalarGridSpec(num_scalar_...  11.2 us
    ppermute x3, starting transfers between devices, along_march(): lax.ppermute(value, 'march', [(i, i + steps) for i in range(count) if 0 <...  10.6 us
    pallas_call x2, Pallas kernels, disc_forces(): pl.pallas_call(disc_kernel, grid=(number // per_step,), out_shape=[near((...  9.46 us
  transfers between devices with their start and end apart: 31, of which 13 were waited for; matrix products, arithmetic and copies ran while one was open for 3% of the time, Pallas kernels for 22%

profile of v9, /device:TPU:2, one launch (start us, length us, event | category | flops | bytes accessed | tf_op | source)
XLA Modules:
  0.0 185.8 jit_solution(13764346707297584225)
XLA Ops:
  7.9 1.0 slice_bitcast_fusion
  8.9 1.9 %collective-permute-start.3 = (f32[128,512]{1,0:T(8,128)S(1)}, f32[128,512]{1,0:T(8,128)S(1)}, u32[]{:S(2)}, u32[]{:S(2)}) collective-permute-start(f32[128,512]{1,0:T(8,128)S(1)} %slice_bitcast_fusion), channel_id=1, source_target_pairs={{0,4},{4,8},{8,12},{12,16},{16,20},{20,24},{24,28},{28,32},{32,36}... | collective-permute-start | bytes 786440 | tf_op jit(solution)/shard_map/ppermute | solution.py:514
  11.8 4.1 %collective-permute-start.2 = (bf16[128,512]{1,0:T(8,128)(2,1)S(1)}, bf16[128,512]{1,0:T(8,128)(2,1)S(1)}, u32[]{:S(2)}, u32[]{:S(2)}) collective-permute-start(bf16[128,512]{1,0:T(8,128)(2,1)S(1)} %fusion.d0), channel_id=1, source_target_pairs={{0,3},{1,0},{2,1},{3,2},{4,7},{5,4},{6,5},{7,6},{8,11},{9,8},{10,9... | collective-permute-start | bytes 393224 | tf_op jit(solution)/shard_map/ppermute | solution.py:505
  16.0 2.7 %collective-permute-done.3.upstream = f32[128,512]{1,0:T(8,128)S(1)} collective-permute-done((f32[128,512]{1,0:T(8,128)S(1)}, f32[128,512]{1,0:T(8,128)S(1)}, u32[]{:S(2)}, u32[]{:S(2)}) %collective-permute-start.3) | collective-permute-done | bytes 262176 | tf_op jit(solution)/shard_map/ppermute | solution.py:514
  18.7 2.7 %shard_map.104 = (f32[128,512]{1,0:T(8,128)S(1)}, f32[136,512]{1,0:T(8,128)S(1)}, f32[136,512]{1,0:T(8,128)S(1)}, f32[136,512]{1,0:T(8,128)S(1)}) custom-call(s32[4]{0:T(128)S(1)} %pad_add_fusion.place, f32[4,128,512]{2,1,0:T(8,128)} %current.4, f32[128,512]{1,0:T(8,128)S(1)} %collective-permute-done.3.upstream, f32[128,512]{1,0:T(8,128)} %inflow.9), custom_call_target="tpu_custom_call" | custom-call | flops 1000000 | bytes 2097152 | tf_op jit(solution)/shard_map/pallas_call | solution.py:436
  21.4 4.0 %collective-permute-start.4 = (f32[136,512]{1,0:T(8,128)S(1)}, f32[136,512]{1,0:T(8,128)S(1)}, u32[]{:S(2)}, u32[]{:S(2)}) collective-permute-start(f32[136,512]{1,0:T(8,128)S(1)} %get-tuple-element.104), channel_id=1, source_target_pairs={{0,2},{1,3},{2,0},{3,1},{4,6},{5,7},{6,4},{7,5},{8,10},{9,11},{10,... | collective-permute-start | bytes 835592 | tf_op jit(solution)/shard_map/ppermute | solution.py:505
  25.4 1.0 collective-permute-start.5
  26.4 2.2 %collective-permute-start.6 = (f32[136,512]{1,0:T(8,128)S(1)}, f32[136,512]{1,0:T(8,128)S(1)}, u32[]{:S(2)}, u32[]{:S(2)}) collective-permute-start(f32[136,512]{1,0:T(8,128)S(1)} %get-tuple-element.106), channel_id=1, source_target_pairs={{0,3},{1,0},{2,1},{3,2},{4,7},{5,4},{6,5},{7,6},{8,11},{9,8},{10,9... | collective-permute-start | bytes 835592 | tf_op jit(solution)/shard_map/ppermute | solution.py:505
  29.3 4.2 %shard_map.105 = (f32[4,128,512]{2,1,0:T(8,128)}, f32[32,16,128]{2,1,0:T(8,128)}) custom-call(s32[4]{0:T(128)S(1)} %pad_add_fusion.place, f32[4,128,512]{2,1,0:T(8,128)} %current.4, f32[4,128,512]{2,1,0:T(8,128)} %damping.1), custom_call_target="tpu_custom_call" | custom-call | flops 4000000 | bytes 3145728 | tf_op jit(solution)/shard_map/pallas_call | solution.py:436
  33.5 5.7 %all-to-all-start = ((f32[32,16,128]{2,1,0:T(8,128)}), f32[32,16,128]{2,1,0:T(8,128)S(1)}, u32[]{:S(2)}, u32[]{:S(2)}) async-start(f32[32,16,128]{2,1,0:T(8,128)} %get-tuple-element.102), calls=%async_computation | async-start | bytes 524288 | tf_op jit(solution)/shard_map/all_to_all | solution.py:519
  39.3 5.6 %shard_map.106 = (f32[128,512]{1,0:T(8,128)S(1)}, f32[128,512]{1,0:T(8,128)S(1)}, f32[128,512]{1,0:T(8,128)S(1)}, f32[128,512]{1,0:T(8,128)S(1)}) custom-call(s32[4]{0:T(128)S(1)} %pad_add_fusion.place, f32[128,512]{1,0:T(8,128)S(1)} %get-tuple-element.103.x0, f32[136,512]{1,0:T(8,128)S(1)} %collective-permute-done.4.x2, ...), custom_call_target="tpu_custom_call" | custom-call | flops 3221225472 | bytes 5242880 | tf_op jit(solution)/shard_map/pallas_call | solution.py:581
  44.9 1.1 collective-permute-done.d1
  49.1 2.0 %collective-permute-start.8 = (f32[128,512]{1,0:T(8,128)S(1)}, f32[128,512]{1,0:T(8,128)S(1)}, u32[]{:S(2)}, u32[]{:S(2)}) collective-permute-start(f32[128,512]{1,0:T(8,128)S(1)} %get-tuple-element.114), channel_id=1, source_target_pairs={{0,1},{1,2},{2,3},{3,0},{4,5},{5,6},{6,7},{7,4},{8,9},{9,10},{10,1... | collective-permute-start | bytes 786440 | tf_op jit(solution)/shard_map/ppermute | solution.py:505
  51.1 1.2 collective-permute-start.9
  52.3 6.2 %all-gather.2.cloned.1.call-done.rest_0_.rest_1_.rest_2_.rest_3_ = bf16[32,512,128]{2,1,0:T(8,128)(2,1)} async-done(((bf16[1,512,128]{2,1,0:T(8,128)(2,1)}), bf16[32,512,128]{2,1,0:T(8,128)(2,1)}) %all-gather.2.cloned.1.call-update) | async-done | bytes 4194320 | tf_op jit(solution)/shard_map/all_gather | solution.py:521
  58.6 4.7 %shard_map.107 = (f32[128,128]{1,0:T(8,128)S(1)}, f32[128,128]{1,0:T(8,128)S(1)}, f32[128,128]{1,0:T(8,128)S(1)}, f32[128,128]{1,0:T(8,128)S(1)}) custom-call(bf16[128,512]{1,0:T(8,128)(2,1)S(1)} %fusion.d0, bf16[128,512]{1,0:T(8,128)(2,1)S(1)} %collective-permute-done.d1, bf16[128,512]{1,0:T(8,128)(2,1)S(1)} %collective-permute-done.1.d2, ...), custom_call_target="tpu_custom_call" | custom-call | flops 2147483648 | bytes 5242880 | tf_op jit(solution)/shard_map/pallas_call | solution.py:459
  63.3 2.7 %collective-permute-start.10 = (f32[128,128]{1,0:T(8,128)S(1)}, f32[128,128]{1,0:T(8,128)S(1)}, u32[]{:S(2)}, u32[]{:S(2)}) collective-permute-start(f32[128,128]{1,0:T(8,128)S(1)} %get-tuple-element.124), channel_id=1, source_target_pairs={{0,3},{1,0},{2,1},{3,2},{4,7},{5,4},{6,5},{7,6},{8,11},{9,8},{10,9... | collective-permute-start | bytes 196616 | tf_op jit(solution)/shard_map/ppermute | solution.py:505
  67.6 3.6 %shard_map.108 = (f32[4,128,512]{2,1,0:T(8,128)}, f32[4,128,512]{2,1,0:T(8,128)S(1)}, f32[128,512]{1,0:T(8,128)S(1)}, f32[128,512]{1,0:T(8,128)S(1)}) custom-call(s32[4]{0:T(128)S(1)} %pad_add_fusion.place, f32[4,128,512]{2,1,0:T(8,128)} %current.4, f32[136,512]{1,0:T(8,128)S(1)} %collective-permute-done.5.x1.before, ...), custom_call_target="tpu_custom_call" | custom-call | flops 8000000 | bytes 4194304 | tf_op jit(solution)/shard_map/pallas_call | solution.py:412
  72.9 1.7 shard_map.109
  74.5 5.9 %all-to-all-start.1 = ((f32[32,16,128]{2,1,0:T(8,128)}), f32[32,16,128]{2,1,0:T(8,128)S(1)}, u32[]{:S(2)}, u32[]{:S(2)}) async-start(f32[32,16,128]{2,1,0:T(8,128)} %get-tuple-element.133), calls=%async_computation.1 | async-start | bytes 524288 | tf_op jit(solution)/shard_map/all_to_all | solution.py:519
  80.4 4.3 %collective-permute-start.13 = (f32[128,512]{1,0:T(8,128)}, f32[128,512]{1,0:T(8,128)}, u32[]{:S(2)}, u32[]{:S(2)}) collective-permute-start(f32[128,512]{1,0:T(8,128)} %get-tuple-element.141), channel_id=1, source_target_pairs={{4,0},{8,4},{12,8},{16,12},{20,16},{24,20},{28,24},{32,28},{36,32}... | collective-permute-start | bytes 786440 | tf_op jit(solution)/shard_map/ppermute | solution.py:514
  84.8 3.4 %all-to-all-done.1.offset = f32[32,16,128]{2,1,0:T(8,128)S(1)} async-done(((f32[32,16,128]{2,1,0:T(8,128)}), f32[32,16,128]{2,1,0:T(8,128)S(1)}, u32[]{:S(2)}, u32[]{:S(2)}) %all-to-all-start.1) | async-done | bytes 262176 | tf_op jit(solution)/shard_map/all_to_all | solution.py:519
  88.9 5.0 %all-to-all-start.2 = ((f32[32,16,128]{2,1,0:T(8,128)}), f32[32,16,128]{2,1,0:T(8,128)S(1)}, u32[]{:S(2)}, u32[]{:S(2)}) async-start(f32[32,16,128]{2,1,0:T(8,128)} %shard_map.110), calls=%async_computation.2 | async-start | bytes 524288 | tf_op jit(solution)/shard_map/all_to_all | solution.py:519
  94.9 1.9 %shard_map.111 = (f32[5,128,512]{2,1,0:T(8,128)S(1)}, f32[4,128,512]{2,1,0:T(8,128)S(1)}) custom-call(s32[4]{0:T(128)S(1)} %pad_add_fusion.place, f32[128,512]{1,0:T(8,128)S(1)} %get-tuple-element.134.rest_0_.p0, f32[128,512]{1,0:T(8,128)S(1)} %collective-permute-done.8.rest_2_.p1, f32[128,512]{1,0:T(8,128)S(1)} %collective-permute-done.7.rest_1_.p2, ...), custom_call_target="tpu_custom_call" | custom-call | flops 4000000 | bytes 4194304 | tf_op jit(solution)/shard_map/pallas_call | solution.py:412
  96.9 4.9 %all-to-all-done.2.entering = f32[32,16,128]{2,1,0:T(8,128)S(1)} async-done(((f32[32,16,128]{2,1,0:T(8,128)}), f32[32,16,128]{2,1,0:T(8,128)S(1)}, u32[]{:S(2)}, u32[]{:S(2)}) %all-to-all-start.2) | async-done | bytes 262176 | tf_op jit(solution)/shard_map/all_to_all | solution.py:519
  101.7 1.2 shard_map.112
  103.7 1.6 collective-permute-start.18
  105.5 3.7 %collective-permute-start.14 = (f32[136,512]{1,0:T(8,128)S(1)}, f32[136,512]{1,0:T(8,128)S(1)}, u32[]{:S(2)}, u32[]{:S(2)}) collective-permute-start(f32[136,512]{1,0:T(8,128)S(1)} %get-tuple-element.152), channel_id=1, source_target_pairs={{0,2},{1,3},{2,0},{3,1},{4,6},{5,7},{6,4},{7,5},{8,10},{9,11},{10,... | collective-permute-start | bytes 835592 | tf_op jit(solution)/shard_map/ppermute | solution.py:505
  109.5 3.0 %collective-permute-start.16 = (f32[136,512]{1,0:T(8,128)S(1)}, f32[136,512]{1,0:T(8,128)S(1)}, u32[]{:S(2)}, u32[]{:S(2)}) collective-permute-start(f32[136,512]{1,0:T(8,128)S(1)} %get-tuple-element.154), channel_id=1, source_target_pairs={{0,3},{1,0},{2,1},{3,2},{4,7},{5,4},{6,5},{7,6},{8,11},{9,8},{10,9... | collective-permute-start | bytes 835592 | tf_op jit(solution)/shard_map/ppermute | solution.py:505
  112.5 4.2 %shard_map.113 = (f32[4,128,512]{2,1,0:T(8,128)}, f32[32,16,128]{2,1,0:T(8,128)}, f32[4,128,512]{2,1,0:T(8,128)}) custom-call(s32[4]{0:T(128)S(1)} %pad_add_fusion.place, f32[4,128,512]{2,1,0:T(8,128)S(1)} %get-tuple-element.148.current, f32[4,128,512]{2,1,0:T(8,128)} %damping.1), custom_call_target="tpu_custom_call" | custom-call | flops 4000000 | bytes 3145728 | tf_op jit(solution)/shard_map/pallas_call | solution.py:436
  116.7 2.2 %collective-permute-done.17.d1 = bf16[128,512]{1,0:T(8,128)(2,1)S(1)} collective-permute-done((bf16[128,512]{1,0:T(8,128)(2,1)S(1)}, bf16[128,512]{1,0:T(8,128)(2,1)S(1)}, u32[]{:S(2)}, u32[]{:S(2)}) %collective-permute-start.17) | collective-permute-done | bytes 131104 | tf_op jit(solution)/shard_map/ppermute | solution.py:505
  118.9 4.8 %shard_map.114 = (f32[128,128]{1,0:T(8,128)S(1)}, f32[128,128]{1,0:T(8,128)S(1)}, f32[128,128]{1,0:T(8,128)S(1)}, f32[128,128]{1,0:T(8,128)S(1)}, bf16[512,512]{...) custom-call(bf16[128,512]{1,0:T(8,128)(2,1)S(1)} %get-tuple-element.160.d0, ...), custom_call_target="tpu_custom_call" | custom-call | flops 2147483648 | bytes 5242880 | tf_op jit(solution)/shard_map/pallas_call | solution.py:459
  123.7 1.7 collective-permute-done.15.x1.before
  125.4 5.0 %shard_map.115 = (f32[160,512]{1,0:T(8,128)S(1)}, f32[160,512]{1,0:T(8,128)S(1)}, f32[160,512]{1,0:T(8,128)}, f32[160,512]{1,0:T(8,128)S(1)}) custom-call(s32[4]{0:T(128)S(1)} %pad_add_fusion.place, f32[128,512]{1,0:T(8,128)S(1)} %get-tuple-element.156.x0, f32[136,512]{1,0:T(8,128)S(1)} %collective-permute-done.14.x2, ...), custom_call_target="tpu_custom_call" | custom-call | flops 3221225472 | bytes 5242880 | tf_op jit(solution)/shard_map/pallas_call | solution.py:412
  130.4 1.7 collective-permute-start.20
  132.0 3.2 %collective-permute-start.22 = (f32[160,512]{1,0:T(8,128)S(1)}, f32[160,512]{1,0:T(8,128)S(1)}, u32[]{:S(2)}, u32[]{:S(2)}) collective-permute-start(f32[160,512]{1,0:T(8,128)S(1)} %get-tuple-element.171), channel_id=1, source_target_pairs={{0,3},{1,0},{2,1},{3,2},{4,7},{5,4},{6,5},{7,6},{8,11},{9,8},{10,9... | collective-permute-start | bytes 983048 | tf_op jit(solution)/shard_map/ppermute | solution.py:505
  135.3 5.1 %all-to-all-start.3 = ((f32[32,16,128]{2,1,0:T(8,128)}), f32[32,16,128]{2,1,0:T(8,128)S(1)}, u32[]{:S(2)}, u32[]{:S(2)}) async-start(f32[32,16,128]{2,1,0:T(8,128)} %get-tuple-element.155), calls=%async_computation.3 | async-start | bytes 524288 | tf_op jit(solution)/shard_map/all_to_all | solution.py:519
  140.3 3.6 %shard_map.116 = (f32[4,128,512]{2,1,0:T(8,128)}, f32[4,128,512]{2,1,0:T(8,128)S(1)}, f32[128,512]{1,0:T(8,128)S(1)}, f32[128,512]{1,0:T(8,128)S(1)}) custom-call(s32[4]{0:T(128)S(1)} %pad_add_fusion.place, f32[4,128,512]{2,1,0:T(8,128)} %get-tuple-element.172.current, f32[136,512]{1,0:T(8,128)S(1)} %collective-permute-done.15.x1.before, ...), custom_call_target="tpu_custom_call" | custom-call | flops 8000000 | bytes 4194304 | tf_op jit(solution)/shard_map/pallas_call | solution.py:412
  144.0 4.6 %collective-permute-done.21.rest_2_.p1 = f32[160,512]{1,0:T(8,128)S(1)} collective-permute-done((f32[160,512]{1,0:T(8,128)S(1)}, f32[160,512]{1,0:T(8,128)S(1)}, u32[]{:S(2)}, u32[]{:S(2)}) %collective-permute-start.21) | collective-permute-done | bytes 327712 | tf_op jit(solution)/shard_map/ppermute | solution.py:505
  148.6 1.5 shard_map.117
  150.1 5.1 %all-to-all-start.4 = ((f32[32,16,128]{2,1,0:T(8,128)}), f32[32,16,128]{2,1,0:T(8,128)S(1)}, u32[]{:S(2)}, u32[]{:S(2)}) async-start(f32[32,16,128]{2,1,0:T(8,128)} %get-tuple-element.179), calls=%async_computation.4 | async-start | bytes 524288 | tf_op jit(solution)/shard_map/all_to_all | solution.py:519
  155.2 4.3 %collective-permute-start.23 = (f32[128,512]{1,0:T(8,128)S(1)}, f32[128,512]{1,0:T(8,128)S(1)}, u32[]{:S(2)}, u32[]{:S(2)}) collective-permute-start(f32[128,512]{1,0:T(8,128)S(1)} %get-tuple-element.187), channel_id=1, source_target_pairs={{4,0},{8,4},{12,8},{16,12},{20,16},{24,20},{28,24},{32,28},{36,32}... | collective-permute-start | bytes 786440 | tf_op jit(solution)/shard_map/ppermute | solution.py:514
  159.6 3.5 %all-to-all-done.4.offset = f32[32,16,128]{2,1,0:T(8,128)S(1)} async-done(((f32[32,16,128]{2,1,0:T(8,128)}), f32[32,16,128]{2,1,0:T(8,128)S(1)}, u32[]{:S(2)}, u32[]{:S(2)}) %all-to-all-start.4) | async-done | bytes 262176 | tf_op jit(solution)/shard_map/all_to_all | solution.py:519
  163.8 5.0 %all-to-all-start.5 = ((f32[32,16,128]{2,1,0:T(8,128)}), f32[32,16,128]{2,1,0:T(8,128)S(1)}, u32[]{:S(2)}, u32[]{:S(2)}) async-start(f32[32,16,128]{2,1,0:T(8,128)} %shard_map.118), calls=%async_computation.5 | async-start | bytes 524288 | tf_op jit(solution)/shard_map/all_to_all | solution.py:519
  168.8 2.8 %shard_map.119 = (f32[4,128,512]{2,1,0:T(8,128)S(1)}, f32[4,128,512]{2,1,0:T(8,128)S(1)}, f32[4,128,512]{2,1,0:T(8,128)}) custom-call(s32[4]{0:T(128)S(1)} %pad_add_fusion.place, f32[160,512]{1,0:T(8,128)S(1)} %get-tuple-element.180.rest_0_.p0, f32[160,512]{1,0:T(8,128)S(1)} %collective-permute-done.21.rest_2_.p1, ...), custom_call_target="tpu_custom_call" | custom-call | flops 4000000 | bytes 4194304 | tf_op jit(solution)/shard_map/pallas_call | solution.py:412
  172.6 4.1 %all-to-all-done.5.entering = f32[32,16,128]{2,1,0:T(8,128)S(1)} async-done(((f32[32,16,128]{2,1,0:T(8,128)}), f32[32,16,128]{2,1,0:T(8,128)S(1)}, u32[]{:S(2)}, u32[]{:S(2)}) %all-to-all-start.5) | async-done | bytes 262176 | tf_op jit(solution)/shard_map/all_to_all | solution.py:519
  176.6 1.2 copy-done.1
  177.8 1.1 shard_map.120
  (48 shorter events, 13.4 us)
Async XLA Ops:
  7.2 51.4 %all-gather.2.cloned.1.call-start = ((), (), s32[]{:S(2)}) async-start(), calls=%async_computation.6 | async-start | bytes 4325376 | tf_op jit(solution)/shard_map/all_gather | solution.py:521
  8.9 9.8 %collective-permute-start.3 = (f32[128,512]{1,0:T(8,128)S(1)}, f32[128,512]{1,0:T(8,128)S(1)}, u32[]{:S(2)}, u32[]{:S(2)}) collective-permute-start(f32[128,512]{1,0:T(8,128)S(1)} %slice_bitcast_fusion), channel_id=1, source_target_pairs={{0,4},{4,8},{8,12},{12,16},{16,20},{20,24},{24,28},{28,32},{32,36}... | collective-permute-start | bytes 786440 | tf_op jit(solution)/shard_map/ppermute | solution.py:514
  11.8 33.1 %collective-permute-start.2 = (bf16[128,512]{1,0:T(8,128)(2,1)S(1)}, bf16[128,512]{1,0:T(8,128)(2,1)S(1)}, u32[]{:S(2)}, u32[]{:S(2)}) collective-permute-start(bf16[128,512]{1,0:T(8,128)(2,1)S(1)} %fusion.d0), channel_id=1, source_target_pairs={{0,3},{1,0},{2,1},{3,2},{4,7},{5,4},{6,5},{7,6},{8,11},{9,8},{10,9... | collective-permute-start | bytes 393224 | tf_op jit(solution)/shard_map/ppermute | solution.py:505
  15.9 29.0 %collective-permute-start.1 = (bf16[128,512]{1,0:T(8,128)(2,1)S(1)}, bf16[128,512]{1,0:T(8,128)(2,1)S(1)}, u32[]{:S(2)}, u32[]{:S(2)}) collective-permute-start(bf16[128,512]{1,0:T(8,128)(2,1)S(1)} %fusion.d0), channel_id=1, source_target_pairs={{0,2},{1,3},{2,0},{3,1},{4,6},{5,7},{6,4},{7,5},{8,10},{9,11},{10,... | collective-permute-start | bytes 393224 | tf_op jit(solution)/shard_map/ppermute | solution.py:505
  21.4 17.8 %collective-permute-start.4 = (f32[136,512]{1,0:T(8,128)S(1)}, f32[136,512]{1,0:T(8,128)S(1)}, u32[]{:S(2)}, u32[]{:S(2)}) collective-permute-start(f32[136,512]{1,0:T(8,128)S(1)} %get-tuple-element.104), channel_id=1, source_target_pairs={{0,2},{1,3},{2,0},{3,1},{4,6},{5,7},{6,4},{7,5},{8,10},{9,11},{10,... | collective-permute-start | bytes 835592 | tf_op jit(solution)/shard_map/ppermute | solution.py:505
  25.4 13.9 %collective-permute-start.5 = (f32[136,512]{1,0:T(8,128)S(1)}, f32[136,512]{1,0:T(8,128)S(1)}, u32[]{:S(2)}, u32[]{:S(2)}) collective-permute-start(f32[136,512]{1,0:T(8,128)S(1)} %get-tuple-element.105), channel_id=1, source_target_pairs={{0,1},{1,2},{2,3},{3,0},{4,5},{5,6},{6,7},{7,4},{8,9},{9,10},{10,1... | collective-permute-start | bytes 835592 | tf_op jit(solution)/shard_map/ppermute | solution.py:505
  26.4 12.9 %collective-permute-start.6 = (f32[136,512]{1,0:T(8,128)S(1)}, f32[136,512]{1,0:T(8,128)S(1)}, u32[]{:S(2)}, u32[]{:S(2)}) collective-permute-start(f32[136,512]{1,0:T(8,128)S(1)} %get-tuple-element.106), channel_id=1, source_target_pairs={{0,3},{1,0},{2,1},{3,2},{4,7},{5,4},{6,5},{7,6},{8,11},{9,8},{10,9... | collective-permute-start | bytes 835592 | tf_op jit(solution)/shard_map/ppermute | solution.py:505
  33.5 13.4 %all-to-all-start = ((f32[32,16,128]{2,1,0:T(8,128)}), f32[32,16,128]{2,1,0:T(8,128)S(1)}, u32[]{:S(2)}, u32[]{:S(2)}) async-start(f32[32,16,128]{2,1,0:T(8,128)} %get-tuple-element.102), calls=%async_computation | async-start | bytes 524288 | tf_op jit(solution)/shard_map/all_to_all | solution.py:519
  39.2 6.8 %collective-permute-start = (bf16[128,512]{1,0:T(8,128)(2,1)S(1)}, bf16[128,512]{1,0:T(8,128)(2,1)S(1)}, u32[]{:S(2)}, u32[]{:S(2)}) collective-permute-start(bf16[128,512]{1,0:T(8,128)(2,1)S(1)} %fusion.d0), channel_id=1, source_target_pairs={{0,1},{1,2},{2,3},{3,0},{4,5},{5,6},{6,7},{7,4},{8,9},{9,10},{10,1... | collective-permute-start | bytes 393224 | tf_op jit(solution)/shard_map/ppermute | solution.py:505
  49.1 17.6 %collective-permute-start.7 = (f32[128,512]{1,0:T(8,128)S(1)}, f32[128,512]{1,0:T(8,128)S(1)}, u32[]{:S(2)}, u32[]{:S(2)}) collective-permute-start(f32[128,512]{1,0:T(8,128)S(1)} %get-tuple-element.113), channel_id=1, source_target_pairs={{0,2},{1,3},{2,0},{3,1},{4,6},{5,7},{6,4},{7,5},{8,10},{9,11},{10,... | collective-permute-start | bytes 786440 | tf_op jit(solution)/shard_map/ppermute | solution.py:505
  49.1 22.2 %collective-permute-start.8 = (f32[128,512]{1,0:T(8,128)S(1)}, f32[128,512]{1,0:T(8,128)S(1)}, u32[]{:S(2)}, u32[]{:S(2)}) collective-permute-start(f32[128,512]{1,0:T(8,128)S(1)} %get-tuple-element.114), channel_id=1, source_target_pairs={{0,1},{1,2},{2,3},{3,0},{4,5},{5,6},{6,7},{7,4},{8,9},{9,10},{10,1... | collective-permute-start | bytes 786440 | tf_op jit(solution)/shard_map/ppermute | solution.py:505
  51.1 20.1 %collective-permute-start.9 = (f32[128,512]{1,0:T(8,128)S(1)}, f32[128,512]{1,0:T(8,128)S(1)}, u32[]{:S(2)}, u32[]{:S(2)}) collective-permute-start(f32[128,512]{1,0:T(8,128)S(1)} %get-tuple-element.115), channel_id=1, source_target_pairs={{0,3},{1,0},{2,1},{3,2},{4,7},{5,4},{6,5},{7,6},{8,11},{9,8},{10,9... | collective-permute-start | bytes 786440 | tf_op jit(solution)/shard_map/ppermute | solution.py:505
  63.3 8.0 %collective-permute-start.10 = (f32[128,128]{1,0:T(8,128)S(1)}, f32[128,128]{1,0:T(8,128)S(1)}, u32[]{:S(2)}, u32[]{:S(2)}) collective-permute-start(f32[128,128]{1,0:T(8,128)S(1)} %get-tuple-element.124), channel_id=1, source_target_pairs={{0,3},{1,0},{2,1},{3,2},{4,7},{5,4},{6,5},{7,6},{8,11},{9,8},{10,9... | collective-permute-start | bytes 196616 | tf_op jit(solution)/shard_map/ppermute | solution.py:505
  66.0 6.2 %collective-permute-start.11 = (f32[128,128]{1,0:T(8,128)S(1)}, f32[128,128]{1,0:T(8,128)S(1)}, u32[]{:S(2)}, u32[]{:S(2)}) collective-permute-start(f32[128,128]{1,0:T(8,128)S(1)} %get-tuple-element.125), channel_id=1, source_target_pairs={{0,2},{1,3},{2,0},{3,1},{4,6},{5,7},{6,4},{7,5},{8,10},{9,11},{10,... | collective-permute-start | bytes 196616 | tf_op jit(solution)/shard_map/ppermute | solution.py:505
  66.7 6.2 %collective-permute-start.12 = (f32[128,128]{1,0:T(8,128)S(1)}, f32[128,128]{1,0:T(8,128)S(1)}, u32[]{:S(2)}, u32[]{:S(2)}) collective-permute-start(f32[128,128]{1,0:T(8,128)S(1)} %get-tuple-element.126), channel_id=1, source_target_pairs={{0,1},{1,2},{2,3},{3,0},{4,5},{5,6},{6,7},{7,4},{8,9},{9,10},{10,1... | collective-permute-start | bytes 196616 | tf_op jit(solution)/shard_map/ppermute | solution.py:505
  71.2 3.3 %copy-start.2 = (f32[128,512]{1,0:T(8,128)}, f32[128,512]{1,0:T(8,128)S(1)}, u32[]{:S(2)}) copy-start(f32[128,512]{1,0:T(8,128)S(1)} %collective-permute-done.9.rest_3_.p3) | copy-start | bytes 786436
  74.5 13.6 %all-to-all-start.1 = ((f32[32,16,128]{2,1,0:T(8,128)}), f32[32,16,128]{2,1,0:T(8,128)S(1)}, u32[]{:S(2)}, u32[]{:S(2)}) async-start(f32[32,16,128]{2,1,0:T(8,128)} %get-tuple-element.133), calls=%async_computation.1 | async-start | bytes 524288 | tf_op jit(solution)/shard_map/all_to_all | solution.py:519
  80.4 16.4 %collective-permute-start.13 = (f32[128,512]{1,0:T(8,128)}, f32[128,512]{1,0:T(8,128)}, u32[]{:S(2)}, u32[]{:S(2)}) collective-permute-start(f32[128,512]{1,0:T(8,128)} %get-tuple-element.141), channel_id=1, source_target_pairs={{4,0},{8,4},{12,8},{16,12},{20,16},{24,20},{28,24},{32,28},{36,32}... | collective-permute-start | bytes 786440 | tf_op jit(solution)/shard_map/ppermute | solution.py:514
  88.9 12.8 %all-to-all-start.2 = ((f32[32,16,128]{2,1,0:T(8,128)}), f32[32,16,128]{2,1,0:T(8,128)S(1)}, u32[]{:S(2)}, u32[]{:S(2)}) async-start(f32[32,16,128]{2,1,0:T(8,128)} %shard_map.110), calls=%async_computation.2 | async-start | bytes 524288 | tf_op jit(solution)/shard_map/all_to_all | solution.py:519
  93.9 1.0 copy-start.3
  103.0 6.5 %collective-permute-start.19 = (bf16[128,512]{1,0:T(8,128)(2,1)S(1)}, bf16[128,512]{1,0:T(8,128)(2,1)S(1)}, u32[]{:S(2)}, u32[]{:S(2)}) collective-permute-start(bf16[128,512]{1,0:T(8,128)(2,1)S(1)} %get-tuple-element.160.d0), channel_id=1, source_target_pairs={{0,3},{1,0},{2,1},{3,2},{4,7},{5,4},{6,5},{7,6},{8,11},{9,8},{10,9... | collective-permute-start | bytes 393224 | tf_op jit(solution)/shard_map/ppermute | solution.py:505
  103.7 13.0 %collective-permute-start.18 = (bf16[128,512]{1,0:T(8,128)(2,1)S(1)}, bf16[128,512]{1,0:T(8,128)(2,1)S(1)}, u32[]{:S(2)}, u32[]{:S(2)}) collective-permute-start(bf16[128,512]{1,0:T(8,128)(2,1)S(1)} %get-tuple-element.160.d0), channel_id=1, source_target_pairs={{0,2},{1,3},{2,0},{3,1},{4,6},{5,7},{6,4},{7,5},{8,10},{9,11},{10,... | collective-permute-start | bytes 393224 | tf_op jit(solution)/shard_map/ppermute | solution.py:505
  105.4 13.5 %collective-permute-start.17 = (bf16[128,512]{1,0:T(8,128)(2,1)S(1)}, bf16[128,512]{1,0:T(8,128)(2,1)S(1)}, u32[]{:S(2)}, u32[]{:S(2)}) collective-permute-start(bf16[128,512]{1,0:T(8,128)(2,1)S(1)} %get-tuple-element.160.d0), channel_id=1, source_target_pairs={{0,1},{1,2},{2,3},{3,0},{4,5},{5,6},{6,7},{7,4},{8,9},{9,10},{10,1... | collective-permute-start | bytes 393224 | tf_op jit(solution)/shard_map/ppermute | solution.py:505
  105.5 18.2 %collective-permute-start.14 = (f32[136,512]{1,0:T(8,128)S(1)}, f32[136,512]{1,0:T(8,128)S(1)}, u32[]{:S(2)}, u32[]{:S(2)}) collective-permute-start(f32[136,512]{1,0:T(8,128)S(1)} %get-tuple-element.152), channel_id=1, source_target_pairs={{0,2},{1,3},{2,0},{3,1},{4,6},{5,7},{6,4},{7,5},{8,10},{9,11},{10,... | collective-permute-start | bytes 835592 | tf_op jit(solution)/shard_map/ppermute | solution.py:505
  109.2 16.2 %collective-permute-start.15 = (f32[136,512]{1,0:T(8,128)S(1)}, f32[136,512]{1,0:T(8,128)S(1)}, u32[]{:S(2)}, u32[]{:S(2)}) collective-permute-start(f32[136,512]{1,0:T(8,128)S(1)} %get-tuple-element.153), channel_id=1, source_target_pairs={{0,1},{1,2},{2,3},{3,0},{4,5},{5,6},{6,7},{7,4},{8,9},{9,10},{10,1... | collective-permute-start | bytes 835592 | tf_op jit(solution)/shard_map/ppermute | solution.py:505
  109.5 15.9 %collective-permute-start.16 = (f32[136,512]{1,0:T(8,128)S(1)}, f32[136,512]{1,0:T(8,128)S(1)}, u32[]{:S(2)}, u32[]{:S(2)}) collective-permute-start(f32[136,512]{1,0:T(8,128)S(1)} %get-tuple-element.154), channel_id=1, source_target_pairs={{0,3},{1,0},{2,1},{3,2},{4,7},{5,4},{6,5},{7,6},{8,11},{9,8},{10,9... | collective-permute-start | bytes 835592 | tf_op jit(solution)/shard_map/ppermute | solution.py:505
  130.4 13.6 %collective-permute-start.20 = (f32[160,512]{1,0:T(8,128)}, f32[160,512]{1,0:T(8,128)S(1)}, u32[]{:S(2)}, u32[]{:S(2)}) collective-permute-start(f32[160,512]{1,0:T(8,128)} %get-tuple-element.169), channel_id=1, source_target_pairs={{0,2},{1,3},{2,0},{3,1},{4,6},{5,7},{6,4},{7,5},{8,10},{9,11},{10,... | collective-permute-start | bytes 983048 | tf_op jit(solution)/shard_map/ppermute | solution.py:505
  132.0 16.6 %collective-permute-start.21 = (f32[160,512]{1,0:T(8,128)S(1)}, f32[160,512]{1,0:T(8,128)S(1)}, u32[]{:S(2)}, u32[]{:S(2)}) collective-permute-start(f32[160,512]{1,0:T(8,128)S(1)} %get-tuple-element.170), channel_id=1, source_target_pairs={{0,1},{1,2},{2,3},{3,0},{4,5},{5,6},{6,7},{7,4},{8,9},{9,10},{10,1... | collective-permute-start | bytes 983048 | tf_op jit(solution)/shard_map/ppermute | solution.py:505
  132.0 16.6 %collective-permute-start.22 = (f32[160,512]{1,0:T(8,128)S(1)}, f32[160,512]{1,0:T(8,128)S(1)}, u32[]{:S(2)}, u32[]{:S(2)}) collective-permute-start(f32[160,512]{1,0:T(8,128)S(1)} %get-tuple-element.171), channel_id=1, source_target_pairs={{0,3},{1,0},{2,1},{3,2},{4,7},{5,4},{6,5},{7,6},{8,11},{9,8},{10,9... | collective-permute-start | bytes 983048 | tf_op jit(solution)/shard_map/ppermute | solution.py:505
  135.3 14.9 %all-to-all-start.3 = ((f32[32,16,128]{2,1,0:T(8,128)}), f32[32,16,128]{2,1,0:T(8,128)S(1)}, u32[]{:S(2)}, u32[]{:S(2)}) async-start(f32[32,16,128]{2,1,0:T(8,128)} %get-tuple-element.155), calls=%async_computation.3 | async-start | bytes 524288 | tf_op jit(solution)/shard_map/all_to_all | solution.py:519
  150.1 12.9 %all-to-all-start.4 = ((f32[32,16,128]{2,1,0:T(8,128)}), f32[32,16,128]{2,1,0:T(8,128)S(1)}, u32[]{:S(2)}, u32[]{:S(2)}) async-start(f32[32,16,128]{2,1,0:T(8,128)} %get-tuple-element.179), calls=%async_computation.4 | async-start | bytes 524288 | tf_op jit(solution)/shard_map/all_to_all | solution.py:519
  155.2 17.3 %collective-permute-start.23 = (f32[128,512]{1,0:T(8,128)S(1)}, f32[128,512]{1,0:T(8,128)S(1)}, u32[]{:S(2)}, u32[]{:S(2)}) collective-permute-start(f32[128,512]{1,0:T(8,128)S(1)} %get-tuple-element.187), channel_id=1, source_target_pairs={{4,0},{8,4},{12,8},{16,12},{20,16},{24,20},{28,24},{32,28},{36,32}... | collective-permute-start | bytes 786440 | tf_op jit(solution)/shard_map/ppermute | solution.py:514
  163.8 12.8 %all-to-all-start.5 = ((f32[32,16,128]{2,1,0:T(8,128)}), f32[32,16,128]{2,1,0:T(8,128)S(1)}, u32[]{:S(2)}, u32[]{:S(2)}) async-start(f32[32,16,128]{2,1,0:T(8,128)} %shard_map.118), calls=%async_computation.5 | async-start | bytes 524288 | tf_op jit(solution)/shard_map/all_to_all | solution.py:519
  171.6 1.0 copy-start
  176.6 1.2 copy-start.1
Sparse Core Ops, SparseCore 0:
  10.3 48.2 all-gather.1

commit v10 on v8

--- a/solution.py
+++ b/solution.py
@@ -168,10 +168,9 @@
 
 
 def near_solve_kernel(
-    place, x0, x1, x2, x3, high, low, inverse, f0, f1, f2, f3, p0, p1, p2, p3, plane
+    place, x0, x1, x2, x3, high, low, inverse, p0, p1, p2, p3, plane
 ):
-    forces = (f0, f1, f2, f3)
-    solve(place, (x0, x1, x2, x3), (high, low, inverse), forces, (p0, p1, p2, p3), plane)
+    solve(place, (x0, x1, x2, x3), (high, low, inverse), (), (p0, p1, p2, p3), plane)
 
 
 def solve(place, inputs, tables_near, forces, outputs, plane, copies=()):
@@ -560,15 +559,15 @@
             forces, near_tables = made[:cross_size], made[cross_size:]
             solved = call(
                 near_solve_kernel,
-                [near((height + height * LANE // width, width))] * cross_size,
-                (place, *arrived, *near_tables, *forces),
+                [near(plane)] * cross_size,
+                (place, *arrived, *near_tables),
                 solve_cost,
                 scalars=1,
                 limit=16,
                 scratch=[pltpu.VMEM((width, width), F32)],
             )
             scales = across_march(scale)
-            forces = []
+            forces, solved = lax.optimization_barrier((turns(forces, -1), solved))
         else:
             scales = across_march(scale)
             solved = pl.pallas_call(

time: 188 us -> 187 us (level)
  waiting for transfers between devices: 39.1 us -> 36.7 us
  starting transfers between devices: 73.4 us -> 75.8 us
  local copies, waits for them, and re-layouts: 7.19 us -> 4.97 us
    ppermute x21 -> x24, waiting for transfers between devices: 12.8 us -> 8.18 us  [turn(): lax.ppermute(value, 'cross', [(i, (i + steps) % cross_size) for i in rang...]
    ppermute x21 -> x24, starting transfers between devices: 31 us -> 33.6 us  [turn(): lax.ppermute(value, 'cross', [(i, (i + steps) % cross_size) for i in rang...]
    unnamed x8 -> x4, local copies, waits for them, and re-layouts: 3.14 us -> 0.95 us
    all_to_all x6, waiting for transfers between devices: 16.7 us -> 18.9 us  [across_march(): lax.all_to_all(value, 'march', split_axis=0, concat_axis=0, tiled=True)]
  transfers between devices with their start and end apart: 31 -> 34, of which waited for: 14 -> 15; matrix products, arithmetic and copies ran while one was open for 3% -> 3% of each run, Pallas kernels for 22% -> 25%
where the time goes in v10:
time: 187 us; the launch traced here: 184 us
  starting transfers between devices  75.8 us (41%)
  Pallas kernels  51.3 us (27%)
  waiting for transfers between devices  36.7 us (20%)
  between operations  14.3 us (8%)
  local copies, waits for them, and re-layouts  4.97 us (3%)
    ppermute x24, starting transfers between devices, turn(): lax.ppermute(value, 'cross', [(i, (i + steps) % cross_size) for i in rang...  33.6 us
    all_to_all x6, starting transfers between devices, across_march(): lax.all_to_all(value, 'march', split_axis=0, concat_axis=0, tiled=True)  31.6 us
    pallas_call x11, Pallas kernels, call(): pl.pallas_call(kernel, out_shape=outs, in_specs=[SMEM] * scalars + [VMEM]...  25.1 us
    all_to_all x6, waiting for transfers between devices, across_march(): lax.all_to_all(value, 'march', split_axis=0, concat_axis=0, tiled=True)  18.9 us
    pallas_call x3, Pallas kernels, by_rows(): pl.pallas_call(kernel, grid_spec=pltpu.PrefetchScalarGridSpec(num_scalar_...  11.2 us
    ppermute x3, starting transfers between devices, along_march(): lax.ppermute(value, 'march', [(i, i + steps) for i in range(count) if 0 <...  10.6 us
    pallas_call x2, Pallas kernels, disc_forces(): pl.pallas_call(disc_kernel, grid=(number // per_step,), out_shape=[near((...  9.52 us
    ppermute x24, waiting for transfers between devices, turn(): lax.ppermute(value, 'cross', [(i, (i + steps) % cross_size) for i in rang...  8.18 us
  transfers between devices with their start and end apart: 34, of which 15 were waited for; matrix products, arithmetic and copies ran while one was open for 3% of the time, Pallas kernels for 25%

profile of v10, /device:TPU:2, one launch (start us, length us, event | category | flops | bytes accessed | tf_op | source)
XLA Modules:
  0.0 183.9 jit_solution(3953530657939455401)
XLA Ops:
  7.9 1.0 slice_bitcast_fusion
  8.9 1.9 %collective-permute-start.3 = (f32[128,512]{1,0:T(8,128)S(1)}, f32[128,512]{1,0:T(8,128)S(1)}, u32[]{:S(2)}, u32[]{:S(2)}) collective-permute-start(f32[128,512]{1,0:T(8,128)S(1)} %slice_bitcast_fusion), channel_id=1, source_target_pairs={{0,4},{4,8},{8,12},{12,16},{16,20},{20,24},{24,28},{28,32},{32,36}... | collective-permute-start | bytes 786440 | tf_op jit(solution)/shard_map/ppermute | solution.py:507
  11.8 4.1 %collective-permute-start.2 = (bf16[128,512]{1,0:T(8,128)(2,1)S(1)}, bf16[128,512]{1,0:T(8,128)(2,1)S(1)}, u32[]{:S(2)}, u32[]{:S(2)}) collective-permute-start(bf16[128,512]{1,0:T(8,128)(2,1)S(1)} %fusion.d0), channel_id=1, source_target_pairs={{0,3},{1,0},{2,1},{3,2},{4,7},{5,4},{6,5},{7,6},{8,11},{9,8},{10,9... | collective-permute-start | bytes 393224 | tf_op jit(solution)/shard_map/ppermute | solution.py:498
  16.0 2.7 %collective-permute-done.3.upstream = f32[128,512]{1,0:T(8,128)S(1)} collective-permute-done((f32[128,512]{1,0:T(8,128)S(1)}, f32[128,512]{1,0:T(8,128)S(1)}, u32[]{:S(2)}, u32[]{:S(2)}) %collective-permute-start.3) | collective-permute-done | bytes 262176 | tf_op jit(solution)/shard_map/ppermute | solution.py:507
  18.7 2.7 %shard_map.104 = (f32[128,512]{1,0:T(8,128)S(1)}, f32[136,512]{1,0:T(8,128)S(1)}, f32[128,512]{1,0:T(8,128)S(1)}, f32[136,512]{1,0:T(8,128)S(1)}) custom-call(s32[4]{0:T(128)S(1)} %pad_add_fusion.place, f32[4,128,512]{2,1,0:T(8,128)} %current.4, f32[128,512]{1,0:T(8,128)S(1)} %collective-permute-done.3.upstream, f32[128,512]{1,0:T(8,128)} %inflow.9), custom_call_target="tpu_custom_call" | custom-call | flops 1000000 | bytes 2097152 | tf_op jit(solution)/shard_map/pallas_call | solution.py:429
  21.4 4.0 %collective-permute-start.5 = (f32[128,512]{1,0:T(8,128)S(1)}, f32[128,512]{1,0:T(8,128)S(1)}, u32[]{:S(2)}, u32[]{:S(2)}) collective-permute-start(f32[128,512]{1,0:T(8,128)S(1)} %get-tuple-element.113), channel_id=1, source_target_pairs={{0,2},{1,3},{2,0},{3,1},{4,6},{5,7},{6,4},{7,5},{8,10},{9,11},{10,... | collective-permute-start | bytes 786440 | tf_op jit(solution)/shard_map/ppermute | solution.py:498
  25.4 1.0 collective-permute-start.4
  26.4 2.2 %collective-permute-start.6 = (f32[136,512]{1,0:T(8,128)S(1)}, f32[136,512]{1,0:T(8,128)S(1)}, u32[]{:S(2)}, u32[]{:S(2)}) collective-permute-start(f32[136,512]{1,0:T(8,128)S(1)} %get-tuple-element.114), channel_id=1, source_target_pairs={{0,3},{1,0},{2,1},{3,2},{4,7},{5,4},{6,5},{7,6},{8,11},{9,8},{10,9... | collective-permute-start | bytes 835592 | tf_op jit(solution)/shard_map/ppermute | solution.py:498
  29.3 4.2 %shard_map.105 = (f32[4,128,512]{2,1,0:T(8,128)}, f32[32,16,128]{2,1,0:T(8,128)}) custom-call(s32[4]{0:T(128)S(1)} %pad_add_fusion.place, f32[4,128,512]{2,1,0:T(8,128)} %current.4, f32[4,128,512]{2,1,0:T(8,128)} %damping.1), custom_call_target="tpu_custom_call" | custom-call | flops 4000000 | bytes 3145728 | tf_op jit(solution)/shard_map/pallas_call | solution.py:429
  33.5 5.7 %all-to-all-start = ((f32[32,16,128]{2,1,0:T(8,128)}), f32[32,16,128]{2,1,0:T(8,128)S(1)}, u32[]{:S(2)}, u32[]{:S(2)}) async-start(f32[32,16,128]{2,1,0:T(8,128)} %get-tuple-element.110), calls=%async_computation | async-start | bytes 524288 | tf_op jit(solution)/shard_map/all_to_all | solution.py:512
  39.3 5.6 %shard_map.106 = (f32[128,512]{1,0:T(8,128)S(1)}, f32[128,512]{1,0:T(8,128)S(1)}, f32[128,512]{1,0:T(8,128)S(1)}, f32[128,512]{1,0:T(8,128)S(1)}) custom-call(s32[4]{0:T(128)S(1)} %pad_add_fusion.place, f32[128,512]{1,0:T(8,128)S(1)} %get-tuple-element.111.x0, f32[136,512]{1,0:T(8,128)S(1)} %collective-permute-done.4.x1.before, ...), custom_call_target="tpu_custom_call" | custom-call | flops 3221225472 | bytes 5242880 | tf_op jit(solution)/shard_map/pallas_call | solution.py:573
  44.9 1.1 collective-permute-done.d1
  49.0 2.6 %collective-permute-start.8 = (f32[128,512]{1,0:T(8,128)S(1)}, f32[128,512]{1,0:T(8,128)S(1)}, u32[]{:S(2)}, u32[]{:S(2)}) collective-permute-start(f32[128,512]{1,0:T(8,128)S(1)} %get-tuple-element.122), channel_id=1, source_target_pairs={{0,2},{1,3},{2,0},{3,1},{4,6},{5,7},{6,4},{7,5},{8,10},{9,11},{10,... | collective-permute-start | bytes 786440 | tf_op jit(solution)/shard_map/ppermute | solution.py:498
  52.3 6.3 %all-gather.2.cloned.1.call-done.rest_0_.rest_1_.rest_2_.rest_3_ = bf16[32,512,128]{2,1,0:T(8,128)(2,1)} async-done(((bf16[1,512,128]{2,1,0:T(8,128)(2,1)}), bf16[32,512,128]{2,1,0:T(8,128)(2,1)}) %all-gather.2.cloned.1.call-update) | async-done | bytes 4194320 | tf_op jit(solution)/shard_map/all_gather | solution.py:514
  58.6 4.7 %shard_map.107 = (f32[128,128]{1,0:T(8,128)S(1)}, f32[128,128]{1,0:T(8,128)S(1)}, f32[128,128]{1,0:T(8,128)S(1)}, f32[128,128]{1,0:T(8,128)S(1)}) custom-call(bf16[128,512]{1,0:T(8,128)(2,1)S(1)} %fusion.d0, bf16[128,512]{1,0:T(8,128)(2,1)S(1)} %collective-permute-done.d1, bf16[128,512]{1,0:T(8,128)(2,1)S(1)} %collective-permute-done.1.d2, ...), custom_call_target="tpu_custom_call" | custom-call | flops 2147483648 | bytes 5242880 | tf_op jit(solution)/shard_map/pallas_call | solution.py:452
  63.3 2.7 %collective-permute-start.10 = (f32[128,128]{1,0:T(8,128)S(1)}, f32[128,128]{1,0:T(8,128)S(1)}, u32[]{:S(2)}, u32[]{:S(2)}) collective-permute-start(f32[128,128]{1,0:T(8,128)S(1)} %get-tuple-element.132), channel_id=1, source_target_pairs={{0,3},{1,0},{2,1},{3,2},{4,7},{5,4},{6,5},{7,6},{8,11},{9,8},{10,9... | collective-permute-start | bytes 196616 | tf_op jit(solution)/shard_map/ppermute | solution.py:498
  67.6 3.6 %shard_map.108 = (f32[4,128,512]{2,1,0:T(8,128)}, f32[4,128,512]{2,1,0:T(8,128)S(1)}, f32[128,512]{1,0:T(8,128)S(1)}, f32[128,512]{1,0:T(8,128)S(1)}) custom-call(s32[4]{0:T(128)S(1)} %pad_add_fusion.place, f32[4,128,512]{2,1,0:T(8,128)} %current.4, f32[136,512]{1,0:T(8,128)S(1)} %collective-permute-done.4.x1.before, ...), custom_call_target="tpu_custom_call" | custom-call | flops 8000000 | bytes 4194304 | tf_op jit(solution)/shard_map/pallas_call | solution.py:405
  72.9 1.6 shard_map.109
  74.5 5.9 %all-to-all-start.1 = ((f32[32,16,128]{2,1,0:T(8,128)}), f32[32,16,128]{2,1,0:T(8,128)S(1)}, u32[]{:S(2)}, u32[]{:S(2)}) async-start(f32[32,16,128]{2,1,0:T(8,128)} %get-tuple-element.141), calls=%async_computation.1 | async-start | bytes 524288 | tf_op jit(solution)/shard_map/all_to_all | solution.py:512
  80.4 4.3 %collective-permute-start.13 = (f32[128,512]{1,0:T(8,128)}, f32[128,512]{1,0:T(8,128)}, u32[]{:S(2)}, u32[]{:S(2)}) collective-permute-start(f32[128,512]{1,0:T(8,128)} %get-tuple-element.149), channel_id=1, source_target_pairs={{4,0},{8,4},{12,8},{16,12},{20,16},{24,20},{28,24},{32,28},{36,32}... | collective-permute-start | bytes 786440 | tf_op jit(solution)/shard_map/ppermute | solution.py:507
  84.8 3.4 %all-to-all-done.1.offset = f32[32,16,128]{2,1,0:T(8,128)S(1)} async-done(((f32[32,16,128]{2,1,0:T(8,128)}), f32[32,16,128]{2,1,0:T(8,128)S(1)}, u32[]{:S(2)}, u32[]{:S(2)}) %all-to-all-start.1) | async-done | bytes 262176 | tf_op jit(solution)/shard_map/all_to_all | solution.py:512
  88.9 5.0 %all-to-all-start.2 = ((f32[32,16,128]{2,1,0:T(8,128)}), f32[32,16,128]{2,1,0:T(8,128)S(1)}, u32[]{:S(2)}, u32[]{:S(2)}) async-start(f32[32,16,128]{2,1,0:T(8,128)} %shard_map.110), calls=%async_computation.2 | async-start | bytes 524288 | tf_op jit(solution)/shard_map/all_to_all | solution.py:512
  94.9 1.9 %shard_map.111 = (f32[5,128,512]{2,1,0:T(8,128)S(1)}, f32[4,128,512]{2,1,0:T(8,128)S(1)}) custom-call(s32[4]{0:T(128)S(1)} %pad_add_fusion.place, f32[128,512]{1,0:T(8,128)S(1)} %get-tuple-element.142.rest_0_.p0, f32[128,512]{1,0:T(8,128)S(1)} %collective-permute-done.7.rest_1_.p1, f32[128,512]{1,0:T(8,128)S(1)} %collective-permute-done.8.rest_2_.p2, ...), custom_call_target="tpu_custom_call" | custom-call | flops 4000000 | bytes 4194304 | tf_op jit(solution)/shard_map/pallas_call | solution.py:405
  96.8 4.9 %all-to-all-done.2.entering = f32[32,16,128]{2,1,0:T(8,128)S(1)} async-done(((f32[32,16,128]{2,1,0:T(8,128)}), f32[32,16,128]{2,1,0:T(8,128)S(1)}, u32[]{:S(2)}, u32[]{:S(2)}) %all-to-all-start.2) | async-done | bytes 262176 | tf_op jit(solution)/shard_map/all_to_all | solution.py:512
  101.7 1.2 shard_map.112
  103.7 1.6 collective-permute-start.18
  105.5 1.7 collective-permute-start.14
  107.2 1.5 collective-permute-start.16
  109.4 1.9 %collective-permute-start.15 = (f32[128,512]{1,0:T(8,128)S(1)}, f32[128,512]{1,0:T(8,128)S(1)}, u32[]{:S(2)}, u32[]{:S(2)}) collective-permute-start(f32[128,512]{1,0:T(8,128)S(1)} %get-tuple-element.161), channel_id=1, source_target_pairs={{0,2},{1,3},{2,0},{3,1},{4,6},{5,7},{6,4},{7,5},{8,10},{9,11},{10,... | collective-permute-start | bytes 786440 | tf_op jit(solution)/shard_map/ppermute | solution.py:498
  111.2 4.2 %shard_map.113 = (f32[4,128,512]{2,1,0:T(8,128)}, f32[32,16,128]{2,1,0:T(8,128)}, f32[4,128,512]{2,1,0:T(8,128)}) custom-call(s32[4]{0:T(128)S(1)} %pad_add_fusion.place, f32[4,128,512]{2,1,0:T(8,128)S(1)} %get-tuple-element.156.current, f32[4,128,512]{2,1,0:T(8,128)} %damping.1), custom_call_target="tpu_custom_call" | custom-call | flops 4000000 | bytes 3145728 | tf_op jit(solution)/shard_map/pallas_call | solution.py:429
  115.5 4.8 %shard_map.114 = (f32[128,128]{1,0:T(8,128)S(1)}, f32[128,128]{1,0:T(8,128)S(1)}, f32[128,128]{1,0:T(8,128)S(1)}, f32[128,128]{1,0:T(8,128)S(1)}, bf16[512,512]{...) custom-call(bf16[128,512]{1,0:T(8,128)(2,1)S(1)} %get-tuple-element.164.d0, ...), custom_call_target="tpu_custom_call" | custom-call | flops 2147483648 | bytes 5242880 | tf_op jit(solution)/shard_map/pallas_call | solution.py:452
  121.0 1.6 collective-permute-start.21
  122.7 3.0 %collective-permute-done.15.x2 = f32[128,512]{1,0:T(8,128)S(1)} collective-permute-done((f32[128,512]{1,0:T(8,128)S(1)}, f32[128,512]{1,0:T(8,128)S(1)}, u32[]{:S(2)}, u32[]{:S(2)}) %collective-permute-start.15) | collective-permute-done | bytes 262176 | tf_op jit(solution)/shard_map/ppermute | solution.py:498
  125.7 5.1 %shard_map.115 = (f32[128,512]{1,0:T(8,128)S(1)}, f32[128,512]{1,0:T(8,128)}, f32[128,512]{1,0:T(8,128)}, f32[128,512]{1,0:T(8,128)}) custom-call(s32[4]{0:T(128)S(1)} %pad_add_fusion.place, f32[128,512]{1,0:T(8,128)S(1)} %get-tuple-element.169.x0, f32[136,512]{1,0:T(8,128)S(1)} %collective-permute-done.14.x1.before, ...), custom_call_target="tpu_custom_call" | custom-call | flops 3221225472 | bytes 5242880 | tf_op jit(solution)/shard_map/pallas_call | solution.py:405
  131.2 1.4 collective-permute-start.23
  132.6 3.1 %collective-permute-start.24 = (f32[128,512]{1,0:T(8,128)}, f32[128,512]{1,0:T(8,128)S(1)}, u32[]{:S(2)}, u32[]{:S(2)}) collective-permute-start(f32[128,512]{1,0:T(8,128)} %get-tuple-element.182), channel_id=1, source_target_pairs={{0,2},{1,3},{2,0},{3,1},{4,6},{5,7},{6,4},{7,5},{8,10},{9,11},{10,... | collective-permute-start | bytes 786440 | tf_op jit(solution)/shard_map/ppermute | solution.py:498
  135.8 5.0 %all-to-all-start.3 = ((f32[32,16,128]{2,1,0:T(8,128)}), f32[32,16,128]{2,1,0:T(8,128)S(1)}, u32[]{:S(2)}, u32[]{:S(2)}) async-start(f32[32,16,128]{2,1,0:T(8,128)} %get-tuple-element.163), calls=%async_computation.3 | async-start | bytes 524288 | tf_op jit(solution)/shard_map/all_to_all | solution.py:512
  140.8 3.6 %shard_map.116 = (f32[4,128,512]{2,1,0:T(8,128)}, f32[4,128,512]{2,1,0:T(8,128)S(1)}, f32[128,512]{1,0:T(8,128)S(1)}, f32[128,512]{1,0:T(8,128)S(1)}) custom-call(s32[4]{0:T(128)S(1)} %pad_add_fusion.place, f32[4,128,512]{2,1,0:T(8,128)} %get-tuple-element.188.current, f32[136,512]{1,0:T(8,128)S(1)} %collective-permute-done.14.x1.before, ...), custom_call_target="tpu_custom_call" | custom-call | flops 8000000 | bytes 4194304 | tf_op jit(solution)/shard_map/pallas_call | solution.py:405
  144.5 1.3 collective-permute-done.24.rest_2_.p2
  145.8 1.6 shard_map.117
  147.4 1.2 all-to-all-done.3.scale
  148.6 5.0 %all-to-all-start.4 = ((f32[32,16,128]{2,1,0:T(8,128)}), f32[32,16,128]{2,1,0:T(8,128)S(1)}, u32[]{:S(2)}, u32[]{:S(2)}) async-start(f32[32,16,128]{2,1,0:T(8,128)} %get-tuple-element.195), calls=%async_computation.4 | async-start | bytes 524288 | tf_op jit(solution)/shard_map/all_to_all | solution.py:512
  153.6 4.3 %collective-permute-start.26 = (f32[128,512]{1,0:T(8,128)}, f32[128,512]{1,0:T(8,128)}, u32[]{:S(2)}, u32[]{:S(2)}) collective-permute-start(f32[128,512]{1,0:T(8,128)} %get-tuple-element.203), channel_id=1, source_target_pairs={{4,0},{8,4},{12,8},{16,12},{20,16},{24,20},{28,24},{32,28},{36,32}... | collective-permute-start | bytes 786440 | tf_op jit(solution)/shard_map/ppermute | solution.py:507
  158.0 3.5 %all-to-all-done.4.offset = f32[32,16,128]{2,1,0:T(8,128)S(1)} async-done(((f32[32,16,128]{2,1,0:T(8,128)}), f32[32,16,128]{2,1,0:T(8,128)S(1)}, u32[]{:S(2)}, u32[]{:S(2)}) %all-to-all-start.4) | async-done | bytes 262176 | tf_op jit(solution)/shard_map/all_to_all | solution.py:512
  162.2 5.0 %all-to-all-start.5 = ((f32[32,16,128]{2,1,0:T(8,128)}), f32[32,16,128]{2,1,0:T(8,128)S(1)}, u32[]{:S(2)}, u32[]{:S(2)}) async-start(f32[32,16,128]{2,1,0:T(8,128)} %shard_map.118), calls=%async_computation.5 | async-start | bytes 524288 | tf_op jit(solution)/shard_map/all_to_all | solution.py:512
  167.2 2.7 %shard_map.119 = (f32[4,128,512]{2,1,0:T(8,128)S(1)}, f32[4,128,512]{2,1,0:T(8,128)S(1)}, f32[4,128,512]{2,1,0:T(8,128)}) custom-call(s32[4]{0:T(128)S(1)} %pad_add_fusion.place, f32[128,512]{1,0:T(8,128)S(1)} %get-tuple-element.196.rest_0_.p0, f32[128,512]{1,0:T(8,128)S(1)} %collective-permute-done.23.rest_1_.p1, ...), custom_call_target="tpu_custom_call" | custom-call | flops 4000000 | bytes 4194304 | tf_op jit(solution)/shard_map/pallas_call | solution.py:405
  169.9 5.1 %all-to-all-done.5.entering = f32[32,16,128]{2,1,0:T(8,128)S(1)} async-done(((f32[32,16,128]{2,1,0:T(8,128)}), f32[32,16,128]{2,1,0:T(8,128)S(1)}, u32[]{:S(2)}, u32[]{:S(2)}) %all-to-all-start.5) | async-done | bytes 262176 | tf_op jit(solution)/shard_map/all_to_all | solution.py:512
  175.0 2.0 %shard_map.120 = f32[4,128,512]{2,1,0:T(8,128)} custom-call(f32[32,16,128]{2,1,0:T(8,128)S(1)} %all-to-all-done.5.entering, f32[4,128,512]{2,1,0:T(8,128)S(1)} %get-tuple-element.202.change, f32[128,512]{1,0:T(8,128)} %collective-permute-done.26.following, f32[4,128,512]{2,1,0:T(8,128)S(1)} %get-tuple-element.204.decay), custom_call_target="tpu_custom_call" | custom-call | flops 4000000 | bytes 5242880 | tf_op jit(solution)/shard_map/pallas_call | solution.py:405
  (50 shorter events, 14.7 us)
Async XLA Ops:
  7.2 51.4 %all-gather.2.cloned.1.call-start = ((), (), s32[]{:S(2)}) async-start(), calls=%async_computation.6 | async-start | bytes 4325376 | tf_op jit(solution)/shard_map/all_gather | solution.py:514
  8.9 9.8 %collective-permute-start.3 = (f32[128,512]{1,0:T(8,128)S(1)}, f32[128,512]{1,0:T(8,128)S(1)}, u32[]{:S(2)}, u32[]{:S(2)}) collective-permute-start(f32[128,512]{1,0:T(8,128)S(1)} %slice_bitcast_fusion), channel_id=1, source_target_pairs={{0,4},{4,8},{8,12},{12,16},{16,20},{20,24},{24,28},{28,32},{32,36}... | collective-permute-start | bytes 786440 | tf_op jit(solution)/shard_map/ppermute | solution.py:507
  11.8 33.1 %collective-permute-start.2 = (bf16[128,512]{1,0:T(8,128)(2,1)S(1)}, bf16[128,512]{1,0:T(8,128)(2,1)S(1)}, u32[]{:S(2)}, u32[]{:S(2)}) collective-permute-start(bf16[128,512]{1,0:T(8,128)(2,1)S(1)} %fusion.d0), channel_id=1, source_target_pairs={{0,3},{1,0},{2,1},{3,2},{4,7},{5,4},{6,5},{7,6},{8,11},{9,8},{10,9... | collective-permute-start | bytes 393224 | tf_op jit(solution)/shard_map/ppermute | solution.py:498
  15.9 29.0 %collective-permute-start.1 = (bf16[128,512]{1,0:T(8,128)(2,1)S(1)}, bf16[128,512]{1,0:T(8,128)(2,1)S(1)}, u32[]{:S(2)}, u32[]{:S(2)}) collective-permute-start(bf16[128,512]{1,0:T(8,128)(2,1)S(1)} %fusion.d0), channel_id=1, source_target_pairs={{0,2},{1,3},{2,0},{3,1},{4,6},{5,7},{6,4},{7,5},{8,10},{9,11},{10,... | collective-permute-start | bytes 393224 | tf_op jit(solution)/shard_map/ppermute | solution.py:498
  21.4 17.8 %collective-permute-start.5 = (f32[128,512]{1,0:T(8,128)S(1)}, f32[128,512]{1,0:T(8,128)S(1)}, u32[]{:S(2)}, u32[]{:S(2)}) collective-permute-start(f32[128,512]{1,0:T(8,128)S(1)} %get-tuple-element.113), channel_id=1, source_target_pairs={{0,2},{1,3},{2,0},{3,1},{4,6},{5,7},{6,4},{7,5},{8,10},{9,11},{10,... | collective-permute-start | bytes 786440 | tf_op jit(solution)/shard_map/ppermute | solution.py:498
  25.4 13.9 %collective-permute-start.4 = (f32[136,512]{1,0:T(8,128)S(1)}, f32[136,512]{1,0:T(8,128)S(1)}, u32[]{:S(2)}, u32[]{:S(2)}) collective-permute-start(f32[136,512]{1,0:T(8,128)S(1)} %get-tuple-element.112), channel_id=1, source_target_pairs={{0,1},{1,2},{2,3},{3,0},{4,5},{5,6},{6,7},{7,4},{8,9},{9,10},{10,1... | collective-permute-start | bytes 835592 | tf_op jit(solution)/shard_map/ppermute | solution.py:498
  26.4 12.9 %collective-permute-start.6 = (f32[136,512]{1,0:T(8,128)S(1)}, f32[136,512]{1,0:T(8,128)S(1)}, u32[]{:S(2)}, u32[]{:S(2)}) collective-permute-start(f32[136,512]{1,0:T(8,128)S(1)} %get-tuple-element.114), channel_id=1, source_target_pairs={{0,3},{1,0},{2,1},{3,2},{4,7},{5,4},{6,5},{7,6},{8,11},{9,8},{10,9... | collective-permute-start | bytes 835592 | tf_op jit(solution)/shard_map/ppermute | solution.py:498
  33.5 13.4 %all-to-all-start = ((f32[32,16,128]{2,1,0:T(8,128)}), f32[32,16,128]{2,1,0:T(8,128)S(1)}, u32[]{:S(2)}, u32[]{:S(2)}) async-start(f32[32,16,128]{2,1,0:T(8,128)} %get-tuple-element.110), calls=%async_computation | async-start | bytes 524288 | tf_op jit(solution)/shard_map/all_to_all | solution.py:512
  39.2 6.8 %collective-permute-start = (bf16[128,512]{1,0:T(8,128)(2,1)S(1)}, bf16[128,512]{1,0:T(8,128)(2,1)S(1)}, u32[]{:S(2)}, u32[]{:S(2)}) collective-permute-start(bf16[128,512]{1,0:T(8,128)(2,1)S(1)} %fusion.d0), channel_id=1, source_target_pairs={{0,1},{1,2},{2,3},{3,0},{4,5},{5,6},{6,7},{7,4},{8,9},{9,10},{10,1... | collective-permute-start | bytes 393224 | tf_op jit(solution)/shard_map/ppermute | solution.py:498
  49.0 17.6 %collective-permute-start.7 = (f32[128,512]{1,0:T(8,128)S(1)}, f32[128,512]{1,0:T(8,128)S(1)}, u32[]{:S(2)}, u32[]{:S(2)}) collective-permute-start(f32[128,512]{1,0:T(8,128)S(1)} %get-tuple-element.121), channel_id=1, source_target_pairs={{0,1},{1,2},{2,3},{3,0},{4,5},{5,6},{6,7},{7,4},{8,9},{9,10},{10,1... | collective-permute-start | bytes 786440 | tf_op jit(solution)/shard_map/ppermute | solution.py:498
  49.0 22.2 %collective-permute-start.8 = (f32[128,512]{1,0:T(8,128)S(1)}, f32[128,512]{1,0:T(8,128)S(1)}, u32[]{:S(2)}, u32[]{:S(2)}) collective-permute-start(f32[128,512]{1,0:T(8,128)S(1)} %get-tuple-element.122), channel_id=1, source_target_pairs={{0,2},{1,3},{2,0},{3,1},{4,6},{5,7},{6,4},{7,5},{8,10},{9,11},{10,... | collective-permute-start | bytes 786440 | tf_op jit(solution)/shard_map/ppermute | solution.py:498
  51.7 19.5 %collective-permute-start.9 = (f32[128,512]{1,0:T(8,128)S(1)}, f32[128,512]{1,0:T(8,128)S(1)}, u32[]{:S(2)}, u32[]{:S(2)}) collective-permute-start(f32[128,512]{1,0:T(8,128)S(1)} %get-tuple-element.123), channel_id=1, source_target_pairs={{0,3},{1,0},{2,1},{3,2},{4,7},{5,4},{6,5},{7,6},{8,11},{9,8},{10,9... | collective-permute-start | bytes 786440 | tf_op jit(solution)/shard_map/ppermute | solution.py:498
  63.3 8.0 %collective-permute-start.10 = (f32[128,128]{1,0:T(8,128)S(1)}, f32[128,128]{1,0:T(8,128)S(1)}, u32[]{:S(2)}, u32[]{:S(2)}) collective-permute-start(f32[128,128]{1,0:T(8,128)S(1)} %get-tuple-element.132), channel_id=1, source_target_pairs={{0,3},{1,0},{2,1},{3,2},{4,7},{5,4},{6,5},{7,6},{8,11},{9,8},{10,9... | collective-permute-start | bytes 196616 | tf_op jit(solution)/shard_map/ppermute | solution.py:498
  66.0 6.2 %collective-permute-start.11 = (f32[128,128]{1,0:T(8,128)S(1)}, f32[128,128]{1,0:T(8,128)S(1)}, u32[]{:S(2)}, u32[]{:S(2)}) collective-permute-start(f32[128,128]{1,0:T(8,128)S(1)} %get-tuple-element.133), channel_id=1, source_target_pairs={{0,2},{1,3},{2,0},{3,1},{4,6},{5,7},{6,4},{7,5},{8,10},{9,11},{10,... | collective-permute-start | bytes 196616 | tf_op jit(solution)/shard_map/ppermute | solution.py:498
  66.7 6.2 %collective-permute-start.12 = (f32[128,128]{1,0:T(8,128)S(1)}, f32[128,128]{1,0:T(8,128)S(1)}, u32[]{:S(2)}, u32[]{:S(2)}) collective-permute-start(f32[128,128]{1,0:T(8,128)S(1)} %get-tuple-element.134), channel_id=1, source_target_pairs={{0,1},{1,2},{2,3},{3,0},{4,5},{5,6},{6,7},{7,4},{8,9},{9,10},{10,1... | collective-permute-start | bytes 196616 | tf_op jit(solution)/shard_map/ppermute | solution.py:498
  71.2 3.3 %copy-start = (f32[128,512]{1,0:T(8,128)}, f32[128,512]{1,0:T(8,128)S(1)}, u32[]{:S(2)}) copy-start(f32[128,512]{1,0:T(8,128)S(1)} %collective-permute-done.9.rest_3_.p3) | copy-start | bytes 786436
  74.5 13.6 %all-to-all-start.1 = ((f32[32,16,128]{2,1,0:T(8,128)}), f32[32,16,128]{2,1,0:T(8,128)S(1)}, u32[]{:S(2)}, u32[]{:S(2)}) async-start(f32[32,16,128]{2,1,0:T(8,128)} %get-tuple-element.141), calls=%async_computation.1 | async-start | bytes 524288 | tf_op jit(solution)/shard_map/all_to_all | solution.py:512
  80.4 16.4 %collective-permute-start.13 = (f32[128,512]{1,0:T(8,128)}, f32[128,512]{1,0:T(8,128)}, u32[]{:S(2)}, u32[]{:S(2)}) collective-permute-start(f32[128,512]{1,0:T(8,128)} %get-tuple-element.149), channel_id=1, source_target_pairs={{4,0},{8,4},{12,8},{16,12},{20,16},{24,20},{28,24},{32,28},{36,32}... | collective-permute-start | bytes 786440 | tf_op jit(solution)/shard_map/ppermute | solution.py:507
  88.9 12.8 %all-to-all-start.2 = ((f32[32,16,128]{2,1,0:T(8,128)}), f32[32,16,128]{2,1,0:T(8,128)S(1)}, u32[]{:S(2)}, u32[]{:S(2)}) async-start(f32[32,16,128]{2,1,0:T(8,128)} %shard_map.110), calls=%async_computation.2 | async-start | bytes 524288 | tf_op jit(solution)/shard_map/all_to_all | solution.py:512
  93.9 1.0 copy-start.1
  103.0 6.4 %collective-permute-start.19 = (bf16[128,512]{1,0:T(8,128)(2,1)S(1)}, bf16[128,512]{1,0:T(8,128)(2,1)S(1)}, u32[]{:S(2)}, u32[]{:S(2)}) collective-permute-start(bf16[128,512]{1,0:T(8,128)(2,1)S(1)} %get-tuple-element.164.d0), channel_id=1, source_target_pairs={{0,3},{1,0},{2,1},{3,2},{4,7},{5,4},{6,5},{7,6},{8,11},{9,8},{10,9... | collective-permute-start | bytes 393224 | tf_op jit(solution)/shard_map/ppermute | solution.py:498
  103.7 11.8 %collective-permute-start.18 = (bf16[128,512]{1,0:T(8,128)(2,1)S(1)}, bf16[128,512]{1,0:T(8,128)(2,1)S(1)}, u32[]{:S(2)}, u32[]{:S(2)}) collective-permute-start(bf16[128,512]{1,0:T(8,128)(2,1)S(1)} %get-tuple-element.164.d0), channel_id=1, source_target_pairs={{0,2},{1,3},{2,0},{3,1},{4,6},{5,7},{6,4},{7,5},{8,10},{9,11},{10,... | collective-permute-start | bytes 393224 | tf_op jit(solution)/shard_map/ppermute | solution.py:498
  105.3 10.1 %collective-permute-start.17 = (bf16[128,512]{1,0:T(8,128)(2,1)S(1)}, bf16[128,512]{1,0:T(8,128)(2,1)S(1)}, u32[]{:S(2)}, u32[]{:S(2)}) collective-permute-start(bf16[128,512]{1,0:T(8,128)(2,1)S(1)} %get-tuple-element.164.d0), channel_id=1, source_target_pairs={{0,1},{1,2},{2,3},{3,0},{4,5},{5,6},{6,7},{7,4},{8,9},{9,10},{10,1... | collective-permute-start | bytes 393224 | tf_op jit(solution)/shard_map/ppermute | solution.py:498
  105.5 20.2 %collective-permute-start.14 = (f32[136,512]{1,0:T(8,128)S(1)}, f32[136,512]{1,0:T(8,128)S(1)}, u32[]{:S(2)}, u32[]{:S(2)}) collective-permute-start(f32[136,512]{1,0:T(8,128)S(1)} %get-tuple-element.160), channel_id=1, source_target_pairs={{0,1},{1,2},{2,3},{3,0},{4,5},{5,6},{6,7},{7,4},{8,9},{9,10},{10,1... | collective-permute-start | bytes 835592 | tf_op jit(solution)/shard_map/ppermute | solution.py:498
  107.2 18.5 %collective-permute-start.16 = (f32[136,512]{1,0:T(8,128)S(1)}, f32[136,512]{1,0:T(8,128)S(1)}, u32[]{:S(2)}, u32[]{:S(2)}) collective-permute-start(f32[136,512]{1,0:T(8,128)S(1)} %get-tuple-element.162), channel_id=1, source_target_pairs={{0,3},{1,0},{2,1},{3,2},{4,7},{5,4},{6,5},{7,6},{8,11},{9,8},{10,9... | collective-permute-start | bytes 835592 | tf_op jit(solution)/shard_map/ppermute | solution.py:498
  109.4 16.3 %collective-permute-start.15 = (f32[128,512]{1,0:T(8,128)S(1)}, f32[128,512]{1,0:T(8,128)S(1)}, u32[]{:S(2)}, u32[]{:S(2)}) collective-permute-start(f32[128,512]{1,0:T(8,128)S(1)} %get-tuple-element.161), channel_id=1, source_target_pairs={{0,2},{1,3},{2,0},{3,1},{4,6},{5,7},{6,4},{7,5},{8,10},{9,11},{10,... | collective-permute-start | bytes 786440 | tf_op jit(solution)/shard_map/ppermute | solution.py:498
  120.3 10.5 %collective-permute-start.20 = (f32[128,128]{1,0:T(8,128)S(1)}, f32[128,128]{1,0:T(8,128)S(1)}, u32[]{:S(2)}, u32[]{:S(2)}) collective-permute-start(f32[128,128]{1,0:T(8,128)S(1)} %get-tuple-element.166), channel_id=1, source_target_pairs={{0,3},{1,0},{2,1},{3,2},{4,7},{5,4},{6,5},{7,6},{8,11},{9,8},{10,9... | collective-permute-start | bytes 196616 | tf_op jit(solution)/shard_map/ppermute | solution.py:498
  121.0 9.8 %collective-permute-start.21 = (f32[128,128]{1,0:T(8,128)S(1)}, f32[128,128]{1,0:T(8,128)S(1)}, u32[]{:S(2)}, u32[]{:S(2)}) collective-permute-start(f32[128,128]{1,0:T(8,128)S(1)} %get-tuple-element.167), channel_id=1, source_target_pairs={{0,2},{1,3},{2,0},{3,1},{4,6},{5,7},{6,4},{7,5},{8,10},{9,11},{10,... | collective-permute-start | bytes 196616 | tf_op jit(solution)/shard_map/ppermute | solution.py:498
  125.7 5.5 %collective-permute-start.22 = (f32[128,128]{1,0:T(8,128)S(1)}, f32[128,128]{1,0:T(8,128)S(1)}, u32[]{:S(2)}, u32[]{:S(2)}) collective-permute-start(f32[128,128]{1,0:T(8,128)S(1)} %get-tuple-element.168), channel_id=1, source_target_pairs={{0,1},{1,2},{2,3},{3,0},{4,5},{5,6},{6,7},{7,4},{8,9},{9,10},{10,1... | collective-permute-start | bytes 196616 | tf_op jit(solution)/shard_map/ppermute | solution.py:498
  131.2 13.3 %collective-permute-start.23 = (f32[128,512]{1,0:T(8,128)}, f32[128,512]{1,0:T(8,128)S(1)}, u32[]{:S(2)}, u32[]{:S(2)}) collective-permute-start(f32[128,512]{1,0:T(8,128)} %get-tuple-element.181), channel_id=1, source_target_pairs={{0,1},{1,2},{2,3},{3,0},{4,5},{5,6},{6,7},{7,4},{8,9},{9,10},{10,1... | collective-permute-start | bytes 786440 | tf_op jit(solution)/shard_map/ppermute | solution.py:498
  132.6 13.2 %collective-permute-start.24 = (f32[128,512]{1,0:T(8,128)}, f32[128,512]{1,0:T(8,128)S(1)}, u32[]{:S(2)}, u32[]{:S(2)}) collective-permute-start(f32[128,512]{1,0:T(8,128)} %get-tuple-element.182), channel_id=1, source_target_pairs={{0,2},{1,3},{2,0},{3,1},{4,6},{5,7},{6,4},{7,5},{8,10},{9,11},{10,... | collective-permute-start | bytes 786440 | tf_op jit(solution)/shard_map/ppermute | solution.py:498
  135.6 10.2 %collective-permute-start.25 = (f32[128,512]{1,0:T(8,128)}, f32[128,512]{1,0:T(8,128)S(1)}, u32[]{:S(2)}, u32[]{:S(2)}) collective-permute-start(f32[128,512]{1,0:T(8,128)} %get-tuple-element.183), channel_id=1, source_target_pairs={{0,3},{1,0},{2,1},{3,2},{4,7},{5,4},{6,5},{7,6},{8,11},{9,8},{10,9... | collective-permute-start | bytes 786440 | tf_op jit(solution)/shard_map/ppermute | solution.py:498
  135.8 12.8 %all-to-all-start.3 = ((f32[32,16,128]{2,1,0:T(8,128)}), f32[32,16,128]{2,1,0:T(8,128)S(1)}, u32[]{:S(2)}, u32[]{:S(2)}) async-start(f32[32,16,128]{2,1,0:T(8,128)} %get-tuple-element.163), calls=%async_computation.3 | async-start | bytes 524288 | tf_op jit(solution)/shard_map/all_to_all | solution.py:512
  148.6 12.8 %all-to-all-start.4 = ((f32[32,16,128]{2,1,0:T(8,128)}), f32[32,16,128]{2,1,0:T(8,128)S(1)}, u32[]{:S(2)}, u32[]{:S(2)}) async-start(f32[32,16,128]{2,1,0:T(8,128)} %get-tuple-element.195), calls=%async_computation.4 | async-start | bytes 524288 | tf_op jit(solution)/shard_map/all_to_all | solution.py:512
  153.6 16.3 %collective-permute-start.26 = (f32[128,512]{1,0:T(8,128)}, f32[128,512]{1,0:T(8,128)}, u32[]{:S(2)}, u32[]{:S(2)}) collective-permute-start(f32[128,512]{1,0:T(8,128)} %get-tuple-element.203), channel_id=1, source_target_pairs={{4,0},{8,4},{12,8},{16,12},{20,16},{24,20},{28,24},{32,28},{36,32}... | collective-permute-start | bytes 786440 | tf_op jit(solution)/shard_map/ppermute | solution.py:507
  162.2 12.8 %all-to-all-start.5 = ((f32[32,16,128]{2,1,0:T(8,128)}), f32[32,16,128]{2,1,0:T(8,128)S(1)}, u32[]{:S(2)}, u32[]{:S(2)}) async-start(f32[32,16,128]{2,1,0:T(8,128)} %shard_map.118), calls=%async_computation.5 | async-start | bytes 524288 | tf_op jit(solution)/shard_map/all_to_all | solution.py:512
Sparse Core Ops, SparseCore 0:
  10.3 48.2 all-gather.1

commit v11 on v10

--- a/solution.py
+++ b/solution.py
@@ -445,7 +445,7 @@
     height, width = rows[0].shape
     count = len(rows)
     number = blades.shape[0]
-    per_step, streams = 8, 4
+    per_step, streams = 16, 4
     fixed = lambda shape: pl.BlockSpec(shape, lambda i: (0,) * len(shape))
     table = lambda k: pl.BlockSpec((per_step, width // streams, LANE), lambda i: (i, k, 0))
     discs = where[0].shape[0]

time: 187 us -> 186 us (level)
    pallas_call x2, Pallas kernels: 9.52 us -> 7.64 us  [disc_forces(): pl.pallas_call(disc_kernel, grid=(number // per_step,), out_shape=[near((...]
  transfers between devices with their start and end apart: 34 -> 34, of which waited for: 15 -> 15; matrix products, arithmetic and copies ran while one was open for 3% -> 3% of each run, Pallas kernels for 25% -> 24%
where the time goes in v11:
time: 186 us; the launch traced here: 183 us
  starting transfers between devices  75.9 us (41%)
  Pallas kernels  49.5 us (27%)
  waiting for transfers between devices  37.6 us (20%)
  between operations  14.3 us (8%)
  local copies, waits for them, and re-layouts  4.97 us (3%)
    ppermute x24, starting transfers between devices, turn(): lax.ppermute(value, 'cross', [(i, (i + steps) % cross_size) for i in rang...  33.7 us
    all_to_all x6, starting transfers between devices, across_march(): lax.all_to_all(value, 'march', split_axis=0, concat_axis=0, tiled=True)  31.6 us
    pallas_call x11, Pallas kernels, call(): pl.pallas_call(kernel, out_shape=outs, in_specs=[SMEM] * scalars + [VMEM]...  25.1 us
    all_to_all x6, waiting for transfers between devices, across_march(): lax.all_to_all(value, 'march', split_axis=0, concat_axis=0, tiled=True)  18.9 us
    pallas_call x3, Pallas kernels, by_rows(): pl.pallas_call(kernel, grid_spec=pltpu.PrefetchScalarGridSpec(num_scalar_...  11.2 us
    ppermute x3, starting transfers between devices, along_march(): lax.ppermute(value, 'march', [(i, i + steps) for i in range(count) if 0 <...  10.6 us
    ppermute x24, waiting for transfers between devices, turn(): lax.ppermute(value, 'cross', [(i, (i + steps) % cross_size) for i in rang...  9.08 us
    pallas_call x2, Pallas kernels, disc_forces(): pl.pallas_call(disc_kernel, grid=(number // per_step,), out_shape=[near((...  7.64 us
  transfers between devices with their start and end apart: 34, of which 15 were waited for; matrix products, arithmetic and copies ran while one was open for 3% of the time, Pallas kernels for 24%

profile of v11, /device:TPU:2, one launch (start us, length us, event | category | flops | bytes accessed | tf_op | source)
XLA Modules:
  0.0 183.1 jit_solution(7523776400729003880)
XLA Ops:
  7.9 1.0 slice_bitcast_fusion
  8.9 1.9 %collective-permute-start.3 = (f32[128,512]{1,0:T(8,128)S(1)}, f32[128,512]{1,0:T(8,128)S(1)}, u32[]{:S(2)}, u32[]{:S(2)}) collective-permute-start(f32[128,512]{1,0:T(8,128)S(1)} %slice_bitcast_fusion), channel_id=1, source_target_pairs={{0,4},{4,8},{8,12},{12,16},{16,20},{20,24},{24,28},{28,32},{32,36}... | collective-permute-start | bytes 786440 | tf_op jit(solution)/shard_map/ppermute | solution.py:507
  11.8 4.1 %collective-permute-start.2 = (bf16[128,512]{1,0:T(8,128)(2,1)S(1)}, bf16[128,512]{1,0:T(8,128)(2,1)S(1)}, u32[]{:S(2)}, u32[]{:S(2)}) collective-permute-start(bf16[128,512]{1,0:T(8,128)(2,1)S(1)} %fusion.d0), channel_id=1, source_target_pairs={{0,3},{1,0},{2,1},{3,2},{4,7},{5,4},{6,5},{7,6},{8,11},{9,8},{10,9... | collective-permute-start | bytes 393224 | tf_op jit(solution)/shard_map/ppermute | solution.py:498
  16.0 2.7 %collective-permute-done.3.upstream = f32[128,512]{1,0:T(8,128)S(1)} collective-permute-done((f32[128,512]{1,0:T(8,128)S(1)}, f32[128,512]{1,0:T(8,128)S(1)}, u32[]{:S(2)}, u32[]{:S(2)}) %collective-permute-start.3) | collective-permute-done | bytes 262176 | tf_op jit(solution)/shard_map/ppermute | solution.py:507
  18.7 2.7 %shard_map.104 = (f32[128,512]{1,0:T(8,128)S(1)}, f32[136,512]{1,0:T(8,128)S(1)}, f32[128,512]{1,0:T(8,128)S(1)}, f32[136,512]{1,0:T(8,128)S(1)}) custom-call(s32[4]{0:T(128)S(1)} %pad_add_fusion.place, f32[4,128,512]{2,1,0:T(8,128)} %current.4, f32[128,512]{1,0:T(8,128)S(1)} %collective-permute-done.3.upstream, f32[128,512]{1,0:T(8,128)} %inflow.9), custom_call_target="tpu_custom_call" | custom-call | flops 1000000 | bytes 2097152 | tf_op jit(solution)/shard_map/pallas_call | solution.py:429
  21.4 4.0 %collective-permute-start.5 = (f32[128,512]{1,0:T(8,128)S(1)}, f32[128,512]{1,0:T(8,128)S(1)}, u32[]{:S(2)}, u32[]{:S(2)}) collective-permute-start(f32[128,512]{1,0:T(8,128)S(1)} %get-tuple-element.113), channel_id=1, source_target_pairs={{0,2},{1,3},{2,0},{3,1},{4,6},{5,7},{6,4},{7,5},{8,10},{9,11},{10,... | collective-permute-start | bytes 786440 | tf_op jit(solution)/shard_map/ppermute | solution.py:498
  25.4 1.0 collective-permute-start.4
  26.4 2.2 %collective-permute-start.6 = (f32[136,512]{1,0:T(8,128)S(1)}, f32[136,512]{1,0:T(8,128)S(1)}, u32[]{:S(2)}, u32[]{:S(2)}) collective-permute-start(f32[136,512]{1,0:T(8,128)S(1)} %get-tuple-element.114), channel_id=1, source_target_pairs={{0,3},{1,0},{2,1},{3,2},{4,7},{5,4},{6,5},{7,6},{8,11},{9,8},{10,9... | collective-permute-start | bytes 835592 | tf_op jit(solution)/shard_map/ppermute | solution.py:498
  29.3 4.2 %shard_map.105 = (f32[4,128,512]{2,1,0:T(8,128)}, f32[32,16,128]{2,1,0:T(8,128)}) custom-call(s32[4]{0:T(128)S(1)} %pad_add_fusion.place, f32[4,128,512]{2,1,0:T(8,128)} %current.4, f32[4,128,512]{2,1,0:T(8,128)} %damping.1), custom_call_target="tpu_custom_call" | custom-call | flops 4000000 | bytes 3145728 | tf_op jit(solution)/shard_map/pallas_call | solution.py:429
  33.5 5.7 %all-to-all-start = ((f32[32,16,128]{2,1,0:T(8,128)}), f32[32,16,128]{2,1,0:T(8,128)S(1)}, u32[]{:S(2)}, u32[]{:S(2)}) async-start(f32[32,16,128]{2,1,0:T(8,128)} %get-tuple-element.110), calls=%async_computation | async-start | bytes 524288 | tf_op jit(solution)/shard_map/all_to_all | solution.py:512
  39.3 5.6 %shard_map.106 = (f32[128,512]{1,0:T(8,128)S(1)}, f32[128,512]{1,0:T(8,128)S(1)}, f32[128,512]{1,0:T(8,128)S(1)}, f32[128,512]{1,0:T(8,128)S(1)}) custom-call(s32[4]{0:T(128)S(1)} %pad_add_fusion.place, f32[128,512]{1,0:T(8,128)S(1)} %get-tuple-element.111.x0, f32[136,512]{1,0:T(8,128)S(1)} %collective-permute-done.4.x1.before, ...), custom_call_target="tpu_custom_call" | custom-call | flops 3221225472 | bytes 5242880 | tf_op jit(solution)/shard_map/pallas_call | solution.py:573
  44.9 1.1 collective-permute-done.d1
  49.0 2.6 %collective-permute-start.8 = (f32[128,512]{1,0:T(8,128)S(1)}, f32[128,512]{1,0:T(8,128)S(1)}, u32[]{:S(2)}, u32[]{:S(2)}) collective-permute-start(f32[128,512]{1,0:T(8,128)S(1)} %get-tuple-element.122), channel_id=1, source_target_pairs={{0,2},{1,3},{2,0},{3,1},{4,6},{5,7},{6,4},{7,5},{8,10},{9,11},{10,... | collective-permute-start | bytes 786440 | tf_op jit(solution)/shard_map/ppermute | solution.py:498
  52.3 6.3 %all-gather.2.cloned.1.call-done.rest_0_.rest_1_.rest_2_.rest_3_ = bf16[32,512,128]{2,1,0:T(8,128)(2,1)} async-done(((bf16[1,512,128]{2,1,0:T(8,128)(2,1)}), bf16[32,512,128]{2,1,0:T(8,128)(2,1)}) %all-gather.2.cloned.1.call-update) | async-done | bytes 4194320 | tf_op jit(solution)/shard_map/all_gather | solution.py:514
  58.6 3.8 %shard_map.107 = (f32[128,128]{1,0:T(8,128)S(1)}, f32[128,128]{1,0:T(8,128)S(1)}, f32[128,128]{1,0:T(8,128)S(1)}, f32[128,128]{1,0:T(8,128)S(1)}) custom-call(bf16[128,512]{1,0:T(8,128)(2,1)S(1)} %fusion.d0, bf16[128,512]{1,0:T(8,128)(2,1)S(1)} %collective-permute-done.d1, bf16[128,512]{1,0:T(8,128)(2,1)S(1)} %collective-permute-done.1.d2, ...), custom_call_target="tpu_custom_call" | custom-call | flops 2147483648 | bytes 5242880 | tf_op jit(solution)/shard_map/pallas_call | solution.py:452
  62.4 2.7 %collective-permute-start.10 = (f32[128,128]{1,0:T(8,128)S(1)}, f32[128,128]{1,0:T(8,128)S(1)}, u32[]{:S(2)}, u32[]{:S(2)}) collective-permute-start(f32[128,128]{1,0:T(8,128)S(1)} %get-tuple-element.132), channel_id=1, source_target_pairs={{0,3},{1,0},{2,1},{3,2},{4,7},{5,4},{6,5},{7,6},{8,11},{9,8},{10,9... | collective-permute-start | bytes 196616 | tf_op jit(solution)/shard_map/ppermute | solution.py:498
  66.7 3.6 %shard_map.108 = (f32[4,128,512]{2,1,0:T(8,128)}, f32[4,128,512]{2,1,0:T(8,128)S(1)}, f32[128,512]{1,0:T(8,128)S(1)}, f32[128,512]{1,0:T(8,128)S(1)}) custom-call(s32[4]{0:T(128)S(1)} %pad_add_fusion.place, f32[4,128,512]{2,1,0:T(8,128)} %current.4, f32[136,512]{1,0:T(8,128)S(1)} %collective-permute-done.4.x1.before, ...), custom_call_target="tpu_custom_call" | custom-call | flops 8000000 | bytes 4194304 | tf_op jit(solution)/shard_map/pallas_call | solution.py:405
  72.0 1.6 shard_map.109
  73.6 5.9 %all-to-all-start.1 = ((f32[32,16,128]{2,1,0:T(8,128)}), f32[32,16,128]{2,1,0:T(8,128)S(1)}, u32[]{:S(2)}, u32[]{:S(2)}) async-start(f32[32,16,128]{2,1,0:T(8,128)} %get-tuple-element.141), calls=%async_computation.1 | async-start | bytes 524288 | tf_op jit(solution)/shard_map/all_to_all | solution.py:512
  79.5 4.3 %collective-permute-start.13 = (f32[128,512]{1,0:T(8,128)}, f32[128,512]{1,0:T(8,128)}, u32[]{:S(2)}, u32[]{:S(2)}) collective-permute-start(f32[128,512]{1,0:T(8,128)} %get-tuple-element.149), channel_id=1, source_target_pairs={{4,0},{8,4},{12,8},{16,12},{20,16},{24,20},{28,24},{32,28},{36,32}... | collective-permute-start | bytes 786440 | tf_op jit(solution)/shard_map/ppermute | solution.py:507
  83.9 3.4 %all-to-all-done.1.offset = f32[32,16,128]{2,1,0:T(8,128)S(1)} async-done(((f32[32,16,128]{2,1,0:T(8,128)}), f32[32,16,128]{2,1,0:T(8,128)S(1)}, u32[]{:S(2)}, u32[]{:S(2)}) %all-to-all-start.1) | async-done | bytes 262176 | tf_op jit(solution)/shard_map/all_to_all | solution.py:512
  88.0 5.0 %all-to-all-start.2 = ((f32[32,16,128]{2,1,0:T(8,128)}), f32[32,16,128]{2,1,0:T(8,128)S(1)}, u32[]{:S(2)}, u32[]{:S(2)}) async-start(f32[32,16,128]{2,1,0:T(8,128)} %shard_map.110), calls=%async_computation.2 | async-start | bytes 524288 | tf_op jit(solution)/shard_map/all_to_all | solution.py:512
  94.0 1.9 %shard_map.111 = (f32[5,128,512]{2,1,0:T(8,128)S(1)}, f32[4,128,512]{2,1,0:T(8,128)S(1)}) custom-call(s32[4]{0:T(128)S(1)} %pad_add_fusion.place, f32[128,512]{1,0:T(8,128)S(1)} %get-tuple-element.142.rest_0_.p0, f32[128,512]{1,0:T(8,128)S(1)} %collective-permute-done.7.rest_1_.p1, f32[128,512]{1,0:T(8,128)S(1)} %collective-permute-done.8.rest_2_.p2, ...), custom_call_target="tpu_custom_call" | custom-call | flops 4000000 | bytes 4194304 | tf_op jit(solution)/shard_map/pallas_call | solution.py:405
  96.0 4.9 %all-to-all-done.2.entering = f32[32,16,128]{2,1,0:T(8,128)S(1)} async-done(((f32[32,16,128]{2,1,0:T(8,128)}), f32[32,16,128]{2,1,0:T(8,128)S(1)}, u32[]{:S(2)}, u32[]{:S(2)}) %all-to-all-start.2) | async-done | bytes 262176 | tf_op jit(solution)/shard_map/all_to_all | solution.py:512
  100.8 1.2 shard_map.112
  102.8 1.6 collective-permute-start.18
  104.6 1.7 collective-permute-start.14
  106.3 1.5 collective-permute-start.16
  108.5 1.9 %collective-permute-start.15 = (f32[128,512]{1,0:T(8,128)S(1)}, f32[128,512]{1,0:T(8,128)S(1)}, u32[]{:S(2)}, u32[]{:S(2)}) collective-permute-start(f32[128,512]{1,0:T(8,128)S(1)} %get-tuple-element.161), channel_id=1, source_target_pairs={{0,2},{1,3},{2,0},{3,1},{4,6},{5,7},{6,4},{7,5},{8,10},{9,11},{10,... | collective-permute-start | bytes 786440 | tf_op jit(solution)/shard_map/ppermute | solution.py:498
  110.3 4.2 %shard_map.113 = (f32[4,128,512]{2,1,0:T(8,128)}, f32[32,16,128]{2,1,0:T(8,128)}, f32[4,128,512]{2,1,0:T(8,128)}) custom-call(s32[4]{0:T(128)S(1)} %pad_add_fusion.place, f32[4,128,512]{2,1,0:T(8,128)S(1)} %get-tuple-element.156.current, f32[4,128,512]{2,1,0:T(8,128)} %damping.1), custom_call_target="tpu_custom_call" | custom-call | flops 4000000 | bytes 3145728 | tf_op jit(solution)/shard_map/pallas_call | solution.py:429
  114.6 3.8 %shard_map.114 = (f32[128,128]{1,0:T(8,128)S(1)}, f32[128,128]{1,0:T(8,128)S(1)}, f32[128,128]{1,0:T(8,128)S(1)}, f32[128,128]{1,0:T(8,128)S(1)}, bf16[512,512]{...) custom-call(bf16[128,512]{1,0:T(8,128)(2,1)S(1)} %get-tuple-element.164.d0, ...), custom_call_target="tpu_custom_call" | custom-call | flops 2147483648 | bytes 5242880 | tf_op jit(solution)/shard_map/pallas_call | solution.py:452
  119.2 1.7 collective-permute-start.21
  120.8 4.0 %collective-permute-done.15.x2 = f32[128,512]{1,0:T(8,128)S(1)} collective-permute-done((f32[128,512]{1,0:T(8,128)S(1)}, f32[128,512]{1,0:T(8,128)S(1)}, u32[]{:S(2)}, u32[]{:S(2)}) %collective-permute-start.15) | collective-permute-done | bytes 262176 | tf_op jit(solution)/shard_map/ppermute | solution.py:498
  124.8 5.1 %shard_map.115 = (f32[128,512]{1,0:T(8,128)S(1)}, f32[128,512]{1,0:T(8,128)}, f32[128,512]{1,0:T(8,128)}, f32[128,512]{1,0:T(8,128)}) custom-call(s32[4]{0:T(128)S(1)} %pad_add_fusion.place, f32[128,512]{1,0:T(8,128)S(1)} %get-tuple-element.169.x0, f32[136,512]{1,0:T(8,128)S(1)} %collective-permute-done.14.x1.before, ...), custom_call_target="tpu_custom_call" | custom-call | flops 3221225472 | bytes 5242880 | tf_op jit(solution)/shard_map/pallas_call | solution.py:405
  130.3 1.4 collective-permute-start.23
  131.7 3.1 %collective-permute-start.24 = (f32[128,512]{1,0:T(8,128)}, f32[128,512]{1,0:T(8,128)S(1)}, u32[]{:S(2)}, u32[]{:S(2)}) collective-permute-start(f32[128,512]{1,0:T(8,128)} %get-tuple-element.182), channel_id=1, source_target_pairs={{0,2},{1,3},{2,0},{3,1},{4,6},{5,7},{6,4},{7,5},{8,10},{9,11},{10,... | collective-permute-start | bytes 786440 | tf_op jit(solution)/shard_map/ppermute | solution.py:498
  134.9 5.0 %all-to-all-start.3 = ((f32[32,16,128]{2,1,0:T(8,128)}), f32[32,16,128]{2,1,0:T(8,128)S(1)}, u32[]{:S(2)}, u32[]{:S(2)}) async-start(f32[32,16,128]{2,1,0:T(8,128)} %get-tuple-element.163), calls=%async_computation.3 | async-start | bytes 524288 | tf_op jit(solution)/shard_map/all_to_all | solution.py:512
  140.0 3.6 %shard_map.116 = (f32[4,128,512]{2,1,0:T(8,128)}, f32[4,128,512]{2,1,0:T(8,128)S(1)}, f32[128,512]{1,0:T(8,128)S(1)}, f32[128,512]{1,0:T(8,128)S(1)}) custom-call(s32[4]{0:T(128)S(1)} %pad_add_fusion.place, f32[4,128,512]{2,1,0:T(8,128)} %get-tuple-element.188.current, f32[136,512]{1,0:T(8,128)S(1)} %collective-permute-done.14.x1.before, ...), custom_call_target="tpu_custom_call" | custom-call | flops 8000000 | bytes 4194304 | tf_op jit(solution)/shard_map/pallas_call | solution.py:405
  143.6 1.3 collective-permute-done.24.rest_2_.p2
  144.9 1.6 shard_map.117
  146.5 1.2 all-to-all-done.3.scale
  147.8 5.0 %all-to-all-start.4 = ((f32[32,16,128]{2,1,0:T(8,128)}), f32[32,16,128]{2,1,0:T(8,128)S(1)}, u32[]{:S(2)}, u32[]{:S(2)}) async-start(f32[32,16,128]{2,1,0:T(8,128)} %get-tuple-element.195), calls=%async_computation.4 | async-start | bytes 524288 | tf_op jit(solution)/shard_map/all_to_all | solution.py:512
  152.8 4.3 %collective-permute-start.26 = (f32[128,512]{1,0:T(8,128)}, f32[128,512]{1,0:T(8,128)}, u32[]{:S(2)}, u32[]{:S(2)}) collective-permute-start(f32[128,512]{1,0:T(8,128)} %get-tuple-element.203), channel_id=1, source_target_pairs={{4,0},{8,4},{12,8},{16,12},{20,16},{24,20},{28,24},{32,28},{36,32}... | collective-permute-start | bytes 786440 | tf_op jit(solution)/shard_map/ppermute | solution.py:507
  157.1 3.5 %all-to-all-done.4.offset = f32[32,16,128]{2,1,0:T(8,128)S(1)} async-done(((f32[32,16,128]{2,1,0:T(8,128)}), f32[32,16,128]{2,1,0:T(8,128)S(1)}, u32[]{:S(2)}, u32[]{:S(2)}) %all-to-all-start.4) | async-done | bytes 262176 | tf_op jit(solution)/shard_map/all_to_all | solution.py:512
  161.3 5.0 %all-to-all-start.5 = ((f32[32,16,128]{2,1,0:T(8,128)}), f32[32,16,128]{2,1,0:T(8,128)S(1)}, u32[]{:S(2)}, u32[]{:S(2)}) async-start(f32[32,16,128]{2,1,0:T(8,128)} %shard_map.118), calls=%async_computation.5 | async-start | bytes 524288 | tf_op jit(solution)/shard_map/all_to_all | solution.py:512
  166.4 2.7 %shard_map.119 = (f32[4,128,512]{2,1,0:T(8,128)S(1)}, f32[4,128,512]{2,1,0:T(8,128)S(1)}, f32[4,128,512]{2,1,0:T(8,128)}) custom-call(s32[4]{0:T(128)S(1)} %pad_add_fusion.place, f32[128,512]{1,0:T(8,128)S(1)} %get-tuple-element.196.rest_0_.p0, f32[128,512]{1,0:T(8,128)S(1)} %collective-permute-done.23.rest_1_.p1, ...), custom_call_target="tpu_custom_call" | custom-call | flops 4000000 | bytes 4194304 | tf_op jit(solution)/shard_map/pallas_call | solution.py:405
  169.1 5.1 %all-to-all-done.5.entering = f32[32,16,128]{2,1,0:T(8,128)S(1)} async-done(((f32[32,16,128]{2,1,0:T(8,128)}), f32[32,16,128]{2,1,0:T(8,128)S(1)}, u32[]{:S(2)}, u32[]{:S(2)}) %all-to-all-start.5) | async-done | bytes 262176 | tf_op jit(solution)/shard_map/all_to_all | solution.py:512
  174.2 2.0 %shard_map.120 = f32[4,128,512]{2,1,0:T(8,128)} custom-call(f32[32,16,128]{2,1,0:T(8,128)S(1)} %all-to-all-done.5.entering, f32[4,128,512]{2,1,0:T(8,128)S(1)} %get-tuple-element.202.change, f32[128,512]{1,0:T(8,128)} %collective-permute-done.26.following, f32[4,128,512]{2,1,0:T(8,128)S(1)} %get-tuple-element.204.decay), custom_call_target="tpu_custom_call" | custom-call | flops 4000000 | bytes 5242880 | tf_op jit(solution)/shard_map/pallas_call | solution.py:405
  (50 shorter events, 14.7 us)
Async XLA Ops:
  7.2 51.4 %all-gather.2.cloned.1.call-start = ((), (), s32[]{:S(2)}) async-start(), calls=%async_computation.6 | async-start | bytes 4325376 | tf_op jit(solution)/shard_map/all_gather | solution.py:514
  8.9 9.8 %collective-permute-start.3 = (f32[128,512]{1,0:T(8,128)S(1)}, f32[128,512]{1,0:T(8,128)S(1)}, u32[]{:S(2)}, u32[]{:S(2)}) collective-permute-start(f32[128,512]{1,0:T(8,128)S(1)} %slice_bitcast_fusion), channel_id=1, source_target_pairs={{0,4},{4,8},{8,12},{12,16},{16,20},{20,24},{24,28},{28,32},{32,36}... | collective-permute-start | bytes 786440 | tf_op jit(solution)/shard_map/ppermute | solution.py:507
  11.8 33.1 %collective-permute-start.2 = (bf16[128,512]{1,0:T(8,128)(2,1)S(1)}, bf16[128,512]{1,0:T(8,128)(2,1)S(1)}, u32[]{:S(2)}, u32[]{:S(2)}) collective-permute-start(bf16[128,512]{1,0:T(8,128)(2,1)S(1)} %fusion.d0), channel_id=1, source_target_pairs={{0,3},{1,0},{2,1},{3,2},{4,7},{5,4},{6,5},{7,6},{8,11},{9,8},{10,9... | collective-permute-start | bytes 393224 | tf_op jit(solution)/shard_map/ppermute | solution.py:498
  15.9 29.0 %collective-permute-start.1 = (bf16[128,512]{1,0:T(8,128)(2,1)S(1)}, bf16[128,512]{1,0:T(8,128)(2,1)S(1)}, u32[]{:S(2)}, u32[]{:S(2)}) collective-permute-start(bf16[128,512]{1,0:T(8,128)(2,1)S(1)} %fusion.d0), channel_id=1, source_target_pairs={{0,2},{1,3},{2,0},{3,1},{4,6},{5,7},{6,4},{7,5},{8,10},{9,11},{10,... | collective-permute-start | bytes 393224 | tf_op jit(solution)/shard_map/ppermute | solution.py:498
  21.4 17.8 %collective-permute-start.5 = (f32[128,512]{1,0:T(8,128)S(1)}, f32[128,512]{1,0:T(8,128)S(1)}, u32[]{:S(2)}, u32[]{:S(2)}) collective-permute-start(f32[128,512]{1,0:T(8,128)S(1)} %get-tuple-element.113), channel_id=1, source_target_pairs={{0,2},{1,3},{2,0},{3,1},{4,6},{5,7},{6,4},{7,5},{8,10},{9,11},{10,... | collective-permute-start | bytes 786440 | tf_op jit(solution)/shard_map/ppermute | solution.py:498
  25.4 13.9 %collective-permute-start.4 = (f32[136,512]{1,0:T(8,128)S(1)}, f32[136,512]{1,0:T(8,128)S(1)}, u32[]{:S(2)}, u32[]{:S(2)}) collective-permute-start(f32[136,512]{1,0:T(8,128)S(1)} %get-tuple-element.112), channel_id=1, source_target_pairs={{0,1},{1,2},{2,3},{3,0},{4,5},{5,6},{6,7},{7,4},{8,9},{9,10},{10,1... | collective-permute-start | bytes 835592 | tf_op jit(solution)/shard_map/ppermute | solution.py:498
  26.4 12.9 %collective-permute-start.6 = (f32[136,512]{1,0:T(8,128)S(1)}, f32[136,512]{1,0:T(8,128)S(1)}, u32[]{:S(2)}, u32[]{:S(2)}) collective-permute-start(f32[136,512]{1,0:T(8,128)S(1)} %get-tuple-element.114), channel_id=1, source_target_pairs={{0,3},{1,0},{2,1},{3,2},{4,7},{5,4},{6,5},{7,6},{8,11},{9,8},{10,9... | collective-permute-start | bytes 835592 | tf_op jit(solution)/shard_map/ppermute | solution.py:498
  33.5 13.4 %all-to-all-start = ((f32[32,16,128]{2,1,0:T(8,128)}), f32[32,16,128]{2,1,0:T(8,128)S(1)}, u32[]{:S(2)}, u32[]{:S(2)}) async-start(f32[32,16,128]{2,1,0:T(8,128)} %get-tuple-element.110), calls=%async_computation | async-start | bytes 524288 | tf_op jit(solution)/shard_map/all_to_all | solution.py:512
  39.2 6.8 %collective-permute-start = (bf16[128,512]{1,0:T(8,128)(2,1)S(1)}, bf16[128,512]{1,0:T(8,128)(2,1)S(1)}, u32[]{:S(2)}, u32[]{:S(2)}) collective-permute-start(bf16[128,512]{1,0:T(8,128)(2,1)S(1)} %fusion.d0), channel_id=1, source_target_pairs={{0,1},{1,2},{2,3},{3,0},{4,5},{5,6},{6,7},{7,4},{8,9},{9,10},{10,1... | collective-permute-start | bytes 393224 | tf_op jit(solution)/shard_map/ppermute | solution.py:498
  49.0 16.7 %collective-permute-start.7 = (f32[128,512]{1,0:T(8,128)S(1)}, f32[128,512]{1,0:T(8,128)S(1)}, u32[]{:S(2)}, u32[]{:S(2)}) collective-permute-start(f32[128,512]{1,0:T(8,128)S(1)} %get-tuple-element.121), channel_id=1, source_target_pairs={{0,1},{1,2},{2,3},{3,0},{4,5},{5,6},{6,7},{7,4},{8,9},{9,10},{10,1... | collective-permute-start | bytes 786440 | tf_op jit(solution)/shard_map/ppermute | solution.py:498
  49.0 21.3 %collective-permute-start.8 = (f32[128,512]{1,0:T(8,128)S(1)}, f32[128,512]{1,0:T(8,128)S(1)}, u32[]{:S(2)}, u32[]{:S(2)}) collective-permute-start(f32[128,512]{1,0:T(8,128)S(1)} %get-tuple-element.122), channel_id=1, source_target_pairs={{0,2},{1,3},{2,0},{3,1},{4,6},{5,7},{6,4},{7,5},{8,10},{9,11},{10,... | collective-permute-start | bytes 786440 | tf_op jit(solution)/shard_map/ppermute | solution.py:498
  51.7 18.6 %collective-permute-start.9 = (f32[128,512]{1,0:T(8,128)S(1)}, f32[128,512]{1,0:T(8,128)S(1)}, u32[]{:S(2)}, u32[]{:S(2)}) collective-permute-start(f32[128,512]{1,0:T(8,128)S(1)} %get-tuple-element.123), channel_id=1, source_target_pairs={{0,3},{1,0},{2,1},{3,2},{4,7},{5,4},{6,5},{7,6},{8,11},{9,8},{10,9... | collective-permute-start | bytes 786440 | tf_op jit(solution)/shard_map/ppermute | solution.py:498
  62.4 8.0 %collective-permute-start.10 = (f32[128,128]{1,0:T(8,128)S(1)}, f32[128,128]{1,0:T(8,128)S(1)}, u32[]{:S(2)}, u32[]{:S(2)}) collective-permute-start(f32[128,128]{1,0:T(8,128)S(1)} %get-tuple-element.132), channel_id=1, source_target_pairs={{0,3},{1,0},{2,1},{3,2},{4,7},{5,4},{6,5},{7,6},{8,11},{9,8},{10,9... | collective-permute-start | bytes 196616 | tf_op jit(solution)/shard_map/ppermute | solution.py:498
  65.1 6.2 %collective-permute-start.11 = (f32[128,128]{1,0:T(8,128)S(1)}, f32[128,128]{1,0:T(8,128)S(1)}, u32[]{:S(2)}, u32[]{:S(2)}) collective-permute-start(f32[128,128]{1,0:T(8,128)S(1)} %get-tuple-element.133), channel_id=1, source_target_pairs={{0,2},{1,3},{2,0},{3,1},{4,6},{5,7},{6,4},{7,5},{8,10},{9,11},{10,... | collective-permute-start | bytes 196616 | tf_op jit(solution)/shard_map/ppermute | solution.py:498
  65.8 6.2 %collective-permute-start.12 = (f32[128,128]{1,0:T(8,128)S(1)}, f32[128,128]{1,0:T(8,128)S(1)}, u32[]{:S(2)}, u32[]{:S(2)}) collective-permute-start(f32[128,128]{1,0:T(8,128)S(1)} %get-tuple-element.134), channel_id=1, source_target_pairs={{0,1},{1,2},{2,3},{3,0},{4,5},{5,6},{6,7},{7,4},{8,9},{9,10},{10,1... | collective-permute-start | bytes 196616 | tf_op jit(solution)/shard_map/ppermute | solution.py:498
  70.3 3.3 %copy-start = (f32[128,512]{1,0:T(8,128)}, f32[128,512]{1,0:T(8,128)S(1)}, u32[]{:S(2)}) copy-start(f32[128,512]{1,0:T(8,128)S(1)} %collective-permute-done.9.rest_3_.p3) | copy-start | bytes 786436
  73.6 13.6 %all-to-all-start.1 = ((f32[32,16,128]{2,1,0:T(8,128)}), f32[32,16,128]{2,1,0:T(8,128)S(1)}, u32[]{:S(2)}, u32[]{:S(2)}) async-start(f32[32,16,128]{2,1,0:T(8,128)} %get-tuple-element.141), calls=%async_computation.1 | async-start | bytes 524288 | tf_op jit(solution)/shard_map/all_to_all | solution.py:512
  79.5 16.4 %collective-permute-start.13 = (f32[128,512]{1,0:T(8,128)}, f32[128,512]{1,0:T(8,128)}, u32[]{:S(2)}, u32[]{:S(2)}) collective-permute-start(f32[128,512]{1,0:T(8,128)} %get-tuple-element.149), channel_id=1, source_target_pairs={{4,0},{8,4},{12,8},{16,12},{20,16},{24,20},{28,24},{32,28},{36,32}... | collective-permute-start | bytes 786440 | tf_op jit(solution)/shard_map/ppermute | solution.py:507
  88.0 12.8 %all-to-all-start.2 = ((f32[32,16,128]{2,1,0:T(8,128)}), f32[32,16,128]{2,1,0:T(8,128)S(1)}, u32[]{:S(2)}, u32[]{:S(2)}) async-start(f32[32,16,128]{2,1,0:T(8,128)} %shard_map.110), calls=%async_computation.2 | async-start | bytes 524288 | tf_op jit(solution)/shard_map/all_to_all | solution.py:512
  93.0 1.0 copy-start.1
  102.1 6.4 %collective-permute-start.19 = (bf16[128,512]{1,0:T(8,128)(2,1)S(1)}, bf16[128,512]{1,0:T(8,128)(2,1)S(1)}, u32[]{:S(2)}, u32[]{:S(2)}) collective-permute-start(bf16[128,512]{1,0:T(8,128)(2,1)S(1)} %get-tuple-element.164.d0), channel_id=1, source_target_pairs={{0,3},{1,0},{2,1},{3,2},{4,7},{5,4},{6,5},{7,6},{8,11},{9,8},{10,9... | collective-permute-start | bytes 393224 | tf_op jit(solution)/shard_map/ppermute | solution.py:498
  102.8 11.8 %collective-permute-start.18 = (bf16[128,512]{1,0:T(8,128)(2,1)S(1)}, bf16[128,512]{1,0:T(8,128)(2,1)S(1)}, u32[]{:S(2)}, u32[]{:S(2)}) collective-permute-start(bf16[128,512]{1,0:T(8,128)(2,1)S(1)} %get-tuple-element.164.d0), channel_id=1, source_target_pairs={{0,2},{1,3},{2,0},{3,1},{4,6},{5,7},{6,4},{7,5},{8,10},{9,11},{10,... | collective-permute-start | bytes 393224 | tf_op jit(solution)/shard_map/ppermute | solution.py:498
  104.5 10.1 %collective-permute-start.17 = (bf16[128,512]{1,0:T(8,128)(2,1)S(1)}, bf16[128,512]{1,0:T(8,128)(2,1)S(1)}, u32[]{:S(2)}, u32[]{:S(2)}) collective-permute-start(bf16[128,512]{1,0:T(8,128)(2,1)S(1)} %get-tuple-element.164.d0), channel_id=1, source_target_pairs={{0,1},{1,2},{2,3},{3,0},{4,5},{5,6},{6,7},{7,4},{8,9},{9,10},{10,1... | collective-permute-start | bytes 393224 | tf_op jit(solution)/shard_map/ppermute | solution.py:498
  104.6 20.2 %collective-permute-start.14 = (f32[136,512]{1,0:T(8,128)S(1)}, f32[136,512]{1,0:T(8,128)S(1)}, u32[]{:S(2)}, u32[]{:S(2)}) collective-permute-start(f32[136,512]{1,0:T(8,128)S(1)} %get-tuple-element.160), channel_id=1, source_target_pairs={{0,1},{1,2},{2,3},{3,0},{4,5},{5,6},{6,7},{7,4},{8,9},{9,10},{10,1... | collective-permute-start | bytes 835592 | tf_op jit(solution)/shard_map/ppermute | solution.py:498
  106.3 18.5 %collective-permute-start.16 = (f32[136,512]{1,0:T(8,128)S(1)}, f32[136,512]{1,0:T(8,128)S(1)}, u32[]{:S(2)}, u32[]{:S(2)}) collective-permute-start(f32[136,512]{1,0:T(8,128)S(1)} %get-tuple-element.162), channel_id=1, source_target_pairs={{0,3},{1,0},{2,1},{3,2},{4,7},{5,4},{6,5},{7,6},{8,11},{9,8},{10,9... | collective-permute-start | bytes 835592 | tf_op jit(solution)/shard_map/ppermute | solution.py:498
  108.5 16.3 %collective-permute-start.15 = (f32[128,512]{1,0:T(8,128)S(1)}, f32[128,512]{1,0:T(8,128)S(1)}, u32[]{:S(2)}, u32[]{:S(2)}) collective-permute-start(f32[128,512]{1,0:T(8,128)S(1)} %get-tuple-element.161), channel_id=1, source_target_pairs={{0,2},{1,3},{2,0},{3,1},{4,6},{5,7},{6,4},{7,5},{8,10},{9,11},{10,... | collective-permute-start | bytes 786440 | tf_op jit(solution)/shard_map/ppermute | solution.py:498
  118.4 11.5 %collective-permute-start.20 = (f32[128,128]{1,0:T(8,128)S(1)}, f32[128,128]{1,0:T(8,128)S(1)}, u32[]{:S(2)}, u32[]{:S(2)}) collective-permute-start(f32[128,128]{1,0:T(8,128)S(1)} %get-tuple-element.166), channel_id=1, source_target_pairs={{0,3},{1,0},{2,1},{3,2},{4,7},{5,4},{6,5},{7,6},{8,11},{9,8},{10,9... | collective-permute-start | bytes 196616 | tf_op jit(solution)/shard_map/ppermute | solution.py:498
  119.2 10.8 %collective-permute-start.21 = (f32[128,128]{1,0:T(8,128)S(1)}, f32[128,128]{1,0:T(8,128)S(1)}, u32[]{:S(2)}, u32[]{:S(2)}) collective-permute-start(f32[128,128]{1,0:T(8,128)S(1)} %get-tuple-element.167), channel_id=1, source_target_pairs={{0,2},{1,3},{2,0},{3,1},{4,6},{5,7},{6,4},{7,5},{8,10},{9,11},{10,... | collective-permute-start | bytes 196616 | tf_op jit(solution)/shard_map/ppermute | solution.py:498
  124.8 5.5 %collective-permute-start.22 = (f32[128,128]{1,0:T(8,128)S(1)}, f32[128,128]{1,0:T(8,128)S(1)}, u32[]{:S(2)}, u32[]{:S(2)}) collective-permute-start(f32[128,128]{1,0:T(8,128)S(1)} %get-tuple-element.168), channel_id=1, source_target_pairs={{0,1},{1,2},{2,3},{3,0},{4,5},{5,6},{6,7},{7,4},{8,9},{9,10},{10,1... | collective-permute-start | bytes 196616 | tf_op jit(solution)/shard_map/ppermute | solution.py:498
  130.3 13.3 %collective-permute-start.23 = (f32[128,512]{1,0:T(8,128)}, f32[128,512]{1,0:T(8,128)S(1)}, u32[]{:S(2)}, u32[]{:S(2)}) collective-permute-start(f32[128,512]{1,0:T(8,128)} %get-tuple-element.181), channel_id=1, source_target_pairs={{0,1},{1,2},{2,3},{3,0},{4,5},{5,6},{6,7},{7,4},{8,9},{9,10},{10,1... | collective-permute-start | bytes 786440 | tf_op jit(solution)/shard_map/ppermute | solution.py:498
  131.7 13.2 %collective-permute-start.24 = (f32[128,512]{1,0:T(8,128)}, f32[128,512]{1,0:T(8,128)S(1)}, u32[]{:S(2)}, u32[]{:S(2)}) collective-permute-start(f32[128,512]{1,0:T(8,128)} %get-tuple-element.182), channel_id=1, source_target_pairs={{0,2},{1,3},{2,0},{3,1},{4,6},{5,7},{6,4},{7,5},{8,10},{9,11},{10,... | collective-permute-start | bytes 786440 | tf_op jit(solution)/shard_map/ppermute | solution.py:498
  134.7 10.2 %collective-permute-start.25 = (f32[128,512]{1,0:T(8,128)}, f32[128,512]{1,0:T(8,128)S(1)}, u32[]{:S(2)}, u32[]{:S(2)}) collective-permute-start(f32[128,512]{1,0:T(8,128)} %get-tuple-element.183), channel_id=1, source_target_pairs={{0,3},{1,0},{2,1},{3,2},{4,7},{5,4},{6,5},{7,6},{8,11},{9,8},{10,9... | collective-permute-start | bytes 786440 | tf_op jit(solution)/shard_map/ppermute | solution.py:498
  134.9 12.8 %all-to-all-start.3 = ((f32[32,16,128]{2,1,0:T(8,128)}), f32[32,16,128]{2,1,0:T(8,128)S(1)}, u32[]{:S(2)}, u32[]{:S(2)}) async-start(f32[32,16,128]{2,1,0:T(8,128)} %get-tuple-element.163), calls=%async_computation.3 | async-start | bytes 524288 | tf_op jit(solution)/shard_map/all_to_all | solution.py:512
  147.8 12.8 %all-to-all-start.4 = ((f32[32,16,128]{2,1,0:T(8,128)}), f32[32,16,128]{2,1,0:T(8,128)S(1)}, u32[]{:S(2)}, u32[]{:S(2)}) async-start(f32[32,16,128]{2,1,0:T(8,128)} %get-tuple-element.195), calls=%async_computation.4 | async-start | bytes 524288 | tf_op jit(solution)/shard_map/all_to_all | solution.py:512
  152.8 16.3 %collective-permute-start.26 = (f32[128,512]{1,0:T(8,128)}, f32[128,512]{1,0:T(8,128)}, u32[]{:S(2)}, u32[]{:S(2)}) collective-permute-start(f32[128,512]{1,0:T(8,128)} %get-tuple-element.203), channel_id=1, source_target_pairs={{4,0},{8,4},{12,8},{16,12},{20,16},{24,20},{28,24},{32,28},{36,32}... | collective-permute-start | bytes 786440 | tf_op jit(solution)/shard_map/ppermute | solution.py:507
  161.3 12.8 %all-to-all-start.5 = ((f32[32,16,128]{2,1,0:T(8,128)}), f32[32,16,128]{2,1,0:T(8,128)S(1)}, u32[]{:S(2)}, u32[]{:S(2)}) async-start(f32[32,16,128]{2,1,0:T(8,128)} %shard_map.118), calls=%async_computation.5 | async-start | bytes 524288 | tf_op jit(solution)/shard_map/all_to_all | solution.py:512
Sparse Core Ops, SparseCore 0:
  10.3 48.2 all-gather.1

commit v12 on v11

--- a/solution.py
+++ b/solution.py
@@ -445,7 +445,7 @@
     height, width = rows[0].shape
     count = len(rows)
     number = blades.shape[0]
-    per_step, streams = 16, 4
+    per_step, streams = 32, 4
     fixed = lambda shape: pl.BlockSpec(shape, lambda i: (0,) * len(shape))
     table = lambda k: pl.BlockSpec((per_step, width // streams, LANE), lambda i: (i, k, 0))
     discs = where[0].shape[0]

time: 186 us -> 187 us (level)
  transfers between devices with their start and end apart: 34 -> 34, of which waited for: 15 -> 15; matrix products, arithmetic and copies ran while one was open for 3% -> 3% of each run, Pallas kernels for 24% -> 25%
where the time goes in v12:
time: 187 us; the launch traced here: 183 us
  starting transfers between devices  75.9 us (41%)
  Pallas kernels  50.2 us (27%)
  waiting for transfers between devices  37.3 us (20%)
  between operations  14.3 us (8%)
  local copies, waits for them, and re-layouts  4.97 us (3%)
    ppermute x24, starting transfers between devices, turn(): lax.ppermute(value, 'cross', [(i, (i + steps) % cross_size) for i in rang...  33.6 us
    all_to_all x6, starting transfers between devices, across_march(): lax.all_to_all(value, 'march', split_axis=0, concat_axis=0, tiled=True)  31.6 us
    pallas_call x11, Pallas kernels, call(): pl.pallas_call(kernel, out_shape=outs, in_specs=[SMEM] * scalars + [VMEM]...  25.1 us
    all_to_all x6, waiting for transfers between devices, across_march(): lax.all_to_all(value, 'march', split_axis=0, concat_axis=0, tiled=True)  18.9 us
    pallas_call x3, Pallas kernels, by_rows(): pl.pallas_call(kernel, grid_spec=pltpu.PrefetchScalarGridSpec(num_scalar_...  11.2 us
    ppermute x3, starting transfers between devices, along_march(): lax.ppermute(value, 'march', [(i, i + steps) for i in range(count) if 0 <...  10.6 us
    ppermute x24, waiting for transfers between devices, turn(): lax.ppermute(value, 'cross', [(i, (i + steps) % cross_size) for i in rang...  8.73 us
    pallas_call x2, Pallas kernels, disc_forces(): pl.pallas_call(disc_kernel, grid=(number // per_step,), out_shape=[near((...  8.42 us
  transfers between devices with their start and end apart: 34, of which 15 were waited for; matrix products, arithmetic and copies ran while one was open for 3% of the time, Pallas kernels for 25%

profile of v12, /device:TPU:2, one launch (start us, length us, event | category | flops | bytes accessed | tf_op | source)
XLA Modules:
  0.0 183.4 jit_solution(15878568015304673788)
XLA Ops:
  7.9 1.0 slice_bitcast_fusion
  8.9 1.9 %collective-permute-start.3 = (f32[128,512]{1,0:T(8,128)S(1)}, f32[128,512]{1,0:T(8,128)S(1)}, u32[]{:S(2)}, u32[]{:S(2)}) collective-permute-start(f32[128,512]{1,0:T(8,128)S(1)} %slice_bitcast_fusion), channel_id=1, source_target_pairs={{0,4},{4,8},{8,12},{12,16},{16,20},{20,24},{24,28},{28,32},{32,36}... | collective-permute-start | bytes 786440 | tf_op jit(solution)/shard_map/ppermute | solution.py:507
  11.8 4.1 %collective-permute-start.2 = (bf16[128,512]{1,0:T(8,128)(2,1)S(1)}, bf16[128,512]{1,0:T(8,128)(2,1)S(1)}, u32[]{:S(2)}, u32[]{:S(2)}) collective-permute-start(bf16[128,512]{1,0:T(8,128)(2,1)S(1)} %fusion.d0), channel_id=1, source_target_pairs={{0,3},{1,0},{2,1},{3,2},{4,7},{5,4},{6,5},{7,6},{8,11},{9,8},{10,9... | collective-permute-start | bytes 393224 | tf_op jit(solution)/shard_map/ppermute | solution.py:498
  16.0 2.7 %collective-permute-done.3.upstream = f32[128,512]{1,0:T(8,128)S(1)} collective-permute-done((f32[128,512]{1,0:T(8,128)S(1)}, f32[128,512]{1,0:T(8,128)S(1)}, u32[]{:S(2)}, u32[]{:S(2)}) %collective-permute-start.3) | collective-permute-done | bytes 262176 | tf_op jit(solution)/shard_map/ppermute | solution.py:507
  18.7 2.7 %shard_map.104 = (f32[128,512]{1,0:T(8,128)S(1)}, f32[136,512]{1,0:T(8,128)S(1)}, f32[128,512]{1,0:T(8,128)S(1)}, f32[136,512]{1,0:T(8,128)S(1)}) custom-call(s32[4]{0:T(128)S(1)} %pad_add_fusion.place, f32[4,128,512]{2,1,0:T(8,128)} %current.4, f32[128,512]{1,0:T(8,128)S(1)} %collective-permute-done.3.upstream, f32[128,512]{1,0:T(8,128)} %inflow.9), custom_call_target="tpu_custom_call" | custom-call | flops 1000000 | bytes 2097152 | tf_op jit(solution)/shard_map/pallas_call | solution.py:429
  21.4 4.0 %collective-permute-start.5 = (f32[128,512]{1,0:T(8,128)S(1)}, f32[128,512]{1,0:T(8,128)S(1)}, u32[]{:S(2)}, u32[]{:S(2)}) collective-permute-start(f32[128,512]{1,0:T(8,128)S(1)} %get-tuple-element.113), channel_id=1, source_target_pairs={{0,2},{1,3},{2,0},{3,1},{4,6},{5,7},{6,4},{7,5},{8,10},{9,11},{10,... | collective-permute-start | bytes 786440 | tf_op jit(solution)/shard_map/ppermute | solution.py:498
  25.4 1.0 collective-permute-start.4
  26.4 2.2 %collective-permute-start.6 = (f32[136,512]{1,0:T(8,128)S(1)}, f32[136,512]{1,0:T(8,128)S(1)}, u32[]{:S(2)}, u32[]{:S(2)}) collective-permute-start(f32[136,512]{1,0:T(8,128)S(1)} %get-tuple-element.114), channel_id=1, source_target_pairs={{0,3},{1,0},{2,1},{3,2},{4,7},{5,4},{6,5},{7,6},{8,11},{9,8},{10,9... | collective-permute-start | bytes 835592 | tf_op jit(solution)/shard_map/ppermute | solution.py:498
  29.3 4.2 %shard_map.105 = (f32[4,128,512]{2,1,0:T(8,128)}, f32[32,16,128]{2,1,0:T(8,128)}) custom-call(s32[4]{0:T(128)S(1)} %pad_add_fusion.place, f32[4,128,512]{2,1,0:T(8,128)} %current.4, f32[4,128,512]{2,1,0:T(8,128)} %damping.1), custom_call_target="tpu_custom_call" | custom-call | flops 4000000 | bytes 3145728 | tf_op jit(solution)/shard_map/pallas_call | solution.py:429
  33.5 5.7 %all-to-all-start = ((f32[32,16,128]{2,1,0:T(8,128)}), f32[32,16,128]{2,1,0:T(8,128)S(1)}, u32[]{:S(2)}, u32[]{:S(2)}) async-start(f32[32,16,128]{2,1,0:T(8,128)} %get-tuple-element.110), calls=%async_computation | async-start | bytes 524288 | tf_op jit(solution)/shard_map/all_to_all | solution.py:512
  39.3 5.6 %shard_map.106 = (f32[128,512]{1,0:T(8,128)S(1)}, f32[128,512]{1,0:T(8,128)S(1)}, f32[128,512]{1,0:T(8,128)S(1)}, f32[128,512]{1,0:T(8,128)S(1)}) custom-call(s32[4]{0:T(128)S(1)} %pad_add_fusion.place, f32[128,512]{1,0:T(8,128)S(1)} %get-tuple-element.111.x0, f32[136,512]{1,0:T(8,128)S(1)} %collective-permute-done.4.x1.before, ...), custom_call_target="tpu_custom_call" | custom-call | flops 3221225472 | bytes 5242880 | tf_op jit(solution)/shard_map/pallas_call | solution.py:573
  44.9 1.1 collective-permute-done.d1
  49.0 2.6 %collective-permute-start.8 = (f32[128,512]{1,0:T(8,128)S(1)}, f32[128,512]{1,0:T(8,128)S(1)}, u32[]{:S(2)}, u32[]{:S(2)}) collective-permute-start(f32[128,512]{1,0:T(8,128)S(1)} %get-tuple-element.122), channel_id=1, source_target_pairs={{0,2},{1,3},{2,0},{3,1},{4,6},{5,7},{6,4},{7,5},{8,10},{9,11},{10,... | collective-permute-start | bytes 786440 | tf_op jit(solution)/shard_map/ppermute | solution.py:498
  52.3 6.3 %all-gather.2.cloned.1.call-done.rest_0_.rest_1_.rest_2_.rest_3_ = bf16[32,512,128]{2,1,0:T(8,128)(2,1)} async-done(((bf16[1,512,128]{2,1,0:T(8,128)(2,1)}), bf16[32,512,128]{2,1,0:T(8,128)(2,1)}) %all-gather.2.cloned.1.call-update) | async-done | bytes 4194320 | tf_op jit(solution)/shard_map/all_gather | solution.py:514
  58.6 4.2 %shard_map.107 = (f32[128,128]{1,0:T(8,128)S(1)}, f32[128,128]{1,0:T(8,128)S(1)}, f32[128,128]{1,0:T(8,128)S(1)}, f32[128,128]{1,0:T(8,128)S(1)}) custom-call(bf16[128,512]{1,0:T(8,128)(2,1)S(1)} %fusion.d0, bf16[128,512]{1,0:T(8,128)(2,1)S(1)} %collective-permute-done.d1, bf16[128,512]{1,0:T(8,128)(2,1)S(1)} %collective-permute-done.1.d2, ...), custom_call_target="tpu_custom_call" | custom-call | flops 2147483648 | bytes 5242880 | tf_op jit(solution)/shard_map/pallas_call | solution.py:452
  62.8 2.7 %collective-permute-start.10 = (f32[128,128]{1,0:T(8,128)S(1)}, f32[128,128]{1,0:T(8,128)S(1)}, u32[]{:S(2)}, u32[]{:S(2)}) collective-permute-start(f32[128,128]{1,0:T(8,128)S(1)} %get-tuple-element.132), channel_id=1, source_target_pairs={{0,3},{1,0},{2,1},{3,2},{4,7},{5,4},{6,5},{7,6},{8,11},{9,8},{10,9... | collective-permute-start | bytes 196616 | tf_op jit(solution)/shard_map/ppermute | solution.py:498
  67.1 3.6 %shard_map.108 = (f32[4,128,512]{2,1,0:T(8,128)}, f32[4,128,512]{2,1,0:T(8,128)S(1)}, f32[128,512]{1,0:T(8,128)S(1)}, f32[128,512]{1,0:T(8,128)S(1)}) custom-call(s32[4]{0:T(128)S(1)} %pad_add_fusion.place, f32[4,128,512]{2,1,0:T(8,128)} %current.4, f32[136,512]{1,0:T(8,128)S(1)} %collective-permute-done.4.x1.before, ...), custom_call_target="tpu_custom_call" | custom-call | flops 8000000 | bytes 4194304 | tf_op jit(solution)/shard_map/pallas_call | solution.py:405
  72.4 1.6 shard_map.109
  74.0 5.9 %all-to-all-start.1 = ((f32[32,16,128]{2,1,0:T(8,128)}), f32[32,16,128]{2,1,0:T(8,128)S(1)}, u32[]{:S(2)}, u32[]{:S(2)}) async-start(f32[32,16,128]{2,1,0:T(8,128)} %get-tuple-element.141), calls=%async_computation.1 | async-start | bytes 524288 | tf_op jit(solution)/shard_map/all_to_all | solution.py:512
  79.9 4.3 %collective-permute-start.13 = (f32[128,512]{1,0:T(8,128)}, f32[128,512]{1,0:T(8,128)}, u32[]{:S(2)}, u32[]{:S(2)}) collective-permute-start(f32[128,512]{1,0:T(8,128)} %get-tuple-element.149), channel_id=1, source_target_pairs={{4,0},{8,4},{12,8},{16,12},{20,16},{24,20},{28,24},{32,28},{36,32}... | collective-permute-start | bytes 786440 | tf_op jit(solution)/shard_map/ppermute | solution.py:507
  84.3 3.4 %all-to-all-done.1.offset = f32[32,16,128]{2,1,0:T(8,128)S(1)} async-done(((f32[32,16,128]{2,1,0:T(8,128)}), f32[32,16,128]{2,1,0:T(8,128)S(1)}, u32[]{:S(2)}, u32[]{:S(2)}) %all-to-all-start.1) | async-done | bytes 262176 | tf_op jit(solution)/shard_map/all_to_all | solution.py:512
  88.4 5.0 %all-to-all-start.2 = ((f32[32,16,128]{2,1,0:T(8,128)}), f32[32,16,128]{2,1,0:T(8,128)S(1)}, u32[]{:S(2)}, u32[]{:S(2)}) async-start(f32[32,16,128]{2,1,0:T(8,128)} %shard_map.110), calls=%async_computation.2 | async-start | bytes 524288 | tf_op jit(solution)/shard_map/all_to_all | solution.py:512
  94.4 1.9 %shard_map.111 = (f32[5,128,512]{2,1,0:T(8,128)S(1)}, f32[4,128,512]{2,1,0:T(8,128)S(1)}) custom-call(s32[4]{0:T(128)S(1)} %pad_add_fusion.place, f32[128,512]{1,0:T(8,128)S(1)} %get-tuple-element.142.rest_0_.p0, f32[128,512]{1,0:T(8,128)S(1)} %collective-permute-done.7.rest_1_.p1, f32[128,512]{1,0:T(8,128)S(1)} %collective-permute-done.8.rest_2_.p2, ...), custom_call_target="tpu_custom_call" | custom-call | flops 4000000 | bytes 4194304 | tf_op jit(solution)/shard_map/pallas_call | solution.py:405
  96.3 4.9 %all-to-all-done.2.entering = f32[32,16,128]{2,1,0:T(8,128)S(1)} async-done(((f32[32,16,128]{2,1,0:T(8,128)}), f32[32,16,128]{2,1,0:T(8,128)S(1)}, u32[]{:S(2)}, u32[]{:S(2)}) %all-to-all-start.2) | async-done | bytes 262176 | tf_op jit(solution)/shard_map/all_to_all | solution.py:512
  101.2 1.2 shard_map.112
  103.2 1.6 collective-permute-start.18
  105.0 1.7 collective-permute-start.14
  106.7 1.5 collective-permute-start.16
  108.9 1.9 %collective-permute-start.15 = (f32[128,512]{1,0:T(8,128)S(1)}, f32[128,512]{1,0:T(8,128)S(1)}, u32[]{:S(2)}, u32[]{:S(2)}) collective-permute-start(f32[128,512]{1,0:T(8,128)S(1)} %get-tuple-element.161), channel_id=1, source_target_pairs={{0,2},{1,3},{2,0},{3,1},{4,6},{5,7},{6,4},{7,5},{8,10},{9,11},{10,... | collective-permute-start | bytes 786440 | tf_op jit(solution)/shard_map/ppermute | solution.py:498
  110.7 4.2 %shard_map.113 = (f32[4,128,512]{2,1,0:T(8,128)}, f32[32,16,128]{2,1,0:T(8,128)}, f32[4,128,512]{2,1,0:T(8,128)}) custom-call(s32[4]{0:T(128)S(1)} %pad_add_fusion.place, f32[4,128,512]{2,1,0:T(8,128)S(1)} %get-tuple-element.156.current, f32[4,128,512]{2,1,0:T(8,128)} %damping.1), custom_call_target="tpu_custom_call" | custom-call | flops 4000000 | bytes 3145728 | tf_op jit(solution)/shard_map/pallas_call | solution.py:429
  115.0 4.2 %shard_map.114 = (f32[128,128]{1,0:T(8,128)S(1)}, f32[128,128]{1,0:T(8,128)S(1)}, f32[128,128]{1,0:T(8,128)S(1)}, f32[128,128]{1,0:T(8,128)S(1)}, bf16[512,512]{...) custom-call(bf16[128,512]{1,0:T(8,128)(2,1)S(1)} %get-tuple-element.164.d0, ...), custom_call_target="tpu_custom_call" | custom-call | flops 2147483648 | bytes 5242880 | tf_op jit(solution)/shard_map/pallas_call | solution.py:452
  119.9 1.6 collective-permute-start.21
  121.6 3.6 %collective-permute-done.15.x2 = f32[128,512]{1,0:T(8,128)S(1)} collective-permute-done((f32[128,512]{1,0:T(8,128)S(1)}, f32[128,512]{1,0:T(8,128)S(1)}, u32[]{:S(2)}, u32[]{:S(2)}) %collective-permute-start.15) | collective-permute-done | bytes 262176 | tf_op jit(solution)/shard_map/ppermute | solution.py:498
  125.2 5.1 %shard_map.115 = (f32[128,512]{1,0:T(8,128)S(1)}, f32[128,512]{1,0:T(8,128)}, f32[128,512]{1,0:T(8,128)}, f32[128,512]{1,0:T(8,128)}) custom-call(s32[4]{0:T(128)S(1)} %pad_add_fusion.place, f32[128,512]{1,0:T(8,128)S(1)} %get-tuple-element.169.x0, f32[136,512]{1,0:T(8,128)S(1)} %collective-permute-done.14.x1.before, ...), custom_call_target="tpu_custom_call" | custom-call | flops 3221225472 | bytes 5242880 | tf_op jit(solution)/shard_map/pallas_call | solution.py:405
  130.7 1.4 collective-permute-start.23
  132.1 3.1 %collective-permute-start.24 = (f32[128,512]{1,0:T(8,128)}, f32[128,512]{1,0:T(8,128)S(1)}, u32[]{:S(2)}, u32[]{:S(2)}) collective-permute-start(f32[128,512]{1,0:T(8,128)} %get-tuple-element.182), channel_id=1, source_target_pairs={{0,2},{1,3},{2,0},{3,1},{4,6},{5,7},{6,4},{7,5},{8,10},{9,11},{10,... | collective-permute-start | bytes 786440 | tf_op jit(solution)/shard_map/ppermute | solution.py:498
  135.3 5.0 %all-to-all-start.3 = ((f32[32,16,128]{2,1,0:T(8,128)}), f32[32,16,128]{2,1,0:T(8,128)S(1)}, u32[]{:S(2)}, u32[]{:S(2)}) async-start(f32[32,16,128]{2,1,0:T(8,128)} %get-tuple-element.163), calls=%async_computation.3 | async-start | bytes 524288 | tf_op jit(solution)/shard_map/all_to_all | solution.py:512
  140.4 3.6 %shard_map.116 = (f32[4,128,512]{2,1,0:T(8,128)}, f32[4,128,512]{2,1,0:T(8,128)S(1)}, f32[128,512]{1,0:T(8,128)S(1)}, f32[128,512]{1,0:T(8,128)S(1)}) custom-call(s32[4]{0:T(128)S(1)} %pad_add_fusion.place, f32[4,128,512]{2,1,0:T(8,128)} %get-tuple-element.188.current, f32[136,512]{1,0:T(8,128)S(1)} %collective-permute-done.14.x1.before, ...), custom_call_target="tpu_custom_call" | custom-call | flops 8000000 | bytes 4194304 | tf_op jit(solution)/shard_map/pallas_call | solution.py:405
  144.0 1.3 collective-permute-done.24.rest_2_.p2
  145.3 1.6 shard_map.117
  146.9 1.2 all-to-all-done.3.scale
  148.1 5.0 %all-to-all-start.4 = ((f32[32,16,128]{2,1,0:T(8,128)}), f32[32,16,128]{2,1,0:T(8,128)S(1)}, u32[]{:S(2)}, u32[]{:S(2)}) async-start(f32[32,16,128]{2,1,0:T(8,128)} %get-tuple-element.195), calls=%async_computation.4 | async-start | bytes 524288 | tf_op jit(solution)/shard_map/all_to_all | solution.py:512
  153.2 4.3 %collective-permute-start.26 = (f32[128,512]{1,0:T(8,128)}, f32[128,512]{1,0:T(8,128)}, u32[]{:S(2)}, u32[]{:S(2)}) collective-permute-start(f32[128,512]{1,0:T(8,128)} %get-tuple-element.203), channel_id=1, source_target_pairs={{4,0},{8,4},{12,8},{16,12},{20,16},{24,20},{28,24},{32,28},{36,32}... | collective-permute-start | bytes 786440 | tf_op jit(solution)/shard_map/ppermute | solution.py:507
  157.5 3.5 %all-to-all-done.4.offset = f32[32,16,128]{2,1,0:T(8,128)S(1)} async-done(((f32[32,16,128]{2,1,0:T(8,128)}), f32[32,16,128]{2,1,0:T(8,128)S(1)}, u32[]{:S(2)}, u32[]{:S(2)}) %all-to-all-start.4) | async-done | bytes 262176 | tf_op jit(solution)/shard_map/all_to_all | solution.py:512
  161.7 5.0 %all-to-all-start.5 = ((f32[32,16,128]{2,1,0:T(8,128)}), f32[32,16,128]{2,1,0:T(8,128)S(1)}, u32[]{:S(2)}, u32[]{:S(2)}) async-start(f32[32,16,128]{2,1,0:T(8,128)} %shard_map.118), calls=%async_computation.5 | async-start | bytes 524288 | tf_op jit(solution)/shard_map/all_to_all | solution.py:512
  166.8 2.7 %shard_map.119 = (f32[4,128,512]{2,1,0:T(8,128)S(1)}, f32[4,128,512]{2,1,0:T(8,128)S(1)}, f32[4,128,512]{2,1,0:T(8,128)}) custom-call(s32[4]{0:T(128)S(1)} %pad_add_fusion.place, f32[128,512]{1,0:T(8,128)S(1)} %get-tuple-element.196.rest_0_.p0, f32[128,512]{1,0:T(8,128)S(1)} %collective-permute-done.23.rest_1_.p1, ...), custom_call_target="tpu_custom_call" | custom-call | flops 4000000 | bytes 4194304 | tf_op jit(solution)/shard_map/pallas_call | solution.py:405
  169.5 5.1 %all-to-all-done.5.entering = f32[32,16,128]{2,1,0:T(8,128)S(1)} async-done(((f32[32,16,128]{2,1,0:T(8,128)}), f32[32,16,128]{2,1,0:T(8,128)S(1)}, u32[]{:S(2)}, u32[]{:S(2)}) %all-to-all-start.5) | async-done | bytes 262176 | tf_op jit(solution)/shard_map/all_to_all | solution.py:512
  174.6 2.0 %shard_map.120 = f32[4,128,512]{2,1,0:T(8,128)} custom-call(f32[32,16,128]{2,1,0:T(8,128)S(1)} %all-to-all-done.5.entering, f32[4,128,512]{2,1,0:T(8,128)S(1)} %get-tuple-element.202.change, f32[128,512]{1,0:T(8,128)} %collective-permute-done.26.following, f32[4,128,512]{2,1,0:T(8,128)S(1)} %get-tuple-element.204.decay), custom_call_target="tpu_custom_call" | custom-call | flops 4000000 | bytes 5242880 | tf_op jit(solution)/shard_map/pallas_call | solution.py:405
  (50 shorter events, 14.7 us)
Async XLA Ops:
  7.2 51.4 %all-gather.2.cloned.1.call-start = ((), (), s32[]{:S(2)}) async-start(), calls=%async_computation.6 | async-start | bytes 4325376 | tf_op jit(solution)/shard_map/all_gather | solution.py:514
  8.9 9.8 %collective-permute-start.3 = (f32[128,512]{1,0:T(8,128)S(1)}, f32[128,512]{1,0:T(8,128)S(1)}, u32[]{:S(2)}, u32[]{:S(2)}) collective-permute-start(f32[128,512]{1,0:T(8,128)S(1)} %slice_bitcast_fusion), channel_id=1, source_target_pairs={{0,4},{4,8},{8,12},{12,16},{16,20},{20,24},{24,28},{28,32},{32,36}... | collective-permute-start | bytes 786440 | tf_op jit(solution)/shard_map/ppermute | solution.py:507
  11.8 33.1 %collective-permute-start.2 = (bf16[128,512]{1,0:T(8,128)(2,1)S(1)}, bf16[128,512]{1,0:T(8,128)(2,1)S(1)}, u32[]{:S(2)}, u32[]{:S(2)}) collective-permute-start(bf16[128,512]{1,0:T(8,128)(2,1)S(1)} %fusion.d0), channel_id=1, source_target_pairs={{0,3},{1,0},{2,1},{3,2},{4,7},{5,4},{6,5},{7,6},{8,11},{9,8},{10,9... | collective-permute-start | bytes 393224 | tf_op jit(solution)/shard_map/ppermute | solution.py:498
  15.9 29.0 %collective-permute-start.1 = (bf16[128,512]{1,0:T(8,128)(2,1)S(1)}, bf16[128,512]{1,0:T(8,128)(2,1)S(1)}, u32[]{:S(2)}, u32[]{:S(2)}) collective-permute-start(bf16[128,512]{1,0:T(8,128)(2,1)S(1)} %fusion.d0), channel_id=1, source_target_pairs={{0,2},{1,3},{2,0},{3,1},{4,6},{5,7},{6,4},{7,5},{8,10},{9,11},{10,... | collective-permute-start | bytes 393224 | tf_op jit(solution)/shard_map/ppermute | solution.py:498
  21.4 17.8 %collective-permute-start.5 = (f32[128,512]{1,0:T(8,128)S(1)}, f32[128,512]{1,0:T(8,128)S(1)}, u32[]{:S(2)}, u32[]{:S(2)}) collective-permute-start(f32[128,512]{1,0:T(8,128)S(1)} %get-tuple-element.113), channel_id=1, source_target_pairs={{0,2},{1,3},{2,0},{3,1},{4,6},{5,7},{6,4},{7,5},{8,10},{9,11},{10,... | collective-permute-start | bytes 786440 | tf_op jit(solution)/shard_map/ppermute | solution.py:498
  25.4 13.9 %collective-permute-start.4 = (f32[136,512]{1,0:T(8,128)S(1)}, f32[136,512]{1,0:T(8,128)S(1)}, u32[]{:S(2)}, u32[]{:S(2)}) collective-permute-start(f32[136,512]{1,0:T(8,128)S(1)} %get-tuple-element.112), channel_id=1, source_target_pairs={{0,1},{1,2},{2,3},{3,0},{4,5},{5,6},{6,7},{7,4},{8,9},{9,10},{10,1... | collective-permute-start | bytes 835592 | tf_op jit(solution)/shard_map/ppermute | solution.py:498
  26.4 12.9 %collective-permute-start.6 = (f32[136,512]{1,0:T(8,128)S(1)}, f32[136,512]{1,0:T(8,128)S(1)}, u32[]{:S(2)}, u32[]{:S(2)}) collective-permute-start(f32[136,512]{1,0:T(8,128)S(1)} %get-tuple-element.114), channel_id=1, source_target_pairs={{0,3},{1,0},{2,1},{3,2},{4,7},{5,4},{6,5},{7,6},{8,11},{9,8},{10,9... | collective-permute-start | bytes 835592 | tf_op jit(solution)/shard_map/ppermute | solution.py:498
  33.5 13.4 %all-to-all-start = ((f32[32,16,128]{2,1,0:T(8,128)}), f32[32,16,128]{2,1,0:T(8,128)S(1)}, u32[]{:S(2)}, u32[]{:S(2)}) async-start(f32[32,16,128]{2,1,0:T(8,128)} %get-tuple-element.110), calls=%async_computation | async-start | bytes 524288 | tf_op jit(solution)/shard_map/all_to_all | solution.py:512
  39.2 6.8 %collective-permute-start = (bf16[128,512]{1,0:T(8,128)(2,1)S(1)}, bf16[128,512]{1,0:T(8,128)(2,1)S(1)}, u32[]{:S(2)}, u32[]{:S(2)}) collective-permute-start(bf16[128,512]{1,0:T(8,128)(2,1)S(1)} %fusion.d0), channel_id=1, source_target_pairs={{0,1},{1,2},{2,3},{3,0},{4,5},{5,6},{6,7},{7,4},{8,9},{9,10},{10,1... | collective-permute-start | bytes 393224 | tf_op jit(solution)/shard_map/ppermute | solution.py:498
  49.0 17.1 %collective-permute-start.7 = (f32[128,512]{1,0:T(8,128)S(1)}, f32[128,512]{1,0:T(8,128)S(1)}, u32[]{:S(2)}, u32[]{:S(2)}) collective-permute-start(f32[128,512]{1,0:T(8,128)S(1)} %get-tuple-element.121), channel_id=1, source_target_pairs={{0,1},{1,2},{2,3},{3,0},{4,5},{5,6},{6,7},{7,4},{8,9},{9,10},{10,1... | collective-permute-start | bytes 786440 | tf_op jit(solution)/shard_map/ppermute | solution.py:498
  49.0 21.7 %collective-permute-start.8 = (f32[128,512]{1,0:T(8,128)S(1)}, f32[128,512]{1,0:T(8,128)S(1)}, u32[]{:S(2)}, u32[]{:S(2)}) collective-permute-start(f32[128,512]{1,0:T(8,128)S(1)} %get-tuple-element.122), channel_id=1, source_target_pairs={{0,2},{1,3},{2,0},{3,1},{4,6},{5,7},{6,4},{7,5},{8,10},{9,11},{10,... | collective-permute-start | bytes 786440 | tf_op jit(solution)/shard_map/ppermute | solution.py:498
  51.7 19.0 %collective-permute-start.9 = (f32[128,512]{1,0:T(8,128)S(1)}, f32[128,512]{1,0:T(8,128)S(1)}, u32[]{:S(2)}, u32[]{:S(2)}) collective-permute-start(f32[128,512]{1,0:T(8,128)S(1)} %get-tuple-element.123), channel_id=1, source_target_pairs={{0,3},{1,0},{2,1},{3,2},{4,7},{5,4},{6,5},{7,6},{8,11},{9,8},{10,9... | collective-permute-start | bytes 786440 | tf_op jit(solution)/shard_map/ppermute | solution.py:498
  62.8 8.0 %collective-permute-start.10 = (f32[128,128]{1,0:T(8,128)S(1)}, f32[128,128]{1,0:T(8,128)S(1)}, u32[]{:S(2)}, u32[]{:S(2)}) collective-permute-start(f32[128,128]{1,0:T(8,128)S(1)} %get-tuple-element.132), channel_id=1, source_target_pairs={{0,3},{1,0},{2,1},{3,2},{4,7},{5,4},{6,5},{7,6},{8,11},{9,8},{10,9... | collective-permute-start | bytes 196616 | tf_op jit(solution)/shard_map/ppermute | solution.py:498
  65.5 6.2 %collective-permute-start.11 = (f32[128,128]{1,0:T(8,128)S(1)}, f32[128,128]{1,0:T(8,128)S(1)}, u32[]{:S(2)}, u32[]{:S(2)}) collective-permute-start(f32[128,128]{1,0:T(8,128)S(1)} %get-tuple-element.133), channel_id=1, source_target_pairs={{0,2},{1,3},{2,0},{3,1},{4,6},{5,7},{6,4},{7,5},{8,10},{9,11},{10,... | collective-permute-start | bytes 196616 | tf_op jit(solution)/shard_map/ppermute | solution.py:498
  66.2 6.2 %collective-permute-start.12 = (f32[128,128]{1,0:T(8,128)S(1)}, f32[128,128]{1,0:T(8,128)S(1)}, u32[]{:S(2)}, u32[]{:S(2)}) collective-permute-start(f32[128,128]{1,0:T(8,128)S(1)} %get-tuple-element.134), channel_id=1, source_target_pairs={{0,1},{1,2},{2,3},{3,0},{4,5},{5,6},{6,7},{7,4},{8,9},{9,10},{10,1... | collective-permute-start | bytes 196616 | tf_op jit(solution)/shard_map/ppermute | solution.py:498
  70.7 3.3 %copy-start = (f32[128,512]{1,0:T(8,128)}, f32[128,512]{1,0:T(8,128)S(1)}, u32[]{:S(2)}) copy-start(f32[128,512]{1,0:T(8,128)S(1)} %collective-permute-done.9.rest_3_.p3) | copy-start | bytes 786436
  74.0 13.6 %all-to-all-start.1 = ((f32[32,16,128]{2,1,0:T(8,128)}), f32[32,16,128]{2,1,0:T(8,128)S(1)}, u32[]{:S(2)}, u32[]{:S(2)}) async-start(f32[32,16,128]{2,1,0:T(8,128)} %get-tuple-element.141), calls=%async_computation.1 | async-start | bytes 524288 | tf_op jit(solution)/shard_map/all_to_all | solution.py:512
  79.9 16.4 %collective-permute-start.13 = (f32[128,512]{1,0:T(8,128)}, f32[128,512]{1,0:T(8,128)}, u32[]{:S(2)}, u32[]{:S(2)}) collective-permute-start(f32[128,512]{1,0:T(8,128)} %get-tuple-element.149), channel_id=1, source_target_pairs={{4,0},{8,4},{12,8},{16,12},{20,16},{24,20},{28,24},{32,28},{36,32}... | collective-permute-start | bytes 786440 | tf_op jit(solution)/shard_map/ppermute | solution.py:507
  88.4 12.8 %all-to-all-start.2 = ((f32[32,16,128]{2,1,0:T(8,128)}), f32[32,16,128]{2,1,0:T(8,128)S(1)}, u32[]{:S(2)}, u32[]{:S(2)}) async-start(f32[32,16,128]{2,1,0:T(8,128)} %shard_map.110), calls=%async_computation.2 | async-start | bytes 524288 | tf_op jit(solution)/shard_map/all_to_all | solution.py:512
  93.4 1.0 copy-start.1
  102.5 6.4 %collective-permute-start.19 = (bf16[128,512]{1,0:T(8,128)(2,1)S(1)}, bf16[128,512]{1,0:T(8,128)(2,1)S(1)}, u32[]{:S(2)}, u32[]{:S(2)}) collective-permute-start(bf16[128,512]{1,0:T(8,128)(2,1)S(1)} %get-tuple-element.164.d0), channel_id=1, source_target_pairs={{0,3},{1,0},{2,1},{3,2},{4,7},{5,4},{6,5},{7,6},{8,11},{9,8},{10,9... | collective-permute-start | bytes 393224 | tf_op jit(solution)/shard_map/ppermute | solution.py:498
  103.2 11.8 %collective-permute-start.18 = (bf16[128,512]{1,0:T(8,128)(2,1)S(1)}, bf16[128,512]{1,0:T(8,128)(2,1)S(1)}, u32[]{:S(2)}, u32[]{:S(2)}) collective-permute-start(bf16[128,512]{1,0:T(8,128)(2,1)S(1)} %get-tuple-element.164.d0), channel_id=1, source_target_pairs={{0,2},{1,3},{2,0},{3,1},{4,6},{5,7},{6,4},{7,5},{8,10},{9,11},{10,... | collective-permute-start | bytes 393224 | tf_op jit(solution)/shard_map/ppermute | solution.py:498
  104.9 10.1 %collective-permute-start.17 = (bf16[128,512]{1,0:T(8,128)(2,1)S(1)}, bf16[128,512]{1,0:T(8,128)(2,1)S(1)}, u32[]{:S(2)}, u32[]{:S(2)}) collective-permute-start(bf16[128,512]{1,0:T(8,128)(2,1)S(1)} %get-tuple-element.164.d0), channel_id=1, source_target_pairs={{0,1},{1,2},{2,3},{3,0},{4,5},{5,6},{6,7},{7,4},{8,9},{9,10},{10,1... | collective-permute-start | bytes 393224 | tf_op jit(solution)/shard_map/ppermute | solution.py:498
  105.0 20.2 %collective-permute-start.14 = (f32[136,512]{1,0:T(8,128)S(1)}, f32[136,512]{1,0:T(8,128)S(1)}, u32[]{:S(2)}, u32[]{:S(2)}) collective-permute-start(f32[136,512]{1,0:T(8,128)S(1)} %get-tuple-element.160), channel_id=1, source_target_pairs={{0,1},{1,2},{2,3},{3,0},{4,5},{5,6},{6,7},{7,4},{8,9},{9,10},{10,1... | collective-permute-start | bytes 835592 | tf_op jit(solution)/shard_map/ppermute | solution.py:498
  106.7 18.5 %collective-permute-start.16 = (f32[136,512]{1,0:T(8,128)S(1)}, f32[136,512]{1,0:T(8,128)S(1)}, u32[]{:S(2)}, u32[]{:S(2)}) collective-permute-start(f32[136,512]{1,0:T(8,128)S(1)} %get-tuple-element.162), channel_id=1, source_target_pairs={{0,3},{1,0},{2,1},{3,2},{4,7},{5,4},{6,5},{7,6},{8,11},{9,8},{10,9... | collective-permute-start | bytes 835592 | tf_op jit(solution)/shard_map/ppermute | solution.py:498
  108.9 16.3 %collective-permute-start.15 = (f32[128,512]{1,0:T(8,128)S(1)}, f32[128,512]{1,0:T(8,128)S(1)}, u32[]{:S(2)}, u32[]{:S(2)}) collective-permute-start(f32[128,512]{1,0:T(8,128)S(1)} %get-tuple-element.161), channel_id=1, source_target_pairs={{0,2},{1,3},{2,0},{3,1},{4,6},{5,7},{6,4},{7,5},{8,10},{9,11},{10,... | collective-permute-start | bytes 786440 | tf_op jit(solution)/shard_map/ppermute | solution.py:498
  119.2 11.1 %collective-permute-start.20 = (f32[128,128]{1,0:T(8,128)S(1)}, f32[128,128]{1,0:T(8,128)S(1)}, u32[]{:S(2)}, u32[]{:S(2)}) collective-permute-start(f32[128,128]{1,0:T(8,128)S(1)} %get-tuple-element.166), channel_id=1, source_target_pairs={{0,3},{1,0},{2,1},{3,2},{4,7},{5,4},{6,5},{7,6},{8,11},{9,8},{10,9... | collective-permute-start | bytes 196616 | tf_op jit(solution)/shard_map/ppermute | solution.py:498
  119.9 10.4 %collective-permute-start.21 = (f32[128,128]{1,0:T(8,128)S(1)}, f32[128,128]{1,0:T(8,128)S(1)}, u32[]{:S(2)}, u32[]{:S(2)}) collective-permute-start(f32[128,128]{1,0:T(8,128)S(1)} %get-tuple-element.167), channel_id=1, source_target_pairs={{0,2},{1,3},{2,0},{3,1},{4,6},{5,7},{6,4},{7,5},{8,10},{9,11},{10,... | collective-permute-start | bytes 196616 | tf_op jit(solution)/shard_map/ppermute | solution.py:498
  125.2 5.5 %collective-permute-start.22 = (f32[128,128]{1,0:T(8,128)S(1)}, f32[128,128]{1,0:T(8,128)S(1)}, u32[]{:S(2)}, u32[]{:S(2)}) collective-permute-start(f32[128,128]{1,0:T(8,128)S(1)} %get-tuple-element.168), channel_id=1, source_target_pairs={{0,1},{1,2},{2,3},{3,0},{4,5},{5,6},{6,7},{7,4},{8,9},{9,10},{10,1... | collective-permute-start | bytes 196616 | tf_op jit(solution)/shard_map/ppermute | solution.py:498
  130.7 13.3 %collective-permute-start.23 = (f32[128,512]{1,0:T(8,128)}, f32[128,512]{1,0:T(8,128)S(1)}, u32[]{:S(2)}, u32[]{:S(2)}) collective-permute-start(f32[128,512]{1,0:T(8,128)} %get-tuple-element.181), channel_id=1, source_target_pairs={{0,1},{1,2},{2,3},{3,0},{4,5},{5,6},{6,7},{7,4},{8,9},{9,10},{10,1... | collective-permute-start | bytes 786440 | tf_op jit(solution)/shard_map/ppermute | solution.py:498
  132.1 13.2 %collective-permute-start.24 = (f32[128,512]{1,0:T(8,128)}, f32[128,512]{1,0:T(8,128)S(1)}, u32[]{:S(2)}, u32[]{:S(2)}) collective-permute-start(f32[128,512]{1,0:T(8,128)} %get-tuple-element.182), channel_id=1, source_target_pairs={{0,2},{1,3},{2,0},{3,1},{4,6},{5,7},{6,4},{7,5},{8,10},{9,11},{10,... | collective-permute-start | bytes 786440 | tf_op jit(solution)/shard_map/ppermute | solution.py:498
  135.1 10.2 %collective-permute-start.25 = (f32[128,512]{1,0:T(8,128)}, f32[128,512]{1,0:T(8,128)S(1)}, u32[]{:S(2)}, u32[]{:S(2)}) collective-permute-start(f32[128,512]{1,0:T(8,128)} %get-tuple-element.183), channel_id=1, source_target_pairs={{0,3},{1,0},{2,1},{3,2},{4,7},{5,4},{6,5},{7,6},{8,11},{9,8},{10,9... | collective-permute-start | bytes 786440 | tf_op jit(solution)/shard_map/ppermute | solution.py:498
  135.3 12.8 %all-to-all-start.3 = ((f32[32,16,128]{2,1,0:T(8,128)}), f32[32,16,128]{2,1,0:T(8,128)S(1)}, u32[]{:S(2)}, u32[]{:S(2)}) async-start(f32[32,16,128]{2,1,0:T(8,128)} %get-tuple-element.163), calls=%async_computation.3 | async-start | bytes 524288 | tf_op jit(solution)/shard_map/all_to_all | solution.py:512
  148.1 12.8 %all-to-all-start.4 = ((f32[32,16,128]{2,1,0:T(8,128)}), f32[32,16,128]{2,1,0:T(8,128)S(1)}, u32[]{:S(2)}, u32[]{:S(2)}) async-start(f32[32,16,128]{2,1,0:T(8,128)} %get-tuple-element.195), calls=%async_computation.4 | async-start | bytes 524288 | tf_op jit(solution)/shard_map/all_to_all | solution.py:512
  153.2 16.3 %collective-permute-start.26 = (f32[128,512]{1,0:T(8,128)}, f32[128,512]{1,0:T(8,128)}, u32[]{:S(2)}, u32[]{:S(2)}) collective-permute-start(f32[128,512]{1,0:T(8,128)} %get-tuple-element.203), channel_id=1, source_target_pairs={{4,0},{8,4},{12,8},{16,12},{20,16},{24,20},{28,24},{32,28},{36,32}... | collective-permute-start | bytes 786440 | tf_op jit(solution)/shard_map/ppermute | solution.py:507
  161.7 12.8 %all-to-all-start.5 = ((f32[32,16,128]{2,1,0:T(8,128)}), f32[32,16,128]{2,1,0:T(8,128)S(1)}, u32[]{:S(2)}, u32[]{:S(2)}) async-start(f32[32,16,128]{2,1,0:T(8,128)} %shard_map.118), calls=%async_computation.5 | async-start | bytes 524288 | tf_op jit(solution)/shard_map/all_to_all | solution.py:512
Sparse Core Ops, SparseCore 0:
  10.3 48.2 all-gather.1
